TPU v7x, 32 devices: a whole 2x2x4 slice. The times are simulated.
32 devices in a mesh: ctx: 16 (over z, y, core), mp: 2 (over x).
Axes of the slice: x: 2, y: 2, z: 4, core: 2. Of those that a mesh axis runs over, the one named last changes fastest.
Arguments:
- queries: bfloat16 [8192, 4096], P('ctx', 'mp'), may hold values from -15 to 15
- keys: bfloat16 [8192, 2048], P('ctx', 'mp'), may hold values from -15 to 15
- values: bfloat16 [8192, 2048], P('ctx', 'mp'), may hold values from -6 to 6
- grad_out: bfloat16 [8192, 4096], P(('ctx', 'mp')), may hold values from -6 to 6
- band_mask: int32 [64, 9], replicated, may hold values from 0 to 1, as said below
- segment_ids: int32 [8192], replicated, may hold values from 0 to 7, never falling along the last dimension, each value on 1 to 4096 neighbouring positions
Outputs:
- attn_out: bfloat16 [8192, 4096], P(('ctx', 'mp'))
- grad_queries: bfloat16 [8192, 4096], P('ctx', 'mp')
- grad_keys: bfloat16 [8192, 2048], P('ctx', 'mp')
- grad_values: bfloat16 [8192, 2048], P('ctx', 'mp')
Inputs may be any that keep to these rules, and one draw needn't show every extreme that they name: band_mask[b, o] is 1 when query block b may see the key block o blocks before it; offset 0 is always 1. `segment_ids`: segment numbers never fall along the sequence.
All inputs are finite; a program needn't handle non-finite values.
Results may differ from a plain program's by a relative error of at most 0.03.
Values may be sent and summed in bfloat16 or wider, within the bound.
No kernel may reach another device: no remote copies, remote signals or barrier semaphores. Data moves between devices by JAX's collectives and lax.ppermute only.
A program may use at most 128 MiB of HBM per device.

v0:
```python
import jax
import jax.numpy as jnp
from jax import lax
from jax.sharding import PartitionSpec as P

Q_HEADS = 32
KV_HEADS = 16
HEAD = 128
WINDOW = 1024
BLOCK = 128


ATTN_SCALE = 168.0 ** (-0.5)
NEG_FILL = -1e30


def shifted(block, axis, distance):
    devices = range(lax.axis_size(axis))
    route = [(i - distance, i) for i in devices if i - distance in devices]
    return lax.ppermute(block, axis, route)


def block_mask(seg_query, seg_key, band_row):
    rows_query = seg_query.shape[0]
    width_keys = seg_key.shape[0]
    distance = WINDOW + jnp.arange(rows_query)[:, None] - jnp.arange(width_keys)[None, :]
    allowed = jnp.repeat(band_row[::-1], BLOCK)
    return (
        (distance >= 0)
        & (distance < WINDOW)
        & (seg_query[:, None] == seg_key[None, :])
        & (allowed[None, :] == 1)
    )


def masked_scores(query_blk, key_slab, valid):
    scores = (
        jnp.einsum("qkgd,skd->kgqs", query_blk, key_slab, preferred_element_type=jnp.float32)
        * ATTN_SCALE
    )
    return jnp.where(valid, scores, NEG_FILL)


def rows_for(reach, local_rows):
    first_row = max(WINDOW - reach * local_rows, 0)
    return WINDOW - (reach - 1) * local_rows - first_row


def body(queries, keys, values, grad_out, band_mask, segment_ids):
    local_rows = queries.shape[0]
    kv_local = keys.shape[1] // HEAD
    q_per_kv = Q_HEADS // KV_HEADS
    span_keys = WINDOW + BLOCK
    block_count = local_rows // BLOCK
    hop_total = (WINDOW + local_rows - 1) // local_rows
    position = lax.axis_index("ctx")
    stacked = jnp.stack([keys, values])
    portions = []
    for reach in range(hop_total, 0, -1):
        needed = rows_for(reach, local_rows)
        received = shifted(stacked, "ctx", reach)
        portions.append(received)
    extended = jnp.concatenate(portions + [stacked], axis=1)
    key_ext = extended[0].reshape(WINDOW + local_rows, kv_local, HEAD)
    value_ext = extended[1].reshape(WINDOW + local_rows, kv_local, HEAD)
    seg_padded = jnp.concatenate([jnp.full((WINDOW,), -1, jnp.int32), segment_ids])
    seg_ext = lax.dynamic_slice_in_dim(seg_padded, position * local_rows, WINDOW + local_rows, 0)
    seg_local = lax.dynamic_slice_in_dim(segment_ids, position * local_rows, local_rows, 0)
    band_local = lax.dynamic_slice_in_dim(band_mask, position * block_count, block_count, 0)
    grad_heads = lax.all_to_all(grad_out, "mp", split_axis=1, concat_axis=0, tiled=True)

    def block_inputs(block_idx):
        start = block_idx * BLOCK
        query_blk = lax.dynamic_slice_in_dim(queries, start, BLOCK, 0).reshape(
            BLOCK, kv_local, q_per_kv, HEAD
        )
        key_slab = lax.dynamic_slice_in_dim(key_ext, start, span_keys, 0)
        value_slab = lax.dynamic_slice_in_dim(value_ext, start, span_keys, 0)
        seg_query = lax.dynamic_slice_in_dim(seg_local, start, BLOCK, 0)
        seg_key = lax.dynamic_slice_in_dim(seg_ext, start, span_keys, 0)
        band_row = lax.dynamic_index_in_dim(band_local, block_idx, 0, keepdims=False)
        return (query_blk, key_slab, value_slab, block_mask(seg_query, seg_key, band_row))

    def forward_step(carry, block_idx):
        query_blk, key_slab, value_slab, valid = block_inputs(block_idx)
        scores = masked_scores(query_blk, key_slab, valid)
        row_max = jnp.max(scores, axis=-1, keepdims=True)
        log_norm = row_max + jnp.log(jnp.sum(jnp.exp(scores - row_max), axis=-1, keepdims=True))
        prob_bf = jnp.exp(scores - log_norm).astype(jnp.bfloat16)
        attended = jnp.einsum(
            "kgqs,skd->qkgd", prob_bf, value_slab, preferred_element_type=jnp.float32
        ).astype(jnp.bfloat16)
        attended = attended.reshape(BLOCK, kv_local * q_per_kv * HEAD)
        return (carry, (attended, log_norm))

    block_ids = jnp.arange(block_count, dtype=jnp.int32)
    unused, saved = lax.scan(forward_step, jnp.int32(0), block_ids)
    attn_out = lax.all_to_all(
        saved[0].reshape(local_rows, -1), "mp", split_axis=0, concat_axis=1, tiled=True
    )

    def backward_step(carry, inputs):
        key_grad, value_grad = carry
        block_idx = inputs[0]
        query_blk, key_slab, value_slab, valid = block_inputs(block_idx)
        prob_bf = jnp.exp(masked_scores(query_blk, key_slab, valid) - inputs[2]).astype(
            jnp.bfloat16
        )
        start = block_idx * BLOCK
        grad_blk = lax.dynamic_slice_in_dim(grad_heads, start, BLOCK, 0).reshape(
            BLOCK, kv_local, q_per_kv, HEAD
        )
        attended_blk = inputs[1].reshape(BLOCK, kv_local, q_per_kv, HEAD)
        delta = jnp.sum(
            grad_blk.astype(jnp.float32) * attended_blk.astype(jnp.float32), axis=-1
        ).transpose(1, 2, 0)[..., None]
        value_part = jnp.einsum(
            "kgqs,qkgd->skd", prob_bf, grad_blk, preferred_element_type=jnp.float32
        )
        grad_prob = jnp.einsum(
            "qkgd,skd->kgqs", grad_blk, value_slab, preferred_element_type=jnp.float32
        )
        grad_score = (prob_bf.astype(jnp.float32) * (grad_prob - delta)).astype(jnp.bfloat16)
        grad_query = (
            jnp.einsum("kgqs,skd->qkgd", grad_score, key_slab, preferred_element_type=jnp.float32)
            * ATTN_SCALE
        )
        grad_query = grad_query.astype(jnp.bfloat16).reshape(BLOCK, kv_local * q_per_kv * HEAD)
        key_part = (
            jnp.einsum("kgqs,qkgd->skd", grad_score, query_blk, preferred_element_type=jnp.float32)
            * ATTN_SCALE
        )
        key_grad = lax.dynamic_update_slice_in_dim(
            key_grad, lax.dynamic_slice_in_dim(key_grad, start, span_keys, 0) + key_part, start, 0
        )
        value_grad = lax.dynamic_update_slice_in_dim(
            value_grad,
            lax.dynamic_slice_in_dim(value_grad, start, span_keys, 0) + value_part,
            start,
            0,
        )
        return ((key_grad, value_grad), grad_query)

    zeros = jnp.zeros((WINDOW + local_rows, kv_local, HEAD), jnp.float32)
    (key_grad, value_grad), grad_blocks = lax.scan(
        backward_step, (zeros, zeros), (block_ids,) + tuple(saved)
    )
    grad_queries = grad_blocks.reshape(local_rows, -1)
    both_grads = jnp.stack([key_grad, value_grad])
    owned = both_grads[:, WINDOW:]
    for reach in range(1, hop_total + 1):
        first_row = max(WINDOW - reach * local_rows, 0)
        last_row = WINDOW - (reach - 1) * local_rows
        needed = last_row - first_row
        returned = shifted(both_grads[:, first_row:last_row], "ctx", -reach)
        owned = owned.at[:, local_rows - needed :].add(returned)
    grad_keys = owned[0].reshape(local_rows, -1).astype(jnp.bfloat16)
    grad_values = owned[1].reshape(local_rows, -1).astype(jnp.bfloat16)
    return (attn_out, grad_queries, grad_keys, grad_values)


def solution(mesh):
    placed = (P("ctx", "mp"), P("ctx", "mp"), P("ctx", "mp"), P(("ctx", "mp"), None), P(), P())
    return jax.shard_map(
        body,
        mesh=mesh,
        in_specs=placed,
        out_specs=(P(("ctx", "mp"), None), P("ctx", "mp"), P("ctx", "mp"), P("ctx", "mp")),
        check_vma=False,
    )
```

profile of v0, /device:TPU:0, one launch (start us, length us, event | category | flops | bytes accessed | tf_op | source)
XLA Modules:
  0.0 439.8 jit_solution(13336724967211372958)
XLA Ops:
  0.6 1.5 copy.99
  2.2 1.5 copy.100
  3.7 1.7 pad_maximum_fusion.1
  5.3 6.2 %collective-permute-start = (bf16[2,512,1024]{1,2,0:T(8,128)(2,1)}, bf16[2,512,1024]{1,2,0:T(8,128)(2,1)}, u32[]{:S(2)}, u32[]{:S(2)}) collective-permute-start(bf16[2,512,1024]{1,2,0:T(8,128)(2,1)} %pad_maximum_fusion.1), channel_id=1, source_target_pairs={{0,4},{2,6},{4,8},{6,10},{8,12},{10,14},{12,16},{14,18},{16,20},{1... | collective-permute-start | bytes 6291464 | tf_op jit(solution)/shard_map/ppermute | solution.py:20
  11.6 2.8 collective-permute-start.1
  14.3 4.1 copy.106
  18.4 5.0 %all-to-all-start.1 = ((bf16[256,2,2048]{0,2,1:T(8,128)(2,1)}), bf16[256,2,2048]{0,2,1:T(8,128)(2,1)}, u32[]{:S(2)}, u32[]{:S(2)}) async-start(bf16[256,2,2048]{0,2,1:T(8,128)(2,1)} %bitcast.205), calls=%async_computation.1 | async-start | bytes 4194304 | tf_op jit(solution)/shard_map/all_to_all | solution.py:70
  23.6 2.9 copy.103
  26.7 21.5 %all-to-all-done.1 = bf16[256,2,2048]{0,2,1:T(8,128)(2,1)} async-done(((bf16[256,2,2048]{0,2,1:T(8,128)(2,1)}), bf16[256,2,2048]{0,2,1:T(8,128)(2,1)}, u32[]{:S(2)}, u32[]{:S(2)}) %all-to-all-start.1) | async-done | bytes 2097184 | tf_op jit(solution)/shard_map/all_to_all | solution.py:70
  48.2 4.0 copy.107
  52.2 4.3 collective-permute-done
  56.5 3.3 maximum_maximum_fusion
  59.8 3.0 fusion.53
  62.9 4.6 %copy.102 = bf16[1536,8,128]{2,0,1:T(8,128)(2,1)} copy(bf16[1536,8,128]{0,2,1:T(8,128)(2,1)} %bitcast.199) | data formatting | bytes 6291456 | tf_op jit(solution)/shard_map/while | solution.py:97
  67.5 52.8 %while.30 = (s32[]{:T(128)}, bf16[4,128,2048]{1,2,0:T(8,128)(2,1)}, f32[4,8,2,128,1]{3,2,1,4,0:T(2,128)S(1)}, s32[4]{0:T(128)S(1)}, bf16[1536,8,128]{0,2,1:T(8,1...) while((s32[]{:T(128)}, bf16[4,128,2048]{1,2,0:T(8,128)(2,1)}, ...), condition=%wide.region_3.4_spmd, body=%wide.region_0.3_spmd.sunk | while | flops 1225767040 | bytes 36556012 | solution.py:97
  72.0 3.1 fusion.91
  75.1 1.2 exponential_reduce_fusion.2
  76.4 3.5 fusion.92
  85.2 3.1 fusion.91
  88.3 1.2 exponential_reduce_fusion.2
  89.6 3.5 fusion.92
  98.4 3.1 fusion.91
  101.5 1.2 exponential_reduce_fusion.2
  102.8 3.5 fusion.92
  111.6 3.1 fusion.91
  114.7 1.2 exponential_reduce_fusion.2
  116.0 3.5 fusion.92
  120.3 3.5 broadcast_in_dim.48
  123.8 3.4 broadcast_in_dim.48.clone
  127.2 135.3 %while.31 = (s32[]{:T(128)}, f32[1536,8,128]{0,2,1:T(8,128)}, f32[1536,8,128]{0,2,1:T(8,128)}, bf16[4,128,2048]{2,1,0:T(8,128)(2,1)}, s32[4]{0:T(128)S(1)}, /*in...) while((s32[]{:T(128)}, f32[1536,8,128]{0,2,1:T(8,128)}, ...), condition=%wide.region_6.7_spmd, body=%wide.region_4.6_spmd.sunk | while | flops 3044915200 | bytes 125398432 | solution.py:145
  131.8 6.1 %fusion.105 = bf16[8,2,128,1152]{2,3,1,0:T(8,128)(2,1)} fusion(bf16[128,8,2,128]{0,3,2,1:T(8,128)(2,1)S(1)} %bitcast.193, f32[8,2,128]{2,1,0:T(2,128)S(1)} %dynamic-slice_bitcast_fusion.2, pred[128,1152]{0,1:T(8,128)(4,1)S(1)} %fusion.104, bf16[1536,8,128]{2,0,1:T(8,128)(2,1)} %get-tuple-element.617, s32[]{:T(128)S(6)} %select_n.68), kind=kOutput, calls=%fused_computation.33.clone.1 | convolution fusion | flops 613416960 | bytes 7757828 | tf_op jit(solution)/shard_map/while/body/eval_jaxpr/qkgd,skd->kgqs/dot_general | solution.py:38
  139.3 1.1 constant_dynamic-slice_fusion.14
  140.6 5.1 %fusion.107 = bf16[8,2,128,1152]{2,3,1,0:T(8,128)(2,1)S(1)} fusion(bf16[8,2,128,1152]{2,3,1,0:T(8,128)(2,1)} %fusion.105, bf16[128,8,2,128]{0,3,2,1:T(8,128)(2,1)S(1)} %bitcast.185, f32[8,2,128]{2,1,0:T(2,128)S(1)} %bitcast.211, bf16[1536,8,128]{0,2,1:T(8,128)(2,1)} %get-tuple-element.619, s32[]{:T(128)S(6)} %select_n.68), kind=kOutput, calls=%fused_computation.29.clone.1 | convolution fusion | flops 613416960 | bytes 12328964 | tf_op jit(solution)/shard_map/while/body/eval_jaxpr/qkgd,skd->kgqs/dot_general | solution.py:120
  145.7 2.1 fusion.108
  147.8 4.5 %fusion.110 = bf16[8,128,2,128]{3,1,2,0:T(8,128)(2,1)S(1)} fusion(bf16[8,2,128,1152]{2,3,1,0:T(8,128)(2,1)S(1)} %fusion.107, bf16[1536,8,128]{2,0,1:T(8,128)(2,1)} %get-tuple-element.617, s32[]{:T(128)S(6)} %select_n.68), kind=kOutput, calls=%fused_computation.47.clone.1 | convolution fusion | flops 604504064 | bytes 7602180 | tf_op jit(solution)/shard_map/while/body/eval_jaxpr/kgqs,skd->qkgd/dot_general | solution.py:125
  153.3 7.6 %fusion.109 = f32[1536,8,128]{0,2,1:T(8,128)} fusion(f32[1536,8,128]{0,2,1:T(8,128)} %get-tuple-element.590, s32[]{:T(128)S(6)} %select_n.68, bf16[128,8,2,128]{0,3,2,1:T(8,128)(2,1)S(1)} %bitcast.186, bf16[8,2,128,1152]{2,3,1,0:T(8,128)(2,1)} %fusion.105), kind=kOutput, calls=%fused_computation.35.clone.1 | convolution fusion | flops 605159424 | bytes 14680068 | tf_op jit(solution)/shard_map/while/body/eval_jaxpr/kgqs,qkgd->skd/dot_general | solution.py:117
  165.6 6.1 %fusion.105 = bf16[8,2,128,1152]{2,3,1,0:T(8,128)(2,1)} fusion(bf16[128,8,2,128]{0,3,2,1:T(8,128)(2,1)S(1)} %bitcast.193, f32[8,2,128]{2,1,0:T(2,128)S(1)} %dynamic-slice_bitcast_fusion.2, pred[128,1152]{0,1:T(8,128)(4,1)S(1)} %fusion.104, bf16[1536,8,128]{2,0,1:T(8,128)(2,1)} %get-tuple-element.617, s32[]{:T(128)S(6)} %select_n.68), kind=kOutput, calls=%fused_computation.33.clone.1 | convolution fusion | flops 613416960 | bytes 7757828 | tf_op jit(solution)/shard_map/while/body/eval_jaxpr/qkgd,skd->kgqs/dot_general | solution.py:38
  173.1 1.1 constant_dynamic-slice_fusion.14
  174.4 5.1 %fusion.107 = bf16[8,2,128,1152]{2,3,1,0:T(8,128)(2,1)S(1)} fusion(bf16[8,2,128,1152]{2,3,1,0:T(8,128)(2,1)} %fusion.105, bf16[128,8,2,128]{0,3,2,1:T(8,128)(2,1)S(1)} %bitcast.185, f32[8,2,128]{2,1,0:T(2,128)S(1)} %bitcast.211, bf16[1536,8,128]{0,2,1:T(8,128)(2,1)} %get-tuple-element.619, s32[]{:T(128)S(6)} %select_n.68), kind=kOutput, calls=%fused_computation.29.clone.1 | convolution fusion | flops 613416960 | bytes 12328964 | tf_op jit(solution)/shard_map/while/body/eval_jaxpr/qkgd,skd->kgqs/dot_general | solution.py:120
  179.5 2.2 fusion.108
  181.6 4.5 %fusion.110 = bf16[8,128,2,128]{3,1,2,0:T(8,128)(2,1)S(1)} fusion(bf16[8,2,128,1152]{2,3,1,0:T(8,128)(2,1)S(1)} %fusion.107, bf16[1536,8,128]{2,0,1:T(8,128)(2,1)} %get-tuple-element.617, s32[]{:T(128)S(6)} %select_n.68), kind=kOutput, calls=%fused_computation.47.clone.1 | convolution fusion | flops 604504064 | bytes 7602180 | tf_op jit(solution)/shard_map/while/body/eval_jaxpr/kgqs,skd->qkgd/dot_general | solution.py:125
  187.2 7.6 %fusion.109 = f32[1536,8,128]{0,2,1:T(8,128)} fusion(f32[1536,8,128]{0,2,1:T(8,128)} %get-tuple-element.590, s32[]{:T(128)S(6)} %select_n.68, bf16[128,8,2,128]{0,3,2,1:T(8,128)(2,1)S(1)} %bitcast.186, bf16[8,2,128,1152]{2,3,1,0:T(8,128)(2,1)} %fusion.105), kind=kOutput, calls=%fused_computation.35.clone.1 | convolution fusion | flops 605159424 | bytes 14680068 | tf_op jit(solution)/shard_map/while/body/eval_jaxpr/kgqs,qkgd->skd/dot_general | solution.py:117
  199.4 6.1 %fusion.105 = bf16[8,2,128,1152]{2,3,1,0:T(8,128)(2,1)} fusion(bf16[128,8,2,128]{0,3,2,1:T(8,128)(2,1)S(1)} %bitcast.193, f32[8,2,128]{2,1,0:T(2,128)S(1)} %dynamic-slice_bitcast_fusion.2, pred[128,1152]{0,1:T(8,128)(4,1)S(1)} %fusion.104, bf16[1536,8,128]{2,0,1:T(8,128)(2,1)} %get-tuple-element.617, s32[]{:T(128)S(6)} %select_n.68), kind=kOutput, calls=%fused_computation.33.clone.1 | convolution fusion | flops 613416960 | bytes 7757828 | tf_op jit(solution)/shard_map/while/body/eval_jaxpr/qkgd,skd->kgqs/dot_general | solution.py:38
  206.9 1.1 constant_dynamic-slice_fusion.14
  208.2 5.1 %fusion.107 = bf16[8,2,128,1152]{2,3,1,0:T(8,128)(2,1)S(1)} fusion(bf16[8,2,128,1152]{2,3,1,0:T(8,128)(2,1)} %fusion.105, bf16[128,8,2,128]{0,3,2,1:T(8,128)(2,1)S(1)} %bitcast.185, f32[8,2,128]{2,1,0:T(2,128)S(1)} %bitcast.211, bf16[1536,8,128]{0,2,1:T(8,128)(2,1)} %get-tuple-element.619, s32[]{:T(128)S(6)} %select_n.68), kind=kOutput, calls=%fused_computation.29.clone.1 | convolution fusion | flops 613416960 | bytes 12328964 | tf_op jit(solution)/shard_map/while/body/eval_jaxpr/qkgd,skd->kgqs/dot_general | solution.py:120
  213.3 2.2 fusion.108
  215.5 4.5 %fusion.110 = bf16[8,128,2,128]{3,1,2,0:T(8,128)(2,1)S(1)} fusion(bf16[8,2,128,1152]{2,3,1,0:T(8,128)(2,1)S(1)} %fusion.107, bf16[1536,8,128]{2,0,1:T(8,128)(2,1)} %get-tuple-element.617, s32[]{:T(128)S(6)} %select_n.68), kind=kOutput, calls=%fused_computation.47.clone.1 | convolution fusion | flops 604504064 | bytes 7602180 | tf_op jit(solution)/shard_map/while/body/eval_jaxpr/kgqs,skd->qkgd/dot_general | solution.py:125
  221.1 7.6 %fusion.109 = f32[1536,8,128]{0,2,1:T(8,128)} fusion(f32[1536,8,128]{0,2,1:T(8,128)} %get-tuple-element.590, s32[]{:T(128)S(6)} %select_n.68, bf16[128,8,2,128]{0,3,2,1:T(8,128)(2,1)S(1)} %bitcast.186, bf16[8,2,128,1152]{2,3,1,0:T(8,128)(2,1)} %fusion.105), kind=kOutput, calls=%fused_computation.35.clone.1 | convolution fusion | flops 605159424 | bytes 14680068 | tf_op jit(solution)/shard_map/while/body/eval_jaxpr/kgqs,qkgd->skd/dot_general | solution.py:117
  233.3 6.1 %fusion.105 = bf16[8,2,128,1152]{2,3,1,0:T(8,128)(2,1)} fusion(bf16[128,8,2,128]{0,3,2,1:T(8,128)(2,1)S(1)} %bitcast.193, f32[8,2,128]{2,1,0:T(2,128)S(1)} %dynamic-slice_bitcast_fusion.2, pred[128,1152]{0,1:T(8,128)(4,1)S(1)} %fusion.104, bf16[1536,8,128]{2,0,1:T(8,128)(2,1)} %get-tuple-element.617, s32[]{:T(128)S(6)} %select_n.68), kind=kOutput, calls=%fused_computation.33.clone.1 | convolution fusion | flops 613416960 | bytes 7757828 | tf_op jit(solution)/shard_map/while/body/eval_jaxpr/qkgd,skd->kgqs/dot_general | solution.py:38
  242.1 5.1 %fusion.107 = bf16[8,2,128,1152]{2,3,1,0:T(8,128)(2,1)S(1)} fusion(bf16[8,2,128,1152]{2,3,1,0:T(8,128)(2,1)} %fusion.105, bf16[128,8,2,128]{0,3,2,1:T(8,128)(2,1)S(1)} %bitcast.185, f32[8,2,128]{2,1,0:T(2,128)S(1)} %bitcast.211, bf16[1536,8,128]{0,2,1:T(8,128)(2,1)} %get-tuple-element.619, s32[]{:T(128)S(6)} %select_n.68), kind=kOutput, calls=%fused_computation.29.clone.1 | convolution fusion | flops 613416960 | bytes 12328964 | tf_op jit(solution)/shard_map/while/body/eval_jaxpr/qkgd,skd->kgqs/dot_general | solution.py:120
  247.2 2.2 fusion.108
  249.3 4.5 %fusion.110 = bf16[8,128,2,128]{3,1,2,0:T(8,128)(2,1)S(1)} fusion(bf16[8,2,128,1152]{2,3,1,0:T(8,128)(2,1)S(1)} %fusion.107, bf16[1536,8,128]{2,0,1:T(8,128)(2,1)} %get-tuple-element.617, s32[]{:T(128)S(6)} %select_n.68), kind=kOutput, calls=%fused_computation.47.clone.1 | convolution fusion | flops 604504064 | bytes 7602180 | tf_op jit(solution)/shard_map/while/body/eval_jaxpr/kgqs,skd->qkgd/dot_general | solution.py:125
  254.9 7.6 %fusion.109 = f32[1536,8,128]{0,2,1:T(8,128)} fusion(f32[1536,8,128]{0,2,1:T(8,128)} %get-tuple-element.590, s32[]{:T(128)S(6)} %select_n.68, bf16[128,8,2,128]{0,3,2,1:T(8,128)(2,1)S(1)} %bitcast.186, bf16[8,2,128,1152]{2,3,1,0:T(8,128)(2,1)} %fusion.105), kind=kOutput, calls=%fused_computation.35.clone.1 | convolution fusion | flops 605159424 | bytes 14680068 | tf_op jit(solution)/shard_map/while/body/eval_jaxpr/kgqs,qkgd->skd/dot_general | solution.py:117
  262.5 6.2 %fusion.47 = (f32[2,512,8,128]{1,3,2,0:T(8,128)}, f32[2,512,8,128]{1,3,2,0:T(8,128)}) fusion(f32[1,1536,8,128]{1,3,2,0:T(8,128)} %bitcast.189, f32[1,1536,8,128]{1,3,2,0:T(8,128)} %bitcast.191), kind=kLoop, calls=%fused_computation.74 | loop fusion | flops 2097152 | bytes 20971520 | tf_op jit(solution)/shard_map/stack | solution.py:149
  268.7 1.3 collective-permute-start.2
  270.0 1.3 collective-permute-start.3
  271.3 2.6 copy.104
  273.9 18.8 %all_to_all.38 = bf16[2,256,2048]{2,1,0:T(8,128)(2,1)S(1)} all-to-all(bf16[2,256,2048]{2,1,0:T(8,128)(2,1)} %bitcast.206), channel_id=1, replica_groups=mesh['ctx'=16,'mp'=2] {'mp'}, dimensions={0} | all-to-all | bytes 4194304 | tf_op jit(solution)/shard_map/all_to_all | solution.py:98
  292.7 2.5 copy.105
  295.2 4.1 copy.115
  299.3 131.8 %collective-permute-done.3 = f32[2,512,8,128]{1,3,2,0:T(8,128)} collective-permute-done((f32[2,512,8,128]{1,3,2,0:T(8,128)}, f32[2,512,8,128]{1,3,2,0:T(8,128)}, u32[]{:S(2)}, u32[]{:S(2)}) %collective-permute-start.3) | collective-permute-done | bytes 4194336 | tf_op jit(solution)/shard_map/ppermute | solution.py:20
  431.1 5.9 %fusion.51 = bf16[2,512,8,128]{1,3,2,0:T(8,128)(2,1)S(1)} fusion(f32[2,512,8,128]{1,3,2,0:T(8,128)} %collective-permute-done.3, f32[2,512,8,128]{1,3,2,0:T(8,128)} %collective-permute-done.2, f32[1,1536,8,128]{1,3,2,0:T(8,128)} %bitcast.190, f32[1,1536,8,128]{1,3,2,0:T(8,128)} %bitcast.192), kind=kLoop, calls=%fused_computation.78 | loop fusion | flops 4194304 | bytes 23068672 | tf_op jit(solution)/shard_map/convert.2
  437.2 1.3 copy.132
  438.5 1.3 copy.133
  (179 shorter events, 30.6 us)
Async XLA Ops:
  0.6 22.8 %copy-start = (s32[64,9]{0,1:T(8,128)S(1)}, s32[64,9]{0,1:T(8,128)}, u32[]{:S(2)}) copy-start(s32[64,9]{0,1:T(8,128)} %param.22) | copy-start | bytes 6916
  3.7 14.8 %copy-start.6 = (bf16[512,1024]{0,1:T(8,128)(2,1)}, bf16[512,1024]{0,1:T(8,128)(2,1)S(1)}, u32[]{:S(2)}) copy-start(bf16[512,1024]{0,1:T(8,128)(2,1)S(1)} %copy.100) | copy-start | bytes 3145732
  5.3 51.2 %collective-permute-start = (bf16[2,512,1024]{1,2,0:T(8,128)(2,1)}, bf16[2,512,1024]{1,2,0:T(8,128)(2,1)}, u32[]{:S(2)}, u32[]{:S(2)}) collective-permute-start(bf16[2,512,1024]{1,2,0:T(8,128)(2,1)} %pad_maximum_fusion.1), channel_id=1, source_target_pairs={{0,4},{2,6},{4,8},{6,10},{8,12},{10,14},{12,16},{14,18},{16,20},{1... | collective-permute-start | bytes 6291464 | tf_op jit(solution)/shard_map/ppermute | solution.py:20
  11.6 45.0 %collective-permute-start.1 = (bf16[2,512,1024]{1,2,0:T(8,128)(2,1)}, bf16[2,512,1024]{1,2,0:T(8,128)(2,1)}, u32[]{:S(2)}, u32[]{:S(2)}) collective-permute-start(bf16[2,512,1024]{1,2,0:T(8,128)(2,1)} %pad_maximum_fusion.1), channel_id=1, source_target_pairs={{0,2},{2,4},{4,6},{6,8},{8,10},{10,12},{12,14},{14,16},{16,18},{18... | collective-permute-start | bytes 6291464 | tf_op jit(solution)/shard_map/ppermute | solution.py:20
  18.4 8.1 %copy-start.7 = (s32[8192]{0:T(1024)S(1)}, s32[8192]{0:T(1024)}, u32[]{:S(2)}) copy-start(s32[8192]{0:T(1024)} %param.23) | copy-start | bytes 98308
  18.4 29.8 %all-to-all-start.1 = ((bf16[256,2,2048]{0,2,1:T(8,128)(2,1)}), bf16[256,2,2048]{0,2,1:T(8,128)(2,1)}, u32[]{:S(2)}, u32[]{:S(2)}) async-start(bf16[256,2,2048]{0,2,1:T(8,128)(2,1)} %bitcast.205), calls=%async_computation.1 | async-start | bytes 4194304 | tf_op jit(solution)/shard_map/all_to_all | solution.py:70
  127.2 10.8 %copy-start.3 = (bf16[512,2048]{0,1:T(8,128)(2,1)}, bf16[512,2048]{0,1:T(8,128)(2,1)S(1)}, u32[]{:S(2)}) copy-start(bf16[512,2048]{0,1:T(8,128)(2,1)S(1)} %get-tuple-element.613) | copy-start | bytes 6291460 | tf_op jit(solution)/shard_map/while
  140.4 5.3 %slice-start = ((s8[6291456]{0:T(1024)(128)(4,1)}), s8[4194304]{0:T(1024)(128)(4,1)S(1)}, s32[]{:S(2)}) async-start(s8[6291456]{0:T(1024)(128)(4,1)} %bitcast.187), calls=%async_computation.2 | async-start | bytes 8388608 | tf_op jit(solution)/shard_map/while
  140.6 5.1 %slice-start.1 = ((s8[6291456]{0:T(1024)(128)(4,1)}), s8[2097152]{0:T(1024)(128)(4,1)S(1)}, s32[]{:S(2)}) async-start(s8[6291456]{0:T(1024)(128)(4,1)} %bitcast.187), calls=%async_computation.3 | async-start | bytes 4194304 | tf_op jit(solution)/shard_map/while
  147.8 4.5 %copy-start.2 = (f32[1536,8,128]{0,2,1:T(8,128)}, f32[1536,8,128]{0,2,1:T(8,128)S(1)}, u32[]{:S(2)}) copy-start(f32[1536,8,128]{0,2,1:T(8,128)S(1)} %fusion.108) | copy-start | bytes 18874372 | tf_op jit(solution)/shard_map/while
  153.3 7.6 %copy-start.4 = (bf16[512,2048]{0,1:T(8,128)(2,1)S(1)}, bf16[512,2048]{0,1:T(8,128)(2,1)}, u32[]{:S(2)}) copy-start(bf16[512,2048]{0,1:T(8,128)(2,1)} %copy-done.3) | copy-start | bytes 6291460 | tf_op jit(solution)/shard_map/while
  161.0 10.8 %copy-start.3 = (bf16[512,2048]{0,1:T(8,128)(2,1)}, bf16[512,2048]{0,1:T(8,128)(2,1)S(1)}, u32[]{:S(2)}) copy-start(bf16[512,2048]{0,1:T(8,128)(2,1)S(1)} %get-tuple-element.613) | copy-start | bytes 6291460 | tf_op jit(solution)/shard_map/while
  174.2 5.3 %slice-start = ((s8[6291456]{0:T(1024)(128)(4,1)}), s8[4194304]{0:T(1024)(128)(4,1)S(1)}, s32[]{:S(2)}) async-start(s8[6291456]{0:T(1024)(128)(4,1)} %bitcast.187), calls=%async_computation.2 | async-start | bytes 8388608 | tf_op jit(solution)/shard_map/while
  174.4 5.1 %slice-start.1 = ((s8[6291456]{0:T(1024)(128)(4,1)}), s8[2097152]{0:T(1024)(128)(4,1)S(1)}, s32[]{:S(2)}) async-start(s8[6291456]{0:T(1024)(128)(4,1)} %bitcast.187), calls=%async_computation.3 | async-start | bytes 4194304 | tf_op jit(solution)/shard_map/while
  181.6 4.5 %copy-start.2 = (f32[1536,8,128]{0,2,1:T(8,128)}, f32[1536,8,128]{0,2,1:T(8,128)S(1)}, u32[]{:S(2)}) copy-start(f32[1536,8,128]{0,2,1:T(8,128)S(1)} %fusion.108) | copy-start | bytes 18874372 | tf_op jit(solution)/shard_map/while
  187.2 7.6 %copy-start.4 = (bf16[512,2048]{0,1:T(8,128)(2,1)S(1)}, bf16[512,2048]{0,1:T(8,128)(2,1)}, u32[]{:S(2)}) copy-start(bf16[512,2048]{0,1:T(8,128)(2,1)} %copy-done.3) | copy-start | bytes 6291460 | tf_op jit(solution)/shard_map/while
  194.8 10.8 %copy-start.3 = (bf16[512,2048]{0,1:T(8,128)(2,1)}, bf16[512,2048]{0,1:T(8,128)(2,1)S(1)}, u32[]{:S(2)}) copy-start(bf16[512,2048]{0,1:T(8,128)(2,1)S(1)} %get-tuple-element.613) | copy-start | bytes 6291460 | tf_op jit(solution)/shard_map/while
  208.0 5.3 %slice-start = ((s8[6291456]{0:T(1024)(128)(4,1)}), s8[4194304]{0:T(1024)(128)(4,1)S(1)}, s32[]{:S(2)}) async-start(s8[6291456]{0:T(1024)(128)(4,1)} %bitcast.187), calls=%async_computation.2 | async-start | bytes 8388608 | tf_op jit(solution)/shard_map/while
  208.2 5.1 %slice-start.1 = ((s8[6291456]{0:T(1024)(128)(4,1)}), s8[2097152]{0:T(1024)(128)(4,1)S(1)}, s32[]{:S(2)}) async-start(s8[6291456]{0:T(1024)(128)(4,1)} %bitcast.187), calls=%async_computation.3 | async-start | bytes 4194304 | tf_op jit(solution)/shard_map/while
  215.5 4.5 %copy-start.2 = (f32[1536,8,128]{0,2,1:T(8,128)}, f32[1536,8,128]{0,2,1:T(8,128)S(1)}, u32[]{:S(2)}) copy-start(f32[1536,8,128]{0,2,1:T(8,128)S(1)} %fusion.108) | copy-start | bytes 18874372 | tf_op jit(solution)/shard_map/while
  221.1 7.6 %copy-start.4 = (bf16[512,2048]{0,1:T(8,128)(2,1)S(1)}, bf16[512,2048]{0,1:T(8,128)(2,1)}, u32[]{:S(2)}) copy-start(bf16[512,2048]{0,1:T(8,128)(2,1)} %copy-done.3) | copy-start | bytes 6291460 | tf_op jit(solution)/shard_map/while
  228.6 10.8 %copy-start.3 = (bf16[512,2048]{0,1:T(8,128)(2,1)}, bf16[512,2048]{0,1:T(8,128)(2,1)S(1)}, u32[]{:S(2)}) copy-start(bf16[512,2048]{0,1:T(8,128)(2,1)S(1)} %get-tuple-element.613) | copy-start | bytes 6291460 | tf_op jit(solution)/shard_map/while
  241.9 5.3 %slice-start = ((s8[6291456]{0:T(1024)(128)(4,1)}), s8[4194304]{0:T(1024)(128)(4,1)S(1)}, s32[]{:S(2)}) async-start(s8[6291456]{0:T(1024)(128)(4,1)} %bitcast.187), calls=%async_computation.2 | async-start | bytes 8388608 | tf_op jit(solution)/shard_map/while
  242.0 5.1 %slice-start.1 = ((s8[6291456]{0:T(1024)(128)(4,1)}), s8[2097152]{0:T(1024)(128)(4,1)S(1)}, s32[]{:S(2)}) async-start(s8[6291456]{0:T(1024)(128)(4,1)} %bitcast.187), calls=%async_computation.3 | async-start | bytes 4194304 | tf_op jit(solution)/shard_map/while
  249.3 4.5 %copy-start.2 = (f32[1536,8,128]{0,2,1:T(8,128)}, f32[1536,8,128]{0,2,1:T(8,128)S(1)}, u32[]{:S(2)}) copy-start(f32[1536,8,128]{0,2,1:T(8,128)S(1)} %fusion.108) | copy-start | bytes 18874372 | tf_op jit(solution)/shard_map/while
  254.9 7.6 %copy-start.4 = (bf16[512,2048]{0,1:T(8,128)(2,1)S(1)}, bf16[512,2048]{0,1:T(8,128)(2,1)}, u32[]{:S(2)}) copy-start(bf16[512,2048]{0,1:T(8,128)(2,1)} %copy-done.3) | copy-start | bytes 6291460 | tf_op jit(solution)/shard_map/while
  262.5 8.8 %copy-start.5 = (bf16[4,128,2048]{1,2,0:T(8,128)(2,1)S(1)}, bf16[4,128,2048]{1,2,0:T(8,128)(2,1)}, u32[]{:S(2)}) copy-start(bf16[4,128,2048]{1,2,0:T(8,128)(2,1)} %get-tuple-element.629) | copy-start | bytes 6291460
  268.7 30.5 %collective-permute-start.2 = (f32[2,512,8,128]{1,3,2,0:T(8,128)}, f32[2,512,8,128]{1,3,2,0:T(8,128)}, u32[]{:S(2)}, u32[]{:S(2)}) collective-permute-start(f32[2,512,8,128]{1,3,2,0:T(8,128)} %get-tuple-element.360), channel_id=1, source_target_pairs={{2,0},{4,2},{6,4},{8,6},{10,8},{12,10},{14,12},{16,14},{18,16},{20... | collective-permute-start | bytes 12582920 | tf_op jit(solution)/shard_map/ppermute | solution.py:20
  270.0 161.1 %collective-permute-start.3 = (f32[2,512,8,128]{1,3,2,0:T(8,128)}, f32[2,512,8,128]{1,3,2,0:T(8,128)}, u32[]{:S(2)}, u32[]{:S(2)}) collective-permute-start(f32[2,512,8,128]{1,3,2,0:T(8,128)} %get-tuple-element.361), channel_id=1, source_target_pairs={{4,0},{6,2},{8,4},{10,6},{12,8},{14,10},{16,12},{18,14},{20,16},{2... | collective-permute-start | bytes 12582920 | tf_op jit(solution)/shard_map/ppermute | solution.py:20
  431.1 8.7 %copy-start.1 = (s32[64,9]{0,1:T(8,128)S(1)}, s32[64,9]{0,1:T(8,128)}, u32[]{:S(2)}) copy-start(s32[64,9]{0,1:T(8,128)} %param.22) | copy-start | bytes 6916
where the time goes:
time: 442 us; the launch traced here: 440 us
  waiting for transfers between devices  158 us (36%)
  matrix products  128 us (29%)
  local copies, waits for them, and re-layouts  66.5 us (15%)
  other arithmetic  29.7 us (7%)
  loops' own time  21.8 us (5%)
  blocking collectives  18.8 us (4%)
  starting transfers between devices  16.5 us (4%)
    ppermute x4, waiting for transfers between devices, shifted(): return lax.ppermute(block, axis, route)  136 us
    dot_general x8, matrix products, masked_scores(): jnp.einsum('qkgd,skd->kgqs', query_blk, key_slab, preferred_element_type=...  37 us
    dot_general x4, matrix products, backward_step(): jnp.einsum('kgqs,qkgd->skd', prob_bf, grad_blk, preferred_element_type=jn...  30.4 us
    all_to_all x1, waiting for transfers between devices, body(): lax.all_to_all(grad_out, 'mp', split_axis=1, concat_axis=0, tiled=True)  21.5 us
    dot_general x4, matrix products, backward_step(): jnp.einsum('qkgd,skd->kgqs', grad_blk, value_slab, preferred_element_type...  20.3 us
    all_to_all x1, blocking collectives, body(): lax.all_to_all(saved[0].reshape(local_rows, -1), 'mp', split_axis=0, conc...  18.8 us
    dot_general x4, matrix products, backward_step(): jnp.einsum('kgqs,skd->qkgd', grad_score, key_slab, preferred_element_type...  17.9 us
    dot_general x4, matrix products, forward_step(): jnp.einsum('kgqs,skd->qkgd', prob_bf, value_slab, preferred_element_type=...  13.9 us
  transfers between devices with their start and end apart: 5, of which 3 were waited for; matrix products, arithmetic and copies ran while one was open for 5% of the time, Pallas kernels for 0%

commit v1 on v0

v1 whole, which is shorter than its diff:
```python
import functools
import math

import jax
import jax.numpy as jnp
from jax import lax
from jax.experimental import pallas as pl
from jax.experimental.pallas import tpu as pltpu
from jax.sharding import PartitionSpec as P

KV_HEADS = 16
GROUP = 2
HEAD = 128
WINDOW = 1024
BLOCK = 128
SPAN = WINDOW // BLOCK + 1
CHUNKS = 2
ATTN_SCALE = 168.0 ** (-0.5)
EXP2_SCALE = ATTN_SCALE * math.log2(math.e)
MASKED = -1e30
FAR = 1 << 20
AXES = ("ctx", "mp")
NT = (((1,), (1,)), ((), ()))
NN = (((1,), (0,)), ((), ()))


def dot(a, b, dims=NN):
    return lax.dot_general(a, b, dims, preferred_element_type=jnp.float32)


def routes(target, n_ctx, n_mp):
    out = []
    for c in range(n_ctx):
        for m in range(n_mp):
            d = target(c, m)
            if 0 <= d[0] < n_ctx:
                out.append((c * n_mp + m, d[0] * n_mp + d[1]))
    return out


def copies_kernel(plan, n_in, sc_ref, *refs):
    sem = refs[-1]
    jobs = []
    for src, src_at, dst, dst_at, rows, cols in plan(sc_ref[0], sc_ref[1]):
        jobs.append(
            pltpu.make_async_copy(
                refs[src].at[pl.ds(0, rows), pl.ds(src_at, cols)],
                refs[n_in + dst].at[pl.ds(0, rows), pl.ds(dst_at, cols)],
                sem.at[len(jobs)],
            )
        )
    for job in jobs:
        job.start()
    for job in jobs:
        job.wait()


def run_copies(plan, place, arrays, outs, count):
    hbm = pl.BlockSpec(memory_space=pl.ANY)
    moved = sum(math.prod(o.shape) * o.dtype.itemsize for o in outs)
    return pl.pallas_call(
        functools.partial(copies_kernel, plan, len(arrays)),
        in_specs=[pl.BlockSpec(memory_space=pltpu.SMEM)] + [hbm] * len(arrays),
        out_specs=[hbm] * len(outs),
        out_shape=outs,
        scratch_shapes=[pltpu.SemaphoreType.DMA((count,))],
        cost_estimate=pl.CostEstimate(flops=0, bytes_accessed=2 * moved, transcendentals=0),
    )(place, *arrays)


def attention_kernel(n_mp, rows, sc_ref, open_ref, lo_ref, *refs):
    n_do = 2 * n_mp
    q_own, q_oth, k_own, k_oth, v_own, v_oth, h_same, h_oth = refs[:8]
    do_in = refs[8 : 8 + n_do]
    outs = refs[8 + n_do : 8 + 2 * n_do + 6]
    o_out = outs[:n_do]
    dq_same, dq_oth, dkv_same, dkv_oth, dh_same, dh_oth = outs[n_do:]
    qs, ks, vs, k_t, v_t, dos, os, dqs, dk, dv, s_ref, e_ref = refs[8 + 2 * n_do + 6 :]
    core, mp = sc_ref[0], sc_ref[1]
    piece = rows // n_mp
    same = pl.ds(pl.multiple_of(core * rows, rows), rows)
    oth = pl.ds(pl.multiple_of((1 - core) * rows, rows), rows)
    same_kv = pl.ds(pl.multiple_of(WINDOW + core * rows, rows), rows)
    oth_kv = pl.ds(pl.multiple_of(WINDOW + (1 - core) * rows, rows), rows)

    def piece_at(dk_, dm):
        k_at = core if dk_ == 0 else 1 - core
        return pl.ds(pl.multiple_of(k_at * rows + lax.rem(mp + dm, n_mp) * piece, piece), piece)

    qs[same, :] = q_own[...]
    qs[oth, :] = q_oth[...]
    ks[same, :] = h_same[:, :HEAD]
    ks[oth, :] = h_oth[:, :HEAD]
    ks[same_kv, :] = k_own[...]
    ks[oth_kv, :] = k_oth[...]
    vs[same, :] = h_same[:, HEAD:]
    vs[oth, :] = h_oth[:, HEAD:]
    vs[same_kv, :] = v_own[...]
    vs[oth_kv, :] = v_oth[...]
    for at in range(n_do):
        dos[piece_at(at // n_mp, n_mp - at % n_mp), :] = do_in[at][...]
    dk[...] = jnp.zeros_like(dk)
    dv[...] = jnp.zeros_like(dv)
    for t in range(ks.shape[0] // 256):
        at = slice(t * 256, t * 256 + 256)
        k_t[:, at] = ks[at, :].T
        v_t[:, at] = vs[at, :].T

    row = lax.broadcasted_iota(jnp.int32, (BLOCK, GROUP * BLOCK), 0)
    lane = lax.broadcasted_iota(jnp.int32, (BLOCK, GROUP * BLOCK), 1)
    causal = row <= lax.rem(lane, BLOCK)

    def block(b, carry):
        at_q = pl.ds(pl.multiple_of(b * BLOCK, BLOCK), BLOCK)
        q_blk = jnp.concatenate([qs[at_q, :HEAD], qs[at_q, HEAD:]], axis=0)
        lo = lo_ref[:, at_q]
        lo = jnp.concatenate([lo, lo], axis=1)
        top = jnp.full((8, GROUP * BLOCK), MASKED, jnp.float32)
        for j in range(SPAN):
            k_at = pl.ds(pl.multiple_of((b + j) * BLOCK, BLOCK), BLOCK)
            part = slice(j * BLOCK, j * BLOCK + BLOCK)
            s = dot(ks[k_at, :], q_blk, NT)
            closed = jnp.where(open_ref[b * SPAN + SPAN - 1 - j] == 1, 0, FAR)
            valid = row >= jnp.maximum(lo - (b + j) * BLOCK, closed)
            if j == SPAN - 1:
                valid = valid & causal
            s = jnp.where(valid, s, MASKED)
            s_ref[part, :] = s
            top = jnp.maximum(top, jnp.max(s.reshape(BLOCK // 8, 8, GROUP * BLOCK), axis=0))
        top = jnp.max(top, axis=0, keepdims=True)
        total = jnp.zeros((8, GROUP * BLOCK), jnp.float32)
        for j in range(SPAN):
            part = slice(j * BLOCK, j * BLOCK + BLOCK)
            e = jnp.exp2((s_ref[part, :] - top) * EXP2_SCALE)
            total = total + jnp.sum(e.reshape(BLOCK // 8, 8, GROUP * BLOCK), axis=0)
            e_ref[part, :] = e.astype(jnp.bfloat16)
        inverse = 1.0 / jnp.sum(total, axis=0, keepdims=True)
        at_keys = pl.ds(pl.multiple_of(b * BLOCK, BLOCK), SPAN * BLOCK)
        o_t = (dot(v_t[:, at_keys], e_ref[...]) * inverse).astype(jnp.bfloat16)
        os[at_q, :HEAD] = o_t[:, :BLOCK].T
        os[at_q, HEAD:] = o_t[:, BLOCK:].T
        do_t = jnp.concatenate([dos[at_q, :HEAD].T, dos[at_q, HEAD:].T], axis=1)
        do_t = (do_t.astype(jnp.float32) * inverse).astype(jnp.bfloat16)
        delta = jnp.sum(
            do_t.astype(jnp.float32) * o_t.astype(jnp.float32), axis=0, keepdims=True
        )
        dq_t = jnp.zeros((HEAD, GROUP * BLOCK), jnp.float32)
        for j in range(SPAN):
            k_at = pl.ds(pl.multiple_of((b + j) * BLOCK, BLOCK), BLOCK)
            part = slice(j * BLOCK, j * BLOCK + BLOCK)
            dp = dot(vs[k_at, :], do_t)
            e = e_ref[part, :]
            ds = (e.astype(jnp.float32) * (dp - delta)).astype(jnp.bfloat16)
            dv[k_at, :] += dot(e, do_t, NT)
            dk[k_at, :] += dot(ds, q_blk)
            dq_t = dq_t + dot(k_t[:, k_at], ds)
        dq_t = (dq_t * ATTN_SCALE).astype(jnp.bfloat16)
        dqs[at_q, :HEAD] = dq_t[:, :BLOCK].T
        dqs[at_q, HEAD:] = dq_t[:, BLOCK:].T
        return carry

    lax.fori_loop(0, qs.shape[0] // BLOCK, block, jnp.int32(0))

    for at in range(n_do):
        o_out[at][...] = os[piece_at(at // n_mp, at % n_mp), :]
    dq_same[...] = dqs[same, :]
    dq_oth[...] = dqs[oth, :]
    for out, at in ((dkv_same, same_kv), (dkv_oth, oth_kv), (dh_same, same), (dh_oth, oth)):
        out[:, :HEAD] = (dk[at, :] * ATTN_SCALE).astype(out.dtype)
        out[:, HEAD:] = dv[at, :].astype(out.dtype)


def attention(n_mp, rows, chunk, heads_core, heads_chunk, place, opened, lo, near, halo, grads):
    heads_mp = 2 * heads_core
    piece = rows // n_mp
    pair = GROUP * HEAD

    def at_head(g, sc, *unused):
        return (0, sc[0] * heads_core + chunk * heads_chunk + g)

    def at_grad(g, sc, *unused):
        return (0, sc[1] * heads_mp + sc[0] * heads_core + chunk * heads_chunk + g)

    def at_local(g, *unused):
        return (0, g)

    in_specs = [pl.BlockSpec((1, 2 * rows), lambda g, *unused: (0, 0))]
    in_specs += [pl.BlockSpec((rows, pair), at_head)] * 2
    in_specs += [pl.BlockSpec((rows, HEAD), at_head)] * 4
    in_specs += [pl.BlockSpec((rows, pair), at_local)] * 2
    in_specs += [pl.BlockSpec((piece, pair), at_grad)]
    in_specs += [pl.BlockSpec((piece, pair), at_local)] * (2 * n_mp - 1)
    out_specs = [pl.BlockSpec((piece, pair), at_local)] * (2 * n_mp)
    out_specs += [pl.BlockSpec((rows, pair), at_local)] * 6
    wide = heads_chunk * pair
    bf, f32 = jnp.bfloat16, jnp.float32
    out_shape = [jax.ShapeDtypeStruct((piece, wide), bf)] * (2 * n_mp)
    out_shape += [jax.ShapeDtypeStruct((rows, wide), t) for t in (bf, bf, f32, bf, bf, bf)]
    tokens, keys, slab = 2 * rows, WINDOW + 2 * rows, SPAN * BLOCK
    flops = heads_chunk * 6 * 2 * GROUP * tokens * slab * HEAD
    return pl.pallas_call(
        functools.partial(attention_kernel, n_mp, rows),
        grid_spec=pltpu.PrefetchScalarGridSpec(
            num_scalar_prefetch=2,
            grid=(heads_chunk,),
            in_specs=in_specs,
            out_specs=out_specs,
            scratch_shapes=[
                pltpu.VMEM((tokens, pair), bf),
                pltpu.VMEM((keys, HEAD), bf),
                pltpu.VMEM((keys, HEAD), bf),
                pltpu.VMEM((HEAD, keys), bf),
                pltpu.VMEM((HEAD, keys), bf),
                pltpu.VMEM((tokens, pair), bf),
                pltpu.VMEM((tokens, pair), bf),
                pltpu.VMEM((tokens, pair), bf),
                pltpu.VMEM((keys, HEAD), f32),
                pltpu.VMEM((keys, HEAD), f32),
                pltpu.VMEM((slab, GROUP * BLOCK), f32),
                pltpu.VMEM((slab, GROUP * BLOCK), bf),
            ],
        ),
        out_shape=out_shape,
        compiler_params=pltpu.CompilerParams(
            dimension_semantics=("arbitrary",), vmem_limit_bytes=48 * 1024 * 1024
        ),
        cost_estimate=pl.CostEstimate(
            flops=flops,
            bytes_accessed=heads_chunk * 12 * rows * pair * 2,
            transcendentals=heads_chunk * GROUP * tokens * slab,
        ),
        name="attention",
    )(place, opened, lo, *near, *halo, *grads)


def sum_kernel(heads, sc_ref, *refs):
    near, far, dk_out, dv_out = refs[0], refs[1], refs[2], refs[3]


def body(queries, keys, values, grad_out, band_mask, segment_ids):
    n_ctx, n_mp = lax.axis_size("ctx"), lax.axis_size("mp")
    rows = queries.shape[0]
    piece = rows // n_mp
    heads_mp = KV_HEADS // n_mp
    heads_core = heads_mp // 2
    heads_chunk = heads_core // CHUNKS
    pair = GROUP * HEAD
    wide = heads_chunk * pair
    bf = jnp.bfloat16
    ctx, mp = lax.axis_index("ctx"), lax.axis_index("mp")
    core, chip = lax.rem(ctx, 2), ctx // 2
    place = jnp.stack([core, mp]).astype(jnp.int32)

    def send(x, target):
        return lax.ppermute(x, AXES, routes(target, n_ctx, n_mp))

    def plan_halo(core, mp):
        jobs = []
        for i in range(CHUNKS):
            for side in range(2):
                half = core if side == 0 else 1 - core
                for g in range(heads_chunk):
                    at = pl.multiple_of((half * heads_core + i * heads_chunk + g) * HEAD, HEAD)
                    for which in range(2):
                        jobs.append(
                            (which, at, 2 * i + side, g * pair + which * HEAD, rows, HEAD)
                        )
        return jobs

    halos = run_copies(
        plan_halo,
        place,
        (keys, values),
        [jax.ShapeDtypeStruct((rows, wide), bf)] * (2 * CHUNKS),
        2 * CHUNKS * heads_chunk * 2,
    )
    partners = [(dk, dm) for dk in range(2) for dm in range(n_mp)]

    def plan_grad(core, mp):
        jobs = []
        for i in range(CHUNKS):
            for at, (dk, dm) in enumerate(partners[1:]):
                core_to = core if dk == 0 else 1 - core
                mp_to = lax.rem(mp + dm, n_mp)
                col = (mp_to * heads_mp + core_to * heads_core + i * heads_chunk) * pair
                jobs.append(
                    (0, pl.multiple_of(col, HEAD), i * (2 * n_mp - 1) + at, 0, piece, wide)
                )
        return jobs

    sent_grads = run_copies(
        plan_grad,
        place,
        (grad_out,),
        [jax.ShapeDtypeStruct((piece, wide), bf)] * (CHUNKS * (2 * n_mp - 1)),
        CHUNKS * (2 * n_mp - 1),
    )

    halo_in, grads_in = [], []
    for i in range(CHUNKS):
        halo_in.append(
            (
                send(halos[2 * i], lambda c, m: (c + 2, m)),
                send(halos[2 * i + 1], lambda c, m: ((c + 2) ^ 1, m)),
            )
        )
        grads_in.append(
            [
                send(sent_grads[i * (2 * n_mp - 1) + at], lambda c, m: (c ^ dk, (m + dm) % n_mp))
                for at, (dk, dm) in enumerate(partners[1:])
            ]
        )
    swap = lambda c, m: (c ^ 1, m)
    near = (
        queries,
        send(queries, swap),
        keys,
        send(keys, swap),
        values,
        send(values, swap),
    )

    tokens = 2 * rows
    padded = jnp.concatenate([jnp.full((WINDOW,), -1, jnp.int32), segment_ids])
    ids = lax.dynamic_slice_in_dim(padded, chip * tokens, WINDOW + tokens, 0)
    before = jnp.sum((ids[:, None] < ids[None, WINDOW:]).astype(jnp.int32), axis=0)
    lo = jnp.maximum(before, jnp.arange(1, tokens + 1, dtype=jnp.int32))[None, :]
    blocks = tokens // BLOCK
    opened = lax.dynamic_slice_in_dim(band_mask, chip * blocks, blocks, 0).reshape(-1)

    out_parts, dq_parts, near_parts, far_parts = [], [], [], []
    for i in range(CHUNKS):
        done = attention(
            n_mp,
            rows,
            i,
            heads_core,
            heads_chunk,
            place,
            opened,
            lo,
            near,
            halo_in[i],
            [grad_out] + grads_in[i],
        )
        o_pieces = done[: 2 * n_mp]
        dq_same, dq_oth, dkv_same, dkv_oth, dh_same, dh_oth = done[2 * n_mp :]
        back_same = send(dh_same, lambda c, m: (c - 2, m))
        back_oth = send(dh_oth, lambda c, m: ((c - 2) ^ 1 if c >= 2 else -1, m))
        out_parts.append(
            [o_pieces[0]]
            + [
                send(o_pieces[1 + at], lambda c, m: (c ^ dk, (m + dm) % n_mp))
                for at, (dk, dm) in enumerate(partners[1:])
            ]
        )
        dq_parts.append((dq_same, send(dq_oth, swap)))
        near_parts.append((dkv_same, send(dkv_oth, swap)))
        far_parts.append((back_same, back_oth))

    arrays = [x for part in out_parts for x in part] + [x for part in dq_parts for x in part]

    def plan_out(core, mp):
        jobs = []
        for i in range(CHUNKS):
            for at, (dk, dm) in enumerate(partners):
                core_from = core if dk == 0 else 1 - core
                mp_from = lax.rem(mp + n_mp - dm, n_mp)
                col = (mp_from * heads_mp + core_from * heads_core + i * heads_chunk) * pair
                jobs.append((i * 2 * n_mp + at, 0, 0, pl.multiple_of(col, HEAD), piece, wide))
        for i in range(CHUNKS):
            for side in range(2):
                half = core if side == 0 else 1 - core
                col = (half * heads_core + i * heads_chunk) * pair
                src = CHUNKS * 2 * n_mp + 2 * i + side
                jobs.append((src, 0, 1, pl.multiple_of(col, HEAD), rows, wide))
        return jobs

    attn_out, grad_queries = run_copies(
        plan_out,
        place,
        arrays,
        [
            jax.ShapeDtypeStruct((piece, n_mp * heads_mp * pair), bf),
            jax.ShapeDtypeStruct(queries.shape, bf),
        ],
        len(arrays),
    )

    def halves(pairs):
        same = jnp.concatenate([p[0].astype(jnp.float32) for p in pairs], axis=1)
        oth = jnp.concatenate([p[1].astype(jnp.float32) for p in pairs], axis=1)
        return same, oth

    near_same, near_oth = halves(near_parts)
    far_same, far_oth = halves(far_parts)
    same, oth = near_same + far_same, near_oth + far_oth
    low = jnp.where(core == 0, same, oth).astype(bf)
    high = jnp.where(core == 0, oth, same).astype(bf)
    both = jnp.concatenate([low, high], axis=1).reshape(rows, heads_mp, 2, HEAD)
    grad_keys = both[:, :, 0].reshape(rows, heads_mp * HEAD)
    grad_values = both[:, :, 1].reshape(rows, heads_mp * HEAD)
    return attn_out, grad_queries, grad_keys, grad_values


def solution(mesh):
    placed = (P("ctx", "mp"), P("ctx", "mp"), P("ctx", "mp"), P(("ctx", "mp"), None), P(), P())
    return jax.shard_map(
        body,
        mesh=mesh,
        in_specs=placed,
        out_specs=(P(("ctx", "mp"), None), P("ctx", "mp"), P("ctx", "mp"), P("ctx", "mp")),
        check_vma=False,
    )
```

time: 442 us -> 438 us (level)
  Pallas kernels: 0 us -> 313 us
  matrix products: 128 us -> 0 us
  waiting for transfers between devices: 158 us -> 49.6 us
  local copies, waits for them, and re-layouts: 66.5 us -> 33.5 us
  other arithmetic: 29.7 us -> 5.91 us
  loops' own time: 21.8 us -> 0 us
  blocking collectives: 18.8 us -> 0 us
  starting transfers between devices: 16.5 us -> 33.2 us
    pallas_call x0 -> x5, Pallas kernels: none -> 313 us  [the longest x3 244 us: run_copies(): pl.pallas_call(functools.partial(copies_kernel, plan, len(arrays)), in_sp...]
    dot_general x28 -> x0, matrix products: 128 us -> none  [the longest x8 37 us: masked_scores(): jnp.einsum('qkgd,skd->kgqs', query_blk, key_slab, preferred_element_type=...]
    ppermute x4 -> x27, waiting for transfers between devices: 136 us -> 49.6 us  [send(): return lax.ppermute(x, AXES, routes(target, n_ctx, n_mp))]
    concatenate x0 -> x16, local copies, waits for them, and re-layouts: none -> 25.7 us  [the longest x8 15.4 us: halves(): same = jnp.concatenate([p[0].astype(jnp.float32) for p in pairs], axis=1)]
    another operation x2 -> x0, loops' own time: 21.8 us -> none  [the longest x1 11.2 us: body(): lax.scan(backward_step, (zeros, zeros), (block_ids,) + tuple(saved))]
    ppermute x4 -> x27, starting transfers between devices: 11.6 us -> 33.2 us  [send(): return lax.ppermute(x, AXES, routes(target, n_ctx, n_mp))]
    all_to_all x1 -> x0, waiting for transfers between devices: 21.5 us -> none  [body(): lax.all_to_all(grad_out, 'mp', split_axis=1, concat_axis=0, tiled=True)]
    all_to_all x1 -> x0, blocking collectives: 18.8 us -> none  [body(): lax.all_to_all(saved[0].reshape(local_rows, -1), 'mp', split_axis=0, conc...]
  transfers between devices with their start and end apart: 5 -> 27, of which waited for: 3 -> 6; matrix products, arithmetic and copies ran while one was open for 5% -> 8% of each run, Pallas kernels for 0% -> 42%
where the time goes in v1:
time: 438 us; the launch traced here: 436 us
  Pallas kernels  313 us (71%)
  waiting for transfers between devices  49.6 us (11%)
  local copies, waits for them, and re-layouts  33.5 us (8%)
  starting transfers between devices  33.2 us (8%)
  other arithmetic  5.91 us (1%)
    pallas_call x3, Pallas kernels, run_copies(): pl.pallas_call(functools.partial(copies_kernel, plan, len(arrays)), in_sp...  244 us
    pallas_call x2, Pallas kernels, attention(): pl.pallas_call(functools.partial(attention_kernel, n_mp, rows), grid_spec...  68.6 us
    ppermute x27, waiting for transfers between devices, send(): return lax.ppermute(x, AXES, routes(target, n_ctx, n_mp))  49.6 us
    ppermute x27, starting transfers between devices, send(): return lax.ppermute(x, AXES, routes(target, n_ctx, n_mp))  33.2 us
    concatenate x8, local copies, waits for them, and re-layouts, halves(): same = jnp.concatenate([p[0].astype(jnp.float32) for p in pairs], axis=1)  15.4 us
    concatenate x8, local copies, waits for them, and re-layouts, halves(): oth = jnp.concatenate([p[1].astype(jnp.float32) for p in pairs], axis=1)  10.4 us
  transfers between devices with their start and end apart: 27, of which 6 were waited for; matrix products, arithmetic and copies ran while one was open for 8% of the time, Pallas kernels for 42%

profile of v1, /device:TPU:0, one launch (start us, length us, event | category | flops | bytes accessed | tf_op | source)
XLA Modules:
  0.0 435.9 jit_solution(5155173495893475120)
XLA Ops:
  0.6 0.5 collective-permute-start
  1.2 0.6 pad_add_fusion.sc_ref
  1.8 49.6 %shard_map.94 = (bf16[256,512]{1,0:T(8,128)(2,1)}, bf16[256,512]{1,0:T(8,128)(2,1)}, bf16[256,512]{1,0:T(8,128)(2,1)}, bf16[256,512]{1,0:T(8,128)(2,1)}, bf16[25...) custom-call(s32[2]{0:T(128)} %pad_add_fusion.sc_ref, bf16[256,4096]{1,0:T(8,128)(2,1)} %refs_8_.3), custom_call_target="tpu_custom_call" | custom-call | bytes 3145728 | tf_op jit(solution)/shard_map/pallas_call | solution.py:61
  51.5 2.6 collective-permute-start.13
  54.0 0.2 collective-permute-start.1
  54.2 0.3 collective-permute-start.2
  54.5 0.2 collective-permute-start.14
  54.7 6.4 %collective-permute-done.13.refs_9_ = bf16[256,512]{1,0:T(8,128)(2,1)S(1)} collective-permute-done((bf16[256,512]{1,0:T(8,128)(2,1)}, bf16[256,512]{1,0:T(8,128)(2,1)S(1)}, u32[]{:S(2)}, u32[]{:S(2)}) %collective-permute-start.13) | collective-permute-done | bytes 262176 | tf_op jit(solution)/shard_map/ppermute | solution.py:255
  61.2 1.0 collective-permute-start.15
  62.2 65.4 %shard_map.93 = (bf16[512,512]{1,0:T(8,128)(2,1)}, bf16[512,512]{1,0:T(8,128)(2,1)}, bf16[512,512]{1,0:T(8,128)(2,1)}, bf16[512,512]{1,0:T(8,128)(2,1)}) custom-call(s32[2]{0:T(128)} %pad_add_fusion.sc_ref, bf16[512,1024]{1,0:T(8,128)(2,1)} %refs_2_.3, bf16[512,1024]{1,0:T(8,128)(2,1)} %refs_4_.3), custom_call_target="tpu_custom_call" | custom-call | bytes 4194304 | tf_op jit(solution)/shard_map/pallas_call | solution.py:61
  127.8 0.1 copy.22
  128.0 3.5 collective-permute-start.11
  131.5 3.6 collective-permute-start.12
  135.1 1.0 convert_reduce_fusion
  136.1 8.0 %collective-permute-done.11.refs_6_ = bf16[512,512]{1,0:T(8,128)(2,1)S(1)} collective-permute-done((bf16[512,512]{1,0:T(8,128)(2,1)}, bf16[512,512]{1,0:T(8,128)(2,1)S(1)}, u32[]{:S(2)}, u32[]{:S(2)}) %collective-permute-start.11) | collective-permute-done | bytes 524320 | tf_op jit(solution)/shard_map/ppermute | solution.py:255
  144.0 0.7 collective-permute-start.5
  144.7 10.4 %collective-permute-done.12.refs_7_ = bf16[512,512]{1,0:T(8,128)(2,1)S(1)} collective-permute-done((bf16[512,512]{1,0:T(8,128)(2,1)}, bf16[512,512]{1,0:T(8,128)(2,1)S(1)}, u32[]{:S(2)}, u32[]{:S(2)}) %collective-permute-start.12) | collective-permute-done | bytes 524320 | tf_op jit(solution)/shard_map/ppermute | solution.py:255
  155.1 0.7 collective-permute-start.7
  155.8 4.0 collective-permute-start.3
  159.8 3.8 collective-permute-start.4
  163.6 34.3 %attention.3 = (bf16[256,512]{1,0:T(8,128)(2,1)S(1)}, bf16[256,512]{1,0:T(8,128)(2,1)S(1)}, bf16[256,512]{1,0:T(8,128)(2,1)S(1)}, bf16[256,512]{1,0:T(8,128)(2,1...) custom-call(s32[2]{0:T(128)S(1)} %copy-done.5, ...), custom_call_target="tpu_custom_call" | custom-call | flops 7247757312 | bytes 6291456 | tf_op jit(solution)/shard_map/attention/pallas_call | solution.py:201
  197.9 0.8 copy-done.1
  198.7 0.7 copy-done.3
  199.4 1.3 collective-permute-start.22
  200.7 0.7 collective-permute-start.24
  201.4 1.3 collective-permute-start.26
  202.7 34.3 %attention.2 = (bf16[256,512]{1,0:T(8,128)(2,1)S(1)}, bf16[256,512]{1,0:T(8,128)(2,1)S(1)}, bf16[256,512]{1,0:T(8,128)(2,1)S(1)}, bf16[256,512]{1,0:T(8,128)(2,1...) custom-call(s32[2]{0:T(128)S(1)} %copy-done.5, ...), custom_call_target="tpu_custom_call" | custom-call | flops 7247757312 | bytes 6291456 | tf_op jit(solution)/shard_map/attention/pallas_call | solution.py:201
  237.0 0.8 copy-done.2
  237.8 0.7 copy-done.4
  238.5 1.3 collective-permute-start.21
  239.8 0.1 collective-permute-start.23
  239.9 1.5 collective-permute-start.25
  241.4 1.7 collective-permute-start.16
  243.2 0.2 collective-permute-start.17
  243.3 12.8 %collective-permute-done.21 = bf16[512,512]{1,0:T(8,128)(2,1)S(1)} collective-permute-done((bf16[512,512]{1,0:T(8,128)(2,1)S(1)}, bf16[512,512]{1,0:T(8,128)(2,1)S(1)}, u32[]{:S(2)}, u32[]{:S(2)}) %collective-permute-start.21) | collective-permute-done | bytes 524320 | tf_op jit(solution)/shard_map/ppermute | solution.py:255
  256.1 0.5 collective-permute-start.18
  256.6 1.3 collective-permute-start.20
  257.9 8.5 %collective-permute-done.25 = bf16[512,512]{1,0:T(8,128)(2,1)S(1)} collective-permute-done((bf16[512,512]{1,0:T(8,128)(2,1)S(1)}, bf16[512,512]{1,0:T(8,128)(2,1)S(1)}, u32[]{:S(2)}, u32[]{:S(2)}) %collective-permute-start.25) | collective-permute-done | bytes 524320 | tf_op jit(solution)/shard_map/ppermute | solution.py:255
  266.5 0.8 copy-done.11
  267.3 0.3 collective-permute-start.19
  267.6 2.8 concatenate.54
  270.4 2.3 copy.24
  272.7 2.8 concatenate.53
  275.5 2.3 copy.23
  277.7 1.2 concatenate.57
  278.9 1.4 copy.26
  280.3 1.2 concatenate.61
  281.5 1.4 copy.28
  282.9 1.2 concatenate.65
  284.1 1.4 copy.30
  285.5 1.2 concatenate.56
  286.7 1.4 copy.25
  288.1 1.2 concatenate.60
  289.3 1.4 copy.27
  290.7 1.2 concatenate.64
  291.9 1.4 copy.29
  293.3 1.7 collective-permute-start.8
  295.0 0.5 collective-permute-start.10
  295.5 3.1 select_convert_fusion
  298.6 1.2 pad_maximum_fusion
  299.8 2.3 copy.32
  302.0 1.3 copy.31
  303.4 3.4 collective-permute-done.10.refs_3_
  306.8 128.9 %shard_map.95 = (bf16[256,4096]{1,0:T(8,128)(2,1)}, bf16[512,2048]{1,0:T(8,128)(2,1)}) custom-call(s32[2]{0:T(128)} %pad_add_fusion.sc_ref, bf16[256,512]{1,0:T(8,128)(2,1)} %copy-done.4, bf16[256,512]{1,0:T(8,128)(2,1)} %copy-done.13, bf16[256,512]{1,0:T(8,128)(2,1)} %collective-permute-done.9.refs_2_, bf16[256,512]{1,0:T(8,128)(2,1)} %collective-permute-done.10.refs_3_, ...), custom_call_target="tpu_custom_call" | custom-call | bytes 8388608 | tf_op jit(solution)/shard_map/pallas_call | solution.py:61
  (59 shorter events, 0.3 us)
Async XLA Ops:
  0.6 127.1 %copy-start = (s32[64,9]{0,1:T(8,128)S(1)}, s32[64,9]{0,1:T(8,128)}, u32[]{:S(2)}) copy-start(s32[64,9]{0,1:T(8,128)} %param.10) | copy-start | bytes 6916
  0.6 159.1 %collective-permute-start = (bf16[512,2048]{1,0:T(8,128)(2,1)}, bf16[512,2048]{1,0:T(8,128)(2,1)}, u32[]{:S(2)}, u32[]{:S(2)}) collective-permute-start(bf16[512,2048]{1,0:T(8,128)(2,1)} %refs_0_.7), channel_id=1, source_target_pairs={{0,2},{1,3},{2,0},{3,1},{4,6},{5,7},{6,4},{7,5},{8,10},{9,11},{10,... | collective-permute-start | bytes 6291464 | tf_op jit(solution)/shard_map/ppermute | solution.py:255
  1.8 126.2 %copy-start.14 = (s32[8192]{0:T(1024)S(1)}, s32[8192]{0:T(1024)}, u32[]{:S(2)}) copy-start(s32[8192]{0:T(1024)} %param.11) | copy-start | bytes 98308
  1.8 161.8 %copy-start.5 = (s32[2]{0:T(128)S(1)}, s32[2]{0:T(128)}, u32[]{:S(2)}) copy-start(s32[2]{0:T(128)} %pad_add_fusion.sc_ref) | copy-start | bytes 28
  51.4 92.6 %copy-start.17 = (bf16[256,512]{1,0:T(8,128)(2,1)S(1)}, bf16[256,512]{1,0:T(8,128)(2,1)}, u32[]{:S(2)}) copy-start(bf16[256,512]{1,0:T(8,128)(2,1)} %get-tuple-element.38) | copy-start | bytes 786436
  51.4 103.7 %copy-start.16 = (bf16[256,512]{1,0:T(8,128)(2,1)S(1)}, bf16[256,512]{1,0:T(8,128)(2,1)}, u32[]{:S(2)}) copy-start(bf16[256,512]{1,0:T(8,128)(2,1)} %get-tuple-element.39) | copy-start | bytes 786436
  51.4 103.7 %copy-start.15 = (bf16[256,512]{1,0:T(8,128)(2,1)S(1)}, bf16[256,512]{1,0:T(8,128)(2,1)}, u32[]{:S(2)}) copy-start(bf16[256,512]{1,0:T(8,128)(2,1)} %get-tuple-element.40) | copy-start | bytes 786436
  51.5 9.7 %collective-permute-start.13 = (bf16[256,512]{1,0:T(8,128)(2,1)}, bf16[256,512]{1,0:T(8,128)(2,1)S(1)}, u32[]{:S(2)}, u32[]{:S(2)}) collective-permute-start(bf16[256,512]{1,0:T(8,128)(2,1)} %get-tuple-element.47), channel_id=1, source_target_pairs={{0,1},{1,0},{2,3},{3,2},{4,5},{5,4},{6,7},{7,6},{8,9},{9,8},{10,11... | collective-permute-start | bytes 786440 | tf_op jit(solution)/shard_map/ppermute | solution.py:255
  54.0 101.1 %collective-permute-start.1 = (bf16[512,1024]{1,0:T(8,128)(2,1)}, bf16[512,1024]{1,0:T(8,128)(2,1)}, u32[]{:S(2)}, u32[]{:S(2)}) collective-permute-start(bf16[512,1024]{1,0:T(8,128)(2,1)} %refs_2_.3), channel_id=1, source_target_pairs={{0,2},{1,3},{2,0},{3,1},{4,6},{5,7},{6,4},{7,5},{8,10},{9,11},{10,... | collective-permute-start | bytes 3145736 | tf_op jit(solution)/shard_map/ppermute | solution.py:255
  54.2 101.6 %collective-permute-start.2 = (bf16[512,1024]{1,0:T(8,128)(2,1)}, bf16[512,1024]{1,0:T(8,128)(2,1)}, u32[]{:S(2)}, u32[]{:S(2)}) collective-permute-start(bf16[512,1024]{1,0:T(8,128)(2,1)} %refs_4_.3), channel_id=1, source_target_pairs={{0,2},{1,3},{2,0},{3,1},{4,6},{5,7},{6,4},{7,5},{8,10},{9,11},{10,... | collective-permute-start | bytes 3145736 | tf_op jit(solution)/shard_map/ppermute | solution.py:255
  54.5 73.4 %collective-permute-start.14 = (bf16[256,512]{1,0:T(8,128)(2,1)}, bf16[256,512]{1,0:T(8,128)(2,1)S(1)}, u32[]{:S(2)}, u32[]{:S(2)}) collective-permute-start(bf16[256,512]{1,0:T(8,128)(2,1)} %get-tuple-element.48), channel_id=1, source_target_pairs={{0,2},{1,3},{2,0},{3,1},{4,6},{5,7},{6,4},{7,5},{8,10},{9,11},{10,... | collective-permute-start | bytes 786440 | tf_op jit(solution)/shard_map/ppermute | solution.py:255
  61.2 70.3 %collective-permute-start.15 = (bf16[256,512]{1,0:T(8,128)(2,1)}, bf16[256,512]{1,0:T(8,128)(2,1)S(1)}, u32[]{:S(2)}, u32[]{:S(2)}) collective-permute-start(bf16[256,512]{1,0:T(8,128)(2,1)} %get-tuple-element.49), channel_id=1, source_target_pairs={{0,3},{1,2},{2,1},{3,0},{4,7},{5,6},{6,5},{7,4},{8,11},{9,10},{10,... | collective-permute-start | bytes 786440 | tf_op jit(solution)/shard_map/ppermute | solution.py:255
  128.0 16.0 %collective-permute-start.11 = (bf16[512,512]{1,0:T(8,128)(2,1)}, bf16[512,512]{1,0:T(8,128)(2,1)S(1)}, u32[]{:S(2)}, u32[]{:S(2)}) collective-permute-start(bf16[512,512]{1,0:T(8,128)(2,1)} %get-tuple-element.45), channel_id=1, source_target_pairs={{0,4},{1,5},{2,6},{3,7},{4,8},{5,9},{6,10},{7,11},{8,12},{9,13},{1... | collective-permute-start | bytes 1572872 | tf_op jit(solution)/shard_map/ppermute | solution.py:255
  131.5 23.6 %collective-permute-start.12 = (bf16[512,512]{1,0:T(8,128)(2,1)}, bf16[512,512]{1,0:T(8,128)(2,1)S(1)}, u32[]{:S(2)}, u32[]{:S(2)}) collective-permute-start(bf16[512,512]{1,0:T(8,128)(2,1)} %get-tuple-element.46), channel_id=1, source_target_pairs={{0,6},{1,7},{2,4},{3,5},{4,10},{5,11},{6,8},{7,9},{8,14},{9,15},{1... | collective-permute-start | bytes 1572872 | tf_op jit(solution)/shard_map/ppermute | solution.py:255
  144.0 55.4 %collective-permute-start.5 = (bf16[256,512]{1,0:T(8,128)(2,1)S(1)}, bf16[256,512]{1,0:T(8,128)(2,1)S(1)}, u32[]{:S(2)}, u32[]{:S(2)}) collective-permute-start(bf16[256,512]{1,0:T(8,128)(2,1)S(1)} %copy-done.17), channel_id=1, source_target_pairs={{0,1},{1,0},{2,3},{3,2},{4,5},{5,4},{6,7},{7,6},{8,9},{9,8},{10,11... | collective-permute-start | bytes 786440 | tf_op jit(solution)/shard_map/ppermute | solution.py:255
  155.1 45.6 %collective-permute-start.6 = (bf16[256,512]{1,0:T(8,128)(2,1)S(1)}, bf16[256,512]{1,0:T(8,128)(2,1)S(1)}, u32[]{:S(2)}, u32[]{:S(2)}) collective-permute-start(bf16[256,512]{1,0:T(8,128)(2,1)S(1)} %copy-done.16), channel_id=1, source_target_pairs={{0,2},{1,3},{2,0},{3,1},{4,6},{5,7},{6,4},{7,5},{8,10},{9,11},{10,... | collective-permute-start | bytes 786440 | tf_op jit(solution)/shard_map/ppermute | solution.py:255
  155.1 46.3 %collective-permute-start.7 = (bf16[256,512]{1,0:T(8,128)(2,1)S(1)}, bf16[256,512]{1,0:T(8,128)(2,1)S(1)}, u32[]{:S(2)}, u32[]{:S(2)}) collective-permute-start(bf16[256,512]{1,0:T(8,128)(2,1)S(1)} %copy-done.15), channel_id=1, source_target_pairs={{0,3},{1,2},{2,1},{3,0},{4,7},{5,6},{6,5},{7,4},{8,11},{9,10},{10,... | collective-permute-start | bytes 786440 | tf_op jit(solution)/shard_map/ppermute | solution.py:255
  155.8 46.9 %collective-permute-start.3 = (bf16[512,512]{1,0:T(8,128)(2,1)}, bf16[512,512]{1,0:T(8,128)(2,1)S(1)}, u32[]{:S(2)}, u32[]{:S(2)}) collective-permute-start(bf16[512,512]{1,0:T(8,128)(2,1)} %get-tuple-element.36), channel_id=1, source_target_pairs={{0,4},{1,5},{2,6},{3,7},{4,8},{5,9},{6,10},{7,11},{8,12},{9,13},{1... | collective-permute-start | bytes 1572872 | tf_op jit(solution)/shard_map/ppermute | solution.py:255
  159.8 43.0 %collective-permute-start.4 = (bf16[512,512]{1,0:T(8,128)(2,1)}, bf16[512,512]{1,0:T(8,128)(2,1)S(1)}, u32[]{:S(2)}, u32[]{:S(2)}) collective-permute-start(bf16[512,512]{1,0:T(8,128)(2,1)} %get-tuple-element.37), channel_id=1, source_target_pairs={{0,6},{1,7},{2,4},{3,5},{4,10},{5,11},{6,8},{7,9},{8,14},{9,15},{1... | collective-permute-start | bytes 1572872 | tf_op jit(solution)/shard_map/ppermute | solution.py:255
  197.9 0.8 copy-start.1
  198.7 0.7 copy-start.3
  199.4 40.5 %collective-permute-start.22 = (bf16[512,512]{1,0:T(8,128)(2,1)S(1)}, bf16[512,512]{1,0:T(8,128)(2,1)S(1)}, u32[]{:S(2)}, u32[]{:S(2)}) collective-permute-start(bf16[512,512]{1,0:T(8,128)(2,1)S(1)} %get-tuple-element.63), channel_id=1, source_target_pairs={{4,0},{5,1},{6,2},{7,3},{8,4},{9,5},{10,6},{11,7},{12,8},{13,9},{1... | collective-permute-start | bytes 1572872 | tf_op jit(solution)/shard_map/ppermute | solution.py:255
  200.7 40.7 %collective-permute-start.24 = (bf16[512,512]{1,0:T(8,128)(2,1)S(1)}, bf16[512,512]{1,0:T(8,128)(2,1)S(1)}, u32[]{:S(2)}, u32[]{:S(2)}) collective-permute-start(bf16[512,512]{1,0:T(8,128)(2,1)S(1)} %get-tuple-element.65), channel_id=1, source_target_pairs={{0,2},{1,3},{2,0},{3,1},{4,6},{5,7},{6,4},{7,5},{8,10},{9,11},{10,... | collective-permute-start | bytes 1572872 | tf_op jit(solution)/shard_map/ppermute | solution.py:255
  201.4 41.7 %collective-permute-start.26 = (bf16[512,512]{1,0:T(8,128)(2,1)S(1)}, bf16[512,512]{1,0:T(8,128)(2,1)S(1)}, u32[]{:S(2)}, u32[]{:S(2)}) collective-permute-start(bf16[512,512]{1,0:T(8,128)(2,1)S(1)} %get-tuple-element.67), channel_id=1, source_target_pairs={{4,2},{5,3},{6,0},{7,1},{8,6},{9,7},{10,4},{11,5},{12,10},{13,11},... | collective-permute-start | bytes 1572872 | tf_op jit(solution)/shard_map/ppermute | solution.py:255
  237.0 0.8 copy-start.2
  237.8 0.7 copy-start.4
  238.5 17.6 %collective-permute-start.21 = (bf16[512,512]{1,0:T(8,128)(2,1)S(1)}, bf16[512,512]{1,0:T(8,128)(2,1)S(1)}, u32[]{:S(2)}, u32[]{:S(2)}) collective-permute-start(bf16[512,512]{1,0:T(8,128)(2,1)S(1)} %get-tuple-element.62), channel_id=1, source_target_pairs={{4,0},{5,1},{6,2},{7,3},{8,4},{9,5},{10,6},{11,7},{12,8},{13,9},{1... | collective-permute-start | bytes 1572872 | tf_op jit(solution)/shard_map/ppermute | solution.py:255
  239.8 16.8 %collective-permute-start.23 = (bf16[512,512]{1,0:T(8,128)(2,1)S(1)}, bf16[512,512]{1,0:T(8,128)(2,1)S(1)}, u32[]{:S(2)}, u32[]{:S(2)}) collective-permute-start(bf16[512,512]{1,0:T(8,128)(2,1)S(1)} %get-tuple-element.64), channel_id=1, source_target_pairs={{0,2},{1,3},{2,0},{3,1},{4,6},{5,7},{6,4},{7,5},{8,10},{9,11},{10,... | collective-permute-start | bytes 1572872 | tf_op jit(solution)/shard_map/ppermute | solution.py:255
  239.9 26.5 %copy-start.6 = (bf16[512,512]{1,0:T(8,128)(2,1)}, bf16[512,512]{1,0:T(8,128)(2,1)S(1)}, u32[]{:S(2)}) copy-start(bf16[512,512]{1,0:T(8,128)(2,1)S(1)} %collective-permute-done.22) | copy-start | bytes 1572868
  239.9 26.5 %collective-permute-start.25 = (bf16[512,512]{1,0:T(8,128)(2,1)S(1)}, bf16[512,512]{1,0:T(8,128)(2,1)S(1)}, u32[]{:S(2)}, u32[]{:S(2)}) collective-permute-start(bf16[512,512]{1,0:T(8,128)(2,1)S(1)} %get-tuple-element.66), channel_id=1, source_target_pairs={{4,2},{5,3},{6,0},{7,1},{8,6},{9,7},{10,4},{11,5},{12,10},{13,11},... | collective-permute-start | bytes 1572872 | tf_op jit(solution)/shard_map/ppermute | solution.py:255
  241.4 25.1 %copy-start.7 = (bf16[512,512]{1,0:T(8,128)(2,1)}, bf16[512,512]{1,0:T(8,128)(2,1)S(1)}, u32[]{:S(2)}) copy-start(bf16[512,512]{1,0:T(8,128)(2,1)S(1)} %collective-permute-done.24) | copy-start | bytes 1572868
  241.4 51.9 %collective-permute-start.16 = (bf16[256,512]{1,0:T(8,128)(2,1)S(1)}, bf16[256,512]{1,0:T(8,128)(2,1)S(1)}, u32[]{:S(2)}, u32[]{:S(2)}) collective-permute-start(bf16[256,512]{1,0:T(8,128)(2,1)S(1)} %get-tuple-element.51), channel_id=1, source_target_pairs={{0,1},{1,0},{2,3},{3,2},{4,5},{5,4},{6,7},{7,6},{8,9},{9,8},{10,11... | collective-permute-start | bytes 786440 | tf_op jit(solution)/shard_map/ppermute | solution.py:255
  243.2 23.3 %copy-start.8 = (bf16[512,512]{1,0:T(8,128)(2,1)}, bf16[512,512]{1,0:T(8,128)(2,1)S(1)}, u32[]{:S(2)}) copy-start(bf16[512,512]{1,0:T(8,128)(2,1)S(1)} %collective-permute-done.26) | copy-start | bytes 1572868
  243.2 51.8 %collective-permute-start.17 = (bf16[256,512]{1,0:T(8,128)(2,1)S(1)}, bf16[256,512]{1,0:T(8,128)(2,1)}, u32[]{:S(2)}, u32[]{:S(2)}) collective-permute-start(bf16[256,512]{1,0:T(8,128)(2,1)S(1)} %get-tuple-element.52), channel_id=1, source_target_pairs={{0,2},{1,3},{2,0},{3,1},{4,6},{5,7},{6,4},{7,5},{8,10},{9,11},{10,... | collective-permute-start | bytes 786440 | tf_op jit(solution)/shard_map/ppermute | solution.py:255
  256.1 10.3 %copy-start.9 = (bf16[512,512]{1,0:T(8,128)(2,1)}, bf16[512,512]{1,0:T(8,128)(2,1)S(1)}, u32[]{:S(2)}) copy-start(bf16[512,512]{1,0:T(8,128)(2,1)S(1)} %collective-permute-done.21) | copy-start | bytes 1572868
  256.1 38.9 %collective-permute-start.18 = (bf16[256,512]{1,0:T(8,128)(2,1)S(1)}, bf16[256,512]{1,0:T(8,128)(2,1)}, u32[]{:S(2)}, u32[]{:S(2)}) collective-permute-start(bf16[256,512]{1,0:T(8,128)(2,1)S(1)} %get-tuple-element.53), channel_id=1, source_target_pairs={{0,3},{1,2},{2,1},{3,0},{4,7},{5,6},{6,5},{7,4},{8,11},{9,10},{10,... | collective-permute-start | bytes 786440 | tf_op jit(solution)/shard_map/ppermute | solution.py:255
  256.6 9.9 %copy-start.10 = (bf16[512,512]{1,0:T(8,128)(2,1)}, bf16[512,512]{1,0:T(8,128)(2,1)S(1)}, u32[]{:S(2)}) copy-start(bf16[512,512]{1,0:T(8,128)(2,1)S(1)} %collective-permute-done.23) | copy-start | bytes 1572868
  256.6 50.2 %collective-permute-start.20 = (bf16[512,512]{1,0:T(8,128)(2,1)S(1)}, bf16[512,512]{1,0:T(8,128)(2,1)}, u32[]{:S(2)}, u32[]{:S(2)}) collective-permute-start(bf16[512,512]{1,0:T(8,128)(2,1)S(1)} %get-tuple-element.57), channel_id=1, source_target_pairs={{0,2},{1,3},{2,0},{3,1},{4,6},{5,7},{6,4},{7,5},{8,10},{9,11},{10,... | collective-permute-start | bytes 1572872 | tf_op jit(solution)/shard_map/ppermute | solution.py:255
  266.5 0.8 copy-start.11
  267.3 39.5 %collective-permute-start.19 = (bf16[512,512]{1,0:T(8,128)(2,1)S(1)}, bf16[512,512]{1,0:T(8,128)(2,1)}, u32[]{:S(2)}, u32[]{:S(2)}) collective-permute-start(bf16[512,512]{1,0:T(8,128)(2,1)S(1)} %get-tuple-element.55), channel_id=1, source_target_pairs={{0,2},{1,3},{2,0},{3,1},{4,6},{5,7},{6,4},{7,5},{8,10},{9,11},{10,... | collective-permute-start | bytes 1572872 | tf_op jit(solution)/shard_map/ppermute | solution.py:255
  293.3 5.3 %copy-start.12 = (bf16[256,512]{1,0:T(8,128)(2,1)}, bf16[256,512]{1,0:T(8,128)(2,1)S(1)}, u32[]{:S(2)}) copy-start(bf16[256,512]{1,0:T(8,128)(2,1)S(1)} %collective-permute-done.16.refs_5_) | copy-start | bytes 786436
  293.3 10.0 %collective-permute-start.8 = (bf16[256,512]{1,0:T(8,128)(2,1)S(1)}, bf16[256,512]{1,0:T(8,128)(2,1)S(1)}, u32[]{:S(2)}, u32[]{:S(2)}) collective-permute-start(bf16[256,512]{1,0:T(8,128)(2,1)S(1)} %get-tuple-element.42), channel_id=1, source_target_pairs={{0,1},{1,0},{2,3},{3,2},{4,5},{5,4},{6,7},{7,6},{8,9},{9,8},{10,11... | collective-permute-start | bytes 786440 | tf_op jit(solution)/shard_map/ppermute | solution.py:255
  295.0 8.4 %collective-permute-start.9 = (bf16[256,512]{1,0:T(8,128)(2,1)S(1)}, bf16[256,512]{1,0:T(8,128)(2,1)}, u32[]{:S(2)}, u32[]{:S(2)}) collective-permute-start(bf16[256,512]{1,0:T(8,128)(2,1)S(1)} %get-tuple-element.43), channel_id=1, source_target_pairs={{0,2},{1,3},{2,0},{3,1},{4,6},{5,7},{6,4},{7,5},{8,10},{9,11},{10,... | collective-permute-start | bytes 786440 | tf_op jit(solution)/shard_map/ppermute | solution.py:255
  295.0 11.8 %collective-permute-start.10 = (bf16[256,512]{1,0:T(8,128)(2,1)S(1)}, bf16[256,512]{1,0:T(8,128)(2,1)}, u32[]{:S(2)}, u32[]{:S(2)}) collective-permute-start(bf16[256,512]{1,0:T(8,128)(2,1)S(1)} %get-tuple-element.44), channel_id=1, source_target_pairs={{0,3},{1,2},{2,1},{3,0},{4,7},{5,6},{6,5},{7,4},{8,11},{9,10},{10,... | collective-permute-start | bytes 786440 | tf_op jit(solution)/shard_map/ppermute | solution.py:255
  303.4 3.5 copy-start.13

commit v2 on v1

--- a/solution.py
+++ b/solution.py
@@ -38,34 +38,139 @@
     return out
 
 
-def copies_kernel(plan, n_in, sc_ref, *refs):
-    sem = refs[-1]
-    jobs = []
-    for src, src_at, dst, dst_at, rows, cols in plan(sc_ref[0], sc_ref[1]):
-        jobs.append(
-            pltpu.make_async_copy(
-                refs[src].at[pl.ds(0, rows), pl.ds(src_at, cols)],
-                refs[n_in + dst].at[pl.ds(0, rows), pl.ds(dst_at, cols)],
-                sem.at[len(jobs)],
-            )
-        )
-    for job in jobs:
-        job.start()
-    for job in jobs:
-        job.wait()
-
-
-def run_copies(plan, place, arrays, outs, count):
-    hbm = pl.BlockSpec(memory_space=pl.ANY)
+def pack_halo_kernel(sc_ref, k_same, v_same, k_oth, v_oth, same, oth):
+    same[:, :HEAD] = k_same[...]
+    same[:, HEAD:] = v_same[...]
+    oth[:, :HEAD] = k_oth[...]
+    oth[:, HEAD:] = v_oth[...]
+
+
+def pack_halo(place, keys, values, chunk, heads_core, heads_chunk):
+    rows, pair = keys.shape[0], 2 * HEAD
+
+    def at_half(side):
+        def index(g, sc):
+            half = sc[0] if side == 0 else 1 - sc[0]
+            return (0, half * heads_core + chunk * heads_chunk + g)
+
+        return index
+
+    return pl.pallas_call(
+        pack_halo_kernel,
+        grid_spec=pltpu.PrefetchScalarGridSpec(
+            num_scalar_prefetch=1,
+            grid=(heads_chunk,),
+            in_specs=[pl.BlockSpec((rows, HEAD), at_half(n // 2)) for n in range(4)],
+            out_specs=[pl.BlockSpec((rows, pair), lambda g, sc: (0, g))] * 2,
+        ),
+        out_shape=[jax.ShapeDtypeStruct((rows, heads_chunk * pair), keys.dtype)] * 2,
+        cost_estimate=pl.CostEstimate(
+            flops=0, bytes_accessed=8 * rows * heads_chunk * pair, transcendentals=0
+        ),
+        name="pack_halo",
+    )(place, keys, values, keys, values)
+
+
+def pack_grad_kernel(n, sc_ref, *refs):
+    for at in range(n):
+        refs[n + at][...] = refs[at][...]
+
+
+def pack_grad(place, grad_out, chunk, heads_core, heads_chunk, n_mp, partners):
+    piece, pair = grad_out.shape[0], GROUP * HEAD
+
+    def at_partner(dk, dm):
+        def index(g, sc):
+            core = sc[0] if dk == 0 else 1 - sc[0]
+            mp = lax.rem(sc[1] + dm, n_mp)
+            return (0, (mp * 2 + core) * heads_core + chunk * heads_chunk + g)
+
+        return index
+
+    n = len(partners)
+    return pl.pallas_call(
+        functools.partial(pack_grad_kernel, n),
+        grid_spec=pltpu.PrefetchScalarGridSpec(
+            num_scalar_prefetch=1,
+            grid=(heads_chunk,),
+            in_specs=[pl.BlockSpec((piece, pair), at_partner(*p)) for p in partners],
+            out_specs=[pl.BlockSpec((piece, pair), lambda g, sc: (0, g))] * n,
+        ),
+        out_shape=[jax.ShapeDtypeStruct((piece, heads_chunk * pair), grad_out.dtype)] * n,
+        cost_estimate=pl.CostEstimate(
+            flops=0, bytes_accessed=4 * n * piece * heads_chunk * pair, transcendentals=0
+        ),
+        name="pack_grad",
+    )(place, *[grad_out] * n)
+
+
+def place_kernel(jobs, n_in, sc_ref, *refs):
+    for src, dst, width, column in jobs:
+        col = pl.multiple_of(column(sc_ref[0], sc_ref[1]), HEAD)
+        refs[n_in + dst][:, pl.ds(col, width)] = refs[src][...]
+
+
+def place_columns(place, arrays, outs, jobs):
+    vmem = pl.BlockSpec(memory_space=pltpu.VMEM)
     moved = sum(math.prod(o.shape) * o.dtype.itemsize for o in outs)
     return pl.pallas_call(
-        functools.partial(copies_kernel, plan, len(arrays)),
-        in_specs=[pl.BlockSpec(memory_space=pltpu.SMEM)] + [hbm] * len(arrays),
-        out_specs=[hbm] * len(outs),
+        functools.partial(place_kernel, jobs, len(arrays)),
+        in_specs=[pl.BlockSpec(memory_space=pltpu.SMEM)] + [vmem] * len(arrays),
+        out_specs=[vmem] * len(outs),
         out_shape=outs,
-        scratch_shapes=[pltpu.SemaphoreType.DMA((count,))],
+        compiler_params=pltpu.CompilerParams(vmem_limit_bytes=32 * 1024 * 1024),
         cost_estimate=pl.CostEstimate(flops=0, bytes_accessed=2 * moved, transcendentals=0),
+        name="place_columns",
     )(place, *arrays)
+
+
+def sum_kernel(sc_ref, near_same, far_same, near_oth, far_oth, *refs):
+    dk, dv = refs[-2:]
+
+    @pl.when(pl.program_id(0) == 0)
+    def _():
+        total = near_same[...] + far_same[...].astype(jnp.float32)
+        dk[...] = total[:, :HEAD].astype(dk.dtype)
+        dv[...] = total[:, HEAD:].astype(dv.dtype)
+
+    @pl.when(pl.program_id(0) == 1)
+    def _():
+        total = near_oth[...].astype(jnp.float32) + far_oth[...].astype(jnp.float32)
+        dk[...] = total[:, :HEAD].astype(dk.dtype)
+        dv[...] = total[:, HEAD:].astype(dv.dtype)
+
+
+def sum_terms(place, chunk, heads_core, heads_chunk, terms, before):
+    rows, pair = terms[0].shape[0], 2 * HEAD
+    last = heads_chunk - 1
+
+    def at_same(side, g, sc):
+        return (0, jnp.where(side == 0, g, last))
+
+    def at_oth(side, g, sc):
+        return (0, jnp.where(side == 1, g, 0))
+
+    def at_out(side, g, sc):
+        half = jnp.where(side == 0, sc[0], 1 - sc[0])
+        return (0, half * heads_core + chunk * heads_chunk + g)
+
+    shape = jax.ShapeDtypeStruct((rows, 2 * heads_core * HEAD), jnp.bfloat16)
+    in_specs = [pl.BlockSpec((rows, pair), at) for at in (at_same, at_same, at_oth, at_oth)]
+    return pl.pallas_call(
+        sum_kernel,
+        grid_spec=pltpu.PrefetchScalarGridSpec(
+            num_scalar_prefetch=1,
+            grid=(2, heads_chunk),
+            in_specs=in_specs + [pl.BlockSpec(memory_space=pl.ANY)] * len(before),
+            out_specs=[pl.BlockSpec((rows, HEAD), at_out)] * 2,
+        ),
+        out_shape=[shape, shape],
+        input_output_aliases={5: 0, 6: 1} if before else {},
+        cost_estimate=pl.CostEstimate(
+            flops=0, bytes_accessed=14 * rows * heads_chunk * pair, transcendentals=0
+        ),
+        name="sum_terms",
+    )(place, *terms, *before)
 
 
 def attention_kernel(n_mp, rows, sc_ref, open_ref, lo_ref, *refs):
@@ -233,10 +338,6 @@
     )(place, opened, lo, *near, *halo, *grads)
 
 
-def sum_kernel(heads, sc_ref, *refs):
-    near, far, dk_out, dv_out = refs[0], refs[1], refs[2], refs[3]
-
-
 def body(queries, keys, values, grad_out, band_mask, segment_ids):
     n_ctx, n_mp = lax.axis_size("ctx"), lax.axis_size("mp")
     rows = queries.shape[0]
@@ -254,59 +355,20 @@
     def send(x, target):
         return lax.ppermute(x, AXES, routes(target, n_ctx, n_mp))
 
-    def plan_halo(core, mp):
-        jobs = []
-        for i in range(CHUNKS):
-            for side in range(2):
-                half = core if side == 0 else 1 - core
-                for g in range(heads_chunk):
-                    at = pl.multiple_of((half * heads_core + i * heads_chunk + g) * HEAD, HEAD)
-                    for which in range(2):
-                        jobs.append(
-                            (which, at, 2 * i + side, g * pair + which * HEAD, rows, HEAD)
-                        )
-        return jobs
-
-    halos = run_copies(
-        plan_halo,
-        place,
-        (keys, values),
-        [jax.ShapeDtypeStruct((rows, wide), bf)] * (2 * CHUNKS),
-        2 * CHUNKS * heads_chunk * 2,
-    )
     partners = [(dk, dm) for dk in range(2) for dm in range(n_mp)]
-
-    def plan_grad(core, mp):
-        jobs = []
-        for i in range(CHUNKS):
-            for at, (dk, dm) in enumerate(partners[1:]):
-                core_to = core if dk == 0 else 1 - core
-                mp_to = lax.rem(mp + dm, n_mp)
-                col = (mp_to * heads_mp + core_to * heads_core + i * heads_chunk) * pair
-                jobs.append(
-                    (0, pl.multiple_of(col, HEAD), i * (2 * n_mp - 1) + at, 0, piece, wide)
-                )
-        return jobs
-
-    sent_grads = run_copies(
-        plan_grad,
-        place,
-        (grad_out,),
-        [jax.ShapeDtypeStruct((piece, wide), bf)] * (CHUNKS * (2 * n_mp - 1)),
-        CHUNKS * (2 * n_mp - 1),
-    )
-
     halo_in, grads_in = [], []
     for i in range(CHUNKS):
+        halo_same, halo_oth = pack_halo(place, keys, values, i, heads_core, heads_chunk)
         halo_in.append(
             (
-                send(halos[2 * i], lambda c, m: (c + 2, m)),
-                send(halos[2 * i + 1], lambda c, m: ((c + 2) ^ 1, m)),
+                send(halo_same, lambda c, m: (c + 2, m)),
+                send(halo_oth, lambda c, m: ((c + 2) ^ 1, m)),
             )
         )
+        sent = pack_grad(place, grad_out, i, heads_core, heads_chunk, n_mp, partners[1:])
         grads_in.append(
             [
-                send(sent_grads[i * (2 * n_mp - 1) + at], lambda c, m: (c ^ dk, (m + dm) % n_mp))
+                send(sent[at], lambda c, m: (c ^ dk, (m + dm) % n_mp))
                 for at, (dk, dm) in enumerate(partners[1:])
             ]
         )
@@ -358,49 +420,44 @@
         near_parts.append((dkv_same, send(dkv_oth, swap)))
         far_parts.append((back_same, back_oth))
 
-    arrays = [x for part in out_parts for x in part] + [x for part in dq_parts for x in part]
-
-    def plan_out(core, mp):
-        jobs = []
-        for i in range(CHUNKS):
-            for at, (dk, dm) in enumerate(partners):
-                core_from = core if dk == 0 else 1 - core
-                mp_from = lax.rem(mp + n_mp - dm, n_mp)
-                col = (mp_from * heads_mp + core_from * heads_core + i * heads_chunk) * pair
-                jobs.append((i * 2 * n_mp + at, 0, 0, pl.multiple_of(col, HEAD), piece, wide))
-        for i in range(CHUNKS):
-            for side in range(2):
-                half = core if side == 0 else 1 - core
-                col = (half * heads_core + i * heads_chunk) * pair
-                src = CHUNKS * 2 * n_mp + 2 * i + side
-                jobs.append((src, 0, 1, pl.multiple_of(col, HEAD), rows, wide))
-        return jobs
-
-    attn_out, grad_queries = run_copies(
-        plan_out,
+    def out_column(chunk, dk, dm):
+        def column(core, mp):
+            core_from = core if dk == 0 else 1 - core
+            mp_from = lax.rem(mp + n_mp - dm, n_mp)
+            return ((mp_from * 2 + core_from) * heads_core + chunk * heads_chunk) * pair
+
+        return column
+
+    def query_column(chunk, side):
+        def column(core, mp):
+            half = core if side == 0 else 1 - core
+            return (half * heads_core + chunk * heads_chunk) * pair
+
+        return column
+
+    arrays, jobs = [], []
+    for i in range(CHUNKS):
+        for at, (dk, dm) in enumerate(partners):
+            jobs.append((len(arrays), 0, wide, out_column(i, dk, dm)))
+            arrays.append(out_parts[i][at])
+        for side in range(2):
+            jobs.append((len(arrays), 1, wide, query_column(i, side)))
+            arrays.append(dq_parts[i][side])
+    attn_out, grad_queries = place_columns(
         place,
         arrays,
         [
             jax.ShapeDtypeStruct((piece, n_mp * heads_mp * pair), bf),
             jax.ShapeDtypeStruct(queries.shape, bf),
         ],
-        len(arrays),
+        jobs,
     )
 
-    def halves(pairs):
-        same = jnp.concatenate([p[0].astype(jnp.float32) for p in pairs], axis=1)
-        oth = jnp.concatenate([p[1].astype(jnp.float32) for p in pairs], axis=1)
-        return same, oth
-
-    near_same, near_oth = halves(near_parts)
-    far_same, far_oth = halves(far_parts)
-    same, oth = near_same + far_same, near_oth + far_oth
-    low = jnp.where(core == 0, same, oth).astype(bf)
-    high = jnp.where(core == 0, oth, same).astype(bf)
-    both = jnp.concatenate([low, high], axis=1).reshape(rows, heads_mp, 2, HEAD)
-    grad_keys = both[:, :, 0].reshape(rows, heads_mp * HEAD)
-    grad_values = both[:, :, 1].reshape(rows, heads_mp * HEAD)
-    return attn_out, grad_queries, grad_keys, grad_values
+    grads_kv = ()
+    for i in range(CHUNKS):
+        terms = (near_parts[i][0], far_parts[i][0], near_parts[i][1], far_parts[i][1])
+        grads_kv = sum_terms(place, i, heads_core, heads_chunk, terms, grads_kv)
+    return attn_out, grad_queries, grads_kv[0], grads_kv[1]
 
 
 def solution(mesh):

time: 438 us -> 195 us (0.45)
  Pallas kernels: 313 us -> 93 us
  local copies, waits for them, and re-layouts: 33.5 us -> 3.61 us
  waiting for transfers between devices: 49.6 us -> 59.5 us
    pallas_call x3 -> x7, Pallas kernels: 244 us -> 24.3 us  [the longest x2 9.36 us: sum_terms(): pl.pallas_call(sum_kernel, grid_spec=pltpu.PrefetchScalarGridSpec(num_sca...]
    concatenate x16 -> x0, local copies, waits for them, and re-layouts: 25.7 us -> none  [the longest x8 15.4 us: halves(): same = jnp.concatenate([p[0].astype(jnp.float32) for p in pairs], axis=1)]
    ppermute x27, waiting for transfers between devices: 49.6 us -> 59.5 us  [send(): return lax.ppermute(x, AXES, routes(target, n_ctx, n_mp))]
  transfers between devices with their start and end apart: 27 -> 27, of which waited for: 6 -> 8; matrix products, arithmetic and copies ran while one was open for 8% -> 1% of each run, Pallas kernels for 42% -> 46%
where the time goes in v2:
time: 195 us; the launch traced here: 193 us
  Pallas kernels  93 us (48%)
  waiting for transfers between devices  59.5 us (31%)
  starting transfers between devices  34.6 us (18%)
  local copies, waits for them, and re-layouts  3.61 us (2%)
    pallas_call x2, Pallas kernels, attention(): pl.pallas_call(functools.partial(attention_kernel, n_mp, rows), grid_spec...  68.7 us
    ppermute x27, waiting for transfers between devices, send(): return lax.ppermute(x, AXES, routes(target, n_ctx, n_mp))  59.5 us
    ppermute x27, starting transfers between devices, send(): return lax.ppermute(x, AXES, routes(target, n_ctx, n_mp))  34.6 us
    pallas_call x2, Pallas kernels, sum_terms(): pl.pallas_call(sum_kernel, grid_spec=pltpu.PrefetchScalarGridSpec(num_sca...  9.36 us
    pallas_call x2, Pallas kernels, pack_halo(): pl.pallas_call(pack_halo_kernel, grid_spec=pltpu.PrefetchScalarGridSpec(n...  5.93 us
    pallas_call x2, Pallas kernels, pack_grad(): pl.pallas_call(functools.partial(pack_grad_kernel, n), grid_spec=pltpu.Pr...  5.54 us
  transfers between devices with their start and end apart: 27, of which 8 were waited for; matrix products, arithmetic and copies ran while one was open for 1% of the time, Pallas kernels for 46%

profile of v2, /device:TPU:0, one launch (start us, length us, event | category | flops | bytes accessed | tf_op | source)
XLA Modules:
  0.0 193.3 jit_solution(16886127661359321240)
XLA Ops:
  0.6 0.0 copy-start
  0.6 0.5 collective-permute-start
  1.2 0.7 pad_add_fusion.sc_ref
  1.8 2.8 %pack_grad.2 = (bf16[256,512]{1,0:T(8,128)(2,1)}, bf16[256,512]{1,0:T(8,128)(2,1)}, bf16[256,512]{1,0:T(8,128)(2,1)}) custom-call(s32[2]{0:T(128)} %pad_add_fusion.sc_ref, bf16[256,4096]{1,0:T(8,128)(2,1)} %refs_8_.3, bf16[256,4096]{1,0:T(8,128)(2,1)} %refs_8_.3, bf16[256,4096]{1,0:T(8,128)(2,1)} %refs_8_.3), custom_call_target="tpu_custom_call" | custom-call | bytes 1572864 | tf_op jit(solution)/shard_map/pack_grad/pallas_call | solution.py:91
  4.7 2.5 %collective-permute-start.5 = (bf16[256,512]{1,0:T(8,128)(2,1)}, bf16[256,512]{1,0:T(8,128)(2,1)S(1)}, u32[]{:S(2)}, u32[]{:S(2)}) collective-permute-start(bf16[256,512]{1,0:T(8,128)(2,1)} %get-tuple-element.42), channel_id=1, source_target_pairs={{0,1},{1,0},{2,3},{3,2},{4,5},{5,4},{6,7},{7,6},{8,9},{9,8},{10,11... | collective-permute-start | bytes 786440 | tf_op jit(solution)/shard_map/ppermute | solution.py:356
  7.2 0.2 collective-permute-start.1
  7.4 0.3 collective-permute-start.2
  7.7 0.2 collective-permute-start.6
  7.9 6.4 %collective-permute-done.5.refs_9_ = bf16[256,512]{1,0:T(8,128)(2,1)S(1)} collective-permute-done((bf16[256,512]{1,0:T(8,128)(2,1)}, bf16[256,512]{1,0:T(8,128)(2,1)S(1)}, u32[]{:S(2)}, u32[]{:S(2)}) %collective-permute-start.5) | collective-permute-done | bytes 262176 | tf_op jit(solution)/shard_map/ppermute | solution.py:356
  14.3 1.1 collective-permute-start.7
  15.4 2.9 %pack_halo.2 = (bf16[512,512]{1,0:T(8,128)(2,1)}, bf16[512,512]{1,0:T(8,128)(2,1)}) custom-call(s32[2]{0:T(128)} %pad_add_fusion.sc_ref, bf16[512,1024]{1,0:T(8,128)(2,1)} %refs_2_.7, bf16[512,1024]{1,0:T(8,128)(2,1)} %refs_4_.3, bf16[512,1024]{1,0:T(8,128)(2,1)} %refs_2_.7, bf16[512,1024]{1,0:T(8,128)(2,1)} %refs_4_.3), custom_call_target="tpu_custom_call" | custom-call | bytes 2097152 | tf_op jit(solution)/shard_map/pack_halo/pallas_call | solution.py:58
  18.3 2.7 %pack_grad.3 = (bf16[256,512]{1,0:T(8,128)(2,1)}, bf16[256,512]{1,0:T(8,128)(2,1)}, bf16[256,512]{1,0:T(8,128)(2,1)}) custom-call(s32[2]{0:T(128)} %pad_add_fusion.sc_ref, bf16[256,4096]{1,0:T(8,128)(2,1)} %refs_8_.3, bf16[256,4096]{1,0:T(8,128)(2,1)} %refs_8_.3, bf16[256,4096]{1,0:T(8,128)(2,1)} %refs_8_.3), custom_call_target="tpu_custom_call" | custom-call | bytes 1572864 | tf_op jit(solution)/shard_map/pack_grad/pallas_call | solution.py:91
  21.0 3.0 %pack_halo.3 = (bf16[512,512]{1,0:T(8,128)(2,1)}, bf16[512,512]{1,0:T(8,128)(2,1)}) custom-call(s32[2]{0:T(128)} %pad_add_fusion.sc_ref, bf16[512,1024]{1,0:T(8,128)(2,1)} %refs_2_.7, bf16[512,1024]{1,0:T(8,128)(2,1)} %refs_4_.3, bf16[512,1024]{1,0:T(8,128)(2,1)} %refs_2_.7, bf16[512,1024]{1,0:T(8,128)(2,1)} %refs_4_.3), custom_call_target="tpu_custom_call" | custom-call | bytes 2097152 | tf_op jit(solution)/shard_map/pack_halo/pallas_call | solution.py:58
  24.1 0.1 constant_dynamic-slice_fusion
  24.2 0.1 copy.13
  24.2 0.1 reshape.27.open_ref
  24.3 0.0 collective-permute-done.6.refs_10_
  24.3 0.0 copy-start.3
  24.4 0.7 copy-done.3
  25.1 3.4 %collective-permute-start.3 = (bf16[512,512]{1,0:T(8,128)(2,1)S(1)}, bf16[512,512]{1,0:T(8,128)(2,1)S(1)}, u32[]{:S(2)}, u32[]{:S(2)}) collective-permute-start(bf16[512,512]{1,0:T(8,128)(2,1)S(1)} %copy-done.16), channel_id=1, source_target_pairs={{0,4},{1,5},{2,6},{3,7},{4,8},{5,9},{6,10},{7,11},{8,12},{9,13},{1... | collective-permute-start | bytes 1572872 | tf_op jit(solution)/shard_map/ppermute | solution.py:356
  28.5 0.0 collective-permute-done.7.refs_11_
  28.5 0.0 copy-start.5
  28.5 0.7 copy-done.5
  29.2 3.5 %collective-permute-start.4 = (bf16[512,512]{1,0:T(8,128)(2,1)S(1)}, bf16[512,512]{1,0:T(8,128)(2,1)S(1)}, u32[]{:S(2)}, u32[]{:S(2)}) collective-permute-start(bf16[512,512]{1,0:T(8,128)(2,1)S(1)} %copy-done.15), channel_id=1, source_target_pairs={{0,6},{1,7},{2,4},{3,5},{4,10},{5,11},{6,8},{7,9},{8,14},{9,15},{1... | collective-permute-start | bytes 1572872 | tf_op jit(solution)/shard_map/ppermute | solution.py:356
  32.8 1.0 convert_reduce_fusion
  33.8 7.0 %collective-permute-done.3.refs_6_ = bf16[512,512]{1,0:T(8,128)(2,1)S(1)} collective-permute-done((bf16[512,512]{1,0:T(8,128)(2,1)S(1)}, bf16[512,512]{1,0:T(8,128)(2,1)S(1)}, u32[]{:S(2)}, u32[]{:S(2)}) %collective-permute-start.3) | collective-permute-done | bytes 524320 | tf_op jit(solution)/shard_map/ppermute | solution.py:356
  40.8 0.7 collective-permute-start.14
  41.5 10.4 %collective-permute-done.4.refs_7_ = bf16[512,512]{1,0:T(8,128)(2,1)S(1)} collective-permute-done((bf16[512,512]{1,0:T(8,128)(2,1)S(1)}, bf16[512,512]{1,0:T(8,128)(2,1)S(1)}, u32[]{:S(2)}, u32[]{:S(2)}) %collective-permute-start.4) | collective-permute-done | bytes 524320 | tf_op jit(solution)/shard_map/ppermute | solution.py:356
  51.9 0.7 collective-permute-start.16
  52.5 4.1 %collective-permute-start.12 = (bf16[512,512]{1,0:T(8,128)(2,1)}, bf16[512,512]{1,0:T(8,128)(2,1)S(1)}, u32[]{:S(2)}, u32[]{:S(2)}) collective-permute-start(bf16[512,512]{1,0:T(8,128)(2,1)} %get-tuple-element.51), channel_id=1, source_target_pairs={{0,4},{1,5},{2,6},{3,7},{4,8},{5,9},{6,10},{7,11},{8,12},{9,13},{1... | collective-permute-start | bytes 1572872 | tf_op jit(solution)/shard_map/ppermute | solution.py:356
  56.6 0.0 collective-permute-done.refs_1_
  56.6 3.8 %collective-permute-start.13 = (bf16[512,512]{1,0:T(8,128)(2,1)}, bf16[512,512]{1,0:T(8,128)(2,1)S(1)}, u32[]{:S(2)}, u32[]{:S(2)}) collective-permute-start(bf16[512,512]{1,0:T(8,128)(2,1)} %get-tuple-element.52), channel_id=1, source_target_pairs={{0,6},{1,7},{2,4},{3,5},{4,10},{5,11},{6,8},{7,9},{8,14},{9,15},{1... | collective-permute-start | bytes 1572872 | tf_op jit(solution)/shard_map/ppermute | solution.py:356
  60.4 0.0 copy-start.4
  60.4 0.9 copy-done.4
  61.4 0.9 copy-done.6
  62.3 34.3 %attention.2 = (bf16[256,512]{1,0:T(8,128)(2,1)S(1)}, bf16[256,512]{1,0:T(8,128)(2,1)}, bf16[256,512]{1,0:T(8,128)(2,1)}, bf16[256,512]{1,0:T(8,128)(2,1)}, bf16...) custom-call(s32[2]{0:T(128)S(1)} %copy-done.1, ...), custom_call_target="tpu_custom_call" | custom-call | flops 7247757312 | bytes 6291456 | tf_op jit(solution)/shard_map/attention/pallas_call | solution.py:306
  96.7 1.3 collective-permute-start.24
  98.0 0.0 collective-permute-done.15.refs_10_
  98.0 0.0 collective-permute-done.16.refs_11_
  98.0 0.0 collective-permute-done.13.refs_7_
  98.0 34.3 %attention.3 = (bf16[256,512]{1,0:T(8,128)(2,1)S(1)}, bf16[256,512]{1,0:T(8,128)(2,1)S(1)}, bf16[256,512]{1,0:T(8,128)(2,1)S(1)}, bf16[256,512]{1,0:T(8,128)(2,1...) custom-call(s32[2]{0:T(128)S(1)} %copy-done.1, ...), custom_call_target="tpu_custom_call" | custom-call | flops 7247757312 | bytes 6291456 | tf_op jit(solution)/shard_map/attention/pallas_call | solution.py:306
  132.4 1.6 collective-permute-start.17
  134.0 0.4 collective-permute-start.18
  134.3 0.2 collective-permute-start.19
  134.5 0.3 collective-permute-start.25
  134.8 6.7 %collective-permute-done.17.refs_7_ = bf16[256,512]{1,0:T(8,128)(2,1)S(1)} collective-permute-done((bf16[256,512]{1,0:T(8,128)(2,1)S(1)}, bf16[256,512]{1,0:T(8,128)(2,1)S(1)}, u32[]{:S(2)}, u32[]{:S(2)}) %collective-permute-start.17) | collective-permute-done | bytes 262176 | tf_op jit(solution)/shard_map/ppermute | solution.py:356
  141.5 1.3 collective-permute-start.26
  142.8 1.3 collective-permute-start.21
  144.1 2.3 %collective-permute-done.19.refs_9_ = bf16[256,512]{1,0:T(8,128)(2,1)S(1)} collective-permute-done((bf16[256,512]{1,0:T(8,128)(2,1)S(1)}, bf16[256,512]{1,0:T(8,128)(2,1)S(1)}, u32[]{:S(2)}, u32[]{:S(2)}) %collective-permute-start.19) | collective-permute-done | bytes 262176 | tf_op jit(solution)/shard_map/ppermute | solution.py:356
  146.5 0.5 collective-permute-start.22
  146.9 1.3 collective-permute-start.23
  148.2 0.0 collective-permute-done.25.near_oth
  148.2 0.1 collective-permute-start.20
  148.4 8.1 %collective-permute-done.26.far_oth = bf16[512,512]{1,0:T(8,128)(2,1)S(1)} collective-permute-done((bf16[512,512]{1,0:T(8,128)(2,1)S(1)}, bf16[512,512]{1,0:T(8,128)(2,1)S(1)}, u32[]{:S(2)}, u32[]{:S(2)}) %collective-permute-start.26) | collective-permute-done | bytes 524320 | tf_op jit(solution)/shard_map/ppermute | solution.py:356
  156.5 2.2 %collective-permute-start.11 = (bf16[512,512]{1,0:T(8,128)(2,1)}, bf16[512,512]{1,0:T(8,128)(2,1)S(1)}, u32[]{:S(2)}, u32[]{:S(2)}) collective-permute-start(bf16[512,512]{1,0:T(8,128)(2,1)} %get-tuple-element.50), channel_id=1, source_target_pairs={{0,2},{1,3},{2,0},{3,1},{4,6},{5,7},{6,4},{7,5},{8,10},{9,11},{10,... | collective-permute-start | bytes 1572872 | tf_op jit(solution)/shard_map/ppermute | solution.py:356
  158.6 11.4 %collective-permute-done.21.far_same = bf16[512,512]{1,0:T(8,128)(2,1)S(1)} collective-permute-done((bf16[512,512]{1,0:T(8,128)(2,1)S(1)}, bf16[512,512]{1,0:T(8,128)(2,1)S(1)}, u32[]{:S(2)}, u32[]{:S(2)}) %collective-permute-start.21) | collective-permute-done | bytes 524320 | tf_op jit(solution)/shard_map/ppermute | solution.py:356
  170.1 1.7 collective-permute-start.8
  171.8 7.2 %collective-permute-done.23.far_oth = bf16[512,512]{1,0:T(8,128)(2,1)S(1)} collective-permute-done((bf16[512,512]{1,0:T(8,128)(2,1)S(1)}, bf16[512,512]{1,0:T(8,128)(2,1)S(1)}, u32[]{:S(2)}, u32[]{:S(2)}) %collective-permute-start.23) | collective-permute-done | bytes 524320 | tf_op jit(solution)/shard_map/ppermute | solution.py:356
  178.9 1.5 collective-permute-start.9
  180.4 4.6 %sum_terms.2 = (bf16[512,1024]{1,0:T(8,128)(2,1)}, bf16[512,1024]{1,0:T(8,128)(2,1)}) custom-call(s32[2]{0:T(128)} %pad_add_fusion.sc_ref, f32[512,512]{1,0:T(8,128)} %get-tuple-element.68.near_same, bf16[512,512]{1,0:T(8,128)(2,1)} %copy-done.11, bf16[512,512]{1,0:T(8,128)(2,1)} %copy-done.12, bf16[512,512]{1,0:T(8,128)(2,1)} %copy-done.13), custom_call_target="tpu_custom_call" | custom-call | bytes 3670016 | tf_op jit(solution)/shard_map/sum_terms/pallas_call | solution.py:159
  185.0 4.7 %sum_terms.3 = (bf16[512,1024]{1,0:T(8,128)(2,1)}, bf16[512,1024]{1,0:T(8,128)(2,1)}) custom-call(s32[2]{0:T(128)} %pad_add_fusion.sc_ref, f32[512,512]{1,0:T(8,128)} %get-tuple-element.64.near_same, bf16[512,512]{1,0:T(8,128)(2,1)} %copy-done.8, bf16[512,512]{1,0:T(8,128)(2,1)} %copy-done.9, ...), custom_call_target="tpu_custom_call", output_to_operand_aliasing={{0}: (5, {}), {1}: (6, {})} | custom-call | bytes 3670016 | tf_op jit(solution)/shard_map/sum_terms/pallas_call | solution.py:159
  189.8 0.0 collective-permute-done.10.refs_3_
  189.8 0.0 collective-permute-done.8.refs_1_
  189.8 3.5 %place_columns.1 = (bf16[256,4096]{1,0:T(8,128)(2,1)}, bf16[512,2048]{1,0:T(8,128)(2,1)}) custom-call(s32[2]{0:T(128)S(1)} %copy-done.2, bf16[256,512]{1,0:T(8,128)(2,1)S(1)} %get-tuple-element.45.refs_0_, bf16[256,512]{1,0:T(8,128)(2,1)} %collective-permute-done.8.refs_1_, bf16[256,512]{1,0:T(8,128)(2,1)} %collective-permute-done.9.refs_2_, ...), custom_call_target="tpu_custom_call" | custom-call | bytes 8388608 | tf_op jit(solution)/shard_map/place_columns/pallas_call | solution.py:116
  (45 shorter events, 0.1 us)
Async XLA Ops:
  0.6 23.4 %copy-start = (s32[64,9]{0,1:T(8,128)S(1)}, s32[64,9]{0,1:T(8,128)}, u32[]{:S(2)}) copy-start(s32[64,9]{0,1:T(8,128)} %param.10) | copy-start | bytes 6916
  0.6 56.0 %collective-permute-start = (bf16[512,2048]{1,0:T(8,128)(2,1)}, bf16[512,2048]{1,0:T(8,128)(2,1)}, u32[]{:S(2)}, u32[]{:S(2)}) collective-permute-start(bf16[512,2048]{1,0:T(8,128)(2,1)} %refs_0_.7), channel_id=1, source_target_pairs={{0,2},{1,3},{2,0},{3,1},{4,6},{5,7},{6,4},{7,5},{8,10},{9,11},{10,... | collective-permute-start | bytes 6291464 | tf_op jit(solution)/shard_map/ppermute | solution.py:356
  1.8 5.3 %copy-start.7 = (bf16[512,1024]{1,0:T(8,128)(2,1)S(1)}, bf16[512,1024]{1,0:T(8,128)(2,1)}, u32[]{:S(2)}) copy-start(bf16[512,1024]{1,0:T(8,128)(2,1)} %refs_2_.7) | copy-start | bytes 3145732
  4.7 9.7 %collective-permute-start.5 = (bf16[256,512]{1,0:T(8,128)(2,1)}, bf16[256,512]{1,0:T(8,128)(2,1)S(1)}, u32[]{:S(2)}, u32[]{:S(2)}) collective-permute-start(bf16[256,512]{1,0:T(8,128)(2,1)} %get-tuple-element.42), channel_id=1, source_target_pairs={{0,1},{1,0},{2,3},{3,2},{4,5},{5,4},{6,7},{7,6},{8,9},{9,8},{10,11... | collective-permute-start | bytes 786440 | tf_op jit(solution)/shard_map/ppermute | solution.py:356
  7.2 44.7 %collective-permute-start.1 = (bf16[512,1024]{1,0:T(8,128)(2,1)S(1)}, bf16[512,1024]{1,0:T(8,128)(2,1)}, u32[]{:S(2)}, u32[]{:S(2)}) collective-permute-start(bf16[512,1024]{1,0:T(8,128)(2,1)S(1)} %copy-done.7), channel_id=1, source_target_pairs={{0,2},{1,3},{2,0},{3,1},{4,6},{5,7},{6,4},{7,5},{8,10},{9,11},{10,... | collective-permute-start | bytes 3145736 | tf_op jit(solution)/shard_map/ppermute | solution.py:356
  7.4 45.1 %collective-permute-start.2 = (bf16[512,1024]{1,0:T(8,128)(2,1)}, bf16[512,1024]{1,0:T(8,128)(2,1)}, u32[]{:S(2)}, u32[]{:S(2)}) collective-permute-start(bf16[512,1024]{1,0:T(8,128)(2,1)} %refs_4_.3), channel_id=1, source_target_pairs={{0,2},{1,3},{2,0},{3,1},{4,6},{5,7},{6,4},{7,5},{8,10},{9,11},{10,... | collective-permute-start | bytes 3145736 | tf_op jit(solution)/shard_map/ppermute | solution.py:356
  7.7 16.7 %collective-permute-start.6 = (bf16[256,512]{1,0:T(8,128)(2,1)}, bf16[256,512]{1,0:T(8,128)(2,1)S(1)}, u32[]{:S(2)}, u32[]{:S(2)}) collective-permute-start(bf16[256,512]{1,0:T(8,128)(2,1)} %get-tuple-element.43), channel_id=1, source_target_pairs={{0,2},{1,3},{2,0},{3,1},{4,6},{5,7},{6,4},{7,5},{8,10},{9,11},{10,... | collective-permute-start | bytes 786440 | tf_op jit(solution)/shard_map/ppermute | solution.py:356
  14.3 14.2 %collective-permute-start.7 = (bf16[256,512]{1,0:T(8,128)(2,1)}, bf16[256,512]{1,0:T(8,128)(2,1)S(1)}, u32[]{:S(2)}, u32[]{:S(2)}) collective-permute-start(bf16[256,512]{1,0:T(8,128)(2,1)} %get-tuple-element.44), channel_id=1, source_target_pairs={{0,3},{1,2},{2,1},{3,0},{4,7},{5,6},{6,5},{7,4},{8,11},{9,10},{10,... | collective-permute-start | bytes 786440 | tf_op jit(solution)/shard_map/ppermute | solution.py:356
  21.0 3.3 %copy-start.14 = (s32[8192]{0:T(1024)S(1)}, s32[8192]{0:T(1024)}, u32[]{:S(2)}) copy-start(s32[8192]{0:T(1024)} %param.11) | copy-start | bytes 98308
  21.0 4.1 %copy-start.16 = (bf16[512,512]{1,0:T(8,128)(2,1)S(1)}, bf16[512,512]{1,0:T(8,128)(2,1)}, u32[]{:S(2)}) copy-start(bf16[512,512]{1,0:T(8,128)(2,1)} %get-tuple-element.40) | copy-start | bytes 1572868
  21.0 8.2 %copy-start.15 = (bf16[512,512]{1,0:T(8,128)(2,1)S(1)}, bf16[512,512]{1,0:T(8,128)(2,1)}, u32[]{:S(2)}) copy-start(bf16[512,512]{1,0:T(8,128)(2,1)} %get-tuple-element.41) | copy-start | bytes 1572868
  21.0 30.8 %copy-start.18 = (bf16[256,512]{1,0:T(8,128)(2,1)S(1)}, bf16[256,512]{1,0:T(8,128)(2,1)}, u32[]{:S(2)}) copy-start(bf16[256,512]{1,0:T(8,128)(2,1)} %get-tuple-element.54) | copy-start | bytes 786436
  21.0 30.8 %copy-start.17 = (bf16[256,512]{1,0:T(8,128)(2,1)S(1)}, bf16[256,512]{1,0:T(8,128)(2,1)}, u32[]{:S(2)}) copy-start(bf16[256,512]{1,0:T(8,128)(2,1)} %get-tuple-element.55) | copy-start | bytes 786436
  21.0 39.4 %copy-start.1 = (s32[2]{0:T(128)S(1)}, s32[2]{0:T(128)}, u32[]{:S(2)}) copy-start(s32[2]{0:T(128)} %pad_add_fusion.sc_ref) | copy-start | bytes 28
  24.3 0.7 copy-start.3
  25.1 15.7 %collective-permute-start.3 = (bf16[512,512]{1,0:T(8,128)(2,1)S(1)}, bf16[512,512]{1,0:T(8,128)(2,1)S(1)}, u32[]{:S(2)}, u32[]{:S(2)}) collective-permute-start(bf16[512,512]{1,0:T(8,128)(2,1)S(1)} %copy-done.16), channel_id=1, source_target_pairs={{0,4},{1,5},{2,6},{3,7},{4,8},{5,9},{6,10},{7,11},{8,12},{9,13},{1... | collective-permute-start | bytes 1572872 | tf_op jit(solution)/shard_map/ppermute | solution.py:356
  28.5 0.7 copy-start.5
  29.2 22.6 %collective-permute-start.4 = (bf16[512,512]{1,0:T(8,128)(2,1)S(1)}, bf16[512,512]{1,0:T(8,128)(2,1)S(1)}, u32[]{:S(2)}, u32[]{:S(2)}) collective-permute-start(bf16[512,512]{1,0:T(8,128)(2,1)S(1)} %copy-done.15), channel_id=1, source_target_pairs={{0,6},{1,7},{2,4},{3,5},{4,10},{5,11},{6,8},{7,9},{8,14},{9,15},{1... | collective-permute-start | bytes 1572872 | tf_op jit(solution)/shard_map/ppermute | solution.py:356
  40.8 55.9 %collective-permute-start.14 = (bf16[256,512]{1,0:T(8,128)(2,1)}, bf16[256,512]{1,0:T(8,128)(2,1)S(1)}, u32[]{:S(2)}, u32[]{:S(2)}) collective-permute-start(bf16[256,512]{1,0:T(8,128)(2,1)} %get-tuple-element.53), channel_id=1, source_target_pairs={{0,1},{1,0},{2,3},{3,2},{4,5},{5,4},{6,7},{7,6},{8,9},{9,8},{10,11... | collective-permute-start | bytes 786440 | tf_op jit(solution)/shard_map/ppermute | solution.py:356
  51.8 46.1 %collective-permute-start.15 = (bf16[256,512]{1,0:T(8,128)(2,1)S(1)}, bf16[256,512]{1,0:T(8,128)(2,1)S(1)}, u32[]{:S(2)}, u32[]{:S(2)}) collective-permute-start(bf16[256,512]{1,0:T(8,128)(2,1)S(1)} %copy-done.18), channel_id=1, source_target_pairs={{0,2},{1,3},{2,0},{3,1},{4,6},{5,7},{6,4},{7,5},{8,10},{9,11},{10,... | collective-permute-start | bytes 786440 | tf_op jit(solution)/shard_map/ppermute | solution.py:356
  51.9 46.1 %collective-permute-start.16 = (bf16[256,512]{1,0:T(8,128)(2,1)S(1)}, bf16[256,512]{1,0:T(8,128)(2,1)S(1)}, u32[]{:S(2)}, u32[]{:S(2)}) collective-permute-start(bf16[256,512]{1,0:T(8,128)(2,1)S(1)} %copy-done.17), channel_id=1, source_target_pairs={{0,3},{1,2},{2,1},{3,0},{4,7},{5,6},{6,5},{7,4},{8,11},{9,10},{10,... | collective-permute-start | bytes 786440 | tf_op jit(solution)/shard_map/ppermute | solution.py:356
  52.5 45.5 %collective-permute-start.12 = (bf16[512,512]{1,0:T(8,128)(2,1)}, bf16[512,512]{1,0:T(8,128)(2,1)S(1)}, u32[]{:S(2)}, u32[]{:S(2)}) collective-permute-start(bf16[512,512]{1,0:T(8,128)(2,1)} %get-tuple-element.51), channel_id=1, source_target_pairs={{0,4},{1,5},{2,6},{3,7},{4,8},{5,9},{6,10},{7,11},{8,12},{9,13},{1... | collective-permute-start | bytes 1572872 | tf_op jit(solution)/shard_map/ppermute | solution.py:356
  56.6 41.4 %collective-permute-start.13 = (bf16[512,512]{1,0:T(8,128)(2,1)}, bf16[512,512]{1,0:T(8,128)(2,1)S(1)}, u32[]{:S(2)}, u32[]{:S(2)}) collective-permute-start(bf16[512,512]{1,0:T(8,128)(2,1)} %get-tuple-element.52), channel_id=1, source_target_pairs={{0,6},{1,7},{2,4},{3,5},{4,10},{5,11},{6,8},{7,9},{8,14},{9,15},{1... | collective-permute-start | bytes 1572872 | tf_op jit(solution)/shard_map/ppermute | solution.py:356
  60.4 1.0 copy-start.4
  61.4 0.9 copy-start.6
  96.7 50.2 %collective-permute-start.24 = (bf16[512,512]{1,0:T(8,128)(2,1)S(1)}, bf16[512,512]{1,0:T(8,128)(2,1)S(1)}, u32[]{:S(2)}, u32[]{:S(2)}) collective-permute-start(bf16[512,512]{1,0:T(8,128)(2,1)S(1)} %get-tuple-element.69), channel_id=1, source_target_pairs={{4,0},{5,1},{6,2},{7,3},{8,4},{9,5},{10,6},{11,7},{12,8},{13,9},{1... | collective-permute-start | bytes 1572872 | tf_op jit(solution)/shard_map/ppermute | solution.py:356
  132.4 9.2 %collective-permute-start.17 = (bf16[256,512]{1,0:T(8,128)(2,1)S(1)}, bf16[256,512]{1,0:T(8,128)(2,1)S(1)}, u32[]{:S(2)}, u32[]{:S(2)}) collective-permute-start(bf16[256,512]{1,0:T(8,128)(2,1)S(1)} %get-tuple-element.57), channel_id=1, source_target_pairs={{0,1},{1,0},{2,3},{3,2},{4,5},{5,4},{6,7},{7,6},{8,9},{9,8},{10,11... | collective-permute-start | bytes 786440 | tf_op jit(solution)/shard_map/ppermute | solution.py:356
  134.0 8.8 %collective-permute-start.18 = (bf16[256,512]{1,0:T(8,128)(2,1)S(1)}, bf16[256,512]{1,0:T(8,128)(2,1)S(1)}, u32[]{:S(2)}, u32[]{:S(2)}) collective-permute-start(bf16[256,512]{1,0:T(8,128)(2,1)S(1)} %get-tuple-element.58), channel_id=1, source_target_pairs={{0,2},{1,3},{2,0},{3,1},{4,6},{5,7},{6,4},{7,5},{8,10},{9,11},{10,... | collective-permute-start | bytes 786440 | tf_op jit(solution)/shard_map/ppermute | solution.py:356
  134.3 12.1 %collective-permute-start.19 = (bf16[256,512]{1,0:T(8,128)(2,1)S(1)}, bf16[256,512]{1,0:T(8,128)(2,1)S(1)}, u32[]{:S(2)}, u32[]{:S(2)}) collective-permute-start(bf16[256,512]{1,0:T(8,128)(2,1)S(1)} %get-tuple-element.59), channel_id=1, source_target_pairs={{0,3},{1,2},{2,1},{3,0},{4,7},{5,6},{6,5},{7,4},{8,11},{9,10},{10,... | collective-permute-start | bytes 786440 | tf_op jit(solution)/shard_map/ppermute | solution.py:356
  134.5 13.7 %collective-permute-start.25 = (bf16[512,512]{1,0:T(8,128)(2,1)S(1)}, bf16[512,512]{1,0:T(8,128)(2,1)S(1)}, u32[]{:S(2)}, u32[]{:S(2)}) collective-permute-start(bf16[512,512]{1,0:T(8,128)(2,1)S(1)} %get-tuple-element.70), channel_id=1, source_target_pairs={{0,2},{1,3},{2,0},{3,1},{4,6},{5,7},{6,4},{7,5},{8,10},{9,11},{10,... | collective-permute-start | bytes 1572872 | tf_op jit(solution)/shard_map/ppermute | solution.py:356
  141.5 14.9 %collective-permute-start.26 = (bf16[512,512]{1,0:T(8,128)(2,1)S(1)}, bf16[512,512]{1,0:T(8,128)(2,1)S(1)}, u32[]{:S(2)}, u32[]{:S(2)}) collective-permute-start(bf16[512,512]{1,0:T(8,128)(2,1)S(1)} %get-tuple-element.71), channel_id=1, source_target_pairs={{4,2},{5,3},{6,0},{7,1},{8,6},{9,7},{10,4},{11,5},{12,10},{13,11},... | collective-permute-start | bytes 1572872 | tf_op jit(solution)/shard_map/ppermute | solution.py:356
  142.8 27.2 %collective-permute-start.21 = (bf16[512,512]{1,0:T(8,128)(2,1)S(1)}, bf16[512,512]{1,0:T(8,128)(2,1)S(1)}, u32[]{:S(2)}, u32[]{:S(2)}) collective-permute-start(bf16[512,512]{1,0:T(8,128)(2,1)S(1)} %get-tuple-element.65), channel_id=1, source_target_pairs={{4,0},{5,1},{6,2},{7,3},{8,4},{9,5},{10,6},{11,7},{12,8},{13,9},{1... | collective-permute-start | bytes 1572872 | tf_op jit(solution)/shard_map/ppermute | solution.py:356
  146.5 23.6 %collective-permute-start.22 = (bf16[512,512]{1,0:T(8,128)(2,1)S(1)}, bf16[512,512]{1,0:T(8,128)(2,1)S(1)}, u32[]{:S(2)}, u32[]{:S(2)}) collective-permute-start(bf16[512,512]{1,0:T(8,128)(2,1)S(1)} %get-tuple-element.66), channel_id=1, source_target_pairs={{0,2},{1,3},{2,0},{3,1},{4,6},{5,7},{6,4},{7,5},{8,10},{9,11},{10,... | collective-permute-start | bytes 1572872 | tf_op jit(solution)/shard_map/ppermute | solution.py:356
  146.9 33.5 %copy-start.11 = (bf16[512,512]{1,0:T(8,128)(2,1)}, bf16[512,512]{1,0:T(8,128)(2,1)S(1)}, u32[]{:S(2)}) copy-start(bf16[512,512]{1,0:T(8,128)(2,1)S(1)} %collective-permute-done.24.far_same) | copy-start | bytes 1572868
  146.9 32.0 %collective-permute-start.23 = (bf16[512,512]{1,0:T(8,128)(2,1)S(1)}, bf16[512,512]{1,0:T(8,128)(2,1)S(1)}, u32[]{:S(2)}, u32[]{:S(2)}) collective-permute-start(bf16[512,512]{1,0:T(8,128)(2,1)S(1)} %get-tuple-element.67), channel_id=1, source_target_pairs={{4,2},{5,3},{6,0},{7,1},{8,6},{9,7},{10,4},{11,5},{12,10},{13,11},... | collective-permute-start | bytes 1572872 | tf_op jit(solution)/shard_map/ppermute | solution.py:356
  148.2 32.2 %copy-start.12 = (bf16[512,512]{1,0:T(8,128)(2,1)}, bf16[512,512]{1,0:T(8,128)(2,1)S(1)}, u32[]{:S(2)}) copy-start(bf16[512,512]{1,0:T(8,128)(2,1)S(1)} %collective-permute-done.25.near_oth) | copy-start | bytes 1572868
  148.2 41.6 %collective-permute-start.20 = (bf16[512,512]{1,0:T(8,128)(2,1)}, bf16[512,512]{1,0:T(8,128)(2,1)S(1)}, u32[]{:S(2)}, u32[]{:S(2)}) collective-permute-start(bf16[512,512]{1,0:T(8,128)(2,1)} %get-tuple-element.61), channel_id=1, source_target_pairs={{0,2},{1,3},{2,0},{3,1},{4,6},{5,7},{6,4},{7,5},{8,10},{9,11},{10,... | collective-permute-start | bytes 1572872 | tf_op jit(solution)/shard_map/ppermute | solution.py:356
  156.5 23.9 %copy-start.13 = (bf16[512,512]{1,0:T(8,128)(2,1)}, bf16[512,512]{1,0:T(8,128)(2,1)S(1)}, u32[]{:S(2)}) copy-start(bf16[512,512]{1,0:T(8,128)(2,1)S(1)} %collective-permute-done.26.far_oth) | copy-start | bytes 1572868
  156.5 33.3 %collective-permute-start.11 = (bf16[512,512]{1,0:T(8,128)(2,1)}, bf16[512,512]{1,0:T(8,128)(2,1)S(1)}, u32[]{:S(2)}, u32[]{:S(2)}) collective-permute-start(bf16[512,512]{1,0:T(8,128)(2,1)} %get-tuple-element.50), channel_id=1, source_target_pairs={{0,2},{1,3},{2,0},{3,1},{4,6},{5,7},{6,4},{7,5},{8,10},{9,11},{10,... | collective-permute-start | bytes 1572872 | tf_op jit(solution)/shard_map/ppermute | solution.py:356
  170.1 8.9 %copy-start.8 = (bf16[512,512]{1,0:T(8,128)(2,1)}, bf16[512,512]{1,0:T(8,128)(2,1)S(1)}, u32[]{:S(2)}) copy-start(bf16[512,512]{1,0:T(8,128)(2,1)S(1)} %collective-permute-done.21.far_same) | copy-start | bytes 1572868
  170.1 19.7 %collective-permute-start.10 = (bf16[256,512]{1,0:T(8,128)(2,1)}, bf16[256,512]{1,0:T(8,128)(2,1)}, u32[]{:S(2)}, u32[]{:S(2)}) collective-permute-start(bf16[256,512]{1,0:T(8,128)(2,1)} %get-tuple-element.48), channel_id=1, source_target_pairs={{0,3},{1,2},{2,1},{3,0},{4,7},{5,6},{6,5},{7,4},{8,11},{9,10},{10,... | collective-permute-start | bytes 786440 | tf_op jit(solution)/shard_map/ppermute | solution.py:356
  170.1 8.9 %copy-start.9 = (bf16[512,512]{1,0:T(8,128)(2,1)}, bf16[512,512]{1,0:T(8,128)(2,1)S(1)}, u32[]{:S(2)}) copy-start(bf16[512,512]{1,0:T(8,128)(2,1)S(1)} %collective-permute-done.22.near_oth) | copy-start | bytes 1572868
  170.1 19.7 %collective-permute-start.8 = (bf16[256,512]{1,0:T(8,128)(2,1)}, bf16[256,512]{1,0:T(8,128)(2,1)}, u32[]{:S(2)}, u32[]{:S(2)}) collective-permute-start(bf16[256,512]{1,0:T(8,128)(2,1)} %get-tuple-element.46), channel_id=1, source_target_pairs={{0,1},{1,0},{2,3},{3,2},{4,5},{5,4},{6,7},{7,6},{8,9},{9,8},{10,11... | collective-permute-start | bytes 786440 | tf_op jit(solution)/shard_map/ppermute | solution.py:356
  178.9 1.5 copy-start.10
  178.9 10.9 %collective-permute-start.9 = (bf16[256,512]{1,0:T(8,128)(2,1)}, bf16[256,512]{1,0:T(8,128)(2,1)}, u32[]{:S(2)}, u32[]{:S(2)}) collective-permute-start(bf16[256,512]{1,0:T(8,128)(2,1)} %get-tuple-element.47), channel_id=1, source_target_pairs={{0,2},{1,3},{2,0},{3,1},{4,6},{5,7},{6,4},{7,5},{8,10},{9,11},{10,... | collective-permute-start | bytes 786440 | tf_op jit(solution)/shard_map/ppermute | solution.py:356
  185.0 4.8 %copy-start.2 = (s32[2]{0:T(128)S(1)}, s32[2]{0:T(128)}, u32[]{:S(2)}) copy-start(s32[2]{0:T(128)} %pad_add_fusion.sc_ref) | copy-start | bytes 28

commit v3 on v2

v3 whole, which is shorter than its diff:
```python
import functools
import math

import jax
import jax.numpy as jnp
from jax import lax
from jax.experimental import pallas as pl
from jax.experimental.pallas import tpu as pltpu
from jax.sharding import PartitionSpec as P

KV_HEADS = 16
GROUP = 2
HEAD = 128
WINDOW = 1024
BLOCK = 128
SPAN = WINDOW // BLOCK + 1
CHUNKS = 2
ATTN_SCALE = 168.0 ** (-0.5)
EXP2_SCALE = ATTN_SCALE * math.log2(math.e)
MASKED = -1e30
FAR = 1 << 20
AXES = ("ctx", "mp")
NT = (((1,), (1,)), ((), ()))
NN = (((1,), (0,)), ((), ()))
LIGHT = pl.CostEstimate(flops=0, bytes_accessed=1024, transcendentals=0)
HEAVY = pl.CostEstimate(flops=25_000_000_000, bytes_accessed=1024, transcendentals=0)


def dot(a, b, dims=NN):
    return lax.dot_general(a, b, dims, preferred_element_type=jnp.float32)


def routes(target, n_ctx, n_mp):
    out = []
    for c in range(n_ctx):
        for m in range(n_mp):
            d = target(c, m)
            if 0 <= d[0] < n_ctx:
                out.append((c * n_mp + m, d[0] * n_mp + d[1]))
    return out


def pack_kernel(joins, n_after, sc_ref, *refs):
    outs = refs[sum(n for n, _ in joins) + n_after :]
    at = 0
    for out, (n, axis) in zip(outs, joins):
        out[...] = jnp.concatenate([ref[...] for ref in refs[at : at + n]], axis=axis)
        at += n


def pack(place, steps, inputs, outputs, after=(), name="pack"):
    flat = [i for group in inputs for i in group]
    joins = [(len(group), out[3]) for group, out in zip(inputs, outputs)]
    hbm = pl.BlockSpec(memory_space=pl.ANY)
    return pl.pallas_call(
        functools.partial(pack_kernel, joins, len(after)),
        grid_spec=pltpu.PrefetchScalarGridSpec(
            num_scalar_prefetch=1,
            grid=(steps,),
            in_specs=[pl.BlockSpec(i[1], i[2]) for i in flat] + [hbm] * len(after),
            out_specs=[pl.BlockSpec(o[1], o[2]) for o in outputs],
        ),
        out_shape=[jax.ShapeDtypeStruct(o[0], jnp.bfloat16) for o in outputs],
        cost_estimate=LIGHT,
        name=name,
    )(place, *[i[0] for i in flat], *after)


def place_kernel(jobs, n_in, sc_ref, *refs):
    for src, rows, src_col, dst, width, column in jobs:
        col = pl.multiple_of(column(sc_ref[0], sc_ref[1]), HEAD)
        at = pl.ds(pl.multiple_of(sc_ref[1] * rows, rows), rows) if rows else slice(None)
        refs[n_in + dst][:, pl.ds(col, width)] = refs[src][at, src_col : src_col + width]


def place_columns(place, arrays, outs, jobs):
    vmem = pl.BlockSpec(memory_space=pltpu.VMEM)
    moved = sum(math.prod(o.shape) * o.dtype.itemsize for o in outs)
    return pl.pallas_call(
        functools.partial(place_kernel, jobs, len(arrays)),
        in_specs=[pl.BlockSpec(memory_space=pltpu.SMEM)] + [vmem] * len(arrays),
        out_specs=[vmem] * len(outs),
        out_shape=outs,
        compiler_params=pltpu.CompilerParams(vmem_limit_bytes=32 * 1024 * 1024),
        cost_estimate=LIGHT,
        name="place_columns",
    )(place, *arrays)


def sum_kernel(sc_ref, near_same, far_same, near_oth, far_oth, *refs):
    dk, dv = refs[-2:]

    @pl.when(pl.program_id(0) == 0)
    def _():
        total = near_same[...] + far_same[...].astype(jnp.float32)
        dk[...] = total[:, :HEAD].astype(dk.dtype)
        dv[...] = total[:, HEAD:].astype(dv.dtype)

    @pl.when(pl.program_id(0) == 1)
    def _():
        total = near_oth[...].astype(jnp.float32) + far_oth[...].astype(jnp.float32)
        dk[...] = total[:, :HEAD].astype(dk.dtype)
        dv[...] = total[:, HEAD:].astype(dv.dtype)


def sum_terms(place, chunk, heads_core, heads_chunk, terms, before, after=()):
    rows, pair = terms[0].shape[0], 2 * HEAD
    last = heads_chunk - 1

    def at_same(side, g, sc):
        return (0, jnp.where(side == 0, g, last))

    def at_oth(side, g, sc):
        return (0, jnp.where(side == 1, g, 0))

    def at_across(side, g, sc):
        return (0, 3 * jnp.where(side == 1, g, 0) + 1)

    def at_out(side, g, sc):
        half = jnp.where(side == 0, sc[0], 1 - sc[0])
        return (0, half * heads_core + chunk * heads_chunk + g)

    shape = jax.ShapeDtypeStruct((rows, 2 * heads_core * HEAD), jnp.bfloat16)
    in_specs = [pl.BlockSpec((rows, pair), at) for at in (at_same, at_same, at_across, at_oth)]
    return pl.pallas_call(
        sum_kernel,
        grid_spec=pltpu.PrefetchScalarGridSpec(
            num_scalar_prefetch=1,
            grid=(2, heads_chunk),
            in_specs=in_specs + [pl.BlockSpec(memory_space=pl.ANY)] * len((*before, *after)),
            out_specs=[pl.BlockSpec((rows, HEAD), at_out)] * 2,
        ),
        out_shape=[shape, shape],
        input_output_aliases={5: 0, 6: 1} if before else {},
        cost_estimate=LIGHT,
        name="sum_terms",
    )(place, *terms, *before, *after)


def attention_kernel(n_mp, rows, sc_ref, open_ref, lo_ref, *refs):
    q_own, k_own, v_own, near, h_same, h_oth, do_own, do_oth = refs[:8]
    do_far = refs[8 : 7 + n_mp]
    refs = refs[7 + n_mp :]
    dq_same, dkv_same, dh_same, dh_oth, across, o_own = refs[:6]
    o_far = refs[6 : 4 + 2 * n_mp]
    qs, ks, vs, k_t, v_t, dos, os, dqs, dk, dv, s_ref, e_ref = refs[4 + 2 * n_mp :]
    core, mp = sc_ref[0], sc_ref[1]
    piece, pair = rows // n_mp, GROUP * HEAD
    same = pl.ds(pl.multiple_of(core * rows, rows), rows)
    oth = pl.ds(pl.multiple_of((1 - core) * rows, rows), rows)
    same_kv = pl.ds(pl.multiple_of(WINDOW + core * rows, rows), rows)
    oth_kv = pl.ds(pl.multiple_of(WINDOW + (1 - core) * rows, rows), rows)

    def piece_at(dk_, dm):
        k_at = core if dk_ == 0 else 1 - core
        return pl.ds(pl.multiple_of(k_at * rows + lax.rem(mp + dm, n_mp) * piece, piece), piece)

    qs[same, :] = q_own[...]
    qs[oth, :] = near[:, :pair]
    ks[same, :] = h_same[:, :HEAD]
    ks[oth, :] = h_oth[:, :HEAD]
    ks[same_kv, :] = k_own[...]
    ks[oth_kv, :] = near[:, pair : pair + HEAD]
    vs[same, :] = h_same[:, HEAD:]
    vs[oth, :] = h_oth[:, HEAD:]
    vs[same_kv, :] = v_own[...]
    vs[oth_kv, :] = near[:, pair + HEAD :]
    dos[piece_at(0, 0), :] = do_own[...]
    dos[piece_at(1, 0), :] = do_oth[...]
    for at in range(n_mp - 1):
        dos[piece_at(0, n_mp - 1 - at), :] = do_far[at][:piece, :]
        dos[piece_at(1, n_mp - 1 - at), :] = do_far[at][piece:, :]
    dk[...] = jnp.zeros_like(dk)
    dv[...] = jnp.zeros_like(dv)
    for t in range(ks.shape[0] // 256):
        at = slice(t * 256, t * 256 + 256)
        k_t[:, at] = ks[at, :].T
        v_t[:, at] = vs[at, :].T

    row = lax.broadcasted_iota(jnp.int32, (BLOCK, GROUP * BLOCK), 0)
    lane = lax.broadcasted_iota(jnp.int32, (BLOCK, GROUP * BLOCK), 1)
    causal = row <= lax.rem(lane, BLOCK)

    def block(b, carry):
        at_q = pl.ds(pl.multiple_of(b * BLOCK, BLOCK), BLOCK)
        q_blk = jnp.concatenate([qs[at_q, :HEAD], qs[at_q, HEAD:]], axis=0)
        lo = lo_ref[:, at_q]
        lo = jnp.concatenate([lo, lo], axis=1)
        top = jnp.full((8, GROUP * BLOCK), MASKED, jnp.float32)
        for j in range(SPAN):
            k_at = pl.ds(pl.multiple_of((b + j) * BLOCK, BLOCK), BLOCK)
            part = slice(j * BLOCK, j * BLOCK + BLOCK)
            s = dot(ks[k_at, :], q_blk, NT)
            closed = jnp.where(open_ref[b * SPAN + SPAN - 1 - j] == 1, 0, FAR)
            valid = row >= jnp.maximum(lo - (b + j) * BLOCK, closed)
            if j == SPAN - 1:
                valid = valid & causal
            s = jnp.where(valid, s, MASKED)
            s_ref[part, :] = s
            top = jnp.maximum(top, jnp.max(s.reshape(BLOCK // 8, 8, GROUP * BLOCK), axis=0))
        top = jnp.max(top, axis=0, keepdims=True)
        total = jnp.zeros((8, GROUP * BLOCK), jnp.float32)
        for j in range(SPAN):
            part = slice(j * BLOCK, j * BLOCK + BLOCK)
            e = jnp.exp2((s_ref[part, :] - top) * EXP2_SCALE)
            total = total + jnp.sum(e.reshape(BLOCK // 8, 8, GROUP * BLOCK), axis=0)
            e_ref[part, :] = e.astype(jnp.bfloat16)
        inverse = 1.0 / jnp.sum(total, axis=0, keepdims=True)
        at_keys = pl.ds(pl.multiple_of(b * BLOCK, BLOCK), SPAN * BLOCK)
        o_t = (dot(v_t[:, at_keys], e_ref[...]) * inverse).astype(jnp.bfloat16)
        os[at_q, :HEAD] = o_t[:, :BLOCK].T
        os[at_q, HEAD:] = o_t[:, BLOCK:].T
        do_t = jnp.concatenate([dos[at_q, :HEAD].T, dos[at_q, HEAD:].T], axis=1)
        do_t = (do_t.astype(jnp.float32) * inverse).astype(jnp.bfloat16)
        delta = jnp.sum(
            do_t.astype(jnp.float32) * o_t.astype(jnp.float32), axis=0, keepdims=True
        )
        dq_t = jnp.zeros((HEAD, GROUP * BLOCK), jnp.float32)
        for j in range(SPAN):
            k_at = pl.ds(pl.multiple_of((b + j) * BLOCK, BLOCK), BLOCK)
            part = slice(j * BLOCK, j * BLOCK + BLOCK)
            dp = dot(vs[k_at, :], do_t)
            e = e_ref[part, :]
            ds = (e.astype(jnp.float32) * (dp - delta)).astype(jnp.bfloat16)
            dv[k_at, :] += dot(e, do_t, NT)
            dk[k_at, :] += dot(ds, q_blk)
            dq_t = dq_t + dot(k_t[:, k_at], ds)
        dq_t = (dq_t * ATTN_SCALE).astype(jnp.bfloat16)
        dqs[at_q, :HEAD] = dq_t[:, :BLOCK].T
        dqs[at_q, HEAD:] = dq_t[:, BLOCK:].T
        return carry

    lax.fori_loop(0, qs.shape[0] // BLOCK, block, jnp.int32(0))

    dq_same[...] = dqs[same, :]
    across[:, :pair] = dqs[oth, :]
    across[:, 2 * pair :] = os[oth, :]
    o_own[...] = os[piece_at(0, 0), :]
    for at in range(n_mp - 1):
        o_far[2 * at][...] = os[piece_at(0, at + 1), :]
        o_far[2 * at + 1][...] = os[piece_at(1, at + 1), :]
    for out, at in ((dkv_same, same_kv), (dh_same, same), (dh_oth, oth)):
        out[:, :HEAD] = (dk[at, :] * ATTN_SCALE).astype(out.dtype)
        out[:, HEAD:] = dv[at, :].astype(out.dtype)
    across[:, pair : pair + HEAD] = (dk[oth_kv, :] * ATTN_SCALE).astype(across.dtype)
    across[:, pair + HEAD : 2 * pair] = dv[oth_kv, :].astype(across.dtype)


def attention(n_mp, rows, chunk, heads_core, heads_chunk, place, opened, lo, own, near, halo, near_do, far_do):
    heads_mp = 2 * heads_core
    piece, pair = rows // n_mp, GROUP * HEAD
    first = chunk * heads_chunk

    def at_head(g, sc, *unused):
        return (0, sc[0] * heads_core + first + g)

    def at_grad(g, sc, *unused):
        return (0, sc[1] * heads_mp + sc[0] * heads_core + first + g)

    def at_near(g, *unused):
        return (0, first + g)

    def at_near_do(g, sc, *unused):
        return (sc[1], first + g)

    def at_local(g, *unused):
        return (0, g)

    in_specs = [pl.BlockSpec((1, 2 * rows), lambda g, *unused: (0, 0))]
    in_specs += [pl.BlockSpec((rows, pair), at_head)]
    in_specs += [pl.BlockSpec((rows, HEAD), at_head)] * 2
    in_specs += [pl.BlockSpec((rows, 2 * pair), at_near)]
    in_specs += [pl.BlockSpec((rows, pair), at_local)] * 2
    in_specs += [pl.BlockSpec((piece, pair), at_grad), pl.BlockSpec((piece, pair), at_near_do)]
    in_specs += [pl.BlockSpec((2 * piece, pair), at_local)] * (n_mp - 1)
    wide = heads_chunk * pair
    bf, f32 = jnp.bfloat16, jnp.float32
    out_specs = [pl.BlockSpec((rows, pair), at_local)] * 4
    out_specs += [pl.BlockSpec((rows, 3 * pair), at_local)]
    out_specs += [pl.BlockSpec((piece, pair), at_local)] * (2 * n_mp - 1)
    out_shape = [jax.ShapeDtypeStruct((rows, wide), t) for t in (bf, f32, bf, bf)]
    out_shape += [jax.ShapeDtypeStruct((rows, 3 * wide), bf)]
    out_shape += [jax.ShapeDtypeStruct((piece, wide), bf)] * (2 * n_mp - 1)
    tokens, keys, slab = 2 * rows, WINDOW + 2 * rows, SPAN * BLOCK
    return pl.pallas_call(
        functools.partial(attention_kernel, n_mp, rows),
        grid_spec=pltpu.PrefetchScalarGridSpec(
            num_scalar_prefetch=2,
            grid=(heads_chunk,),
            in_specs=in_specs,
            out_specs=out_specs,
            scratch_shapes=[
                pltpu.VMEM((tokens, pair), bf),
                pltpu.VMEM((keys, HEAD), bf),
                pltpu.VMEM((keys, HEAD), bf),
                pltpu.VMEM((HEAD, keys), bf),
                pltpu.VMEM((HEAD, keys), bf),
                pltpu.VMEM((tokens, pair), bf),
                pltpu.VMEM((tokens, pair), bf),
                pltpu.VMEM((tokens, pair), bf),
                pltpu.VMEM((keys, HEAD), f32),
                pltpu.VMEM((keys, HEAD), f32),
                pltpu.VMEM((slab, GROUP * BLOCK), f32),
                pltpu.VMEM((slab, GROUP * BLOCK), bf),
            ],
        ),
        out_shape=out_shape,
        compiler_params=pltpu.CompilerParams(vmem_limit_bytes=48 * 1024 * 1024),
        cost_estimate=HEAVY if chunk else LIGHT,
        name="attention",
    )(place, opened, lo, *own, near, *halo, *near_do, *far_do)


def body(queries, keys, values, grad_out, band_mask, segment_ids):
    n_ctx, n_mp = lax.axis_size("ctx"), lax.axis_size("mp")
    rows = queries.shape[0]
    piece = rows // n_mp
    heads_mp = KV_HEADS // n_mp
    heads_core = heads_mp // 2
    heads_chunk = heads_core // CHUNKS
    pair = GROUP * HEAD
    wide = heads_chunk * pair
    bf = jnp.bfloat16
    ctx, mp = lax.axis_index("ctx"), lax.axis_index("mp")
    core, chip = lax.rem(ctx, 2), ctx // 2
    place = jnp.stack([core, mp]).astype(jnp.int32)

    def send(x, target):
        return lax.ppermute(x, AXES, routes(target, n_ctx, n_mp))

    def half_at(side, first):
        return lambda g, sc: (0, (sc[0] if side == 0 else 1 - sc[0]) * heads_core + first + g)

    def local_at(g, sc):
        return (0, g)

    def pack_halo(first, after):
        sides = [
            [(x, (rows, HEAD), half_at(side, first)) for x in (keys, values)] for side in range(2)
        ]
        out = ((rows, wide), (rows, pair), local_at, 1)
        return pack(place, heads_chunk, sides, [out] * 2, after, "pack_halo")

    def grad_at(dm, side, first):
        def index(g, sc):
            core_to = sc[0] if side == 0 else 1 - sc[0]
            return (0, (lax.rem(sc[1] + dm, n_mp) * 2 + core_to) * heads_core + first + g)

        return index

    halos = [pack_halo(0, ())]
    (near_do,) = pack(
        place,
        heads_core,
        [
            [
                (
                    grad_out,
                    (piece, pair),
                    lambda g, sc, m=m: (0, (m * 2 + 1 - sc[0]) * heads_core + g),
                )
                for m in range(n_mp)
            ]
        ],
        [((rows, heads_core * pair), (rows, pair), local_at, 0)],
        halos[0],
        "pack_near_grad",
    )
    swap = lambda c, m: (c ^ 1, m)
    near_do = send(near_do, swap)
    (near,) = pack(
        place,
        heads_core,
        [
            [(queries, (rows, pair), half_at(1, 0))]
            + [(x, (rows, HEAD), half_at(1, 0)) for x in (keys, values)]
        ],
        [((rows, heads_core * 2 * pair), (rows, 2 * pair), local_at, 1)],
        halos[0],
        "pack_near",
    )
    near = send(near, swap)
    halo_in, far_do = [], []
    for i in range(CHUNKS):
        first = i * heads_chunk
        if i:
            halos.append(pack_halo(first, sent))
        halo_in.append(
            (
                send(halos[i][0], lambda c, m: (c + 2, m)),
                send(halos[i][1], lambda c, m: ((c + 2) ^ 1, m)),
            )
        )
        sent = pack(
            place,
            heads_chunk,
            [
                [
                    (grad_out, (piece, pair), grad_at(dm, 0, first)),
                    (
                        near_do,
                        (piece, pair),
                        lambda g, sc, dm=dm: (lax.rem(sc[1] + dm, n_mp), first + g),
                    ),
                ]
                for dm in range(1, n_mp)
            ],
            [((2 * piece, wide), (2 * piece, pair), local_at, 0)] * (n_mp - 1),
            halos[i] if i else (),
            "pack_far_grad",
        )
        far_do.append(
            [
                send(sent[dm - 1], lambda c, m: (c, (m + dm) % n_mp))
                for dm in range(1, n_mp)
            ]
        )

    tokens = 2 * rows
    padded = jnp.concatenate([jnp.full((WINDOW,), -1, jnp.int32), segment_ids])
    ids = lax.dynamic_slice_in_dim(padded, chip * tokens, WINDOW + tokens, 0)
    before = jnp.sum((ids[:, None] < ids[None, WINDOW:]).astype(jnp.int32), axis=0)
    lo = jnp.maximum(before, jnp.arange(1, tokens + 1, dtype=jnp.int32))[None, :]
    blocks = tokens // BLOCK
    opened = lax.dynamic_slice_in_dim(band_mask, chip * blocks, blocks, 0).reshape(-1)

    out_parts, dq_parts, across_parts, near_parts, far_parts = [], [], [], [], []
    for i in range(CHUNKS):
        dq_same, dkv_same, dh_same, dh_oth, across, o_own, *o_far = attention(
            n_mp,
            rows,
            i,
            heads_core,
            heads_chunk,
            place,
            opened,
            lo,
            (queries, keys, values),
            near,
            halo_in[i],
            (grad_out, near_do),
            far_do[i],
        )
        if i:
            earlier = (far_parts[-1], out_parts[-1], across_parts[-1])
            (dh_same, dh_oth, o_far, across), earlier = lax.optimization_barrier(
                ((dh_same, dh_oth, o_far, across), earlier)
            )
            far_parts[-1], out_parts[-1], across_parts[-1] = earlier
        far_parts.append(
            (
                send(dh_same, lambda c, m: (c - 2, m)),
                send(dh_oth, lambda c, m: ((c - 2) ^ 1 if c >= 2 else -1, m)),
            )
        )
        o_parts = [o_own]
        for dm in range(1, n_mp):
            o_parts.append(send(o_far[2 * dm - 2], lambda c, m: (c, (m + dm) % n_mp)))
            o_parts.append(send(o_far[2 * dm - 1], lambda c, m: (c ^ 1, (m + dm) % n_mp)))
        out_parts.append(o_parts)
        across_parts.append(send(across, swap))
        dq_parts.append(dq_same)
        near_parts.append(dkv_same)

    def out_column(chunk, dk, dm, g=0):
        def column(core, mp):
            core_from = core if dk == 0 else 1 - core
            mp_from = lax.rem(mp + n_mp - dm, n_mp)
            return ((mp_from * 2 + core_from) * heads_core + chunk * heads_chunk + g) * pair

        return column

    def query_column(chunk, side, g=0):
        def column(core, mp):
            half = core if side == 0 else 1 - core
            return (half * heads_core + chunk * heads_chunk + g) * pair

        return column

    arrays, jobs = [], []
    for i in range(CHUNKS):
        for at, part in enumerate(out_parts[i]):
            dk, dm = (at + 1) % 2 if at else 0, (at + 1) // 2
            jobs.append((len(arrays), 0, 0, 0, wide, out_column(i, dk, dm)))
            arrays.append(part)
        jobs.append((len(arrays), 0, 0, 1, wide, query_column(i, 0)))
        arrays.append(dq_parts[i])
        for g in range(heads_chunk):
            at = 3 * g * pair
            jobs.append((len(arrays), 0, at, 1, pair, query_column(i, 1, g)))
            jobs.append((len(arrays), piece, at + 2 * pair, 0, pair, out_column(i, 1, 0, g)))
        arrays.append(across_parts[i])
    attn_out, grad_queries = place_columns(
        place,
        arrays,
        [
            jax.ShapeDtypeStruct((piece, n_mp * heads_mp * pair), bf),
            jax.ShapeDtypeStruct(queries.shape, bf),
        ],
        jobs,
    )

    grads_kv = ()
    for i in range(CHUNKS):
        terms = (near_parts[i], far_parts[i][0], across_parts[i], far_parts[i][1])
        after = (attn_out,) if i == CHUNKS - 1 else ()
        grads_kv = sum_terms(place, i, heads_core, heads_chunk, terms, grads_kv, after)
    return attn_out, grad_queries, grads_kv[0], grads_kv[1]


def solution(mesh):
    placed = (P("ctx", "mp"), P("ctx", "mp"), P("ctx", "mp"), P(("ctx", "mp"), None), P(), P())
    return jax.shard_map(
        body,
        mesh=mesh,
        in_specs=placed,
        out_specs=(P(("ctx", "mp"), None), P("ctx", "mp"), P("ctx", "mp"), P("ctx", "mp")),
        check_vma=False,
    )
```

time: 195 us -> 159 us (0.82)
  waiting for transfers between devices: 59.5 us -> 16.7 us
  Pallas kernels: 93 us -> 101 us
  starting transfers between devices: 34.6 us -> 27.1 us
  local copies, waits for them, and re-layouts: 3.61 us -> 9.52 us
    ppermute x27 -> x18, waiting for transfers between devices: 59.5 us -> 16.7 us  [send(): return lax.ppermute(x, AXES, routes(target, n_ctx, n_mp))]
    pallas_call x4 -> x6, Pallas kernels: 11.5 us -> 19.5 us  [pack(): pl.pallas_call(functools.partial(pack_kernel, joins, len(after)), grid_sp...]
    ppermute x27 -> x18, starting transfers between devices: 34.6 us -> 27.1 us  [send(): return lax.ppermute(x, AXES, routes(target, n_ctx, n_mp))]
    unnamed x38 -> x42, local copies, waits for them, and re-layouts: 3.35 us -> 9.27 us
  transfers between devices with their start and end apart: 27 -> 18, of which waited for: 8 -> 4; matrix products, arithmetic and copies ran while one was open for 1% -> 1% of each run, Pallas kernels for 46% -> 57%
where the time goes in v3:
time: 159 us; the launch traced here: 157 us
  Pallas kernels  101 us (64%)
  starting transfers between devices  27.1 us (17%)
  waiting for transfers between devices  16.7 us (11%)
  local copies, waits for them, and re-layouts  9.52 us (6%)
    pallas_call x2, Pallas kernels, attention(): pl.pallas_call(functools.partial(attention_kernel, n_mp, rows), grid_spec...  68.6 us
    ppermute x18, starting transfers between devices, send(): return lax.ppermute(x, AXES, routes(target, n_ctx, n_mp))  27.1 us
    pallas_call x6, Pallas kernels, pack(): pl.pallas_call(functools.partial(pack_kernel, joins, len(after)), grid_sp...  19.5 us
    ppermute x18, waiting for transfers between devices, send(): return lax.ppermute(x, AXES, routes(target, n_ctx, n_mp))  16.7 us
    unnamed x42, local copies, waits for them, and re-layouts  9.27 us
    pallas_call x2, Pallas kernels, sum_terms(): pl.pallas_call(sum_kernel, grid_spec=pltpu.PrefetchScalarGridSpec(num_sca...  9.25 us
    pallas_call x1, Pallas kernels, place_columns(): pl.pallas_call(functools.partial(place_kernel, jobs, len(arrays)), in_spe...  4.04 us
  transfers between devices with their start and end apart: 18, of which 4 were waited for; matrix products, arithmetic and copies ran while one was open for 1% of the time, Pallas kernels for 57%

profile of v3, /device:TPU:0, one launch (start us, length us, event | category | flops | bytes accessed | tf_op | source)
XLA Modules:
  0.0 157.1 jit_solution(6555215680144418168)
XLA Ops:
  0.6 0.0 copy-start
  0.7 0.6 pad_add_fusion.sc_ref
  1.2 2.9 %pack_halo.2 = (bf16[512,512]{1,0:T(8,128)(2,1)}, bf16[512,512]{1,0:T(8,128)(2,1)}) custom-call(s32[2]{0:T(128)} %pad_add_fusion.sc_ref, bf16[512,1024]{1,0:T(8,128)(2,1)} %refs_1_.11, bf16[512,1024]{1,0:T(8,128)(2,1)} %refs_2_.9, bf16[512,1024]{1,0:T(8,128)(2,1)} %refs_1_.11, bf16[512,1024]{1,0:T(8,128)(2,1)} %refs_2_.9), custom_call_target="tpu_custom_call" | custom-call | bytes 1024 | tf_op jit(solution)/shard_map/pack_halo/pallas_call | solution.py:55
  4.1 4.5 %pack_near.1 = bf16[512,2048]{1,0:T(8,128)(2,1)} custom-call(s32[2]{0:T(128)} %pad_add_fusion.sc_ref, bf16[512,2048]{1,0:T(8,128)(2,1)} %refs_0_.15, bf16[512,1024]{1,0:T(8,128)(2,1)} %refs_1_.11, bf16[512,1024]{1,0:T(8,128)(2,1)} %refs_2_.9, bf16[512,512]{1,0:T(8,128)(2,1)} %get-tuple-element.41.refs_3_.refs_2_, ...), custom_call_target="tpu_custom_call" | custom-call | bytes 1024 | tf_op jit(solution)/shard_map/pack_near/pallas_call | solution.py:55
  8.6 0.5 collective-permute-start
  9.0 4.1 %pack_near_grad.1 = bf16[512,1024]{1,0:T(8,128)(2,1)} custom-call(s32[2]{0:T(128)} %pad_add_fusion.sc_ref, bf16[256,4096]{1,0:T(8,128)(2,1)} %refs_6_.3, bf16[256,4096]{1,0:T(8,128)(2,1)} %refs_6_.3, bf16[512,512]{1,0:T(8,128)(2,1)} %get-tuple-element.41.refs_3_.refs_2_, bf16[512,512]{1,0:T(8,128)(2,1)} %get-tuple-element.42.refs_4_.refs_3_), custom_call_target="tpu_custom_call" | custom-call | bytes 1024 | tf_op jit(solution)/shard_map/pack_near_grad/pallas_call | solution.py:55
  13.1 0.2 collective-permute-start.1
  13.3 4.8 %collective-permute-start.5 = (bf16[512,512]{1,0:T(8,128)(2,1)}, bf16[512,512]{1,0:T(8,128)(2,1)S(1)}, u32[]{:S(2)}, u32[]{:S(2)}) collective-permute-start(bf16[512,512]{1,0:T(8,128)(2,1)} %get-tuple-element.41.refs_3_.refs_2_), channel_id=1, source_target_pairs={{0,4},{1,5},{2,6},{3,7},{4,8},{5,9},{6,10},{7,11},{8,12},{9,13},{1... | collective-permute-start | bytes 1572872 | tf_op jit(solution)/shard_map/ppermute | solution.py:329
  18.1 2.9 %collective-permute-start.6 = (bf16[512,512]{1,0:T(8,128)(2,1)S(1)}, bf16[512,512]{1,0:T(8,128)(2,1)S(1)}, u32[]{:S(2)}, u32[]{:S(2)}) collective-permute-start(bf16[512,512]{1,0:T(8,128)(2,1)S(1)} %copy-done.17), channel_id=1, source_target_pairs={{0,6},{1,7},{2,4},{3,5},{4,10},{5,11},{6,8},{7,9},{8,14},{9,15},{1... | collective-permute-start | bytes 1572872 | tf_op jit(solution)/shard_map/ppermute | solution.py:329
  21.0 0.1 constant_dynamic-slice_fusion
  21.1 0.1 copy.13
  21.2 0.1 reshape.27.open_ref
  21.3 0.0 collective-permute-done.1.refs_1_.refs_7_
  21.3 0.0 copy-start.16
  21.3 1.0 copy-done.16
  22.3 2.5 %pack_far_grad.2.refs_4_ = bf16[512,512]{1,0:T(8,128)(2,1)} custom-call(s32[2]{0:T(128)} %pad_add_fusion.sc_ref, bf16[256,4096]{1,0:T(8,128)(2,1)} %refs_6_.3, bf16[512,1024]{1,0:T(8,128)(2,1)} %copy-done.16), custom_call_target="tpu_custom_call" | custom-call | bytes 1024 | tf_op jit(solution)/shard_map/pack_far_grad/pallas_call | solution.py:55
  24.8 1.5 collective-permute-start.7
  26.3 2.9 %pack_halo.3 = (bf16[512,512]{1,0:T(8,128)(2,1)}, bf16[512,512]{1,0:T(8,128)(2,1)}) custom-call(s32[2]{0:T(128)} %pad_add_fusion.sc_ref, bf16[512,1024]{1,0:T(8,128)(2,1)} %refs_1_.11, bf16[512,1024]{1,0:T(8,128)(2,1)} %refs_2_.9, bf16[512,1024]{1,0:T(8,128)(2,1)} %refs_1_.11, bf16[512,1024]{1,0:T(8,128)(2,1)} %refs_2_.9, bf16[512,512]{1,0:T(8,128)(2,1)} %pack_far_grad.2.refs_4_), custom_call_target="tpu_custom_call" | custom-call | bytes 1024 | tf_op jit(solution)/shard_map/pack_halo/pallas_call | solution.py:55
  29.1 4.2 %collective-permute-start.2 = (bf16[512,512]{1,0:T(8,128)(2,1)}, bf16[512,512]{1,0:T(8,128)(2,1)}, u32[]{:S(2)}, u32[]{:S(2)}) collective-permute-start(bf16[512,512]{1,0:T(8,128)(2,1)} %get-tuple-element.43.refs_2_), channel_id=1, source_target_pairs={{0,4},{1,5},{2,6},{3,7},{4,8},{5,9},{6,10},{7,11},{8,12},{9,13},{1... | collective-permute-start | bytes 1572872 | tf_op jit(solution)/shard_map/ppermute | solution.py:329
  33.4 2.7 %pack_far_grad.3 = bf16[512,512]{1,0:T(8,128)(2,1)} custom-call(s32[2]{0:T(128)} %pad_add_fusion.sc_ref, bf16[256,4096]{1,0:T(8,128)(2,1)} %refs_6_.3, bf16[512,1024]{1,0:T(8,128)(2,1)} %copy-done.16, bf16[512,512]{1,0:T(8,128)(2,1)} %get-tuple-element.43.refs_2_, bf16[512,512]{1,0:T(8,128)(2,1)} %get-tuple-element.44.refs_3_), custom_call_target="tpu_custom_call" | custom-call | bytes 1024 | tf_op jit(solution)/shard_map/pack_far_grad/pallas_call | solution.py:55
  36.0 0.0 collective-permute-done.5.refs_4_
  36.0 2.3 %collective-permute-start.3 = (bf16[512,512]{1,0:T(8,128)(2,1)}, bf16[512,512]{1,0:T(8,128)(2,1)S(1)}, u32[]{:S(2)}, u32[]{:S(2)}) collective-permute-start(bf16[512,512]{1,0:T(8,128)(2,1)} %get-tuple-element.44.refs_3_), channel_id=1, source_target_pairs={{0,6},{1,7},{2,4},{3,5},{4,10},{5,11},{6,8},{7,9},{8,14},{9,15},{1... | collective-permute-start | bytes 1572872 | tf_op jit(solution)/shard_map/ppermute | solution.py:329
  38.4 3.4 %collective-permute-done.6.refs_5_ = bf16[512,512]{1,0:T(8,128)(2,1)S(1)} collective-permute-done((bf16[512,512]{1,0:T(8,128)(2,1)S(1)}, bf16[512,512]{1,0:T(8,128)(2,1)S(1)}, u32[]{:S(2)}, u32[]{:S(2)}) %collective-permute-start.6) | collective-permute-done | bytes 524320 | tf_op jit(solution)/shard_map/ppermute | solution.py:329
  41.8 1.5 collective-permute-start.4
  43.3 1.0 convert_reduce_fusion
  44.3 0.0 collective-permute-done.7.refs_8_
  44.3 0.0 collective-permute-done.refs_3_
  44.3 34.2 %attention.3 = (bf16[512,512]{1,0:T(8,128)(2,1)S(1)}, f32[512,512]{1,0:T(8,128)S(1)}, bf16[512,512]{1,0:T(8,128)(2,1)S(1)}, bf16[512,512]{1,0:T(8,128)(2,1)S(1)}...) custom-call(s32[2]{0:T(128)S(1)} %copy-done.14, ...), custom_call_target="tpu_custom_call" | custom-call | bytes 1024 | tf_op jit(solution)/shard_map/attention/pallas_call | solution.py:285
  78.5 1.0 copy-done.5
  79.5 0.5 collective-permute-start.10
  80.0 0.0 collective-permute-start.11
  80.0 0.0 collective-permute-done.4.refs_8_
  80.0 1.3 collective-permute-start.8
  81.3 0.0 collective-permute-done.2.refs_4_
  81.3 1.3 collective-permute-start.9
  82.6 0.0 collective-permute-done.3.refs_5_
  82.6 1.7 %collective-permute-start.12 = (bf16[512,1536]{1,0:T(8,128)(2,1)}, bf16[512,1536]{1,0:T(8,128)(2,1)S(1)}, u32[]{:S(2)}, u32[]{:S(2)}) collective-permute-start(bf16[512,1536]{1,0:T(8,128)(2,1)} %get-tuple-element.55), channel_id=1, source_target_pairs={{0,2},{1,3},{2,0},{3,1},{4,6},{5,7},{6,4},{7,5},{8,10},{9,11},{10,... | collective-permute-start | bytes 4718600 | tf_op jit(solution)/shard_map/ppermute | solution.py:329
  84.3 34.4 %attention.2 = (bf16[512,512]{1,0:T(8,128)(2,1)S(1)}, f32[512,512]{1,0:T(8,128)S(1)}, bf16[512,512]{1,0:T(8,128)(2,1)}, bf16[512,512]{1,0:T(8,128)(2,1)}, bf16[5...) custom-call(s32[2]{0:T(128)S(1)} %copy-done.14, ...), custom_call_target="tpu_custom_call" | custom-call | flops 24999999488 | bytes 1024 | tf_op jit(solution)/shard_map/attention/pallas_call | solution.py:285
  118.7 1.0 copy-done.4
  119.7 0.8 copy-done.6
  120.5 0.7 copy-done.12
  121.2 0.0 collective-permute-done.10.refs_1_
  121.2 0.7 copy-done.8
  122.0 0.0 collective-permute-done.11.refs_2_
  122.0 0.7 copy-done.10
  122.7 0.0 collective-permute-done.8.far_same
  122.7 0.0 collective-permute-done.12.refs_4_.near_oth
  122.7 0.8 copy-done.18
  123.5 0.2 copy-done.19
  123.7 0.0 collective-permute-start.15
  123.7 1.3 collective-permute-start.16
  125.0 1.3 collective-permute-start.17
  126.3 0.6 collective-permute-start.13
  126.9 1.3 collective-permute-start.14
  128.2 4.6 %sum_terms.2 = (bf16[512,1024]{1,0:T(8,128)(2,1)}, bf16[512,1024]{1,0:T(8,128)(2,1)}) custom-call(s32[2]{0:T(128)} %pad_add_fusion.sc_ref, f32[512,512]{1,0:T(8,128)} %copy-done.5, bf16[512,512]{1,0:T(8,128)(2,1)} %copy-done.18, bf16[512,1536]{1,0:T(8,128)(2,1)} %copy-done.2, bf16[512,512]{1,0:T(8,128)(2,1)} %copy-done.19), custom_call_target="tpu_custom_call" | custom-call | bytes 1024 | tf_op jit(solution)/shard_map/sum_terms/pallas_call | solution.py:125
  132.8 3.0 %collective-permute-done.13.refs_6_ = bf16[256,512]{1,0:T(8,128)(2,1)} collective-permute-done((bf16[256,512]{1,0:T(8,128)(2,1)}, bf16[256,512]{1,0:T(8,128)(2,1)}, u32[]{:S(2)}, u32[]{:S(2)}) %collective-permute-start.13) | collective-permute-done | bytes 262176 | tf_op jit(solution)/shard_map/ppermute | solution.py:329
  135.8 4.8 %collective-permute-done.14.refs_7_ = bf16[256,512]{1,0:T(8,128)(2,1)} collective-permute-done((bf16[256,512]{1,0:T(8,128)(2,1)}, bf16[256,512]{1,0:T(8,128)(2,1)}, u32[]{:S(2)}, u32[]{:S(2)}) %collective-permute-start.14) | collective-permute-done | bytes 262176 | tf_op jit(solution)/shard_map/ppermute | solution.py:329
  140.6 0.0 copy-start.3
  140.6 1.4 copy-done.3
  142.0 0.9 copy-done.13
  142.9 4.0 %place_columns.1 = (bf16[256,4096]{1,0:T(8,128)(2,1)}, bf16[512,2048]{1,0:T(8,128)(2,1)}) custom-call(s32[2]{0:T(128)S(1)} %copy-done.15, bf16[256,512]{1,0:T(8,128)(2,1)S(1)} %get-tuple-element.56.refs_0_, bf16[256,512]{1,0:T(8,128)(2,1)S(1)} %copy-done.9, bf16[256,512]{1,0:T(8,128)(2,1)S(1)} %copy-done.11, bf16[512,512]{1,0:T(8,128)(2,1)S(1)} %get-tuple-element.59.refs_3_, ...), custom_call_target="tpu_custom_call" | custom-call | bytes 1024 | tf_op jit(solution)/shard_map/place_columns/pallas_call | solution.py:79
  147.0 0.0 collective-permute-done.16.far_same
  147.0 5.5 %collective-permute-done.17.far_oth = bf16[512,512]{1,0:T(8,128)(2,1)} collective-permute-done((bf16[512,512]{1,0:T(8,128)(2,1)}, bf16[512,512]{1,0:T(8,128)(2,1)}, u32[]{:S(2)}, u32[]{:S(2)}) %collective-permute-start.17) | collective-permute-done | bytes 524320 | tf_op jit(solution)/shard_map/ppermute | solution.py:329
  152.5 4.6 %sum_terms.3 = (bf16[512,1024]{1,0:T(8,128)(2,1)}, bf16[512,1024]{1,0:T(8,128)(2,1)}) custom-call(s32[2]{0:T(128)} %pad_add_fusion.sc_ref, f32[512,512]{1,0:T(8,128)} %copy-done.4, bf16[512,512]{1,0:T(8,128)(2,1)} %collective-permute-done.16.far_same, ...), custom_call_target="tpu_custom_call", output_to_operand_aliasing={{0}: (5, {}), {1}: (6, {})} | custom-call | bytes 1024 | tf_op jit(solution)/shard_map/sum_terms/pallas_call | solution.py:125
  (33 shorter events, 0.1 us)
Async XLA Ops:
  0.6 20.4 %copy-start = (s32[64,9]{0,1:T(8,128)S(1)}, s32[64,9]{0,1:T(8,128)}, u32[]{:S(2)}) copy-start(s32[64,9]{0,1:T(8,128)} %param.10) | copy-start | bytes 6916
  8.6 9.5 %copy-start.17 = (bf16[512,512]{1,0:T(8,128)(2,1)S(1)}, bf16[512,512]{1,0:T(8,128)(2,1)}, u32[]{:S(2)}) copy-start(bf16[512,512]{1,0:T(8,128)(2,1)} %get-tuple-element.42.refs_4_.refs_3_) | copy-start | bytes 1572868
  8.6 12.7 %copy-start.20 = (s32[8192]{0:T(1024)S(1)}, s32[8192]{0:T(1024)}, u32[]{:S(2)}) copy-start(s32[8192]{0:T(1024)} %param.11) | copy-start | bytes 98308
  8.6 35.7 %collective-permute-start = (bf16[512,2048]{1,0:T(8,128)(2,1)}, bf16[512,2048]{1,0:T(8,128)(2,1)}, u32[]{:S(2)}, u32[]{:S(2)}) collective-permute-start(bf16[512,2048]{1,0:T(8,128)(2,1)} %pack_near.1), channel_id=1, source_target_pairs={{0,2},{1,3},{2,0},{3,1},{4,6},{5,7},{6,4},{7,5},{8,10},{9,11},{10,... | collective-permute-start | bytes 6291464 | tf_op jit(solution)/shard_map/ppermute | solution.py:329
  13.1 8.2 %collective-permute-start.1 = (bf16[512,1024]{1,0:T(8,128)(2,1)}, bf16[512,1024]{1,0:T(8,128)(2,1)S(1)}, u32[]{:S(2)}, u32[]{:S(2)}) collective-permute-start(bf16[512,1024]{1,0:T(8,128)(2,1)} %pack_near_grad.1), channel_id=1, source_target_pairs={{0,2},{1,3},{2,0},{3,1},{4,6},{5,7},{6,4},{7,5},{8,10},{9,11},{10,... | collective-permute-start | bytes 3145736 | tf_op jit(solution)/shard_map/ppermute | solution.py:329
  13.3 22.7 %collective-permute-start.5 = (bf16[512,512]{1,0:T(8,128)(2,1)}, bf16[512,512]{1,0:T(8,128)(2,1)S(1)}, u32[]{:S(2)}, u32[]{:S(2)}) collective-permute-start(bf16[512,512]{1,0:T(8,128)(2,1)} %get-tuple-element.41.refs_3_.refs_2_), channel_id=1, source_target_pairs={{0,4},{1,5},{2,6},{3,7},{4,8},{5,9},{6,10},{7,11},{8,12},{9,13},{1... | collective-permute-start | bytes 1572872 | tf_op jit(solution)/shard_map/ppermute | solution.py:329
  18.1 23.7 %collective-permute-start.6 = (bf16[512,512]{1,0:T(8,128)(2,1)S(1)}, bf16[512,512]{1,0:T(8,128)(2,1)S(1)}, u32[]{:S(2)}, u32[]{:S(2)}) collective-permute-start(bf16[512,512]{1,0:T(8,128)(2,1)S(1)} %copy-done.17), channel_id=1, source_target_pairs={{0,6},{1,7},{2,4},{3,5},{4,10},{5,11},{6,8},{7,9},{8,14},{9,15},{1... | collective-permute-start | bytes 1572872 | tf_op jit(solution)/shard_map/ppermute | solution.py:329
  21.3 1.0 copy-start.16
  24.8 19.5 %collective-permute-start.7 = (bf16[512,512]{1,0:T(8,128)(2,1)}, bf16[512,512]{1,0:T(8,128)(2,1)S(1)}, u32[]{:S(2)}, u32[]{:S(2)}) collective-permute-start(bf16[512,512]{1,0:T(8,128)(2,1)} %pack_far_grad.2.refs_4_), channel_id=1, source_target_pairs={{0,1},{1,0},{2,3},{3,2},{4,5},{5,4},{6,7},{7,6},{8,9},{9,8},{10,11... | collective-permute-start | bytes 1572872 | tf_op jit(solution)/shard_map/ppermute | solution.py:329
  29.1 52.1 %collective-permute-start.2 = (bf16[512,512]{1,0:T(8,128)(2,1)}, bf16[512,512]{1,0:T(8,128)(2,1)}, u32[]{:S(2)}, u32[]{:S(2)}) collective-permute-start(bf16[512,512]{1,0:T(8,128)(2,1)} %get-tuple-element.43.refs_2_), channel_id=1, source_target_pairs={{0,4},{1,5},{2,6},{3,7},{4,8},{5,9},{6,10},{7,11},{8,12},{9,13},{1... | collective-permute-start | bytes 1572872 | tf_op jit(solution)/shard_map/ppermute | solution.py:329
  33.4 10.9 %copy-start.1 = (bf16[512,1024]{1,0:T(8,128)(2,1)S(1)}, bf16[512,1024]{1,0:T(8,128)(2,1)}, u32[]{:S(2)}) copy-start(bf16[512,1024]{1,0:T(8,128)(2,1)} %refs_1_.11) | copy-start | bytes 3145732
  33.4 10.9 %copy-start.14 = (s32[2]{0:T(128)S(1)}, s32[2]{0:T(128)}, u32[]{:S(2)}) copy-start(s32[2]{0:T(128)} %pad_add_fusion.sc_ref) | copy-start | bytes 28
  36.0 46.6 %collective-permute-start.3 = (bf16[512,512]{1,0:T(8,128)(2,1)}, bf16[512,512]{1,0:T(8,128)(2,1)S(1)}, u32[]{:S(2)}, u32[]{:S(2)}) collective-permute-start(bf16[512,512]{1,0:T(8,128)(2,1)} %get-tuple-element.44.refs_3_), channel_id=1, source_target_pairs={{0,6},{1,7},{2,4},{3,5},{4,10},{5,11},{6,8},{7,9},{8,14},{9,15},{1... | collective-permute-start | bytes 1572872 | tf_op jit(solution)/shard_map/ppermute | solution.py:329
  41.8 38.2 %collective-permute-start.4 = (bf16[512,512]{1,0:T(8,128)(2,1)}, bf16[512,512]{1,0:T(8,128)(2,1)S(1)}, u32[]{:S(2)}, u32[]{:S(2)}) collective-permute-start(bf16[512,512]{1,0:T(8,128)(2,1)} %pack_far_grad.3), channel_id=1, source_target_pairs={{0,1},{1,0},{2,3},{3,2},{4,5},{5,4},{6,7},{7,6},{8,9},{9,8},{10,11... | collective-permute-start | bytes 1572872 | tf_op jit(solution)/shard_map/ppermute | solution.py:329
  78.4 1.0 copy-start.5
  79.5 41.8 %collective-permute-start.10 = (bf16[256,512]{1,0:T(8,128)(2,1)S(1)}, bf16[256,512]{1,0:T(8,128)(2,1)S(1)}, u32[]{:S(2)}, u32[]{:S(2)}) collective-permute-start(bf16[256,512]{1,0:T(8,128)(2,1)S(1)} %get-tuple-element.53), channel_id=1, source_target_pairs={{0,1},{1,0},{2,3},{3,2},{4,5},{5,4},{6,7},{7,6},{8,9},{9,8},{10,11... | collective-permute-start | bytes 786440 | tf_op jit(solution)/shard_map/ppermute | solution.py:329
  80.0 42.0 %collective-permute-start.11 = (bf16[256,512]{1,0:T(8,128)(2,1)S(1)}, bf16[256,512]{1,0:T(8,128)(2,1)S(1)}, u32[]{:S(2)}, u32[]{:S(2)}) collective-permute-start(bf16[256,512]{1,0:T(8,128)(2,1)S(1)} %get-tuple-element.54), channel_id=1, source_target_pairs={{0,3},{1,2},{2,1},{3,0},{4,7},{5,6},{6,5},{7,4},{8,11},{9,10},{10,... | collective-permute-start | bytes 786440 | tf_op jit(solution)/shard_map/ppermute | solution.py:329
  80.0 42.7 %collective-permute-start.8 = (bf16[512,512]{1,0:T(8,128)(2,1)S(1)}, bf16[512,512]{1,0:T(8,128)(2,1)S(1)}, u32[]{:S(2)}, u32[]{:S(2)}) collective-permute-start(bf16[512,512]{1,0:T(8,128)(2,1)S(1)} %get-tuple-element.50), channel_id=1, source_target_pairs={{4,0},{5,1},{6,2},{7,3},{8,4},{9,5},{10,6},{11,7},{12,8},{13,9},{1... | collective-permute-start | bytes 1572872 | tf_op jit(solution)/shard_map/ppermute | solution.py:329
  81.3 41.4 %collective-permute-start.9 = (bf16[512,512]{1,0:T(8,128)(2,1)S(1)}, bf16[512,512]{1,0:T(8,128)(2,1)S(1)}, u32[]{:S(2)}, u32[]{:S(2)}) collective-permute-start(bf16[512,512]{1,0:T(8,128)(2,1)S(1)} %get-tuple-element.51), channel_id=1, source_target_pairs={{4,2},{5,3},{6,0},{7,1},{8,6},{9,7},{10,4},{11,5},{12,10},{13,11},... | collective-permute-start | bytes 1572872 | tf_op jit(solution)/shard_map/ppermute | solution.py:329
  82.6 40.1 %collective-permute-start.12 = (bf16[512,1536]{1,0:T(8,128)(2,1)}, bf16[512,1536]{1,0:T(8,128)(2,1)S(1)}, u32[]{:S(2)}, u32[]{:S(2)}) collective-permute-start(bf16[512,1536]{1,0:T(8,128)(2,1)} %get-tuple-element.55), channel_id=1, source_target_pairs={{0,2},{1,3},{2,0},{3,1},{4,6},{5,7},{6,4},{7,5},{8,10},{9,11},{10,... | collective-permute-start | bytes 4718600 | tf_op jit(solution)/shard_map/ppermute | solution.py:329
  118.7 1.0 copy-start.4
  119.7 0.8 copy-start.6
  120.5 0.7 copy-start.12
  121.2 19.3 %copy-start.15 = (s32[2]{0:T(128)S(1)}, s32[2]{0:T(128)}, u32[]{:S(2)}) copy-start(s32[2]{0:T(128)} %pad_add_fusion.sc_ref) | copy-start | bytes 28
  121.2 0.7 copy-start.8
  121.9 18.6 %copy-start.7 = (bf16[512,512]{1,0:T(8,128)(2,1)S(1)}, bf16[512,512]{1,0:T(8,128)(2,1)}, u32[]{:S(2)}) copy-start(bf16[512,512]{1,0:T(8,128)(2,1)} %copy-done.6) | copy-start | bytes 1572868
  122.0 0.7 copy-start.10
  122.7 17.9 %copy-start.9 = (bf16[256,512]{1,0:T(8,128)(2,1)S(1)}, bf16[256,512]{1,0:T(8,128)(2,1)}, u32[]{:S(2)}) copy-start(bf16[256,512]{1,0:T(8,128)(2,1)} %copy-done.8) | copy-start | bytes 786436
  122.7 0.8 copy-start.18
  122.7 17.9 %copy-start.11 = (bf16[256,512]{1,0:T(8,128)(2,1)S(1)}, bf16[256,512]{1,0:T(8,128)(2,1)}, u32[]{:S(2)}) copy-start(bf16[256,512]{1,0:T(8,128)(2,1)} %copy-done.10) | copy-start | bytes 786436
  122.7 1.0 copy-start.19
  123.5 4.7 %copy-start.2 = (bf16[512,1536]{1,0:T(8,128)(2,1)}, bf16[512,1536]{1,0:T(8,128)(2,1)S(1)}, u32[]{:S(2)}) copy-start(bf16[512,1536]{1,0:T(8,128)(2,1)S(1)} %collective-permute-done.12.refs_4_.near_oth) | copy-start | bytes 4718596
  123.7 16.9 %collective-permute-start.15 = (bf16[512,1536]{1,0:T(8,128)(2,1)}, bf16[512,1536]{1,0:T(8,128)(2,1)}, u32[]{:S(2)}, u32[]{:S(2)}) collective-permute-start(bf16[512,1536]{1,0:T(8,128)(2,1)} %get-tuple-element.65), channel_id=1, source_target_pairs={{0,2},{1,3},{2,0},{3,1},{4,6},{5,7},{6,4},{7,5},{8,10},{9,11},{10,... | collective-permute-start | bytes 4718600 | tf_op jit(solution)/shard_map/ppermute | solution.py:329
  123.7 23.3 %collective-permute-start.16 = (bf16[512,512]{1,0:T(8,128)(2,1)}, bf16[512,512]{1,0:T(8,128)(2,1)}, u32[]{:S(2)}, u32[]{:S(2)}) collective-permute-start(bf16[512,512]{1,0:T(8,128)(2,1)} %get-tuple-element.69), channel_id=1, source_target_pairs={{4,0},{5,1},{6,2},{7,3},{8,4},{9,5},{10,6},{11,7},{12,8},{13,9},{1... | collective-permute-start | bytes 1572872 | tf_op jit(solution)/shard_map/ppermute | solution.py:329
  125.0 27.5 %collective-permute-start.17 = (bf16[512,512]{1,0:T(8,128)(2,1)}, bf16[512,512]{1,0:T(8,128)(2,1)}, u32[]{:S(2)}, u32[]{:S(2)}) collective-permute-start(bf16[512,512]{1,0:T(8,128)(2,1)} %get-tuple-element.70), channel_id=1, source_target_pairs={{4,2},{5,3},{6,0},{7,1},{8,6},{9,7},{10,4},{11,5},{12,10},{13,11},... | collective-permute-start | bytes 1572872 | tf_op jit(solution)/shard_map/ppermute | solution.py:329
  126.3 9.5 %collective-permute-start.13 = (bf16[256,512]{1,0:T(8,128)(2,1)}, bf16[256,512]{1,0:T(8,128)(2,1)}, u32[]{:S(2)}, u32[]{:S(2)}) collective-permute-start(bf16[256,512]{1,0:T(8,128)(2,1)} %get-tuple-element.62), channel_id=1, source_target_pairs={{0,1},{1,0},{2,3},{3,2},{4,5},{5,4},{6,7},{7,6},{8,9},{9,8},{10,11... | collective-permute-start | bytes 786440 | tf_op jit(solution)/shard_map/ppermute | solution.py:329
  126.9 13.7 %collective-permute-start.14 = (bf16[256,512]{1,0:T(8,128)(2,1)}, bf16[256,512]{1,0:T(8,128)(2,1)}, u32[]{:S(2)}, u32[]{:S(2)}) collective-permute-start(bf16[256,512]{1,0:T(8,128)(2,1)} %get-tuple-element.63), channel_id=1, source_target_pairs={{0,3},{1,2},{2,1},{3,0},{4,7},{5,6},{6,5},{7,4},{8,11},{9,10},{10,... | collective-permute-start | bytes 786440 | tf_op jit(solution)/shard_map/ppermute | solution.py:329
  140.6 1.4 copy-start.3
  142.0 0.9 copy-start.13

commit v4 on v3

v4 whole, which is shorter than its diff:
```python
import functools
import math

import jax
import jax.numpy as jnp
from jax import lax
from jax.experimental import pallas as pl
from jax.experimental.pallas import tpu as pltpu
from jax.sharding import PartitionSpec as P

KV_HEADS = 16
GROUP = 2
HEAD = 128
WINDOW = 1024
BLOCK = 128
SPAN = WINDOW // BLOCK + 1
CHUNKS = 2
ATTN_SCALE = 168.0 ** (-0.5)
EXP2_SCALE = ATTN_SCALE * math.log2(math.e)
MASKED = -1e30
FAR = 1 << 20
AXES = ("ctx", "mp")
NT = (((1,), (1,)), ((), ()))
NN = (((1,), (0,)), ((), ()))
LIGHT = pl.CostEstimate(flops=0, bytes_accessed=1024, transcendentals=0)
VMEM_LIMIT = 63 * 1024 * 1024
HEAVY = pl.CostEstimate(flops=25_000_000_000, bytes_accessed=1024, transcendentals=0)


def dot(a, b, dims=NN):
    return lax.dot_general(a, b, dims, preferred_element_type=jnp.float32)


def routes(target, n_ctx, n_mp):
    out = []
    for c in range(n_ctx):
        for m in range(n_mp):
            d = target(c, m)
            if 0 <= d[0] < n_ctx:
                out.append((c * n_mp + m, d[0] * n_mp + d[1]))
    return out


def gather_kernel(plan, n_in, shapes, sc_ref, *refs):
    n = len(shapes)
    outs, images, sems = refs[n_in : n_in + n], refs[n_in + n : n_in + 2 * n], refs[-2:]
    into = [[] for _ in shapes]
    count = 0
    for src, dst, src_at, dst_at, size in plan(sc_ref[0], sc_ref[1]):
        copy = pltpu.make_async_copy(
            refs[src].at[tuple(pl.ds(at, by) for at, by in zip(src_at, size))],
            images[dst].at[tuple(pl.ds(at, by) for at, by in zip(dst_at, size))],
            sems[0].at[count],
        )
        copy.start()
        into[dst].append(copy)
        count += 1
    written = []
    for dst in range(n):
        for copy in into[dst]:
            copy.wait()
        written.append(pltpu.make_async_copy(images[dst], outs[dst], sems[1].at[dst]))
        written[-1].start()
    for copy in written:
        copy.wait()


def gather(plan, count, place, arrays, shapes, cost, after=(), name="gather"):
    hbm = pl.BlockSpec(memory_space=pl.ANY)
    return pl.pallas_call(
        functools.partial(gather_kernel, plan, len(arrays) + len(after), shapes),
        in_specs=[pl.BlockSpec(memory_space=pltpu.SMEM)] + [hbm] * (len(arrays) + len(after)),
        out_specs=[hbm] * len(shapes),
        out_shape=[jax.ShapeDtypeStruct(shape, jnp.bfloat16) for shape in shapes],
        scratch_shapes=[pltpu.VMEM(shape, jnp.bfloat16) for shape in shapes]
        + [pltpu.SemaphoreType.DMA((count,)), pltpu.SemaphoreType.DMA((len(shapes),))],
        compiler_params=pltpu.CompilerParams(vmem_limit_bytes=VMEM_LIMIT),
        cost_estimate=cost,
        name=name,
    )(place, *arrays, *after)


def attention_kernel(n_mp, rows, sc_ref, open_ref, lo_ref, *refs):
    q_own, k_own, v_own, q_near, k_near, v_near = refs[:6]
    kh_same, vh_same, kh_oth, vh_oth, do_own, do_oth = refs[6:12]
    do_far = refs[12 : 10 + 2 * n_mp]
    refs = refs[10 + 2 * n_mp :]
    dq_same, dkv_same, dh_same, dh_oth, across, o_own = refs[:6]
    o_far = refs[6 : 4 + 2 * n_mp]
    qs, ks, vs, k_t, v_t, dos, os, dqs, dk, dv = refs[4 + 2 * n_mp : 14 + 2 * n_mp]
    s_refs, e_refs, ds_refs = refs[-6:-4], refs[-4:-2], refs[-2:]
    core, mp = sc_ref[0], sc_ref[1]
    piece, pair = rows // n_mp, GROUP * HEAD
    same = pl.ds(pl.multiple_of(core * rows, rows), rows)
    oth = pl.ds(pl.multiple_of((1 - core) * rows, rows), rows)
    same_kv = pl.ds(pl.multiple_of(WINDOW + core * rows, rows), rows)
    oth_kv = pl.ds(pl.multiple_of(WINDOW + (1 - core) * rows, rows), rows)

    def piece_at(dk_, dm):
        k_at = core if dk_ == 0 else 1 - core
        return pl.ds(pl.multiple_of(k_at * rows + lax.rem(mp + dm, n_mp) * piece, piece), piece)

    qs[same, :] = q_own[...]
    qs[oth, :] = q_near[...]
    ks[same, :] = kh_same[...]
    ks[oth, :] = kh_oth[...]
    ks[same_kv, :] = k_own[...]
    ks[oth_kv, :] = k_near[...]
    vs[same, :] = vh_same[...]
    vs[oth, :] = vh_oth[...]
    vs[same_kv, :] = v_own[...]
    vs[oth_kv, :] = v_near[...]
    dos[piece_at(0, 0), :] = do_own[...]
    dos[piece_at(1, 0), :] = do_oth[...]
    for at in range(n_mp - 1):
        dos[piece_at(0, n_mp - 1 - at), :] = do_far[2 * at][...]
        dos[piece_at(1, n_mp - 1 - at), :] = do_far[2 * at + 1][...]
    dk[...] = jnp.zeros_like(dk)
    dv[...] = jnp.zeros_like(dv)
    for t in range(ks.shape[0] // 256):
        at = slice(t * 256, t * 256 + 256)
        k_t[:, at] = ks[at, :].T
        v_t[:, at] = vs[at, :].T

    width = GROUP * BLOCK
    row = lax.broadcasted_iota(jnp.int32, (BLOCK, width), 0)
    lane = lax.broadcasted_iota(jnp.int32, (BLOCK, width), 1)
    causal = row <= lax.rem(lane, BLOCK)

    def by_rows(x, reduce):
        return reduce(x.reshape(BLOCK // 8, 8, width), axis=0)

    def forward(b):
        s_ref, e_ref = s_refs[b % 2], e_refs[b % 2]
        at_q = slice(b * BLOCK, b * BLOCK + BLOCK)
        q_blk = jnp.concatenate([qs[at_q, :HEAD], qs[at_q, HEAD:]], axis=0)
        lo = jnp.concatenate([lo_ref[:, at_q]] * GROUP, axis=1)
        top = jnp.full((8, width), MASKED, jnp.float32)
        for j in range(SPAN):
            part = slice(j * BLOCK, j * BLOCK + BLOCK)
            s = dot(ks[(b + j) * BLOCK : (b + j + 1) * BLOCK, :], q_blk, NT)
            closed = jnp.where(open_ref[b * SPAN + SPAN - 1 - j] == 1, 0, FAR)
            valid = row >= jnp.maximum(lo - (b + j) * BLOCK, closed)
            if j == SPAN - 1:
                valid = valid & causal
            s = jnp.where(valid, s, MASKED)
            s_ref[part, :] = s
            top = jnp.maximum(top, by_rows(s, jnp.max))
        top = jnp.max(top, axis=0, keepdims=True)
        total = jnp.zeros((8, width), jnp.float32)
        for j in range(SPAN):
            part = slice(j * BLOCK, j * BLOCK + BLOCK)
            e = jnp.exp2((s_ref[part, :] - top) * EXP2_SCALE)
            total = total + by_rows(e, jnp.sum)
            e_ref[part, :] = e.astype(jnp.bfloat16)
        return q_blk, 1.0 / jnp.sum(total, axis=0, keepdims=True)

    def backward(b, q_blk, inverse):
        e_ref, ds_ref = e_refs[b % 2], ds_refs[b % 2]
        at_q = slice(b * BLOCK, b * BLOCK + BLOCK)
        at_keys = slice(b * BLOCK, (b + SPAN) * BLOCK)
        o_t = (dot(v_t[:, at_keys], e_ref[...]) * inverse).astype(jnp.bfloat16)
        os[at_q, :HEAD] = o_t[:, :BLOCK].T
        os[at_q, HEAD:] = o_t[:, BLOCK:].T
        do_t = jnp.concatenate([dos[at_q, :HEAD].T, dos[at_q, HEAD:].T], axis=1)
        do_t = (do_t.astype(jnp.float32) * inverse).astype(jnp.bfloat16)
        delta = jnp.sum(
            do_t.astype(jnp.float32) * o_t.astype(jnp.float32), axis=0, keepdims=True
        )
        for j in range(SPAN):
            part = slice(j * BLOCK, j * BLOCK + BLOCK)
            dp = dot(vs[(b + j) * BLOCK : (b + j + 1) * BLOCK, :], do_t)
            ds_ref[part, :] = (e_ref[part, :].astype(jnp.float32) * (dp - delta)).astype(
                jnp.bfloat16
            )
        dv[at_keys, :] += dot(e_ref[...], do_t, NT)
        dk[at_keys, :] += dot(ds_ref[...], q_blk)
        dq_t = (dot(k_t[:, at_keys], ds_ref[...]) * ATTN_SCALE).astype(jnp.bfloat16)
        dqs[at_q, :HEAD] = dq_t[:, :BLOCK].T
        dqs[at_q, HEAD:] = dq_t[:, BLOCK:].T

    blocks = qs.shape[0] // BLOCK
    ahead = forward(0)
    for b in range(blocks):
        now, ahead = ahead, forward(b + 1) if b + 1 < blocks else None
        backward(b, *now)

    dq_same[...] = dqs[same, :]
    wide = across.shape[1] // 3
    at_g = pl.multiple_of(pl.program_id(0) * pair, pair)
    across[:, pl.ds(at_g, pair)] = dqs[oth, :]
    across[:, pl.ds(2 * wide + at_g, pair)] = os[oth, :]
    o_own[...] = os[piece_at(0, 0), :]
    for at in range(n_mp - 1):
        o_far[2 * at][...] = os[piece_at(0, at + 1), :]
        o_far[2 * at + 1][...] = os[piece_at(1, at + 1), :]
    for out, at in ((dkv_same, same_kv), (dh_same, same), (dh_oth, oth)):
        out[:, :HEAD] = (dk[at, :] * ATTN_SCALE).astype(out.dtype)
        out[:, HEAD:] = dv[at, :].astype(out.dtype)
    across[:, pl.ds(wide + at_g, HEAD)] = (dk[oth_kv, :] * ATTN_SCALE).astype(across.dtype)
    across[:, pl.ds(wide + at_g + HEAD, HEAD)] = dv[oth_kv, :].astype(across.dtype)


def attention(n_mp, rows, chunk, heads, place, opened, lo, own, near, halo, grad_out, far_do):
    heads_mp = 2 * CHUNKS * heads
    piece, pair = rows // n_mp, GROUP * HEAD
    heads_chunk, first = heads, chunk * heads

    def at_head(g, sc, *unused):
        return (0, 2 * first + sc[0] * heads + g)

    def at_grad(g, sc, *unused):
        return (0, sc[1] * heads_mp + 2 * first + sc[0] * heads + g)

    def at_near(column):
        return lambda g, *unused: (0, column + first + g)

    def at_near_do(g, *unused):
        return (chunk, CHUNKS * 2 * heads + g)

    def at_halo(which):
        return lambda g, sc, *unused: (0, which * 2 * heads + sc[0] * heads + g)

    def at_local(g, *unused):
        return (0, g)

    in_specs = [pl.BlockSpec((1, 2 * rows), lambda g, *unused: (0, 0))]
    in_specs += [pl.BlockSpec((rows, pair), at_head)]
    in_specs += [pl.BlockSpec((rows, HEAD), at_head)] * 2
    in_specs += [pl.BlockSpec((rows, pair), at_near(0))]
    in_specs += [pl.BlockSpec((rows, HEAD), at_near(n * CHUNKS * heads)) for n in (2, 3)]
    in_specs += [pl.BlockSpec((rows, HEAD), at_halo(n)) for n in (0, 1, 0, 1)]
    in_specs += [pl.BlockSpec((piece, pair), at_grad), pl.BlockSpec((piece, pair), at_near_do)]
    in_specs += [pl.BlockSpec((piece, pair), at_local)] * (2 * n_mp - 2)
    wide = heads_chunk * pair
    bf, f32 = jnp.bfloat16, jnp.float32
    out_specs = [pl.BlockSpec((rows, pair), at_local)] * 4
    out_specs += [pl.BlockSpec((rows, 3 * wide), lambda g, *unused: (0, 0))]
    out_specs += [pl.BlockSpec((piece, pair), at_local)] * (2 * n_mp - 1)
    out_shape = [jax.ShapeDtypeStruct((rows, wide), t) for t in (bf, bf, bf, bf)]
    out_shape += [jax.ShapeDtypeStruct((rows, 3 * wide), bf)]
    out_shape += [jax.ShapeDtypeStruct((piece, wide), bf)] * (2 * n_mp - 1)
    tokens, keys, slab = 2 * rows, WINDOW + 2 * rows, SPAN * BLOCK
    return pl.pallas_call(
        functools.partial(attention_kernel, n_mp, rows),
        grid_spec=pltpu.PrefetchScalarGridSpec(
            num_scalar_prefetch=2,
            grid=(heads_chunk,),
            in_specs=in_specs,
            out_specs=out_specs,
            scratch_shapes=[
                pltpu.VMEM((tokens, pair), bf),
                pltpu.VMEM((keys, HEAD), bf),
                pltpu.VMEM((keys, HEAD), bf),
                pltpu.VMEM((HEAD, keys), bf),
                pltpu.VMEM((HEAD, keys), bf),
                pltpu.VMEM((tokens, pair), bf),
                pltpu.VMEM((tokens, pair), bf),
                pltpu.VMEM((tokens, pair), bf),
                pltpu.VMEM((keys, HEAD), f32),
                pltpu.VMEM((keys, HEAD), f32),
            ]
            + [pltpu.VMEM((slab, GROUP * BLOCK), t) for t in (f32, f32, bf, bf, bf, bf)],
        ),
        out_shape=out_shape,
        compiler_params=pltpu.CompilerParams(vmem_limit_bytes=VMEM_LIMIT),
        cost_estimate=HEAVY if chunk else LIGHT,
        name="attention",
    )(place, opened, lo, *own, near, near, near, halo[0], halo[0], halo[1], halo[1], grad_out, near, *far_do)


def sum_kernel(heads, sc_ref, near_same, far_same, near_oth, far_oth, *refs):
    dk, dv = refs[-2:]

    def add(near, far):
        for g in range(heads):
            at = 2 * g * HEAD
            to = slice(g * HEAD, g * HEAD + HEAD)
            for out, col in ((dk, at), (dv, at + HEAD)):
                terms = [x[:, col : col + HEAD].astype(jnp.float32) for x in (near, far)]
                out[:, to] = (terms[0] + terms[1]).astype(out.dtype)

    @pl.when(pl.program_id(0) == 0)
    def _():
        add(near_same, far_same)

    @pl.when(pl.program_id(0) == 1)
    def _():
        add(near_oth, far_oth)


def sum_terms(place, chunk, heads, n_heads, terms, before, after=()):
    rows, wide = terms[0].shape

    def at_first(side, sc):
        return (0, 0)

    def at_across(side, sc):
        return (0, 1)

    def at_out(side, sc):
        return (0, 2 * chunk + jnp.where(side == 0, sc[0], 1 - sc[0]))

    shape = jax.ShapeDtypeStruct((rows, n_heads * HEAD), jnp.bfloat16)
    in_specs = [pl.BlockSpec((rows, wide), at) for at in (at_first, at_first, at_across, at_first)]
    return pl.pallas_call(
        functools.partial(sum_kernel, heads),
        grid_spec=pltpu.PrefetchScalarGridSpec(
            num_scalar_prefetch=1,
            grid=(2,),
            in_specs=in_specs + [pl.BlockSpec(memory_space=pl.ANY)] * len((*before, *after)),
            out_specs=[pl.BlockSpec((rows, heads * HEAD), at_out)] * 2,
        ),
        out_shape=[shape, shape],
        input_output_aliases={5: 0, 6: 1} if before else {},
        compiler_params=pltpu.CompilerParams(vmem_limit_bytes=VMEM_LIMIT),
        cost_estimate=LIGHT,
        name="sum_terms",
    )(place, *terms, *before, *after)


def body(queries, keys, values, grad_out, band_mask, segment_ids):
    n_ctx, n_mp = lax.axis_size("ctx"), lax.axis_size("mp")
    rows = queries.shape[0]
    piece = rows // n_mp
    heads_mp = KV_HEADS // n_mp
    heads = heads_mp // (2 * CHUNKS)
    pair = GROUP * HEAD
    wide = heads * pair
    bf = jnp.bfloat16
    ctx, mp = lax.axis_index("ctx"), lax.axis_index("mp")
    core, chip = lax.rem(ctx, 2), ctx // 2
    place = jnp.stack([core, mp]).astype(jnp.int32)

    def send(x, target):
        return lax.ppermute(x, AXES, routes(target, n_ctx, n_mp))

    swap = lambda c, m: (c ^ 1, m)

    def first_head(chunk, core):
        return (2 * chunk + core) * heads

    def col(head, width):
        return pl.multiple_of(head * width, HEAD)

    def plan_halo(chunk):
        def plan(core, mp):
            at, by = first_head(chunk, 0) * HEAD, 2 * heads * HEAD
            return [(n, 0, (0, at), (0, n * by), (rows, by)) for n in range(2)]

        return plan

    def pack_halo(chunk, after):
        shape = (rows, 4 * heads * HEAD)
        (packed,) = gather(
            plan_halo(chunk), 2, place, (keys, values), [shape], HEAVY, after, "pack_halo"
        )
        return packed

    far = [(dk, dm) for dm in range(1, n_mp) for dk in range(2)]
    n_far = len(far)

    def plan_near(core, mp):
        jobs = []
        for at, (dk, dm) in enumerate(far):
            mp_to, core_to = lax.rem(mp + dm, n_mp), core if dk == 0 else 1 - core
            for i in range(CHUNKS):
                src = col(mp_to * heads_mp + first_head(i, core_to), pair)
                jobs.append((3, i * n_far + at, (0, src), (0, 0), (piece, wide)))
        for n, width, to in ((0, pair, 0), (1, HEAD, CHUNKS * wide), (2, HEAD, 3 * CHUNKS * wide // 2)):
            for i in range(CHUNKS):
                src = col(first_head(i, 1 - core), width)
                by = heads * width
                jobs.append((n, CHUNKS * n_far, (0, src), (0, to + i * by), (rows, by)))
        for i in range(CHUNKS):
            src = col(mp * heads_mp + first_head(i, 1 - core), pair)
            jobs.append((3, CHUNKS * n_far, (0, src), (i * piece, 2 * CHUNKS * wide), (piece, wide)))
        return jobs

    halo = pack_halo(0, ())
    *far_do, near = gather(
        plan_near,
        CHUNKS * (n_far + 4),
        place,
        (queries, keys, values, grad_out),
        [(piece, wide)] * (CHUNKS * n_far) + [(rows, (2 * CHUNKS + 1) * wide)],
        HEAVY,
        (halo,),
        "pack_near",
    )
    far_do = [
        [
            send(x, lambda c, m: (c ^ dk, (m + dm) % n_mp))
            for x, (dk, dm) in zip(far_do[i * n_far : (i + 1) * n_far], far)
        ]
        for i in range(CHUNKS)
    ]
    halos = [halo] + [pack_halo(i, (near,)) for i in range(1, CHUNKS)]
    halo_in = [send(halo, lambda c, m: (c + 2, m)) for halo in halos]
    near = send(near, swap)

    tokens = 2 * rows
    padded = jnp.concatenate([jnp.full((WINDOW,), -1, jnp.int32), segment_ids])
    ids = lax.dynamic_slice_in_dim(padded, chip * tokens, WINDOW + tokens, 0)
    before = jnp.sum((ids[:, None] < ids[None, WINDOW:]).astype(jnp.int32), axis=0)
    lo = jnp.maximum(before, jnp.arange(1, tokens + 1, dtype=jnp.int32))[None, :]
    blocks = tokens // BLOCK
    opened = lax.dynamic_slice_in_dim(band_mask, chip * blocks, blocks, 0).reshape(-1)

    out_parts, dq_parts, across_parts, near_parts, far_parts = [], [], [], [], []
    for i in range(CHUNKS):
        ahead = halos[i + 1 :]
        halo, far_do[i], dq_parts, ahead, lo, opened = lax.optimization_barrier(
            (halo_in[i], far_do[i], dq_parts, ahead, lo, opened)
        )
        halo = (halo, send(halo, swap))
        dq_same, dkv_same, dh_same, dh_oth, across, o_own, *o_far = attention(
            n_mp,
            rows,
            i,
            heads,
            place,
            opened,
            lo,
            (queries, keys, values),
            near,
            halo,
            grad_out,
            far_do[i],
        )
        if i:
            earlier = (far_parts[-1], out_parts[-1], across_parts[-1])
            (dh_same, dh_oth, o_far, across), earlier = lax.optimization_barrier(
                ((dh_same, dh_oth, o_far, across), earlier)
            )
            far_parts[-1], out_parts[-1], across_parts[-1] = earlier
        far_parts.append(
            (
                send(dh_same, lambda c, m: (c - 2, m)),
                send(dh_oth, lambda c, m: ((c - 2) ^ 1 if c >= 2 else -1, m)),
            )
        )
        o_parts = [o_own]
        for dm in range(1, n_mp):
            o_parts.append(send(o_far[2 * dm - 2], lambda c, m: (c, (m + dm) % n_mp)))
            o_parts.append(send(o_far[2 * dm - 1], lambda c, m: (c ^ 1, (m + dm) % n_mp)))
        out_parts.append(o_parts)
        across_parts.append(send(across, swap))
        dq_parts.append(dq_same)
        near_parts.append(dkv_same)

    arrays = [
        x for o, a, q in zip(out_parts, across_parts, dq_parts) for x in (*o, a, q)
    ]

    def plan_out(core, mp):
        jobs, at = [], 0
        for i in range(CHUNKS):
            for dk, dm in [(0, 0)] + far:
                mp_from, core_from = lax.rem(mp + n_mp - dm, n_mp), core if dk == 0 else 1 - core
                to = col(mp_from * heads_mp + first_head(i, core_from), pair)
                jobs.append((at, 0, (0, 0), (0, to), (piece, wide)))
                at += 1
            to = col(mp * heads_mp + first_head(i, 1 - core), pair)
            rows_at = pl.multiple_of(mp * piece, piece)
            jobs.append((at, 0, (rows_at, 2 * wide), (0, to), (piece, wide)))
            to = col(first_head(i, 1 - core), pair)
            jobs.append((at, 1, (0, 0), (0, to), (rows, wide)))
            to = col(first_head(i, core), pair)
            jobs.append((at + 1, 1, (0, 0), (0, to), (rows, wide)))
            at += 2
        return jobs

    attn_out, grad_queries = gather(
        plan_out,
        CHUNKS * (n_far + 4),
        place,
        arrays,
        [(piece, n_mp * heads_mp * pair), (rows, heads_mp * pair)],
        LIGHT,
        (),
        "put_together",
    )

    grads_kv = ()
    for i in range(CHUNKS):
        terms = (near_parts[i], far_parts[i][0], across_parts[i], far_parts[i][1])
        after = (attn_out,) if i == CHUNKS - 1 else ()
        grads_kv = sum_terms(place, i, heads, heads_mp, terms, grads_kv, after)
    return attn_out, grad_queries, grads_kv[0], grads_kv[1]


def solution(mesh):
    placed = (P("ctx", "mp"), P("ctx", "mp"), P("ctx", "mp"), P(("ctx", "mp"), None), P(), P())
    return jax.shard_map(
        body,
        mesh=mesh,
        in_specs=placed,
        out_specs=(P(("ctx", "mp"), None), P("ctx", "mp"), P("ctx", "mp"), P("ctx", "mp")),
        check_vma=False,
    )
```

time: 159 us -> 122 us (0.77); the launches traced: 157 us -> 122 us
  Pallas kernels: 101 us -> 64.1 us
  waiting for transfers between devices: 16.7 us -> 28.6 us
  local copies, waits for them, and re-layouts: 9.52 us -> 0.87 us
  starting transfers between devices: 27.1 us -> 25.1 us
    pallas_call x2, Pallas kernels: 68.6 us -> 42.3 us  [attention(): pl.pallas_call(functools.partial(attention_kernel, n_mp, rows), grid_spec...]
    ppermute x18 -> x19, waiting for transfers between devices: 16.7 us -> 28.6 us  [send(): return lax.ppermute(x, AXES, routes(target, n_ctx, n_mp))]
    pallas_call x9 -> x6, Pallas kernels: 32.8 us -> 21.8 us  [the longest x4 15.1 us: gather(): pl.pallas_call(functools.partial(gather_kernel, plan, len(arrays) + len(a...]
    unnamed x42 -> x14, local copies, waits for them, and re-layouts: 9.27 us -> 0.03 us
    ppermute x18 -> x19, starting transfers between devices: 27.1 us -> 25.1 us  [send(): return lax.ppermute(x, AXES, routes(target, n_ctx, n_mp))]
  transfers between devices with their start and end apart: 18 -> 19, of which waited for: 4 -> 7; matrix products, arithmetic and copies ran while one was open for 1% -> 2% of each run, Pallas kernels for 57% -> 48%
where the time goes in v4:
time: 122 us
  Pallas kernels  64.1 us (53%)
  waiting for transfers between devices  28.6 us (23%)
  starting transfers between devices  25.1 us (21%)
  other arithmetic  2.25 us (2%)
    pallas_call x2, Pallas kernels, attention(): pl.pallas_call(functools.partial(attention_kernel, n_mp, rows), grid_spec...  42.3 us
    ppermute x19, waiting for transfers between devices, send(): return lax.ppermute(x, AXES, routes(target, n_ctx, n_mp))  28.6 us
    ppermute x19, starting transfers between devices, send(): return lax.ppermute(x, AXES, routes(target, n_ctx, n_mp))  25.1 us
    pallas_call x4, Pallas kernels, gather(): pl.pallas_call(functools.partial(gather_kernel, plan, len(arrays) + len(a...  15.1 us
    pallas_call x2, Pallas kernels, sum_terms(): pl.pallas_call(functools.partial(sum_kernel, heads), grid_spec=pltpu.Pref...  6.71 us
  transfers between devices with their start and end apart: 19, of which 7 were waited for; matrix products, arithmetic and copies ran while one was open for 2% of the time, Pallas kernels for 48%

profile of v4, /device:TPU:0, one launch (start us, length us, event | category | flops | bytes accessed | tf_op | source)
XLA Modules:
  0.0 121.8 jit_solution(15902476340469469567)
XLA Ops:
  0.6 0.0 copy-start
  0.7 0.7 pad_add_fusion.sc_ref
  1.3 2.9 %pack_halo.2.refs_4_ = bf16[512,1024]{1,0:T(8,128)(2,1)} custom-call(s32[2]{0:T(128)} %pad_add_fusion.sc_ref, bf16[512,1024]{1,0:T(8,128)(2,1)} %refs_1_.9, bf16[512,1024]{1,0:T(8,128)(2,1)} %refs_2_.5), custom_call_target="tpu_custom_call" | custom-call | flops 24999999488 | bytes 1024 | tf_op jit(solution)/shard_map/pack_halo/pallas_call | solution.py:70
  4.2 5.8 %collective-permute-start.3 = (bf16[512,1024]{1,0:T(8,128)(2,1)}, bf16[512,1024]{1,0:T(8,128)(2,1)}, u32[]{:S(2)}, u32[]{:S(2)}) collective-permute-start(bf16[512,1024]{1,0:T(8,128)(2,1)} %pack_halo.2.refs_4_), channel_id=1, source_target_pairs={{0,4},{1,5},{2,6},{3,7},{4,8},{5,9},{6,10},{7,11},{8,12},{9,13},{1... | collective-permute-start | bytes 3145736 | tf_op jit(solution)/shard_map/ppermute | solution.py:336
  10.0 4.7 %pack_near.1 = (bf16[256,512]{1,0:T(8,128)(2,1)}, bf16[256,512]{1,0:T(8,128)(2,1)}, bf16[256,512]{1,0:T(8,128)(2,1)}, bf16[256,512]{1,0:T(8,128)(2,1)}, bf16[512,2560]{1,0:T(8,128)(2,1)}) custom-call(s32[2]{0:T(128)} %pad_add_fusion.sc_ref, bf16[512,2048]{1,0:T(8,128)(2,1)} %refs_0_.9, bf16[512,1024]{1,0:T(8,128)(2,1)} %refs_1_.9, ...), custom_call_target="tpu_custom_call" | custom-call | flops 24999999488 | bytes 1024 | tf_op jit(solution)/shard_map/pack_near/pallas_call | solution.py:70
  14.8 1.6 %collective-permute-start.4 = (bf16[256,512]{1,0:T(8,128)(2,1)}, bf16[256,512]{1,0:T(8,128)(2,1)S(1)}, u32[]{:S(2)}, u32[]{:S(2)}) collective-permute-start(bf16[256,512]{1,0:T(8,128)(2,1)} %get-tuple-element.56), channel_id=1, source_target_pairs={{0,1},{1,0},{2,3},{3,2},{4,5},{5,4},{6,7},{7,6},{8,9},{9,8},{10,11... | collective-permute-start | bytes 786440 | tf_op jit(solution)/shard_map/ppermute | solution.py:336
  16.3 0.0 collective-permute-start.5
  16.3 0.0 copy-start.5
  16.3 0.0 copy-start.6
  16.3 0.6 collective-permute-start.6
  17.0 2.9 %pack_halo.3 = bf16[512,1024]{1,0:T(8,128)(2,1)} custom-call(s32[2]{0:T(128)} %pad_add_fusion.sc_ref, bf16[512,1024]{1,0:T(8,128)(2,1)} %refs_1_.9, bf16[512,1024]{1,0:T(8,128)(2,1)} %refs_2_.5, bf16[512,2560]{1,0:T(8,128)(2,1)} %get-tuple-element.53.refs_2_), custom_call_target="tpu_custom_call" | custom-call | flops 24999999488 | bytes 1024 | tf_op jit(solution)/shard_map/pack_halo/pallas_call | solution.py:70
  19.9 0.0 copy-done.5
  19.9 1.0 convert_reduce_fusion
  20.9 0.0 copy-done
  20.9 0.1 constant_dynamic-slice_fusion
  21.0 0.1 copy.13
  21.1 0.7 reshape.27.open_ref
  21.7 0.6 add_maximum_fusion.lo_ref
  22.3 1.9 %collective-permute-done.4.refs_12_ = bf16[256,512]{1,0:T(8,128)(2,1)S(1)} collective-permute-done((bf16[256,512]{1,0:T(8,128)(2,1)}, bf16[256,512]{1,0:T(8,128)(2,1)S(1)}, u32[]{:S(2)}, u32[]{:S(2)}) %collective-permute-start.4) | collective-permute-done | bytes 262176 | tf_op jit(solution)/shard_map/ppermute | solution.py:336
  24.3 3.3 %collective-permute-done.5.refs_13_ = bf16[256,512]{1,0:T(8,128)(2,1)S(1)} collective-permute-done((bf16[256,512]{1,0:T(8,128)(2,1)}, bf16[256,512]{1,0:T(8,128)(2,1)S(1)}, u32[]{:S(2)}, u32[]{:S(2)}) %collective-permute-start.5) | collective-permute-done | bytes 262176 | tf_op jit(solution)/shard_map/ppermute | solution.py:336
  27.5 4.2 %collective-permute-done.3.refs_6_.refs_7_ = bf16[512,1024]{1,0:T(8,128)(2,1)} collective-permute-done((bf16[512,1024]{1,0:T(8,128)(2,1)}, bf16[512,1024]{1,0:T(8,128)(2,1)}, u32[]{:S(2)}, u32[]{:S(2)}) %collective-permute-start.3) | collective-permute-done | bytes 1048608 | tf_op jit(solution)/shard_map/ppermute | solution.py:336
  31.8 0.0 collective-permute-start.7
  31.8 5.4 %collective-permute-start = (bf16[512,1024]{1,0:T(8,128)(2,1)}, bf16[512,1024]{1,0:T(8,128)(2,1)}, u32[]{:S(2)}, u32[]{:S(2)}) collective-permute-start(bf16[512,1024]{1,0:T(8,128)(2,1)} %pack_halo.3), channel_id=1, source_target_pairs={{0,4},{1,5},{2,6},{3,7},{4,8},{5,9},{6,10},{7,11},{8,12},{9,13},{1... | collective-permute-start | bytes 3145736 | tf_op jit(solution)/shard_map/ppermute | solution.py:336
  37.1 1.5 %collective-permute-start.1 = (bf16[256,512]{1,0:T(8,128)(2,1)}, bf16[256,512]{1,0:T(8,128)(2,1)}, u32[]{:S(2)}, u32[]{:S(2)}) collective-permute-start(bf16[256,512]{1,0:T(8,128)(2,1)} %get-tuple-element.54), channel_id=1, source_target_pairs={{0,1},{1,0},{2,3},{3,2},{4,5},{5,4},{6,7},{7,6},{8,9},{9,8},{10,11... | collective-permute-start | bytes 786440 | tf_op jit(solution)/shard_map/ppermute | solution.py:336
  38.6 0.0 copy-done.6
  38.6 0.1 collective-permute-start.2
  38.7 0.0 collective-permute-done.7.refs_8_.refs_9_
  38.7 0.0 collective-permute-done.6.refs_3_.refs_4_.refs_5_.refs_11_
  38.7 0.0 copy-done.2
  38.7 0.0 copy-done.3
  38.8 21.2 %attention.2 = (bf16[512,512]{1,0:T(8,128)(2,1)}, bf16[512,512]{1,0:T(8,128)(2,1)}, bf16[512,512]{1,0:T(8,128)(2,1)}, bf16[512,512]{1,0:T(8,128)(2,1)}, bf16[512...) custom-call(s32[2]{0:T(128)} %pad_add_fusion.sc_ref, ...), custom_call_target="tpu_custom_call" | custom-call | bytes 1024 | tf_op jit(solution)/shard_map/attention/pallas_call | solution.py:244
  59.9 0.0 collective-permute-done.1.refs_12_
  59.9 0.0 collective-permute-done.2.refs_13_
  59.9 0.0 collective-permute-done.refs_6_.refs_7_
  59.9 0.6 collective-permute-start.8
  60.6 1.5 %collective-permute-start.11 = (bf16[256,512]{1,0:T(8,128)(2,1)}, bf16[256,512]{1,0:T(8,128)(2,1)S(1)}, u32[]{:S(2)}, u32[]{:S(2)}) collective-permute-start(bf16[256,512]{1,0:T(8,128)(2,1)} %get-tuple-element.77), channel_id=1, source_target_pairs={{0,1},{1,0},{2,3},{3,2},{4,5},{5,4},{6,7},{7,6},{8,9},{9,8},{10,11... | collective-permute-start | bytes 786440 | tf_op jit(solution)/shard_map/ppermute | solution.py:336
  62.1 0.0 collective-permute-start.12
  62.1 1.3 %collective-permute-start.9 = (bf16[512,512]{1,0:T(8,128)(2,1)}, bf16[512,512]{1,0:T(8,128)(2,1)S(1)}, u32[]{:S(2)}, u32[]{:S(2)}) collective-permute-start(bf16[512,512]{1,0:T(8,128)(2,1)} %get-tuple-element.74), channel_id=1, source_target_pairs={{4,0},{5,1},{6,2},{7,3},{8,4},{9,5},{10,6},{11,7},{12,8},{13,9},{1... | collective-permute-start | bytes 1572872 | tf_op jit(solution)/shard_map/ppermute | solution.py:336
  63.4 1.5 %collective-permute-start.10 = (bf16[512,512]{1,0:T(8,128)(2,1)}, bf16[512,512]{1,0:T(8,128)(2,1)}, u32[]{:S(2)}, u32[]{:S(2)}) collective-permute-start(bf16[512,512]{1,0:T(8,128)(2,1)} %get-tuple-element.75), channel_id=1, source_target_pairs={{4,2},{5,3},{6,0},{7,1},{8,6},{9,7},{10,4},{11,5},{12,10},{13,11},... | collective-permute-start | bytes 1572872 | tf_op jit(solution)/shard_map/ppermute | solution.py:336
  64.8 0.0 collective-permute-done.8.refs_8_.refs_9_
  64.8 0.7 collective-permute-start.13
  65.6 21.2 %attention.3 = (bf16[512,512]{1,0:T(8,128)(2,1)}, bf16[512,512]{1,0:T(8,128)(2,1)}, bf16[512,512]{1,0:T(8,128)(2,1)}, bf16[512,512]{1,0:T(8,128)(2,1)}, bf16[512...) custom-call(s32[2]{0:T(128)} %pad_add_fusion.sc_ref, ...), custom_call_target="tpu_custom_call" | custom-call | flops 24999999488 | bytes 1024 | tf_op jit(solution)/shard_map/attention/pallas_call | solution.py:244
  86.8 0.0 collective-permute-done.11.refs_1_
  86.8 0.0 copy-start.4
  86.8 0.0 collective-permute-done.12.refs_2_
  86.8 0.0 collective-permute-done.9.far_same
  86.8 0.0 copy-start.1
  86.8 2.8 %collective-permute-done.10.far_oth = bf16[512,512]{1,0:T(8,128)(2,1)} collective-permute-done((bf16[512,512]{1,0:T(8,128)(2,1)}, bf16[512,512]{1,0:T(8,128)(2,1)}, u32[]{:S(2)}, u32[]{:S(2)}) %collective-permute-start.10) | collective-permute-done | bytes 524320 | tf_op jit(solution)/shard_map/ppermute | solution.py:336
  89.7 0.0 collective-permute-done.13.refs_3_.near_oth
  89.7 0.1 collective-permute-start.16
  89.8 1.3 %collective-permute-start.17 = (bf16[512,512]{1,0:T(8,128)(2,1)}, bf16[512,512]{1,0:T(8,128)(2,1)}, u32[]{:S(2)}, u32[]{:S(2)}) collective-permute-start(bf16[512,512]{1,0:T(8,128)(2,1)} %get-tuple-element.93), channel_id=1, source_target_pairs={{4,0},{5,1},{6,2},{7,3},{8,4},{9,5},{10,6},{11,7},{12,8},{13,9},{1... | collective-permute-start | bytes 1572872 | tf_op jit(solution)/shard_map/ppermute | solution.py:336
  91.1 1.3 %collective-permute-start.18 = (bf16[512,512]{1,0:T(8,128)(2,1)}, bf16[512,512]{1,0:T(8,128)(2,1)}, u32[]{:S(2)}, u32[]{:S(2)}) collective-permute-start(bf16[512,512]{1,0:T(8,128)(2,1)} %get-tuple-element.94), channel_id=1, source_target_pairs={{4,2},{5,3},{6,0},{7,1},{8,6},{9,7},{10,4},{11,5},{12,10},{13,11},... | collective-permute-start | bytes 1572872 | tf_op jit(solution)/shard_map/ppermute | solution.py:336
  92.4 1.6 %collective-permute-start.14 = (bf16[256,512]{1,0:T(8,128)(2,1)}, bf16[256,512]{1,0:T(8,128)(2,1)}, u32[]{:S(2)}, u32[]{:S(2)}) collective-permute-start(bf16[256,512]{1,0:T(8,128)(2,1)} %get-tuple-element.86), channel_id=1, source_target_pairs={{0,1},{1,0},{2,3},{3,2},{4,5},{5,4},{6,7},{7,6},{8,9},{9,8},{10,11... | collective-permute-start | bytes 786440 | tf_op jit(solution)/shard_map/ppermute | solution.py:336
  94.0 0.2 collective-permute-start.15
  94.2 0.0 copy-done.1
  94.2 3.4 %sum_terms.2 = (bf16[512,1024]{1,0:T(8,128)(2,1)}, bf16[512,1024]{1,0:T(8,128)(2,1)}) custom-call(s32[2]{0:T(128)} %pad_add_fusion.sc_ref, bf16[512,512]{1,0:T(8,128)(2,1)} %get-tuple-element.95.near_same, bf16[512,512]{1,0:T(8,128)(2,1)} %copy-done.1, bf16[512,1536]{1,0:T(8,128)(2,1)} %collective-permute-done.13.refs_3_.near_oth, ...), custom_call_target="tpu_custom_call" | custom-call | bytes 1024 | tf_op jit(solution)/shard_map/sum_terms/pallas_call | solution.py:306
  97.5 4.4 %collective-permute-done.14.refs_6_ = bf16[256,512]{1,0:T(8,128)(2,1)} collective-permute-done((bf16[256,512]{1,0:T(8,128)(2,1)}, bf16[256,512]{1,0:T(8,128)(2,1)}, u32[]{:S(2)}, u32[]{:S(2)}) %collective-permute-start.14) | collective-permute-done | bytes 262176 | tf_op jit(solution)/shard_map/ppermute | solution.py:336
  101.9 4.5 %collective-permute-done.15.refs_7_ = bf16[256,512]{1,0:T(8,128)(2,1)} collective-permute-done((bf16[256,512]{1,0:T(8,128)(2,1)}, bf16[256,512]{1,0:T(8,128)(2,1)}, u32[]{:S(2)}, u32[]{:S(2)}) %collective-permute-start.15) | collective-permute-done | bytes 262176 | tf_op jit(solution)/shard_map/ppermute | solution.py:336
  106.4 0.0 collective-permute-done.16.refs_8_.near_oth
  106.4 0.0 copy-done.4
  106.4 4.6 %put_together.1 = (bf16[256,4096]{1,0:T(8,128)(2,1)}, bf16[512,2048]{1,0:T(8,128)(2,1)}) custom-call(s32[2]{0:T(128)} %pad_add_fusion.sc_ref, bf16[256,512]{1,0:T(8,128)(2,1)} %get-tuple-element.80.refs_0_, bf16[256,512]{1,0:T(8,128)(2,1)} %copy-done.4, bf16[256,512]{1,0:T(8,128)(2,1)} %collective-permute-done.12.refs_2_, ...), custom_call_target="tpu_custom_call" | custom-call | bytes 1024 | tf_op jit(solution)/shard_map/put_together/pallas_call | solution.py:70
  111.0 0.0 collective-permute-done.17.far_same
  111.1 7.4 %collective-permute-done.18.far_oth = bf16[512,512]{1,0:T(8,128)(2,1)} collective-permute-done((bf16[512,512]{1,0:T(8,128)(2,1)}, bf16[512,512]{1,0:T(8,128)(2,1)}, u32[]{:S(2)}, u32[]{:S(2)}) %collective-permute-start.18) | collective-permute-done | bytes 524320 | tf_op jit(solution)/shard_map/ppermute | solution.py:336
  118.4 3.4 %sum_terms.3 = (bf16[512,1024]{1,0:T(8,128)(2,1)}, bf16[512,1024]{1,0:T(8,128)(2,1)}) custom-call(s32[2]{0:T(128)} %pad_add_fusion.sc_ref, bf16[512,512]{1,0:T(8,128)(2,1)} %get-tuple-element.92.near_same, bf16[512,512]{1,0:T(8,128)(2,1)} %collective-permute-done.17.far_same, ...), custom_call_target="tpu_custom_call", output_to_operand_aliasing={{0}: (5, {}), {1}: (6, {})} | custom-call | bytes 1024 | tf_op jit(solution)/shard_map/sum_terms/pallas_call | solution.py:306
  (4 shorter events, 0.0 us)
Async XLA Ops:
  0.6 20.3 %copy-start = (s32[64,9]{0,1:T(8,128)S(1)}, s32[64,9]{0,1:T(8,128)}, u32[]{:S(2)}) copy-start(s32[64,9]{0,1:T(8,128)} %param.10) | copy-start | bytes 6916
  4.2 27.6 %collective-permute-start.3 = (bf16[512,1024]{1,0:T(8,128)(2,1)}, bf16[512,1024]{1,0:T(8,128)(2,1)}, u32[]{:S(2)}, u32[]{:S(2)}) collective-permute-start(bf16[512,1024]{1,0:T(8,128)(2,1)} %pack_halo.2.refs_4_), channel_id=1, source_target_pairs={{0,4},{1,5},{2,6},{3,7},{4,8},{5,9},{6,10},{7,11},{8,12},{9,13},{1... | collective-permute-start | bytes 3145736 | tf_op jit(solution)/shard_map/ppermute | solution.py:336
  14.8 9.5 %collective-permute-start.4 = (bf16[256,512]{1,0:T(8,128)(2,1)}, bf16[256,512]{1,0:T(8,128)(2,1)S(1)}, u32[]{:S(2)}, u32[]{:S(2)}) collective-permute-start(bf16[256,512]{1,0:T(8,128)(2,1)} %get-tuple-element.56), channel_id=1, source_target_pairs={{0,1},{1,0},{2,3},{3,2},{4,5},{5,4},{6,7},{7,6},{8,9},{9,8},{10,11... | collective-permute-start | bytes 786440 | tf_op jit(solution)/shard_map/ppermute | solution.py:336
  16.3 11.2 %collective-permute-start.5 = (bf16[256,512]{1,0:T(8,128)(2,1)}, bf16[256,512]{1,0:T(8,128)(2,1)S(1)}, u32[]{:S(2)}, u32[]{:S(2)}) collective-permute-start(bf16[256,512]{1,0:T(8,128)(2,1)} %get-tuple-element.57), channel_id=1, source_target_pairs={{0,3},{1,2},{2,1},{3,0},{4,7},{5,6},{6,5},{7,4},{8,11},{9,10},{10,... | collective-permute-start | bytes 786440 | tf_op jit(solution)/shard_map/ppermute | solution.py:336
  16.3 3.5 %copy-start.5 = (s32[8192]{0:T(1024)S(1)}, s32[8192]{0:T(1024)}, u32[]{:S(2)}) copy-start(s32[8192]{0:T(1024)} %param.11) | copy-start | bytes 98308
  16.3 22.3 %copy-start.6 = (bf16[256,512]{1,0:T(8,128)(2,1)S(1)}, bf16[256,512]{1,0:T(8,128)(2,1)}, u32[]{:S(2)}) copy-start(bf16[256,512]{1,0:T(8,128)(2,1)} %get-tuple-element.55) | copy-start | bytes 786436
  16.3 22.4 %collective-permute-start.6 = (bf16[512,2560]{1,0:T(8,128)(2,1)}, bf16[512,2560]{1,0:T(8,128)(2,1)}, u32[]{:S(2)}, u32[]{:S(2)}) collective-permute-start(bf16[512,2560]{1,0:T(8,128)(2,1)} %get-tuple-element.53.refs_2_), channel_id=1, source_target_pairs={{0,2},{1,3},{2,0},{3,1},{4,6},{5,7},{6,4},{7,5},{8,10},{9,11},{10,... | collective-permute-start | bytes 7864328 | tf_op jit(solution)/shard_map/ppermute | solution.py:336
  24.3 14.5 %copy-start.2 = (bf16[256,512]{1,0:T(8,128)(2,1)}, bf16[256,512]{1,0:T(8,128)(2,1)S(1)}, u32[]{:S(2)}) copy-start(bf16[256,512]{1,0:T(8,128)(2,1)S(1)} %collective-permute-done.4.refs_12_) | copy-start | bytes 786436
  27.5 11.2 %copy-start.3 = (bf16[256,512]{1,0:T(8,128)(2,1)}, bf16[256,512]{1,0:T(8,128)(2,1)S(1)}, u32[]{:S(2)}) copy-start(bf16[256,512]{1,0:T(8,128)(2,1)S(1)} %collective-permute-done.5.refs_13_) | copy-start | bytes 786436
  31.8 7.0 %collective-permute-start.7 = (bf16[512,1024]{1,0:T(8,128)(2,1)}, bf16[512,1024]{1,0:T(8,128)(2,1)}, u32[]{:S(2)}, u32[]{:S(2)}) collective-permute-start(bf16[512,1024]{1,0:T(8,128)(2,1)} %collective-permute-done.3.refs_6_.refs_7_), channel_id=1, source_target_pairs={{0,2},{1,3},{2,0},{3,1},{4,6},{5,7},{6,4},{7,5},{8,10},{9,11},{10,... | collective-permute-start | bytes 3145736 | tf_op jit(solution)/shard_map/ppermute | solution.py:336
  31.8 28.1 %collective-permute-start = (bf16[512,1024]{1,0:T(8,128)(2,1)}, bf16[512,1024]{1,0:T(8,128)(2,1)}, u32[]{:S(2)}, u32[]{:S(2)}) collective-permute-start(bf16[512,1024]{1,0:T(8,128)(2,1)} %pack_halo.3), channel_id=1, source_target_pairs={{0,4},{1,5},{2,6},{3,7},{4,8},{5,9},{6,10},{7,11},{8,12},{9,13},{1... | collective-permute-start | bytes 3145736 | tf_op jit(solution)/shard_map/ppermute | solution.py:336
  37.1 22.8 %collective-permute-start.1 = (bf16[256,512]{1,0:T(8,128)(2,1)}, bf16[256,512]{1,0:T(8,128)(2,1)}, u32[]{:S(2)}, u32[]{:S(2)}) collective-permute-start(bf16[256,512]{1,0:T(8,128)(2,1)} %get-tuple-element.54), channel_id=1, source_target_pairs={{0,1},{1,0},{2,3},{3,2},{4,5},{5,4},{6,7},{7,6},{8,9},{9,8},{10,11... | collective-permute-start | bytes 786440 | tf_op jit(solution)/shard_map/ppermute | solution.py:336
  38.6 21.3 %collective-permute-start.2 = (bf16[256,512]{1,0:T(8,128)(2,1)S(1)}, bf16[256,512]{1,0:T(8,128)(2,1)}, u32[]{:S(2)}, u32[]{:S(2)}) collective-permute-start(bf16[256,512]{1,0:T(8,128)(2,1)S(1)} %copy-done.6), channel_id=1, source_target_pairs={{0,3},{1,2},{2,1},{3,0},{4,7},{5,6},{6,5},{7,4},{8,11},{9,10},{10,... | collective-permute-start | bytes 786440 | tf_op jit(solution)/shard_map/ppermute | solution.py:336
  59.9 4.9 %collective-permute-start.8 = (bf16[512,1024]{1,0:T(8,128)(2,1)}, bf16[512,1024]{1,0:T(8,128)(2,1)}, u32[]{:S(2)}, u32[]{:S(2)}) collective-permute-start(bf16[512,1024]{1,0:T(8,128)(2,1)} %collective-permute-done.refs_6_.refs_7_), channel_id=1, source_target_pairs={{0,2},{1,3},{2,0},{3,1},{4,6},{5,7},{6,4},{7,5},{8,10},{9,11},{10,... | collective-permute-start | bytes 3145736 | tf_op jit(solution)/shard_map/ppermute | solution.py:336
  60.6 26.2 %collective-permute-start.11 = (bf16[256,512]{1,0:T(8,128)(2,1)}, bf16[256,512]{1,0:T(8,128)(2,1)S(1)}, u32[]{:S(2)}, u32[]{:S(2)}) collective-permute-start(bf16[256,512]{1,0:T(8,128)(2,1)} %get-tuple-element.77), channel_id=1, source_target_pairs={{0,1},{1,0},{2,3},{3,2},{4,5},{5,4},{6,7},{7,6},{8,9},{9,8},{10,11... | collective-permute-start | bytes 786440 | tf_op jit(solution)/shard_map/ppermute | solution.py:336
  62.1 24.7 %collective-permute-start.12 = (bf16[256,512]{1,0:T(8,128)(2,1)}, bf16[256,512]{1,0:T(8,128)(2,1)}, u32[]{:S(2)}, u32[]{:S(2)}) collective-permute-start(bf16[256,512]{1,0:T(8,128)(2,1)} %get-tuple-element.78), channel_id=1, source_target_pairs={{0,3},{1,2},{2,1},{3,0},{4,7},{5,6},{6,5},{7,4},{8,11},{9,10},{10,... | collective-permute-start | bytes 786440 | tf_op jit(solution)/shard_map/ppermute | solution.py:336
  62.1 24.7 %collective-permute-start.9 = (bf16[512,512]{1,0:T(8,128)(2,1)}, bf16[512,512]{1,0:T(8,128)(2,1)S(1)}, u32[]{:S(2)}, u32[]{:S(2)}) collective-permute-start(bf16[512,512]{1,0:T(8,128)(2,1)} %get-tuple-element.74), channel_id=1, source_target_pairs={{4,0},{5,1},{6,2},{7,3},{8,4},{9,5},{10,6},{11,7},{12,8},{13,9},{1... | collective-permute-start | bytes 1572872 | tf_op jit(solution)/shard_map/ppermute | solution.py:336
  63.4 26.3 %collective-permute-start.10 = (bf16[512,512]{1,0:T(8,128)(2,1)}, bf16[512,512]{1,0:T(8,128)(2,1)}, u32[]{:S(2)}, u32[]{:S(2)}) collective-permute-start(bf16[512,512]{1,0:T(8,128)(2,1)} %get-tuple-element.75), channel_id=1, source_target_pairs={{4,2},{5,3},{6,0},{7,1},{8,6},{9,7},{10,4},{11,5},{12,10},{13,11},... | collective-permute-start | bytes 1572872 | tf_op jit(solution)/shard_map/ppermute | solution.py:336
  64.8 24.8 %collective-permute-start.13 = (bf16[512,1536]{1,0:T(8,128)(2,1)}, bf16[512,1536]{1,0:T(8,128)(2,1)}, u32[]{:S(2)}, u32[]{:S(2)}) collective-permute-start(bf16[512,1536]{1,0:T(8,128)(2,1)} %get-tuple-element.79), channel_id=1, source_target_pairs={{0,2},{1,3},{2,0},{3,1},{4,6},{5,7},{6,4},{7,5},{8,10},{9,11},{10,... | collective-permute-start | bytes 4718600 | tf_op jit(solution)/shard_map/ppermute | solution.py:336
  86.8 19.6 %copy-start.4 = (bf16[256,512]{1,0:T(8,128)(2,1)}, bf16[256,512]{1,0:T(8,128)(2,1)S(1)}, u32[]{:S(2)}) copy-start(bf16[256,512]{1,0:T(8,128)(2,1)S(1)} %collective-permute-done.11.refs_1_) | copy-start | bytes 786436
  86.8 7.4 %copy-start.1 = (bf16[512,512]{1,0:T(8,128)(2,1)}, bf16[512,512]{1,0:T(8,128)(2,1)S(1)}, u32[]{:S(2)}) copy-start(bf16[512,512]{1,0:T(8,128)(2,1)S(1)} %collective-permute-done.9.far_same) | copy-start | bytes 1572868
  89.7 16.7 %collective-permute-start.16 = (bf16[512,1536]{1,0:T(8,128)(2,1)}, bf16[512,1536]{1,0:T(8,128)(2,1)}, u32[]{:S(2)}, u32[]{:S(2)}) collective-permute-start(bf16[512,1536]{1,0:T(8,128)(2,1)} %get-tuple-element.88), channel_id=1, source_target_pairs={{0,2},{1,3},{2,0},{3,1},{4,6},{5,7},{6,4},{7,5},{8,10},{9,11},{10,... | collective-permute-start | bytes 4718600 | tf_op jit(solution)/shard_map/ppermute | solution.py:336
  89.8 21.2 %collective-permute-start.17 = (bf16[512,512]{1,0:T(8,128)(2,1)}, bf16[512,512]{1,0:T(8,128)(2,1)}, u32[]{:S(2)}, u32[]{:S(2)}) collective-permute-start(bf16[512,512]{1,0:T(8,128)(2,1)} %get-tuple-element.93), channel_id=1, source_target_pairs={{4,0},{5,1},{6,2},{7,3},{8,4},{9,5},{10,6},{11,7},{12,8},{13,9},{1... | collective-permute-start | bytes 1572872 | tf_op jit(solution)/shard_map/ppermute | solution.py:336
  91.1 27.3 %collective-permute-start.18 = (bf16[512,512]{1,0:T(8,128)(2,1)}, bf16[512,512]{1,0:T(8,128)(2,1)}, u32[]{:S(2)}, u32[]{:S(2)}) collective-permute-start(bf16[512,512]{1,0:T(8,128)(2,1)} %get-tuple-element.94), channel_id=1, source_target_pairs={{4,2},{5,3},{6,0},{7,1},{8,6},{9,7},{10,4},{11,5},{12,10},{13,11},... | collective-permute-start | bytes 1572872 | tf_op jit(solution)/shard_map/ppermute | solution.py:336
  92.4 9.5 %collective-permute-start.14 = (bf16[256,512]{1,0:T(8,128)(2,1)}, bf16[256,512]{1,0:T(8,128)(2,1)}, u32[]{:S(2)}, u32[]{:S(2)}) collective-permute-start(bf16[256,512]{1,0:T(8,128)(2,1)} %get-tuple-element.86), channel_id=1, source_target_pairs={{0,1},{1,0},{2,3},{3,2},{4,5},{5,4},{6,7},{7,6},{8,9},{9,8},{10,11... | collective-permute-start | bytes 786440 | tf_op jit(solution)/shard_map/ppermute | solution.py:336
  94.0 12.4 %collective-permute-start.15 = (bf16[256,512]{1,0:T(8,128)(2,1)}, bf16[256,512]{1,0:T(8,128)(2,1)}, u32[]{:S(2)}, u32[]{:S(2)}) collective-permute-start(bf16[256,512]{1,0:T(8,128)(2,1)} %get-tuple-element.87), channel_id=1, source_target_pairs={{0,3},{1,2},{2,1},{3,0},{4,7},{5,6},{6,5},{7,4},{8,11},{9,10},{10,... | collective-permute-start | bytes 786440 | tf_op jit(solution)/shard_map/ppermute | solution.py:336

commit v5 on v4

--- a/solution.py
+++ b/solution.py
@@ -23,7 +23,7 @@
 NT = (((1,), (1,)), ((), ()))
 NN = (((1,), (0,)), ((), ()))
 LIGHT = pl.CostEstimate(flops=0, bytes_accessed=1024, transcendentals=0)
-VMEM_LIMIT = 63 * 1024 * 1024
+VMEM_LIMIT = (64 * 1024 - 128) * 1024
 HEAVY = pl.CostEstimate(flops=25_000_000_000, bytes_accessed=1024, transcendentals=0)
 
 
@@ -80,14 +80,16 @@
     )(place, *arrays, *after)
 
 
-def attention_kernel(n_mp, rows, sc_ref, open_ref, lo_ref, *refs):
+def attention_kernel(n_mp, rows, whole, sc_ref, open_ref, lo_ref, *refs):
     q_own, k_own, v_own, q_near, k_near, v_near = refs[:6]
     kh_same, vh_same, kh_oth, vh_oth, do_own, do_oth = refs[6:12]
     do_far = refs[12 : 10 + 2 * n_mp]
     refs = refs[10 + 2 * n_mp :]
-    dq_same, dkv_same, dh_same, dh_oth, across, o_own = refs[:6]
-    o_far = refs[6 : 4 + 2 * n_mp]
-    qs, ks, vs, k_t, v_t, dos, os, dqs, dk, dv = refs[4 + 2 * n_mp : 14 + 2 * n_mp]
+    n_back = 1 if whole else 2
+    dq_same, dkv_same, across, o_own, *o_far = refs[: 2 + 2 * n_mp]
+    back = refs[2 + 2 * n_mp : 2 + 2 * n_mp + n_back]
+    refs = refs[2 + 2 * n_mp + n_back :]
+    qs, ks, vs, k_t, v_t, dos, os, dqs, dk, dv = refs[:10]
     s_refs, e_refs, ds_refs = refs[-6:-4], refs[-4:-2], refs[-2:]
     core, mp = sc_ref[0], sc_ref[1]
     piece, pair = rows // n_mp, GROUP * HEAD
@@ -194,14 +196,15 @@
     for at in range(n_mp - 1):
         o_far[2 * at][...] = os[piece_at(0, at + 1), :]
         o_far[2 * at + 1][...] = os[piece_at(1, at + 1), :]
-    for out, at in ((dkv_same, same_kv), (dh_same, same), (dh_oth, oth)):
+    ats = (slice(0, 2 * rows),) if whole else (same, oth)
+    for out, at in ((dkv_same, same_kv), *zip(back, ats)):
         out[:, :HEAD] = (dk[at, :] * ATTN_SCALE).astype(out.dtype)
         out[:, HEAD:] = dv[at, :].astype(out.dtype)
     across[:, pl.ds(wide + at_g, HEAD)] = (dk[oth_kv, :] * ATTN_SCALE).astype(across.dtype)
     across[:, pl.ds(wide + at_g + HEAD, HEAD)] = dv[oth_kv, :].astype(across.dtype)
 
 
-def attention(n_mp, rows, chunk, heads, place, opened, lo, own, near, halo, grad_out, far_do):
+def attention(n_mp, rows, whole, chunk, heads, place, opened, lo, own, near, halo, grad_out, far_do):
     heads_mp = 2 * CHUNKS * heads
     piece, pair = rows // n_mp, GROUP * HEAD
     heads_chunk, first = heads, chunk * heads
@@ -218,31 +221,38 @@
     def at_near_do(g, *unused):
         return (chunk, CHUNKS * 2 * heads + g)
 
-    def at_halo(which):
-        return lambda g, sc, *unused: (0, which * 2 * heads + sc[0] * heads + g)
+    def at_halo(which, side):
+        skip = 2 * heads if side and chunk else 0
+        return lambda g, *unused: (0, skip + which * heads + g)
 
     def at_local(g, *unused):
         return (0, g)
+
+    def at_handed(g, *unused):
+        return (0, heads + g)
 
     in_specs = [pl.BlockSpec((1, 2 * rows), lambda g, *unused: (0, 0))]
     in_specs += [pl.BlockSpec((rows, pair), at_head)]
     in_specs += [pl.BlockSpec((rows, HEAD), at_head)] * 2
     in_specs += [pl.BlockSpec((rows, pair), at_near(0))]
     in_specs += [pl.BlockSpec((rows, HEAD), at_near(n * CHUNKS * heads)) for n in (2, 3)]
-    in_specs += [pl.BlockSpec((rows, HEAD), at_halo(n)) for n in (0, 1, 0, 1)]
+    in_specs += [pl.BlockSpec((rows, HEAD), at_halo(n % 2, n // 2)) for n in range(4)]
     in_specs += [pl.BlockSpec((piece, pair), at_grad), pl.BlockSpec((piece, pair), at_near_do)]
-    in_specs += [pl.BlockSpec((piece, pair), at_local)] * (2 * n_mp - 2)
+    in_specs += [pl.BlockSpec((piece, pair), at) for at in (at_local, at_handed)] * (n_mp - 1)
     wide = heads_chunk * pair
     bf, f32 = jnp.bfloat16, jnp.float32
-    out_specs = [pl.BlockSpec((rows, pair), at_local)] * 4
+    out_specs = [pl.BlockSpec((rows, pair), at_local)] * 2
     out_specs += [pl.BlockSpec((rows, 3 * wide), lambda g, *unused: (0, 0))]
     out_specs += [pl.BlockSpec((piece, pair), at_local)] * (2 * n_mp - 1)
-    out_shape = [jax.ShapeDtypeStruct((rows, wide), t) for t in (bf, bf, bf, bf)]
+    out_shape = [jax.ShapeDtypeStruct((rows, wide), bf)] * 2
     out_shape += [jax.ShapeDtypeStruct((rows, 3 * wide), bf)]
     out_shape += [jax.ShapeDtypeStruct((piece, wide), bf)] * (2 * n_mp - 1)
+    n_back, rows_back = (1, 2 * rows) if whole else (2, rows)
+    out_specs += [pl.BlockSpec((rows_back, pair), at_local)] * n_back
+    out_shape += [jax.ShapeDtypeStruct((rows_back, wide), bf)] * n_back
     tokens, keys, slab = 2 * rows, WINDOW + 2 * rows, SPAN * BLOCK
     return pl.pallas_call(
-        functools.partial(attention_kernel, n_mp, rows),
+        functools.partial(attention_kernel, n_mp, rows, whole),
         grid_spec=pltpu.PrefetchScalarGridSpec(
             num_scalar_prefetch=2,
             grid=(heads_chunk,),
@@ -269,50 +279,43 @@
     )(place, opened, lo, *own, near, near, near, halo[0], halo[0], halo[1], halo[1], grad_out, near, *far_do)
 
 
-def sum_kernel(heads, sc_ref, near_same, far_same, near_oth, far_oth, *refs):
+def sum_kernel(heads, sc_ref, near, far, *refs):
     dk, dv = refs[-2:]
-
-    def add(near, far):
-        for g in range(heads):
-            at = 2 * g * HEAD
-            to = slice(g * HEAD, g * HEAD + HEAD)
-            for out, col in ((dk, at), (dv, at + HEAD)):
-                terms = [x[:, col : col + HEAD].astype(jnp.float32) for x in (near, far)]
-                out[:, to] = (terms[0] + terms[1]).astype(out.dtype)
-
-    @pl.when(pl.program_id(0) == 0)
-    def _():
-        add(near_same, far_same)
-
-    @pl.when(pl.program_id(0) == 1)
-    def _():
-        add(near_oth, far_oth)
-
-
-def sum_terms(place, chunk, heads, n_heads, terms, before, after=()):
-    rows, wide = terms[0].shape
-
-    def at_first(side, sc):
-        return (0, 0)
-
-    def at_across(side, sc):
-        return (0, 1)
-
-    def at_out(side, sc):
-        return (0, 2 * chunk + jnp.where(side == 0, sc[0], 1 - sc[0]))
+    for g in range(heads):
+        at = 2 * g * HEAD
+        to = slice(g * HEAD, g * HEAD + HEAD)
+        for out, col in ((dk, at), (dv, at + HEAD)):
+            terms = [x[:, col : col + HEAD].astype(jnp.float32) for x in (near, far)]
+            out[:, to] = (terms[0] + terms[1]).astype(out.dtype)
+
+
+def sum_terms(place, chunk, side, heads, n_heads, terms, before, after=()):
+    rows = terms[0].shape[0]
+    wide = 2 * heads * HEAD
+    by_core = terms[1].shape[0] > rows
+
+    def at_near(n, sc):
+        return (0, side)
+
+    def at_far(n, sc):
+        return (sc[0] if by_core else 0, 0)
+
+    def at_out(n, sc):
+        return (0, 2 * chunk + (sc[0] if side == 0 else 1 - sc[0]))
 
     shape = jax.ShapeDtypeStruct((rows, n_heads * HEAD), jnp.bfloat16)
-    in_specs = [pl.BlockSpec((rows, wide), at) for at in (at_first, at_first, at_across, at_first)]
+    hbm = pl.BlockSpec(memory_space=pl.ANY)
     return pl.pallas_call(
         functools.partial(sum_kernel, heads),
         grid_spec=pltpu.PrefetchScalarGridSpec(
             num_scalar_prefetch=1,
-            grid=(2,),
-            in_specs=in_specs + [pl.BlockSpec(memory_space=pl.ANY)] * len((*before, *after)),
+            grid=(1,),
+            in_specs=[pl.BlockSpec((rows, wide), at) for at in (at_near, at_far)]
+            + [hbm] * len((*before, *after)),
             out_specs=[pl.BlockSpec((rows, heads * HEAD), at_out)] * 2,
         ),
         out_shape=[shape, shape],
-        input_output_aliases={5: 0, 6: 1} if before else {},
+        input_output_aliases={3: 0, 4: 1} if before else {},
         compiler_params=pltpu.CompilerParams(vmem_limit_bytes=VMEM_LIMIT),
         cost_estimate=LIGHT,
         name="sum_terms",
@@ -345,28 +348,33 @@
 
     def plan_halo(chunk):
         def plan(core, mp):
-            at, by = first_head(chunk, 0) * HEAD, 2 * heads * HEAD
-            return [(n, 0, (0, at), (0, n * by), (rows, by)) for n in range(2)]
+            jobs, by = [], heads * HEAD
+            for side in range(2):
+                src = col(first_head(chunk, core if side == 0 else 1 - core), HEAD)
+                for n in range(2):
+                    dst, to = (side, n) if chunk == 0 else (0, 2 * side + n)
+                    jobs.append((n, dst, (0, src), (0, to * by), (rows, by)))
+            return jobs
 
         return plan
 
     def pack_halo(chunk, after):
-        shape = (rows, 4 * heads * HEAD)
-        (packed,) = gather(
-            plan_halo(chunk), 2, place, (keys, values), [shape], HEAVY, after, "pack_halo"
-        )
-        return packed
+        shapes = [(rows, wide)] * 2 if chunk == 0 else [(rows, 2 * wide)]
+        return gather(plan_halo(chunk), 4, place, (keys, values), shapes, HEAVY, after, "pack_halo")
 
     far = [(dk, dm) for dm in range(1, n_mp) for dk in range(2)]
-    n_far = len(far)
+    n_far = n_mp - 1
 
     def plan_near(core, mp):
         jobs = []
-        for at, (dk, dm) in enumerate(far):
-            mp_to, core_to = lax.rem(mp + dm, n_mp), core if dk == 0 else 1 - core
+        for dm in range(1, n_mp):
+            mp_to = lax.rem(mp + dm, n_mp)
             for i in range(CHUNKS):
-                src = col(mp_to * heads_mp + first_head(i, core_to), pair)
-                jobs.append((3, i * n_far + at, (0, src), (0, 0), (piece, wide)))
+                for side in range(2):
+                    core_to = core if side == 0 else 1 - core
+                    src = col(mp_to * heads_mp + first_head(i, core_to), pair)
+                    at = i * n_far + dm - 1
+                    jobs.append((3, at, (0, src), (0, side * wide), (piece, wide)))
         for n, width, to in ((0, pair, 0), (1, HEAD, CHUNKS * wide), (2, HEAD, 3 * CHUNKS * wide // 2)):
             for i in range(CHUNKS):
                 src = col(first_head(i, 1 - core), width)
@@ -377,26 +385,28 @@
             jobs.append((3, CHUNKS * n_far, (0, src), (i * piece, 2 * CHUNKS * wide), (piece, wide)))
         return jobs
 
-    halo = pack_halo(0, ())
+    halos = [pack_halo(0, ())]
     *far_do, near = gather(
         plan_near,
-        CHUNKS * (n_far + 4),
+        CHUNKS * (2 * n_far + 4),
         place,
         (queries, keys, values, grad_out),
-        [(piece, wide)] * (CHUNKS * n_far) + [(rows, (2 * CHUNKS + 1) * wide)],
+        [(piece, 2 * wide)] * (CHUNKS * n_far) + [(rows, (2 * CHUNKS + 1) * wide)],
         HEAVY,
-        (halo,),
+        halos[0],
         "pack_near",
     )
     far_do = [
         [
-            send(x, lambda c, m: (c ^ dk, (m + dm) % n_mp))
-            for x, (dk, dm) in zip(far_do[i * n_far : (i + 1) * n_far], far)
+            send(far_do[i * n_far + dm - 1], lambda c, m: (c, (m + dm) % n_mp))
+            for dm in range(1, n_mp)
         ]
         for i in range(CHUNKS)
     ]
-    halos = [halo] + [pack_halo(i, (near,)) for i in range(1, CHUNKS)]
-    halo_in = [send(halo, lambda c, m: (c + 2, m)) for halo in halos]
+    halos += [pack_halo(i, (near,)) for i in range(1, CHUNKS)]
+    halo_in = [
+        [send(x, lambda c, m: ((c + 2) ^ side, m)) for side, x in enumerate(halo)] for halo in halos
+    ]
     near = send(near, swap)
 
     tokens = 2 * rows
@@ -409,14 +419,17 @@
 
     out_parts, dq_parts, across_parts, near_parts, far_parts = [], [], [], [], []
     for i in range(CHUNKS):
-        ahead = halos[i + 1 :]
-        halo, far_do[i], dq_parts, ahead, lo, opened = lax.optimization_barrier(
-            (halo_in[i], far_do[i], dq_parts, ahead, lo, opened)
-        )
-        halo = (halo, send(halo, swap))
-        dq_same, dkv_same, dh_same, dh_oth, across, o_own, *o_far = attention(
+        halo, ahead = halo_in[i], halos[i + 1 :]
+        if i:
+            halo, far_do[i], dq_parts = lax.optimization_barrier((halo, far_do[i], dq_parts))
+        else:
+            far_do[i], ahead, lo, opened = lax.optimization_barrier((far_do[i], ahead, lo, opened))
+        halo = (halo[0], halo[1] if i == 0 else send(halo[0], swap))
+        last = i == CHUNKS - 1
+        dq_same, dkv_same, across, o_own, *o_far = attention(
             n_mp,
             rows,
+            not last,
             i,
             heads,
             place,
@@ -426,20 +439,23 @@
             near,
             halo,
             grad_out,
-            far_do[i],
+            [y for x in far_do[i] for y in (x, send(x, swap))],
         )
+        n_far_o = 2 * n_mp - 2
+        o_far, back = o_far[:n_far_o], o_far[n_far_o:]
         if i:
-            earlier = (far_parts[-1], out_parts[-1], across_parts[-1])
-            (dh_same, dh_oth, o_far, across), earlier = lax.optimization_barrier(
-                ((dh_same, dh_oth, o_far, across), earlier)
+            earlier = (out_parts[-1], far_parts[-1])
+            (back, o_far, across), earlier = lax.optimization_barrier(((back, o_far, across), earlier))
+            out_parts[-1], far_parts[-1] = earlier
+        if last:
+            far_parts.append(
+                [
+                    send(back[0], lambda c, m: (c - 2, m)),
+                    send(back[1], lambda c, m: ((c - 2) ^ 1 if c >= 2 else -1, m)),
+                ]
             )
-            far_parts[-1], out_parts[-1], across_parts[-1] = earlier
-        far_parts.append(
-            (
-                send(dh_same, lambda c, m: (c - 2, m)),
-                send(dh_oth, lambda c, m: ((c - 2) ^ 1 if c >= 2 else -1, m)),
-            )
-        )
+        else:
+            far_parts.append([send(back[0], lambda c, m: (c - 2, m))])
         o_parts = [o_own]
         for dm in range(1, n_mp):
             o_parts.append(send(o_far[2 * dm - 2], lambda c, m: (c, (m + dm) % n_mp)))
@@ -473,7 +489,7 @@
 
     attn_out, grad_queries = gather(
         plan_out,
-        CHUNKS * (n_far + 4),
+        CHUNKS * (len(far) + 4),
         place,
         arrays,
         [(piece, n_mp * heads_mp * pair), (rows, heads_mp * pair)],
@@ -484,9 +500,11 @@
 
     grads_kv = ()
     for i in range(CHUNKS):
-        terms = (near_parts[i], far_parts[i][0], across_parts[i], far_parts[i][1])
-        after = (attn_out,) if i == CHUNKS - 1 else ()
-        grads_kv = sum_terms(place, i, heads, heads_mp, terms, grads_kv, after)
+        far_i = far_parts[i] if len(far_parts[i]) > 1 else [*far_parts[i], send(far_parts[i][0], swap)]
+        for side, near_i in enumerate((near_parts[i], across_parts[i])):
+            after = (attn_out,) if i == CHUNKS - 1 and side == 1 else ()
+            terms = (near_i, far_i[side])
+            grads_kv = sum_terms(place, i, side, heads, heads_mp, terms, grads_kv, after)
     return attn_out, grad_queries, grads_kv[0], grads_kv[1]
 
 

time: 122 us -> 116 us (0.951)
  waiting for transfers between devices: 28.6 us -> 17.9 us
  Pallas kernels: 64.1 us -> 68.1 us
    ppermute x19, waiting for transfers between devices: 28.6 us -> 17.9 us  [send(): return lax.ppermute(x, AXES, routes(target, n_ctx, n_mp))]
    pallas_call x2 -> x4, Pallas kernels: 6.71 us -> 11 us  [sum_terms(): pl.pallas_call(functools.partial(sum_kernel, heads), grid_spec=pltpu.Pref...]
  transfers between devices with their start and end apart: 19 -> 19, of which waited for: 7 -> 7; matrix products, arithmetic and copies ran while one was open for 2% -> 2% of each run, Pallas kernels for 48% -> 54%
where the time goes in v5:
time: 116 us; the launch traced here: 115 us
  Pallas kernels  68.1 us (59%)
  starting transfers between devices  25.6 us (22%)
  waiting for transfers between devices  17.9 us (15%)
  other arithmetic  2.19 us (2%)
    pallas_call x2, Pallas kernels, attention(): pl.pallas_call(functools.partial(attention_kernel, n_mp, rows, whole), gr...  42.2 us
    ppermute x19, starting transfers between devices, send(): return lax.ppermute(x, AXES, routes(target, n_ctx, n_mp))  25.6 us
    ppermute x19, waiting for transfers between devices, send(): return lax.ppermute(x, AXES, routes(target, n_ctx, n_mp))  17.9 us
    pallas_call x4, Pallas kernels, gather(): pl.pallas_call(functools.partial(gather_kernel, plan, len(arrays) + len(a...  14.8 us
    pallas_call x4, Pallas kernels, sum_terms(): pl.pallas_call(functools.partial(sum_kernel, heads), grid_spec=pltpu.Pref...  11 us
  transfers between devices with their start and end apart: 19, of which 7 were waited for; matrix products, arithmetic and copies ran while one was open for 2% of the time, Pallas kernels for 54%

profile of v5, /device:TPU:0, one launch (start us, length us, event | category | flops | bytes accessed | tf_op | source)
XLA Modules:
  0.0 115.4 jit_solution(11052758044361253363)
XLA Ops:
  0.6 0.0 copy-start
  0.7 0.6 pad_add_fusion.sc_ref
  1.3 2.7 %pack_halo.2 = (bf16[512,512]{1,0:T(8,128)(2,1)}, bf16[512,512]{1,0:T(8,128)(2,1)}) custom-call(s32[2]{0:T(128)} %pad_add_fusion.sc_ref, bf16[512,1024]{1,0:T(8,128)(2,1)} %refs_1_.9, bf16[512,1024]{1,0:T(8,128)(2,1)} %refs_2_.5), custom_call_target="tpu_custom_call" | custom-call | flops 24999999488 | bytes 1024 | tf_op jit(solution)/shard_map/pack_halo/pallas_call | solution.py:70
  4.0 5.7 %collective-permute-start.4 = (bf16[512,512]{1,0:T(8,128)(2,1)}, bf16[512,512]{1,0:T(8,128)(2,1)}, u32[]{:S(2)}, u32[]{:S(2)}) collective-permute-start(bf16[512,512]{1,0:T(8,128)(2,1)} %get-tuple-element.49.refs_4_), channel_id=1, source_target_pairs={{0,4},{1,5},{2,6},{3,7},{4,8},{5,9},{6,10},{7,11},{8,12},{9,13},{1... | collective-permute-start | bytes 1572872 | tf_op jit(solution)/shard_map/ppermute | solution.py:339
  9.6 2.7 %collective-permute-start.5 = (bf16[512,512]{1,0:T(8,128)(2,1)}, bf16[512,512]{1,0:T(8,128)(2,1)}, u32[]{:S(2)}, u32[]{:S(2)}) collective-permute-start(bf16[512,512]{1,0:T(8,128)(2,1)} %get-tuple-element.50.refs_5_), channel_id=1, source_target_pairs={{0,6},{1,7},{2,4},{3,5},{4,10},{5,11},{6,8},{7,9},{8,14},{9,15},{1... | collective-permute-start | bytes 1572872 | tf_op jit(solution)/shard_map/ppermute | solution.py:339
  12.3 4.6 %pack_near.1 = (bf16[256,1024]{1,0:T(8,128)(2,1)}, bf16[256,1024]{1,0:T(8,128)(2,1)}, bf16[512,2560]{1,0:T(8,128)(2,1)}) custom-call(s32[2]{0:T(128)} %pad_add_fusion.sc_ref, bf16[512,2048]{1,0:T(8,128)(2,1)} %refs_0_.9, bf16[512,1024]{1,0:T(8,128)(2,1)} %refs_1_.9, bf16[512,1024]{1,0:T(8,128)(2,1)} %refs_2_.5, bf16[256,4096]{1,0:T(8,128)(2,1)} %refs_10_.3, ...), custom_call_target="tpu_custom_call" | custom-call | flops 24999999488 | bytes 1024 | tf_op jit(solution)/shard_map/pack_near/pallas_call | solution.py:70
  16.9 1.6 %collective-permute-start = (bf16[256,1024]{1,0:T(8,128)(2,1)}, bf16[256,1024]{1,0:T(8,128)(2,1)}, u32[]{:S(2)}, u32[]{:S(2)}) collective-permute-start(bf16[256,1024]{1,0:T(8,128)(2,1)} %get-tuple-element.51), channel_id=1, source_target_pairs={{0,1},{1,0},{2,3},{3,2},{4,5},{5,4},{6,7},{7,6},{8,9},{9,8},{10,11... | collective-permute-start | bytes 1572872 | tf_op jit(solution)/shard_map/ppermute | solution.py:339
  18.5 0.0 copy-start.1
  18.5 0.7 collective-permute-start.1
  19.2 2.9 %pack_halo.3 = bf16[512,1024]{1,0:T(8,128)(2,1)} custom-call(s32[2]{0:T(128)} %pad_add_fusion.sc_ref, bf16[512,1024]{1,0:T(8,128)(2,1)} %refs_1_.9, bf16[512,1024]{1,0:T(8,128)(2,1)} %refs_2_.5, bf16[512,2560]{1,0:T(8,128)(2,1)} %get-tuple-element.52.refs_2_), custom_call_target="tpu_custom_call" | custom-call | flops 24999999488 | bytes 1024 | tf_op jit(solution)/shard_map/pack_halo/pallas_call | solution.py:70
  22.1 3.5 %collective-permute-start.2 = (bf16[512,1024]{1,0:T(8,128)(2,1)}, bf16[512,1024]{1,0:T(8,128)(2,1)}, u32[]{:S(2)}, u32[]{:S(2)}) collective-permute-start(bf16[512,1024]{1,0:T(8,128)(2,1)} %pack_halo.3), channel_id=1, source_target_pairs={{0,4},{1,5},{2,6},{3,7},{4,8},{5,9},{6,10},{7,11},{8,12},{9,13},{1... | collective-permute-start | bytes 3145736 | tf_op jit(solution)/shard_map/ppermute | solution.py:339
  25.6 0.0 copy-done
  25.6 0.1 constant_dynamic-slice_fusion
  25.7 0.1 copy.17
  25.8 0.7 reshape.27.open_ref
  26.4 0.0 copy-done.1
  26.4 1.0 convert_reduce_fusion
  27.4 0.6 add_maximum_fusion.lo_ref
  28.0 4.1 %collective-permute-done.refs_12_ = bf16[256,1024]{1,0:T(8,128)(2,1)} collective-permute-done((bf16[256,1024]{1,0:T(8,128)(2,1)}, bf16[256,1024]{1,0:T(8,128)(2,1)}, u32[]{:S(2)}, u32[]{:S(2)}) %collective-permute-start) | collective-permute-done | bytes 524320 | tf_op jit(solution)/shard_map/ppermute | solution.py:339
  32.1 0.1 collective-permute-start.6
  32.2 0.0 collective-permute-done.4.refs_6_.refs_7_
  32.2 1.5 %collective-permute-start.3 = (bf16[256,1024]{1,0:T(8,128)(2,1)}, bf16[256,1024]{1,0:T(8,128)(2,1)}, u32[]{:S(2)}, u32[]{:S(2)}) collective-permute-start(bf16[256,1024]{1,0:T(8,128)(2,1)} %get-tuple-element.55), channel_id=1, source_target_pairs={{0,1},{1,0},{2,3},{3,2},{4,5},{5,4},{6,7},{7,6},{8,9},{9,8},{10,11... | collective-permute-start | bytes 1572872 | tf_op jit(solution)/shard_map/ppermute | solution.py:339
  33.7 0.0 collective-permute-done.5.refs_8_.refs_9_
  33.7 0.7 collective-permute-done.6.refs_13_
  34.4 0.0 collective-permute-done.1.refs_3_.refs_4_.refs_5_.refs_11_
  34.4 21.1 %attention.2 = (bf16[512,512]{1,0:T(8,128)(2,1)}, bf16[512,512]{1,0:T(8,128)(2,1)}, bf16[512,1536]{1,0:T(8,128)(2,1)}, bf16[256,512]{1,0:T(8,128)(2,1)}, bf16[25...) custom-call(s32[2]{0:T(128)} %pad_add_fusion.sc_ref, s32[72]{0:T(128)} %reshape.27.open_ref, ...), custom_call_target="tpu_custom_call" | custom-call | bytes 1024 | tf_op jit(solution)/shard_map/attention/pallas_call | solution.py:254
  55.4 0.0 collective-permute-done.3.refs_12_
  55.4 0.0 collective-permute-done.2.refs_6_.refs_7_
  55.4 0.2 collective-permute-start.7
  55.6 0.4 collective-permute-start.8
  56.0 1.5 %collective-permute-start.9 = (bf16[256,512]{1,0:T(8,128)(2,1)}, bf16[256,512]{1,0:T(8,128)(2,1)}, u32[]{:S(2)}, u32[]{:S(2)}) collective-permute-start(bf16[256,512]{1,0:T(8,128)(2,1)} %get-tuple-element.66), channel_id=1, source_target_pairs={{0,1},{1,0},{2,3},{3,2},{4,5},{5,4},{6,7},{7,6},{8,9},{9,8},{10,11... | collective-permute-start | bytes 786440 | tf_op jit(solution)/shard_map/ppermute | solution.py:339
  57.5 0.0 collective-permute-start.10
  57.5 1.5 %collective-permute-start.11 = (bf16[1024,512]{1,0:T(8,128)(2,1)}, bf16[1024,512]{1,0:T(8,128)(2,1)}, u32[]{:S(2)}, u32[]{:S(2)}) collective-permute-start(bf16[1024,512]{1,0:T(8,128)(2,1)} %get-tuple-element.68), channel_id=1, source_target_pairs={{4,0},{5,1},{6,2},{7,3},{8,4},{9,5},{10,6},{11,7},{12,8},{13,9},{1... | collective-permute-start | bytes 3145736 | tf_op jit(solution)/shard_map/ppermute | solution.py:339
  59.0 0.3 collective-permute-done.8.refs_13_
  59.3 0.4 collective-permute-start.12
  59.7 0.0 collective-permute-done.7.refs_8_.refs_9_
  59.7 21.2 %attention.3 = (bf16[512,512]{1,0:T(8,128)(2,1)}, bf16[512,512]{1,0:T(8,128)(2,1)}, bf16[512,1536]{1,0:T(8,128)(2,1)}, bf16[256,512]{1,0:T(8,128)(2,1)}, bf16[25...) custom-call(s32[2]{0:T(128)} %pad_add_fusion.sc_ref, ...), custom_call_target="tpu_custom_call" | custom-call | flops 24999999488 | bytes 1024 | tf_op jit(solution)/shard_map/attention/pallas_call | solution.py:254
  80.9 0.0 collective-permute-done.9.refs_1_
  80.9 0.0 collective-permute-done.10.refs_2_
  80.9 4.5 %collective-permute-done.11.far = bf16[1024,512]{1,0:T(8,128)(2,1)} collective-permute-done((bf16[1024,512]{1,0:T(8,128)(2,1)}, bf16[1024,512]{1,0:T(8,128)(2,1)}, u32[]{:S(2)}, u32[]{:S(2)}) %collective-permute-start.11) | collective-permute-done | bytes 1048608 | tf_op jit(solution)/shard_map/ppermute | solution.py:339
  85.4 0.0 collective-permute-start.15
  85.4 0.5 collective-permute-start.18
  85.9 1.3 %collective-permute-start.17 = (bf16[512,512]{1,0:T(8,128)(2,1)}, bf16[512,512]{1,0:T(8,128)(2,1)}, u32[]{:S(2)}, u32[]{:S(2)}) collective-permute-start(bf16[512,512]{1,0:T(8,128)(2,1)} %get-tuple-element.83), channel_id=1, source_target_pairs={{4,0},{5,1},{6,2},{7,3},{8,4},{9,5},{10,6},{11,7},{12,8},{13,9},{1... | collective-permute-start | bytes 1572872 | tf_op jit(solution)/shard_map/ppermute | solution.py:339
  87.2 1.3 %collective-permute-start.16 = (bf16[512,512]{1,0:T(8,128)(2,1)}, bf16[512,512]{1,0:T(8,128)(2,1)}, u32[]{:S(2)}, u32[]{:S(2)}) collective-permute-start(bf16[512,512]{1,0:T(8,128)(2,1)} %get-tuple-element.81), channel_id=1, source_target_pairs={{4,2},{5,3},{6,0},{7,1},{8,6},{9,7},{10,4},{11,5},{12,10},{13,11},... | collective-permute-start | bytes 1572872 | tf_op jit(solution)/shard_map/ppermute | solution.py:339
  88.5 0.0 collective-permute-done.12.refs_3_.near
  88.5 1.6 %collective-permute-start.13 = (bf16[256,512]{1,0:T(8,128)(2,1)}, bf16[256,512]{1,0:T(8,128)(2,1)}, u32[]{:S(2)}, u32[]{:S(2)}) collective-permute-start(bf16[256,512]{1,0:T(8,128)(2,1)} %get-tuple-element.75), channel_id=1, source_target_pairs={{0,1},{1,0},{2,3},{3,2},{4,5},{5,4},{6,7},{7,6},{8,9},{9,8},{10,11... | collective-permute-start | bytes 786440 | tf_op jit(solution)/shard_map/ppermute | solution.py:339
  90.1 0.6 collective-permute-done.18.far
  90.7 1.3 %collective-permute-start.14 = (bf16[256,512]{1,0:T(8,128)(2,1)}, bf16[256,512]{1,0:T(8,128)(2,1)}, u32[]{:S(2)}, u32[]{:S(2)}) collective-permute-start(bf16[256,512]{1,0:T(8,128)(2,1)} %get-tuple-element.76), channel_id=1, source_target_pairs={{0,3},{1,2},{2,1},{3,0},{4,7},{5,6},{6,5},{7,4},{8,11},{9,10},{10,... | collective-permute-start | bytes 786440 | tf_op jit(solution)/shard_map/ppermute | solution.py:339
  91.9 2.8 %sum_terms.4 = (bf16[512,1024]{1,0:T(8,128)(2,1)}, bf16[512,1024]{1,0:T(8,128)(2,1)}) custom-call(s32[2]{0:T(128)} %pad_add_fusion.sc_ref, bf16[512,512]{1,0:T(8,128)(2,1)} %get-tuple-element.85.near, bf16[1024,512]{1,0:T(8,128)(2,1)} %collective-permute-done.11.far), custom_call_target="tpu_custom_call" | custom-call | bytes 1024 | tf_op jit(solution)/shard_map/sum_terms/pallas_call | solution.py:308
  94.7 2.8 %sum_terms.5 = (bf16[512,1024]{1,0:T(8,128)(2,1)}, bf16[512,1024]{1,0:T(8,128)(2,1)}) custom-call(s32[2]{0:T(128)} %pad_add_fusion.sc_ref, bf16[512,1536]{1,0:T(8,128)(2,1)} %collective-permute-done.12.refs_3_.near, bf16[1024,512]{1,0:T(8,128)(2,1)} %collective-permute-done.18.far, ...), custom_call_target="tpu_custom_call", output_to_operand_aliasing={{0}: (3, {}), {1}: (4, {})} | custom-call | bytes 1024 | tf_op jit(solution)/shard_map/sum_terms/pallas_call | solution.py:308
  97.5 5.4 %collective-permute-done.17.far = bf16[512,512]{1,0:T(8,128)(2,1)} collective-permute-done((bf16[512,512]{1,0:T(8,128)(2,1)}, bf16[512,512]{1,0:T(8,128)(2,1)}, u32[]{:S(2)}, u32[]{:S(2)}) %collective-permute-start.17) | collective-permute-done | bytes 524320 | tf_op jit(solution)/shard_map/ppermute | solution.py:339
  102.9 2.8 %sum_terms.6 = (bf16[512,1024]{1,0:T(8,128)(2,1)}, bf16[512,1024]{1,0:T(8,128)(2,1)}) custom-call(s32[2]{0:T(128)} %pad_add_fusion.sc_ref, bf16[512,512]{1,0:T(8,128)(2,1)} %get-tuple-element.82.near, bf16[512,512]{1,0:T(8,128)(2,1)} %collective-permute-done.17.far, ...), custom_call_target="tpu_custom_call", output_to_operand_aliasing={{0}: (3, {}), {1}: (4, {})} | custom-call | bytes 1024 | tf_op jit(solution)/shard_map/sum_terms/pallas_call | solution.py:308
  105.7 0.0 collective-permute-done.13.refs_6_
  105.7 0.0 collective-permute-done.14.refs_7_
  105.7 0.0 collective-permute-done.15.refs_8_.near
  105.7 4.6 %put_together.1 = (bf16[256,4096]{1,0:T(8,128)(2,1)}, bf16[512,2048]{1,0:T(8,128)(2,1)}) custom-call(s32[2]{0:T(128)} %pad_add_fusion.sc_ref, bf16[256,512]{1,0:T(8,128)(2,1)} %get-tuple-element.69.refs_0_, bf16[256,512]{1,0:T(8,128)(2,1)} %collective-permute-done.9.refs_1_, bf16[256,512]{1,0:T(8,128)(2,1)} %collective-permute-done.10.refs_2_, ...), custom_call_target="tpu_custom_call" | custom-call | bytes 1024 | tf_op jit(solution)/shard_map/put_together/pallas_call | solution.py:70
  110.3 2.3 %collective-permute-done.16.far = bf16[512,512]{1,0:T(8,128)(2,1)} collective-permute-done((bf16[512,512]{1,0:T(8,128)(2,1)}, bf16[512,512]{1,0:T(8,128)(2,1)}, u32[]{:S(2)}, u32[]{:S(2)}) %collective-permute-start.16) | collective-permute-done | bytes 524320 | tf_op jit(solution)/shard_map/ppermute | solution.py:339
  112.6 2.8 %sum_terms.7 = (bf16[512,1024]{1,0:T(8,128)(2,1)}, bf16[512,1024]{1,0:T(8,128)(2,1)}) custom-call(s32[2]{0:T(128)} %pad_add_fusion.sc_ref, bf16[512,1536]{1,0:T(8,128)(2,1)} %collective-permute-done.15.refs_8_.near, bf16[512,512]{1,0:T(8,128)(2,1)} %collective-permute-done.16.far, ...), custom_call_target="tpu_custom_call", output_to_operand_aliasing={{0}: (3, {}), {1}: (4, {})} | custom-call | bytes 1024 | tf_op jit(solution)/shard_map/sum_terms/pallas_call | solution.py:308
  (2 shorter events, 0.0 us)
Async XLA Ops:
  0.6 25.0 %copy-start = (s32[64,9]{0,1:T(8,128)S(1)}, s32[64,9]{0,1:T(8,128)}, u32[]{:S(2)}) copy-start(s32[64,9]{0,1:T(8,128)} %param.10) | copy-start | bytes 6916
  4.0 28.2 %collective-permute-start.4 = (bf16[512,512]{1,0:T(8,128)(2,1)}, bf16[512,512]{1,0:T(8,128)(2,1)}, u32[]{:S(2)}, u32[]{:S(2)}) collective-permute-start(bf16[512,512]{1,0:T(8,128)(2,1)} %get-tuple-element.49.refs_4_), channel_id=1, source_target_pairs={{0,4},{1,5},{2,6},{3,7},{4,8},{5,9},{6,10},{7,11},{8,12},{9,13},{1... | collective-permute-start | bytes 1572872 | tf_op jit(solution)/shard_map/ppermute | solution.py:339
  9.6 24.1 %collective-permute-start.5 = (bf16[512,512]{1,0:T(8,128)(2,1)}, bf16[512,512]{1,0:T(8,128)(2,1)}, u32[]{:S(2)}, u32[]{:S(2)}) collective-permute-start(bf16[512,512]{1,0:T(8,128)(2,1)} %get-tuple-element.50.refs_5_), channel_id=1, source_target_pairs={{0,6},{1,7},{2,4},{3,5},{4,10},{5,11},{6,8},{7,9},{8,14},{9,15},{1... | collective-permute-start | bytes 1572872 | tf_op jit(solution)/shard_map/ppermute | solution.py:339
  16.9 15.2 %collective-permute-start = (bf16[256,1024]{1,0:T(8,128)(2,1)}, bf16[256,1024]{1,0:T(8,128)(2,1)}, u32[]{:S(2)}, u32[]{:S(2)}) collective-permute-start(bf16[256,1024]{1,0:T(8,128)(2,1)} %get-tuple-element.51), channel_id=1, source_target_pairs={{0,1},{1,0},{2,3},{3,2},{4,5},{5,4},{6,7},{7,6},{8,9},{9,8},{10,11... | collective-permute-start | bytes 1572872 | tf_op jit(solution)/shard_map/ppermute | solution.py:339
  18.5 7.9 %copy-start.1 = (s32[8192]{0:T(1024)S(1)}, s32[8192]{0:T(1024)}, u32[]{:S(2)}) copy-start(s32[8192]{0:T(1024)} %param.11) | copy-start | bytes 98308
  18.5 15.9 %collective-permute-start.1 = (bf16[512,2560]{1,0:T(8,128)(2,1)}, bf16[512,2560]{1,0:T(8,128)(2,1)}, u32[]{:S(2)}, u32[]{:S(2)}) collective-permute-start(bf16[512,2560]{1,0:T(8,128)(2,1)} %get-tuple-element.52.refs_2_), channel_id=1, source_target_pairs={{0,2},{1,3},{2,0},{3,1},{4,6},{5,7},{6,4},{7,5},{8,10},{9,11},{10,... | collective-permute-start | bytes 7864328 | tf_op jit(solution)/shard_map/ppermute | solution.py:339
  22.1 33.4 %collective-permute-start.2 = (bf16[512,1024]{1,0:T(8,128)(2,1)}, bf16[512,1024]{1,0:T(8,128)(2,1)}, u32[]{:S(2)}, u32[]{:S(2)}) collective-permute-start(bf16[512,1024]{1,0:T(8,128)(2,1)} %pack_halo.3), channel_id=1, source_target_pairs={{0,4},{1,5},{2,6},{3,7},{4,8},{5,9},{6,10},{7,11},{8,12},{9,13},{1... | collective-permute-start | bytes 3145736 | tf_op jit(solution)/shard_map/ppermute | solution.py:339
  32.1 2.3 %collective-permute-start.6 = (bf16[256,1024]{1,0:T(8,128)(2,1)}, bf16[256,1024]{1,0:T(8,128)(2,1)}, u32[]{:S(2)}, u32[]{:S(2)}) collective-permute-start(bf16[256,1024]{1,0:T(8,128)(2,1)} %collective-permute-done.refs_12_), channel_id=1, source_target_pairs={{0,2},{1,3},{2,0},{3,1},{4,6},{5,7},{6,4},{7,5},{8,10},{9,11},{10,... | collective-permute-start | bytes 1572872 | tf_op jit(solution)/shard_map/ppermute | solution.py:339
  32.2 23.2 %collective-permute-start.3 = (bf16[256,1024]{1,0:T(8,128)(2,1)}, bf16[256,1024]{1,0:T(8,128)(2,1)}, u32[]{:S(2)}, u32[]{:S(2)}) collective-permute-start(bf16[256,1024]{1,0:T(8,128)(2,1)} %get-tuple-element.55), channel_id=1, source_target_pairs={{0,1},{1,0},{2,3},{3,2},{4,5},{5,4},{6,7},{7,6},{8,9},{9,8},{10,11... | collective-permute-start | bytes 1572872 | tf_op jit(solution)/shard_map/ppermute | solution.py:339
  55.4 4.3 %collective-permute-start.7 = (bf16[512,1024]{1,0:T(8,128)(2,1)}, bf16[512,1024]{1,0:T(8,128)(2,1)}, u32[]{:S(2)}, u32[]{:S(2)}) collective-permute-start(bf16[512,1024]{1,0:T(8,128)(2,1)} %collective-permute-done.2.refs_6_.refs_7_), channel_id=1, source_target_pairs={{0,2},{1,3},{2,0},{3,1},{4,6},{5,7},{6,4},{7,5},{8,10},{9,11},{10,... | collective-permute-start | bytes 3145736 | tf_op jit(solution)/shard_map/ppermute | solution.py:339
  55.6 3.6 %collective-permute-start.8 = (bf16[256,1024]{1,0:T(8,128)(2,1)}, bf16[256,1024]{1,0:T(8,128)(2,1)}, u32[]{:S(2)}, u32[]{:S(2)}) collective-permute-start(bf16[256,1024]{1,0:T(8,128)(2,1)} %collective-permute-done.3.refs_12_), channel_id=1, source_target_pairs={{0,2},{1,3},{2,0},{3,1},{4,6},{5,7},{6,4},{7,5},{8,10},{9,11},{10,... | collective-permute-start | bytes 1572872 | tf_op jit(solution)/shard_map/ppermute | solution.py:339
  56.0 24.9 %collective-permute-start.9 = (bf16[256,512]{1,0:T(8,128)(2,1)}, bf16[256,512]{1,0:T(8,128)(2,1)}, u32[]{:S(2)}, u32[]{:S(2)}) collective-permute-start(bf16[256,512]{1,0:T(8,128)(2,1)} %get-tuple-element.66), channel_id=1, source_target_pairs={{0,1},{1,0},{2,3},{3,2},{4,5},{5,4},{6,7},{7,6},{8,9},{9,8},{10,11... | collective-permute-start | bytes 786440 | tf_op jit(solution)/shard_map/ppermute | solution.py:339
  57.5 23.4 %collective-permute-start.10 = (bf16[256,512]{1,0:T(8,128)(2,1)}, bf16[256,512]{1,0:T(8,128)(2,1)}, u32[]{:S(2)}, u32[]{:S(2)}) collective-permute-start(bf16[256,512]{1,0:T(8,128)(2,1)} %get-tuple-element.67), channel_id=1, source_target_pairs={{0,3},{1,2},{2,1},{3,0},{4,7},{5,6},{6,5},{7,4},{8,11},{9,10},{10,... | collective-permute-start | bytes 786440 | tf_op jit(solution)/shard_map/ppermute | solution.py:339
  57.5 27.9 %collective-permute-start.11 = (bf16[1024,512]{1,0:T(8,128)(2,1)}, bf16[1024,512]{1,0:T(8,128)(2,1)}, u32[]{:S(2)}, u32[]{:S(2)}) collective-permute-start(bf16[1024,512]{1,0:T(8,128)(2,1)} %get-tuple-element.68), channel_id=1, source_target_pairs={{4,0},{5,1},{6,2},{7,3},{8,4},{9,5},{10,6},{11,7},{12,8},{13,9},{1... | collective-permute-start | bytes 3145736 | tf_op jit(solution)/shard_map/ppermute | solution.py:339
  59.3 29.3 %collective-permute-start.12 = (bf16[512,1536]{1,0:T(8,128)(2,1)}, bf16[512,1536]{1,0:T(8,128)(2,1)}, u32[]{:S(2)}, u32[]{:S(2)}) collective-permute-start(bf16[512,1536]{1,0:T(8,128)(2,1)} %get-tuple-element.72), channel_id=1, source_target_pairs={{0,2},{1,3},{2,0},{3,1},{4,6},{5,7},{6,4},{7,5},{8,10},{9,11},{10,... | collective-permute-start | bytes 4718600 | tf_op jit(solution)/shard_map/ppermute | solution.py:339
  85.4 20.2 %collective-permute-start.15 = (bf16[512,1536]{1,0:T(8,128)(2,1)}, bf16[512,1536]{1,0:T(8,128)(2,1)}, u32[]{:S(2)}, u32[]{:S(2)}) collective-permute-start(bf16[512,1536]{1,0:T(8,128)(2,1)} %get-tuple-element.77), channel_id=1, source_target_pairs={{0,2},{1,3},{2,0},{3,1},{4,6},{5,7},{6,4},{7,5},{8,10},{9,11},{10,... | collective-permute-start | bytes 4718600 | tf_op jit(solution)/shard_map/ppermute | solution.py:339
  85.4 5.2 %collective-permute-start.18 = (bf16[1024,512]{1,0:T(8,128)(2,1)}, bf16[1024,512]{1,0:T(8,128)(2,1)}, u32[]{:S(2)}, u32[]{:S(2)}) collective-permute-start(bf16[1024,512]{1,0:T(8,128)(2,1)} %collective-permute-done.11.far), channel_id=1, source_target_pairs={{0,2},{1,3},{2,0},{3,1},{4,6},{5,7},{6,4},{7,5},{8,10},{9,11},{10,... | collective-permute-start | bytes 3145736 | tf_op jit(solution)/shard_map/ppermute | solution.py:339
  85.9 17.0 %collective-permute-start.17 = (bf16[512,512]{1,0:T(8,128)(2,1)}, bf16[512,512]{1,0:T(8,128)(2,1)}, u32[]{:S(2)}, u32[]{:S(2)}) collective-permute-start(bf16[512,512]{1,0:T(8,128)(2,1)} %get-tuple-element.83), channel_id=1, source_target_pairs={{4,0},{5,1},{6,2},{7,3},{8,4},{9,5},{10,6},{11,7},{12,8},{13,9},{1... | collective-permute-start | bytes 1572872 | tf_op jit(solution)/shard_map/ppermute | solution.py:339
  87.2 25.4 %collective-permute-start.16 = (bf16[512,512]{1,0:T(8,128)(2,1)}, bf16[512,512]{1,0:T(8,128)(2,1)}, u32[]{:S(2)}, u32[]{:S(2)}) collective-permute-start(bf16[512,512]{1,0:T(8,128)(2,1)} %get-tuple-element.81), channel_id=1, source_target_pairs={{4,2},{5,3},{6,0},{7,1},{8,6},{9,7},{10,4},{11,5},{12,10},{13,11},... | collective-permute-start | bytes 1572872 | tf_op jit(solution)/shard_map/ppermute | solution.py:339
  88.5 17.1 %collective-permute-start.13 = (bf16[256,512]{1,0:T(8,128)(2,1)}, bf16[256,512]{1,0:T(8,128)(2,1)}, u32[]{:S(2)}, u32[]{:S(2)}) collective-permute-start(bf16[256,512]{1,0:T(8,128)(2,1)} %get-tuple-element.75), channel_id=1, source_target_pairs={{0,1},{1,0},{2,3},{3,2},{4,5},{5,4},{6,7},{7,6},{8,9},{9,8},{10,11... | collective-permute-start | bytes 786440 | tf_op jit(solution)/shard_map/ppermute | solution.py:339
  90.7 15.0 %collective-permute-start.14 = (bf16[256,512]{1,0:T(8,128)(2,1)}, bf16[256,512]{1,0:T(8,128)(2,1)}, u32[]{:S(2)}, u32[]{:S(2)}) collective-permute-start(bf16[256,512]{1,0:T(8,128)(2,1)} %get-tuple-element.76), channel_id=1, source_target_pairs={{0,3},{1,2},{2,1},{3,0},{4,7},{5,6},{6,5},{7,4},{8,11},{9,10},{10,... | collective-permute-start | bytes 786440 | tf_op jit(solution)/shard_map/ppermute | solution.py:339

commit v6 on v5

--- a/solution.py
+++ b/solution.py
@@ -41,12 +41,12 @@
     return out
 
 
-def gather_kernel(plan, n_in, shapes, sc_ref, *refs):
+def gather_kernel(plan, n_in, shapes, *refs):
     n = len(shapes)
     outs, images, sems = refs[n_in : n_in + n], refs[n_in + n : n_in + 2 * n], refs[-2:]
     into = [[] for _ in shapes]
     count = 0
-    for src, dst, src_at, dst_at, size in plan(sc_ref[0], sc_ref[1]):
+    for src, dst, src_at, dst_at, size in plan(lax.rem(lax.axis_index("ctx"), 2), lax.axis_index("mp")):
         copy = pltpu.make_async_copy(
             refs[src].at[tuple(pl.ds(at, by) for at, by in zip(src_at, size))],
             images[dst].at[tuple(pl.ds(at, by) for at, by in zip(dst_at, size))],
@@ -65,11 +65,11 @@
         copy.wait()
 
 
-def gather(plan, count, place, arrays, shapes, cost, after=(), name="gather"):
+def gather(plan, count, arrays, shapes, cost, after=(), name="gather"):
     hbm = pl.BlockSpec(memory_space=pl.ANY)
     return pl.pallas_call(
         functools.partial(gather_kernel, plan, len(arrays) + len(after), shapes),
-        in_specs=[pl.BlockSpec(memory_space=pltpu.SMEM)] + [hbm] * (len(arrays) + len(after)),
+        in_specs=[hbm] * (len(arrays) + len(after)),
         out_specs=[hbm] * len(shapes),
         out_shape=[jax.ShapeDtypeStruct(shape, jnp.bfloat16) for shape in shapes],
         scratch_shapes=[pltpu.VMEM(shape, jnp.bfloat16) for shape in shapes]
@@ -77,7 +77,7 @@
         compiler_params=pltpu.CompilerParams(vmem_limit_bytes=VMEM_LIMIT),
         cost_estimate=cost,
         name=name,
-    )(place, *arrays, *after)
+    )(*arrays, *after)
 
 
 def attention_kernel(n_mp, rows, whole, sc_ref, open_ref, lo_ref, *refs):
@@ -86,9 +86,9 @@
     do_far = refs[12 : 10 + 2 * n_mp]
     refs = refs[10 + 2 * n_mp :]
     n_back = 1 if whole else 2
-    dq_same, dkv_same, across, o_own, *o_far = refs[: 2 + 2 * n_mp]
-    back = refs[2 + 2 * n_mp : 2 + 2 * n_mp + n_back]
-    refs = refs[2 + 2 * n_mp + n_back :]
+    dq_same, dkv_same, across, o_own, o_oth, *o_far = refs[: 3 + 2 * n_mp]
+    back = refs[3 + 2 * n_mp : 3 + 2 * n_mp + n_back]
+    refs = refs[3 + 2 * n_mp + n_back :]
     qs, ks, vs, k_t, v_t, dos, os, dqs, dk, dv = refs[:10]
     s_refs, e_refs, ds_refs = refs[-6:-4], refs[-4:-2], refs[-2:]
     core, mp = sc_ref[0], sc_ref[1]
@@ -188,11 +188,11 @@
         backward(b, *now)
 
     dq_same[...] = dqs[same, :]
-    wide = across.shape[1] // 3
+    wide = across.shape[1] // 2
     at_g = pl.multiple_of(pl.program_id(0) * pair, pair)
     across[:, pl.ds(at_g, pair)] = dqs[oth, :]
-    across[:, pl.ds(2 * wide + at_g, pair)] = os[oth, :]
     o_own[...] = os[piece_at(0, 0), :]
+    o_oth[...] = os[piece_at(1, 0), :]
     for at in range(n_mp - 1):
         o_far[2 * at][...] = os[piece_at(0, at + 1), :]
         o_far[2 * at + 1][...] = os[piece_at(1, at + 1), :]
@@ -242,11 +242,11 @@
     wide = heads_chunk * pair
     bf, f32 = jnp.bfloat16, jnp.float32
     out_specs = [pl.BlockSpec((rows, pair), at_local)] * 2
-    out_specs += [pl.BlockSpec((rows, 3 * wide), lambda g, *unused: (0, 0))]
-    out_specs += [pl.BlockSpec((piece, pair), at_local)] * (2 * n_mp - 1)
+    out_specs += [pl.BlockSpec((rows, 2 * wide), lambda g, *unused: (0, 0))]
+    out_specs += [pl.BlockSpec((piece, pair), at_local)] * (2 * n_mp)
     out_shape = [jax.ShapeDtypeStruct((rows, wide), bf)] * 2
-    out_shape += [jax.ShapeDtypeStruct((rows, 3 * wide), bf)]
-    out_shape += [jax.ShapeDtypeStruct((piece, wide), bf)] * (2 * n_mp - 1)
+    out_shape += [jax.ShapeDtypeStruct((rows, 2 * wide), bf)]
+    out_shape += [jax.ShapeDtypeStruct((piece, wide), bf)] * (2 * n_mp)
     n_back, rows_back = (1, 2 * rows) if whole else (2, rows)
     out_specs += [pl.BlockSpec((rows_back, pair), at_local)] * n_back
     out_shape += [jax.ShapeDtypeStruct((rows_back, wide), bf)] * n_back
@@ -279,47 +279,41 @@
     )(place, opened, lo, *own, near, near, near, halo[0], halo[0], halo[1], halo[1], grad_out, near, *far_do)
 
 
-def sum_kernel(heads, sc_ref, near, far, *refs):
+def sum_kernel(heads, sc_ref, *refs):
     dk, dv = refs[-2:]
-    for g in range(heads):
-        at = 2 * g * HEAD
-        to = slice(g * HEAD, g * HEAD + HEAD)
-        for out, col in ((dk, at), (dv, at + HEAD)):
-            terms = [x[:, col : col + HEAD].astype(jnp.float32) for x in (near, far)]
-            out[:, to] = (terms[0] + terms[1]).astype(out.dtype)
-
-
-def sum_terms(place, chunk, side, heads, n_heads, terms, before, after=()):
-    rows = terms[0].shape[0]
-    wide = 2 * heads * HEAD
-    by_core = terms[1].shape[0] > rows
-
-    def at_near(n, sc):
-        return (0, side)
-
-    def at_far(n, sc):
-        return (sc[0] if by_core else 0, 0)
-
-    def at_out(n, sc):
-        return (0, 2 * chunk + (sc[0] if side == 0 else 1 - sc[0]))
+    core = sc_ref[0]
+    for at in range(heads * 2):
+        near, far = refs[2 * at : 2 * at + 2]
+        half = core if at % 2 == 0 else 1 - core
+        to = pl.ds(pl.multiple_of((half * heads + at // 2) * HEAD, HEAD), HEAD)
+        total = near[...].astype(jnp.float32) + far[...].astype(jnp.float32)
+        dk[:, to] = total[:, :HEAD].astype(dk.dtype)
+        dv[:, to] = total[:, HEAD:].astype(dv.dtype)
+
+
+def sum_terms(place, chunk, heads, n_heads, terms, before, after):
+    pair = 2 * HEAD
+    rows = terms[0][0].shape[0]
+    hbm = pl.BlockSpec(memory_space=pl.ANY)
+
+    def spec(x, by_core, column):
+        return pl.BlockSpec((rows, pair), lambda g, sc: (sc[0] if by_core else 0, column))
 
     shape = jax.ShapeDtypeStruct((rows, n_heads * HEAD), jnp.bfloat16)
-    hbm = pl.BlockSpec(memory_space=pl.ANY)
     return pl.pallas_call(
         functools.partial(sum_kernel, heads),
         grid_spec=pltpu.PrefetchScalarGridSpec(
             num_scalar_prefetch=1,
             grid=(1,),
-            in_specs=[pl.BlockSpec((rows, wide), at) for at in (at_near, at_far)]
-            + [hbm] * len((*before, *after)),
-            out_specs=[pl.BlockSpec((rows, heads * HEAD), at_out)] * 2,
+            in_specs=[spec(*t) for t in terms] + [hbm] * len((*before, *after)),
+            out_specs=[pl.BlockSpec((rows, 2 * heads * HEAD), lambda g, sc: (0, chunk))] * 2,
         ),
         out_shape=[shape, shape],
-        input_output_aliases={3: 0, 4: 1} if before else {},
+        input_output_aliases={len(terms) + 1: 0, len(terms) + 2: 1} if before else {},
         compiler_params=pltpu.CompilerParams(vmem_limit_bytes=VMEM_LIMIT),
         cost_estimate=LIGHT,
         name="sum_terms",
-    )(place, *terms, *before, *after)
+    )(place, *[t[0] for t in terms], *before, *after)
 
 
 def body(queries, keys, values, grad_out, band_mask, segment_ids):
@@ -360,7 +354,7 @@
 
     def pack_halo(chunk, after):
         shapes = [(rows, wide)] * 2 if chunk == 0 else [(rows, 2 * wide)]
-        return gather(plan_halo(chunk), 4, place, (keys, values), shapes, HEAVY, after, "pack_halo")
+        return gather(plan_halo(chunk), 4, (keys, values), shapes, HEAVY, after, "pack_halo")
 
     far = [(dk, dm) for dm in range(1, n_mp) for dk in range(2)]
     n_far = n_mp - 1
@@ -389,7 +383,6 @@
     *far_do, near = gather(
         plan_near,
         CHUNKS * (2 * n_far + 4),
-        place,
         (queries, keys, values, grad_out),
         [(piece, 2 * wide)] * (CHUNKS * n_far) + [(rows, (2 * CHUNKS + 1) * wide)],
         HEAVY,
@@ -441,12 +434,12 @@
             grad_out,
             [y for x in far_do[i] for y in (x, send(x, swap))],
         )
-        n_far_o = 2 * n_mp - 2
+        n_far_o = 2 * n_mp - 1
         o_far, back = o_far[:n_far_o], o_far[n_far_o:]
         if i:
-            earlier = (out_parts[-1], far_parts[-1])
+            earlier = (out_parts[-1], across_parts[-1])
             (back, o_far, across), earlier = lax.optimization_barrier(((back, o_far, across), earlier))
-            out_parts[-1], far_parts[-1] = earlier
+            out_parts[-1], across_parts[-1] = earlier
         if last:
             far_parts.append(
                 [
@@ -456,11 +449,14 @@
             )
         else:
             far_parts.append([send(back[0], lambda c, m: (c - 2, m))])
-        o_parts = [o_own]
-        for dm in range(1, n_mp):
-            o_parts.append(send(o_far[2 * dm - 2], lambda c, m: (c, (m + dm) % n_mp)))
-            o_parts.append(send(o_far[2 * dm - 1], lambda c, m: (c ^ 1, (m + dm) % n_mp)))
-        out_parts.append(o_parts)
+        o_parts = [
+            send(o_far[1 + at], lambda c, m: (c ^ dk, (m + dm) % n_mp))
+            for at, (dk, dm) in enumerate(far)
+        ]
+        o_oth = o_far[0]
+        if last:
+            o_oth, o_parts[0] = lax.optimization_barrier((o_oth, o_parts[0]))
+        out_parts.append([o_own, send(o_oth, swap), *o_parts])
         across_parts.append(send(across, swap))
         dq_parts.append(dq_same)
         near_parts.append(dkv_same)
@@ -472,14 +468,11 @@
     def plan_out(core, mp):
         jobs, at = [], 0
         for i in range(CHUNKS):
-            for dk, dm in [(0, 0)] + far:
+            for dk, dm in [(0, 0), (1, 0)] + far:
                 mp_from, core_from = lax.rem(mp + n_mp - dm, n_mp), core if dk == 0 else 1 - core
                 to = col(mp_from * heads_mp + first_head(i, core_from), pair)
                 jobs.append((at, 0, (0, 0), (0, to), (piece, wide)))
                 at += 1
-            to = col(mp * heads_mp + first_head(i, 1 - core), pair)
-            rows_at = pl.multiple_of(mp * piece, piece)
-            jobs.append((at, 0, (rows_at, 2 * wide), (0, to), (piece, wide)))
             to = col(first_head(i, 1 - core), pair)
             jobs.append((at, 1, (0, 0), (0, to), (rows, wide)))
             to = col(first_head(i, core), pair)
@@ -490,7 +483,6 @@
     attn_out, grad_queries = gather(
         plan_out,
         CHUNKS * (len(far) + 4),
-        place,
         arrays,
         [(piece, n_mp * heads_mp * pair), (rows, heads_mp * pair)],
         LIGHT,
@@ -500,11 +492,19 @@
 
     grads_kv = ()
     for i in range(CHUNKS):
-        far_i = far_parts[i] if len(far_parts[i]) > 1 else [*far_parts[i], send(far_parts[i][0], swap)]
-        for side, near_i in enumerate((near_parts[i], across_parts[i])):
-            after = (attn_out,) if i == CHUNKS - 1 and side == 1 else ()
-            terms = (near_i, far_i[side])
-            grads_kv = sum_terms(place, i, side, heads, heads_mp, terms, grads_kv, after)
+        terms = []
+        if i < CHUNKS - 1:
+            back, far_parts[-1][0] = lax.optimization_barrier((far_parts[i][0], far_parts[-1][0]))
+            handed = [
+                send(lax.dynamic_slice(back, ((1 - core) * rows, g * pair), (rows, pair)), swap)
+                for g in range(heads)
+            ]
+        for g in range(heads):
+            last = i == CHUNKS - 1
+            terms += [(near_parts[i], False, g), (far_parts[i][0], not last, g)]
+            terms += [(across_parts[i], False, heads + g)]
+            terms += [(far_parts[i][1], False, g) if last else (handed[g], False, 0)]
+        grads_kv = sum_terms(place, i, heads, heads_mp, terms, grads_kv, (attn_out,))
     return attn_out, grad_queries, grads_kv[0], grads_kv[1]
 
 

time: 116 us -> 114 us (0.983)
  the two profiles are of different devices: /device:TPU:0 before, /device:TPU:15 now
where the time goes in v6:
time: 114 us
  Pallas kernels  61.1 us (54%)
  starting transfers between devices  27.6 us (24%)
  waiting for transfers between devices  19.5 us (17%)
  local copies, waits for them, and re-layouts  2.59 us (2%)
  other arithmetic  2.25 us (2%)
    pallas_call x2, Pallas kernels, attention(): pl.pallas_call(functools.partial(attention_kernel, n_mp, rows, whole), gr...  42.1 us
    ppermute x22, starting transfers between devices, send(): return lax.ppermute(x, AXES, routes(target, n_ctx, n_mp))  27.6 us
    ppermute x22, waiting for transfers between devices, send(): return lax.ppermute(x, AXES, routes(target, n_ctx, n_mp))  19.5 us
    pallas_call x4, Pallas kernels, gather(): pl.pallas_call(functools.partial(gather_kernel, plan, len(arrays) + len(a...  12.2 us
    pallas_call x2, Pallas kernels, sum_terms(): pl.pallas_call(functools.partial(sum_kernel, heads), grid_spec=pltpu.Pref...  6.83 us
  transfers between devices with their start and end apart: 22, of which 6 were waited for; matrix products, arithmetic and copies ran while one was open for 4% of the time, Pallas kernels for 49%

profile of v6, /device:TPU:15, one launch (start us, length us, event | category | flops | bytes accessed | tf_op | source)
XLA Modules:
  0.0 113.9 jit_solution(16570315853125028985)
XLA Ops:
  0.6 0.0 copy-start
  0.6 2.1 %pack_halo.2 = (bf16[512,512]{1,0:T(8,128)(2,1)}, bf16[512,512]{1,0:T(8,128)(2,1)}) custom-call(bf16[512,1024]{1,0:T(8,128)(2,1)} %refs_1_.9, bf16[512,1024]{1,0:T(8,128)(2,1)} %refs_2_.5), custom_call_target="tpu_custom_call" | custom-call | flops 24999999488 | bytes 1024 | tf_op jit(solution)/shard_map/pack_halo/pallas_call | solution.py:70
  2.7 3.1 %collective-permute-start.4 = (bf16[512,512]{1,0:T(8,128)(2,1)}, bf16[512,512]{1,0:T(8,128)(2,1)}, u32[]{:S(2)}, u32[]{:S(2)}) collective-permute-start(bf16[512,512]{1,0:T(8,128)(2,1)} %get-tuple-element.53.refs_4_), channel_id=1, source_target_pairs={{0,4},{1,5},{2,6},{3,7},{4,8},{5,9},{6,10},{7,11},{8,12},{9,13},{1... | collective-permute-start | bytes 1572872 | tf_op jit(solution)/shard_map/ppermute | solution.py:333
  5.9 4.0 %collective-permute-start.5 = (bf16[512,512]{1,0:T(8,128)(2,1)}, bf16[512,512]{1,0:T(8,128)(2,1)}, u32[]{:S(2)}, u32[]{:S(2)}) collective-permute-start(bf16[512,512]{1,0:T(8,128)(2,1)} %get-tuple-element.54.refs_5_), channel_id=1, source_target_pairs={{0,6},{1,7},{2,4},{3,5},{4,10},{5,11},{6,8},{7,9},{8,14},{9,15},{1... | collective-permute-start | bytes 1572872 | tf_op jit(solution)/shard_map/ppermute | solution.py:333
  9.9 3.9 %pack_near.1 = (bf16[256,1024]{1,0:T(8,128)(2,1)}, bf16[256,1024]{1,0:T(8,128)(2,1)}, bf16[512,2560]{1,0:T(8,128)(2,1)}) custom-call(bf16[512,2048]{1,0:T(8,128)(2,1)} %refs_0_.9, bf16[512,1024]{1,0:T(8,128)(2,1)} %refs_1_.9, bf16[512,1024]{1,0:T(8,128)(2,1)} %refs_2_.5, bf16[256,4096]{1,0:T(8,128)(2,1)} %refs_10_.3, ...), custom_call_target="tpu_custom_call" | custom-call | flops 24999999488 | bytes 1024 | tf_op jit(solution)/shard_map/pack_near/pallas_call | solution.py:70
  13.8 0.3 collective-permute-start
  14.1 0.0 copy-start.1
  14.1 0.0 collective-permute-start.1
  14.1 2.2 %pack_halo.3 = bf16[512,1024]{1,0:T(8,128)(2,1)} custom-call(bf16[512,1024]{1,0:T(8,128)(2,1)} %refs_1_.9, bf16[512,1024]{1,0:T(8,128)(2,1)} %refs_2_.5, bf16[512,2560]{1,0:T(8,128)(2,1)} %get-tuple-element.56.refs_2_), custom_call_target="tpu_custom_call" | custom-call | flops 24999999488 | bytes 1024 | tf_op jit(solution)/shard_map/pack_halo/pallas_call | solution.py:70
  16.4 3.1 %collective-permute-start.2 = (bf16[512,1024]{1,0:T(8,128)(2,1)}, bf16[512,1024]{1,0:T(8,128)(2,1)}, u32[]{:S(2)}, u32[]{:S(2)}) collective-permute-start(bf16[512,1024]{1,0:T(8,128)(2,1)} %pack_halo.3), channel_id=1, source_target_pairs={{0,4},{1,5},{2,6},{3,7},{4,8},{5,9},{6,10},{7,11},{8,12},{9,13},{1... | collective-permute-start | bytes 3145736 | tf_op jit(solution)/shard_map/ppermute | solution.py:333
  19.6 0.0 copy-done
  19.6 0.1 constant_dynamic-slice_fusion.2
  19.6 0.1 copy.13
  19.7 0.6 reshape.27.open_ref
  20.3 0.0 copy-done.1
  20.3 1.0 convert_reduce_fusion
  21.3 0.6 add_maximum_fusion.lo_ref
  21.9 6.2 %collective-permute-done.refs_12_ = bf16[256,1024]{1,0:T(8,128)(2,1)} collective-permute-done((bf16[256,1024]{1,0:T(8,128)(2,1)}, bf16[256,1024]{1,0:T(8,128)(2,1)}, u32[]{:S(2)}, u32[]{:S(2)}) %collective-permute-start) | collective-permute-done | bytes 524320 | tf_op jit(solution)/shard_map/ppermute | solution.py:333
  28.1 0.4 collective-permute-start.6
  28.5 0.0 collective-permute-done.4.refs_6_.refs_7_
  28.5 0.3 collective-permute-start.3
  28.8 0.7 pad_add_fusion.sc_ref
  29.5 1.5 %collective-permute-done.5.refs_8_.refs_9_ = bf16[512,512]{1,0:T(8,128)(2,1)} collective-permute-done((bf16[512,512]{1,0:T(8,128)(2,1)}, bf16[512,512]{1,0:T(8,128)(2,1)}, u32[]{:S(2)}, u32[]{:S(2)}) %collective-permute-start.5) | collective-permute-done | bytes 524320 | tf_op jit(solution)/shard_map/ppermute | solution.py:333
  31.0 0.0 collective-permute-done.6.refs_13_
  31.0 0.0 collective-permute-done.1.refs_3_.refs_4_.refs_5_.refs_11_
  31.0 20.9 %attention.2 = (bf16[512,512]{1,0:T(8,128)(2,1)}, bf16[512,512]{1,0:T(8,128)(2,1)}, bf16[512,1024]{1,0:T(8,128)(2,1)}, bf16[256,512]{1,0:T(8,128)(2,1)}, bf16[25...) custom-call(s32[2]{0:T(128)} %pad_add_fusion.sc_ref, ...), custom_call_target="tpu_custom_call" | custom-call | bytes 1024 | tf_op jit(solution)/shard_map/attention/pallas_call | solution.py:254
  51.9 0.0 collective-permute-done.3.refs_12_
  51.9 0.0 collective-permute-done.2.refs_6_.refs_7_
  51.9 1.0 collective-permute-start.7
  53.0 0.0 collective-permute-start.8
  53.0 0.5 collective-permute-start.9
  53.5 0.3 collective-permute-start.10
  53.7 1.4 %collective-permute-start.11 = (bf16[256,512]{1,0:T(8,128)(2,1)}, bf16[256,512]{1,0:T(8,128)(2,1)}, u32[]{:S(2)}, u32[]{:S(2)}) collective-permute-start(bf16[256,512]{1,0:T(8,128)(2,1)} %get-tuple-element.73), channel_id=1, source_target_pairs={{0,3},{1,2},{2,1},{3,0},{4,7},{5,6},{6,5},{7,4},{8,11},{9,10},{10,... | collective-permute-start | bytes 786440 | tf_op jit(solution)/shard_map/ppermute | solution.py:333
  55.1 1.2 %collective-permute-done.8.refs_13_ = bf16[256,1024]{1,0:T(8,128)(2,1)} collective-permute-done((bf16[256,1024]{1,0:T(8,128)(2,1)}, bf16[256,1024]{1,0:T(8,128)(2,1)}, u32[]{:S(2)}, u32[]{:S(2)}) %collective-permute-start.8) | collective-permute-done | bytes 524320 | tf_op jit(solution)/shard_map/ppermute | solution.py:333
  56.4 0.4 collective-permute-start.12
  56.7 0.0 collective-permute-done.7.refs_8_.refs_9_
  56.7 3.2 %collective-permute-start.17 = (bf16[1024,512]{1,0:T(8,128)(2,1)}, bf16[1024,512]{1,0:T(8,128)(2,1)}, u32[]{:S(2)}, u32[]{:S(2)}) collective-permute-start(bf16[1024,512]{1,0:T(8,128)(2,1)} %get-tuple-element.92), channel_id=1, source_target_pairs={{4,0},{5,1},{6,2},{7,3},{8,4},{9,5},{10,6},{11,7},{12,8},{13,9},{1... | collective-permute-start | bytes 3145736 | tf_op jit(solution)/shard_map/ppermute | solution.py:333
  59.9 21.1 %attention.3 = (bf16[512,512]{1,0:T(8,128)(2,1)}, bf16[512,512]{1,0:T(8,128)(2,1)}, bf16[512,1024]{1,0:T(8,128)(2,1)}, bf16[256,512]{1,0:T(8,128)(2,1)}, bf16[25...) custom-call(s32[2]{0:T(128)} %pad_add_fusion.sc_ref, ...), custom_call_target="tpu_custom_call" | custom-call | flops 24999999488 | bytes 1024 | tf_op jit(solution)/shard_map/attention/pallas_call | solution.py:254
  81.1 0.0 collective-permute-done.9.refs_1_
  81.1 0.0 collective-permute-done.10.refs_2_
  81.1 0.0 collective-permute-done.11.refs_3_
  81.1 0.0 collective-permute-done.12.refs_4_.refs_2_.refs_6_
  81.1 0.5 collective-permute-start.16
  81.6 2.1 %collective-permute-start.18 = (bf16[512,512]{1,0:T(8,128)(2,1)}, bf16[512,512]{1,0:T(8,128)(2,1)}, u32[]{:S(2)}, u32[]{:S(2)}) collective-permute-start(bf16[512,512]{1,0:T(8,128)(2,1)} %get-tuple-element.93), channel_id=1, source_target_pairs={{4,0},{5,1},{6,2},{7,3},{8,4},{9,5},{10,6},{11,7},{12,8},{13,9},{1... | collective-permute-start | bytes 1572872 | tf_op jit(solution)/shard_map/ppermute | solution.py:333
  83.8 0.3 collective-permute-start.13
  84.1 1.7 %collective-permute-start.15 = (bf16[256,512]{1,0:T(8,128)(2,1)}, bf16[256,512]{1,0:T(8,128)(2,1)}, u32[]{:S(2)}, u32[]{:S(2)}) collective-permute-start(bf16[256,512]{1,0:T(8,128)(2,1)} %get-tuple-element.86), channel_id=1, source_target_pairs={{0,3},{1,2},{2,1},{3,0},{4,7},{5,6},{6,5},{7,4},{8,11},{9,10},{10,... | collective-permute-start | bytes 786440 | tf_op jit(solution)/shard_map/ppermute | solution.py:333
  85.8 5.9 %collective-permute-done.13.refs_8_ = bf16[256,512]{1,0:T(8,128)(2,1)} collective-permute-done((bf16[256,512]{1,0:T(8,128)(2,1)}, bf16[256,512]{1,0:T(8,128)(2,1)}, u32[]{:S(2)}, u32[]{:S(2)}) %collective-permute-start.13) | collective-permute-done | bytes 262176 | tf_op jit(solution)/shard_map/ppermute | solution.py:333
  91.7 3.7 %collective-permute-start.19 = (bf16[512,512]{1,0:T(8,128)(2,1)}, bf16[512,512]{1,0:T(8,128)(2,1)}, u32[]{:S(2)}, u32[]{:S(2)}) collective-permute-start(bf16[512,512]{1,0:T(8,128)(2,1)} %get-tuple-element.95), channel_id=1, source_target_pairs={{4,2},{5,3},{6,0},{7,1},{8,6},{9,7},{10,4},{11,5},{12,10},{13,11},... | collective-permute-start | bytes 1572872 | tf_op jit(solution)/shard_map/ppermute | solution.py:333
  95.4 0.0 collective-permute-done.17.refs_1_.refs_5_
  95.5 0.2 collective-permute-start.14
  95.6 2.6 %collective-permute-done.18.refs_1_.refs_5_ = bf16[512,512]{1,0:T(8,128)(2,1)} collective-permute-done((bf16[512,512]{1,0:T(8,128)(2,1)}, bf16[512,512]{1,0:T(8,128)(2,1)}, u32[]{:S(2)}, u32[]{:S(2)}) %collective-permute-start.18) | collective-permute-done | bytes 524320 | tf_op jit(solution)/shard_map/ppermute | solution.py:333
  98.2 1.9 %constant_dynamic-slice_fusion = (bf16[512,256]{1,0:T(8,128)(2,1)}, bf16[512,256]{1,0:T(8,128)(2,1)}) fusion(bf16[1024,512]{1,0:T(8,128)(2,1)} %collective-permute-done.17.refs_1_.refs_5_, s32[]{:T(128)S(6)} %select_n.18), kind=kLoop, calls=%fused_computation.5 | loop fusion | bytes 1048580 | tf_op jit(solution)/shard_map/dynamic_slice | solution.py:499
  100.1 0.8 collective-permute-start.21
  100.9 0.0 collective-permute-done.15.refs_9_
  100.9 0.1 collective-permute-start.20
  101.0 0.0 collective-permute-done.14.refs_7_
  101.0 0.0 collective-permute-done.16.refs_10_.refs_2_.refs_6_
  101.0 3.9 %put_together.1 = (bf16[256,4096]{1,0:T(8,128)(2,1)}, bf16[512,2048]{1,0:T(8,128)(2,1)}) custom-call(bf16[256,512]{1,0:T(8,128)(2,1)} %get-tuple-element.75.refs_0_, bf16[256,512]{1,0:T(8,128)(2,1)} %collective-permute-done.9.refs_1_, bf16[256,512]{1,0:T(8,128)(2,1)} %collective-permute-done.10.refs_2_, bf16[256,512]{1,0:T(8,128)(2,1)} %collective-permute-done.11.refs_3_, ...), custom_call_target="tpu_custom_call" | custom-call | bytes 1024 | tf_op jit(solution)/shard_map/put_together/pallas_call | solution.py:70
  104.9 0.0 collective-permute-done.21.refs_7_
  105.0 0.0 collective-permute-done.20.refs_3_
  105.0 3.4 %sum_terms.2 = (bf16[512,1024]{1,0:T(8,128)(2,1)}, bf16[512,1024]{1,0:T(8,128)(2,1)}) custom-call(s32[2]{0:T(128)} %pad_add_fusion.sc_ref, bf16[512,512]{1,0:T(8,128)(2,1)} %get-tuple-element.96.refs_0_.refs_4_, bf16[1024,512]{1,0:T(8,128)(2,1)} %collective-permute-done.17.refs_1_.refs_5_, bf16[512,1024]{1,0:T(8,128)(2,1)} %collective-permute-done.12.refs_4_.refs_2_.refs_6_, ...), custom_call_target="tpu_custom_call" | custom-call | bytes 1024 | tf_op jit(solution)/shard_map/sum_terms/pallas_call | solution.py:303
  108.4 2.1 %collective-permute-done.19.refs_3_.refs_7_ = bf16[512,512]{1,0:T(8,128)(2,1)} collective-permute-done((bf16[512,512]{1,0:T(8,128)(2,1)}, bf16[512,512]{1,0:T(8,128)(2,1)}, u32[]{:S(2)}, u32[]{:S(2)}) %collective-permute-start.19) | collective-permute-done | bytes 524320 | tf_op jit(solution)/shard_map/ppermute | solution.py:333
  110.5 3.4 %sum_terms.3 = (bf16[512,1024]{1,0:T(8,128)(2,1)}, bf16[512,1024]{1,0:T(8,128)(2,1)}) custom-call(s32[2]{0:T(128)} %pad_add_fusion.sc_ref, bf16[512,512]{1,0:T(8,128)(2,1)} %get-tuple-element.91.refs_0_.refs_4_, bf16[512,512]{1,0:T(8,128)(2,1)} %collective-permute-done.18.refs_1_.refs_5_, ...), custom_call_target="tpu_custom_call", output_to_operand_aliasing={{0}: (9, {}), {1}: (10, {})} | custom-call | bytes 1024 | tf_op jit(solution)/shard_map/sum_terms/pallas_call | solution.py:303
  (2 shorter events, 0.0 us)
Async XLA Ops:
  0.6 18.9 %copy-start = (s32[64,9]{0,1:T(8,128)S(1)}, s32[64,9]{0,1:T(8,128)}, u32[]{:S(2)}) copy-start(s32[64,9]{0,1:T(8,128)} %param.10) | copy-start | bytes 6916
  2.7 25.8 %collective-permute-start.4 = (bf16[512,512]{1,0:T(8,128)(2,1)}, bf16[512,512]{1,0:T(8,128)(2,1)}, u32[]{:S(2)}, u32[]{:S(2)}) collective-permute-start(bf16[512,512]{1,0:T(8,128)(2,1)} %get-tuple-element.53.refs_4_), channel_id=1, source_target_pairs={{0,4},{1,5},{2,6},{3,7},{4,8},{5,9},{6,10},{7,11},{8,12},{9,13},{1... | collective-permute-start | bytes 1572872 | tf_op jit(solution)/shard_map/ppermute | solution.py:333
  5.9 25.1 %collective-permute-start.5 = (bf16[512,512]{1,0:T(8,128)(2,1)}, bf16[512,512]{1,0:T(8,128)(2,1)}, u32[]{:S(2)}, u32[]{:S(2)}) collective-permute-start(bf16[512,512]{1,0:T(8,128)(2,1)} %get-tuple-element.54.refs_5_), channel_id=1, source_target_pairs={{0,6},{1,7},{2,4},{3,5},{4,10},{5,11},{6,8},{7,9},{8,14},{9,15},{1... | collective-permute-start | bytes 1572872 | tf_op jit(solution)/shard_map/ppermute | solution.py:333
  13.8 14.3 %collective-permute-start = (bf16[256,1024]{1,0:T(8,128)(2,1)}, bf16[256,1024]{1,0:T(8,128)(2,1)}, u32[]{:S(2)}, u32[]{:S(2)}) collective-permute-start(bf16[256,1024]{1,0:T(8,128)(2,1)} %get-tuple-element.55), channel_id=1, source_target_pairs={{0,1},{1,0},{2,3},{3,2},{4,5},{5,4},{6,7},{7,6},{8,9},{9,8},{10,11... | collective-permute-start | bytes 1572872 | tf_op jit(solution)/shard_map/ppermute | solution.py:333
  14.1 6.1 %copy-start.1 = (s32[8192]{0:T(1024)S(1)}, s32[8192]{0:T(1024)}, u32[]{:S(2)}) copy-start(s32[8192]{0:T(1024)} %param.11) | copy-start | bytes 98308
  14.1 16.8 %collective-permute-start.1 = (bf16[512,2560]{1,0:T(8,128)(2,1)}, bf16[512,2560]{1,0:T(8,128)(2,1)}, u32[]{:S(2)}, u32[]{:S(2)}) collective-permute-start(bf16[512,2560]{1,0:T(8,128)(2,1)} %get-tuple-element.56.refs_2_), channel_id=1, source_target_pairs={{0,2},{1,3},{2,0},{3,1},{4,6},{5,7},{6,4},{7,5},{8,10},{9,11},{10,... | collective-permute-start | bytes 7864328 | tf_op jit(solution)/shard_map/ppermute | solution.py:333
  16.4 35.6 %collective-permute-start.2 = (bf16[512,1024]{1,0:T(8,128)(2,1)}, bf16[512,1024]{1,0:T(8,128)(2,1)}, u32[]{:S(2)}, u32[]{:S(2)}) collective-permute-start(bf16[512,1024]{1,0:T(8,128)(2,1)} %pack_halo.3), channel_id=1, source_target_pairs={{0,4},{1,5},{2,6},{3,7},{4,8},{5,9},{6,10},{7,11},{8,12},{9,13},{1... | collective-permute-start | bytes 3145736 | tf_op jit(solution)/shard_map/ppermute | solution.py:333
  28.1 2.8 %collective-permute-start.6 = (bf16[256,1024]{1,0:T(8,128)(2,1)}, bf16[256,1024]{1,0:T(8,128)(2,1)}, u32[]{:S(2)}, u32[]{:S(2)}) collective-permute-start(bf16[256,1024]{1,0:T(8,128)(2,1)} %collective-permute-done.refs_12_), channel_id=1, source_target_pairs={{0,2},{1,3},{2,0},{3,1},{4,6},{5,7},{6,4},{7,5},{8,10},{9,11},{10,... | collective-permute-start | bytes 1572872 | tf_op jit(solution)/shard_map/ppermute | solution.py:333
  28.5 23.4 %collective-permute-start.3 = (bf16[256,1024]{1,0:T(8,128)(2,1)}, bf16[256,1024]{1,0:T(8,128)(2,1)}, u32[]{:S(2)}, u32[]{:S(2)}) collective-permute-start(bf16[256,1024]{1,0:T(8,128)(2,1)} %get-tuple-element.59), channel_id=1, source_target_pairs={{0,1},{1,0},{2,3},{3,2},{4,5},{5,4},{6,7},{7,6},{8,9},{9,8},{10,11... | collective-permute-start | bytes 1572872 | tf_op jit(solution)/shard_map/ppermute | solution.py:333
  51.9 4.8 %collective-permute-start.7 = (bf16[512,1024]{1,0:T(8,128)(2,1)}, bf16[512,1024]{1,0:T(8,128)(2,1)}, u32[]{:S(2)}, u32[]{:S(2)}) collective-permute-start(bf16[512,1024]{1,0:T(8,128)(2,1)} %collective-permute-done.2.refs_6_.refs_7_), channel_id=1, source_target_pairs={{0,2},{1,3},{2,0},{3,1},{4,6},{5,7},{6,4},{7,5},{8,10},{9,11},{10,... | collective-permute-start | bytes 3145736 | tf_op jit(solution)/shard_map/ppermute | solution.py:333
  53.0 3.4 %collective-permute-start.8 = (bf16[256,1024]{1,0:T(8,128)(2,1)}, bf16[256,1024]{1,0:T(8,128)(2,1)}, u32[]{:S(2)}, u32[]{:S(2)}) collective-permute-start(bf16[256,1024]{1,0:T(8,128)(2,1)} %collective-permute-done.3.refs_12_), channel_id=1, source_target_pairs={{0,2},{1,3},{2,0},{3,1},{4,6},{5,7},{6,4},{7,5},{8,10},{9,11},{10,... | collective-permute-start | bytes 1572872 | tf_op jit(solution)/shard_map/ppermute | solution.py:333
  53.0 28.1 %collective-permute-start.9 = (bf16[256,512]{1,0:T(8,128)(2,1)}, bf16[256,512]{1,0:T(8,128)(2,1)}, u32[]{:S(2)}, u32[]{:S(2)}) collective-permute-start(bf16[256,512]{1,0:T(8,128)(2,1)} %get-tuple-element.71), channel_id=1, source_target_pairs={{0,2},{1,3},{2,0},{3,1},{4,6},{5,7},{6,4},{7,5},{8,10},{9,11},{10,... | collective-permute-start | bytes 786440 | tf_op jit(solution)/shard_map/ppermute | solution.py:333
  53.5 27.6 %collective-permute-start.10 = (bf16[256,512]{1,0:T(8,128)(2,1)}, bf16[256,512]{1,0:T(8,128)(2,1)}, u32[]{:S(2)}, u32[]{:S(2)}) collective-permute-start(bf16[256,512]{1,0:T(8,128)(2,1)} %get-tuple-element.72), channel_id=1, source_target_pairs={{0,1},{1,0},{2,3},{3,2},{4,5},{5,4},{6,7},{7,6},{8,9},{9,8},{10,11... | collective-permute-start | bytes 786440 | tf_op jit(solution)/shard_map/ppermute | solution.py:333
  53.7 27.4 %collective-permute-start.11 = (bf16[256,512]{1,0:T(8,128)(2,1)}, bf16[256,512]{1,0:T(8,128)(2,1)}, u32[]{:S(2)}, u32[]{:S(2)}) collective-permute-start(bf16[256,512]{1,0:T(8,128)(2,1)} %get-tuple-element.73), channel_id=1, source_target_pairs={{0,3},{1,2},{2,1},{3,0},{4,7},{5,6},{6,5},{7,4},{8,11},{9,10},{10,... | collective-permute-start | bytes 786440 | tf_op jit(solution)/shard_map/ppermute | solution.py:333
  56.4 24.8 %collective-permute-start.12 = (bf16[512,1024]{1,0:T(8,128)(2,1)}, bf16[512,1024]{1,0:T(8,128)(2,1)}, u32[]{:S(2)}, u32[]{:S(2)}) collective-permute-start(bf16[512,1024]{1,0:T(8,128)(2,1)} %get-tuple-element.74), channel_id=1, source_target_pairs={{0,2},{1,3},{2,0},{3,1},{4,6},{5,7},{6,4},{7,5},{8,10},{9,11},{10,... | collective-permute-start | bytes 3145736 | tf_op jit(solution)/shard_map/ppermute | solution.py:333
  56.7 38.7 %collective-permute-start.17 = (bf16[1024,512]{1,0:T(8,128)(2,1)}, bf16[1024,512]{1,0:T(8,128)(2,1)}, u32[]{:S(2)}, u32[]{:S(2)}) collective-permute-start(bf16[1024,512]{1,0:T(8,128)(2,1)} %get-tuple-element.92), channel_id=1, source_target_pairs={{4,0},{5,1},{6,2},{7,3},{8,4},{9,5},{10,6},{11,7},{12,8},{13,9},{1... | collective-permute-start | bytes 3145736 | tf_op jit(solution)/shard_map/ppermute | solution.py:333
  81.1 19.9 %collective-permute-start.16 = (bf16[512,1024]{1,0:T(8,128)(2,1)}, bf16[512,1024]{1,0:T(8,128)(2,1)}, u32[]{:S(2)}, u32[]{:S(2)}) collective-permute-start(bf16[512,1024]{1,0:T(8,128)(2,1)} %get-tuple-element.87), channel_id=1, source_target_pairs={{0,2},{1,3},{2,0},{3,1},{4,6},{5,7},{6,4},{7,5},{8,10},{9,11},{10,... | collective-permute-start | bytes 3145736 | tf_op jit(solution)/shard_map/ppermute | solution.py:333
  81.6 16.6 %collective-permute-start.18 = (bf16[512,512]{1,0:T(8,128)(2,1)}, bf16[512,512]{1,0:T(8,128)(2,1)}, u32[]{:S(2)}, u32[]{:S(2)}) collective-permute-start(bf16[512,512]{1,0:T(8,128)(2,1)} %get-tuple-element.93), channel_id=1, source_target_pairs={{4,0},{5,1},{6,2},{7,3},{8,4},{9,5},{10,6},{11,7},{12,8},{13,9},{1... | collective-permute-start | bytes 1572872 | tf_op jit(solution)/shard_map/ppermute | solution.py:333
  83.8 7.9 %collective-permute-start.13 = (bf16[256,512]{1,0:T(8,128)(2,1)}, bf16[256,512]{1,0:T(8,128)(2,1)}, u32[]{:S(2)}, u32[]{:S(2)}) collective-permute-start(bf16[256,512]{1,0:T(8,128)(2,1)} %get-tuple-element.83), channel_id=1, source_target_pairs={{0,1},{1,0},{2,3},{3,2},{4,5},{5,4},{6,7},{7,6},{8,9},{9,8},{10,11... | collective-permute-start | bytes 786440 | tf_op jit(solution)/shard_map/ppermute | solution.py:333
  84.1 16.8 %collective-permute-start.15 = (bf16[256,512]{1,0:T(8,128)(2,1)}, bf16[256,512]{1,0:T(8,128)(2,1)}, u32[]{:S(2)}, u32[]{:S(2)}) collective-permute-start(bf16[256,512]{1,0:T(8,128)(2,1)} %get-tuple-element.86), channel_id=1, source_target_pairs={{0,3},{1,2},{2,1},{3,0},{4,7},{5,6},{6,5},{7,4},{8,11},{9,10},{10,... | collective-permute-start | bytes 786440 | tf_op jit(solution)/shard_map/ppermute | solution.py:333
  91.7 18.8 %collective-permute-start.19 = (bf16[512,512]{1,0:T(8,128)(2,1)}, bf16[512,512]{1,0:T(8,128)(2,1)}, u32[]{:S(2)}, u32[]{:S(2)}) collective-permute-start(bf16[512,512]{1,0:T(8,128)(2,1)} %get-tuple-element.95), channel_id=1, source_target_pairs={{4,2},{5,3},{6,0},{7,1},{8,6},{9,7},{10,4},{11,5},{12,10},{13,11},... | collective-permute-start | bytes 1572872 | tf_op jit(solution)/shard_map/ppermute | solution.py:333
  95.5 5.5 %collective-permute-start.14 = (bf16[256,512]{1,0:T(8,128)(2,1)}, bf16[256,512]{1,0:T(8,128)(2,1)}, u32[]{:S(2)}, u32[]{:S(2)}) collective-permute-start(bf16[256,512]{1,0:T(8,128)(2,1)} %get-tuple-element.84), channel_id=1, source_target_pairs={{0,2},{1,3},{2,0},{3,1},{4,6},{5,7},{6,4},{7,5},{8,10},{9,11},{10,... | collective-permute-start | bytes 786440 | tf_op jit(solution)/shard_map/ppermute | solution.py:333
  100.1 4.9 %collective-permute-start.21 = (bf16[512,256]{1,0:T(8,128)(2,1)}, bf16[512,256]{1,0:T(8,128)(2,1)}, u32[]{:S(2)}, u32[]{:S(2)}) collective-permute-start(bf16[512,256]{1,0:T(8,128)(2,1)} %get-tuple-element.102), channel_id=1, source_target_pairs={{0,2},{1,3},{2,0},{3,1},{4,6},{5,7},{6,4},{7,5},{8,10},{9,11},{10,... | collective-permute-start | bytes 786440 | tf_op jit(solution)/shard_map/ppermute | solution.py:333
  100.9 4.0 %collective-permute-start.20 = (bf16[512,256]{1,0:T(8,128)(2,1)}, bf16[512,256]{1,0:T(8,128)(2,1)}, u32[]{:S(2)}, u32[]{:S(2)}) collective-permute-start(bf16[512,256]{1,0:T(8,128)(2,1)} %get-tuple-element.103), channel_id=1, source_target_pairs={{0,2},{1,3},{2,0},{3,1},{4,6},{5,7},{6,4},{7,5},{8,10},{9,11},{10,... | collective-permute-start | bytes 786440 | tf_op jit(solution)/shard_map/ppermute | solution.py:333

commit v7 on v6

--- a/solution.py
+++ b/solution.py
@@ -24,6 +24,7 @@
 NN = (((1,), (0,)), ((), ()))
 LIGHT = pl.CostEstimate(flops=0, bytes_accessed=1024, transcendentals=0)
 VMEM_LIMIT = (64 * 1024 - 128) * 1024
+MEDIUM = pl.CostEstimate(flops=4_000_000_000, bytes_accessed=1024, transcendentals=0)
 HEAVY = pl.CostEstimate(flops=25_000_000_000, bytes_accessed=1024, transcendentals=0)
 
 
@@ -117,8 +118,6 @@
     for at in range(n_mp - 1):
         dos[piece_at(0, n_mp - 1 - at), :] = do_far[2 * at][...]
         dos[piece_at(1, n_mp - 1 - at), :] = do_far[2 * at + 1][...]
-    dk[...] = jnp.zeros_like(dk)
-    dv[...] = jnp.zeros_like(dv)
     for t in range(ks.shape[0] // 256):
         at = slice(t * 256, t * 256 + 256)
         k_t[:, at] = ks[at, :].T
@@ -175,8 +174,12 @@
             ds_ref[part, :] = (e_ref[part, :].astype(jnp.float32) * (dp - delta)).astype(
                 jnp.bfloat16
             )
-        dv[at_keys, :] += dot(e_ref[...], do_t, NT)
-        dk[at_keys, :] += dot(ds_ref[...], q_blk)
+        for total, part in ((dv, dot(e_ref[...], do_t, NT)), (dk, dot(ds_ref[...], q_blk))):
+            met = 0 if b == 0 else WINDOW
+            seen, fresh = slice(b * BLOCK, b * BLOCK + met), slice(b * BLOCK + met, (b + SPAN) * BLOCK)
+            if met:
+                total[seen, :] += part[:met]
+            total[fresh, :] = part[met:]
         dq_t = (dot(k_t[:, at_keys], ds_ref[...]) * ATTN_SCALE).astype(jnp.bfloat16)
         dqs[at_q, :HEAD] = dq_t[:, :BLOCK].T
         dqs[at_q, HEAD:] = dq_t[:, BLOCK:].T
@@ -274,7 +277,7 @@
         ),
         out_shape=out_shape,
         compiler_params=pltpu.CompilerParams(vmem_limit_bytes=VMEM_LIMIT),
-        cost_estimate=HEAVY if chunk else LIGHT,
+        cost_estimate=MEDIUM if chunk else LIGHT,
         name="attention",
     )(place, opened, lo, *own, near, near, near, halo[0], halo[0], halo[1], halo[1], grad_out, near, *far_do)
 
@@ -455,7 +458,7 @@
         ]
         o_oth = o_far[0]
         if last:
-            o_oth, o_parts[0] = lax.optimization_barrier((o_oth, o_parts[0]))
+            o_oth, far_parts[-2][0] = lax.optimization_barrier((o_oth, far_parts[-2][0]))
         out_parts.append([o_own, send(o_oth, swap), *o_parts])
         across_parts.append(send(across, swap))
         dq_parts.append(dq_same)

time: 114 us -> 113 us (level)
  the two profiles are of different devices: /device:TPU:15 before, /device:TPU:0 now
where the time goes in v7:
time: 113 us
  Pallas kernels  61.4 us (54%)
  starting transfers between devices  25.2 us (22%)
  waiting for transfers between devices  20.4 us (18%)
  local copies, waits for them, and re-layouts  2.59 us (2%)
  other arithmetic  2.25 us (2%)
    pallas_call x2, Pallas kernels, attention(): pl.pallas_call(functools.partial(attention_kernel, n_mp, rows, whole), gr...  42.4 us
    ppermute x22, starting transfers between devices, send(): return lax.ppermute(x, AXES, routes(target, n_ctx, n_mp))  25.2 us
    ppermute x22, waiting for transfers between devices, send(): return lax.ppermute(x, AXES, routes(target, n_ctx, n_mp))  20.4 us
    pallas_call x4, Pallas kernels, gather(): pl.pallas_call(functools.partial(gather_kernel, plan, len(arrays) + len(a...  12.1 us
    pallas_call x2, Pallas kernels, sum_terms(): pl.pallas_call(functools.partial(sum_kernel, heads), grid_spec=pltpu.Pref...  6.83 us
  transfers between devices with their start and end apart: 22, of which 3 were waited for; matrix products, arithmetic and copies ran while one was open for 4% of the time, Pallas kernels for 50%

profile of v7, /device:TPU:0, one launch (start us, length us, event | category | flops | bytes accessed | tf_op | source)
XLA Modules:
  0.0 112.6 jit_solution(7147529189740934146)
XLA Ops:
  0.6 0.0 copy-start
  0.6 2.1 %pack_halo.2 = (bf16[512,512]{1,0:T(8,128)(2,1)}, bf16[512,512]{1,0:T(8,128)(2,1)}) custom-call(bf16[512,1024]{1,0:T(8,128)(2,1)} %refs_1_.9, bf16[512,1024]{1,0:T(8,128)(2,1)} %refs_2_.5), custom_call_target="tpu_custom_call" | custom-call | flops 24999999488 | bytes 1024 | tf_op jit(solution)/shard_map/pack_halo/pallas_call | solution.py:71
  2.7 5.7 %collective-permute-start.4 = (bf16[512,512]{1,0:T(8,128)(2,1)}, bf16[512,512]{1,0:T(8,128)(2,1)}, u32[]{:S(2)}, u32[]{:S(2)}) collective-permute-start(bf16[512,512]{1,0:T(8,128)(2,1)} %get-tuple-element.53.refs_4_), channel_id=1, source_target_pairs={{0,4},{1,5},{2,6},{3,7},{4,8},{5,9},{6,10},{7,11},{8,12},{9,13},{1... | collective-permute-start | bytes 1572872 | tf_op jit(solution)/shard_map/ppermute | solution.py:336
  8.4 2.7 %collective-permute-start.5 = (bf16[512,512]{1,0:T(8,128)(2,1)}, bf16[512,512]{1,0:T(8,128)(2,1)}, u32[]{:S(2)}, u32[]{:S(2)}) collective-permute-start(bf16[512,512]{1,0:T(8,128)(2,1)} %get-tuple-element.54.refs_5_), channel_id=1, source_target_pairs={{0,6},{1,7},{2,4},{3,5},{4,10},{5,11},{6,8},{7,9},{8,14},{9,15},{1... | collective-permute-start | bytes 1572872 | tf_op jit(solution)/shard_map/ppermute | solution.py:336
  11.1 3.9 %pack_near.1 = (bf16[256,1024]{1,0:T(8,128)(2,1)}, bf16[256,1024]{1,0:T(8,128)(2,1)}, bf16[512,2560]{1,0:T(8,128)(2,1)}) custom-call(bf16[512,2048]{1,0:T(8,128)(2,1)} %refs_0_.9, bf16[512,1024]{1,0:T(8,128)(2,1)} %refs_1_.9, bf16[512,1024]{1,0:T(8,128)(2,1)} %refs_2_.5, bf16[256,4096]{1,0:T(8,128)(2,1)} %refs_10_.3, ...), custom_call_target="tpu_custom_call" | custom-call | flops 24999999488 | bytes 1024 | tf_op jit(solution)/shard_map/pack_near/pallas_call | solution.py:71
  15.0 1.6 %collective-permute-start = (bf16[256,1024]{1,0:T(8,128)(2,1)}, bf16[256,1024]{1,0:T(8,128)(2,1)}, u32[]{:S(2)}, u32[]{:S(2)}) collective-permute-start(bf16[256,1024]{1,0:T(8,128)(2,1)} %get-tuple-element.55), channel_id=1, source_target_pairs={{0,1},{1,0},{2,3},{3,2},{4,5},{5,4},{6,7},{7,6},{8,9},{9,8},{10,11... | collective-permute-start | bytes 1572872 | tf_op jit(solution)/shard_map/ppermute | solution.py:336
  16.5 0.0 copy-start.1
  16.5 0.7 collective-permute-start.1
  17.2 2.2 %pack_halo.3 = bf16[512,1024]{1,0:T(8,128)(2,1)} custom-call(bf16[512,1024]{1,0:T(8,128)(2,1)} %refs_1_.9, bf16[512,1024]{1,0:T(8,128)(2,1)} %refs_2_.5, bf16[512,2560]{1,0:T(8,128)(2,1)} %get-tuple-element.56.refs_2_), custom_call_target="tpu_custom_call" | custom-call | flops 24999999488 | bytes 1024 | tf_op jit(solution)/shard_map/pack_halo/pallas_call | solution.py:71
  19.4 3.6 %collective-permute-start.2 = (bf16[512,1024]{1,0:T(8,128)(2,1)}, bf16[512,1024]{1,0:T(8,128)(2,1)}, u32[]{:S(2)}, u32[]{:S(2)}) collective-permute-start(bf16[512,1024]{1,0:T(8,128)(2,1)} %pack_halo.3), channel_id=1, source_target_pairs={{0,4},{1,5},{2,6},{3,7},{4,8},{5,9},{6,10},{7,11},{8,12},{9,13},{1... | collective-permute-start | bytes 3145736 | tf_op jit(solution)/shard_map/ppermute | solution.py:336
  23.0 0.0 copy-done
  23.0 0.1 constant_dynamic-slice_fusion.2
  23.1 0.1 copy.13
  23.2 0.6 reshape.27.open_ref
  23.7 0.0 copy-done.1
  23.8 1.0 convert_reduce_fusion
  24.7 0.6 add_maximum_fusion.lo_ref
  25.3 4.8 %collective-permute-done.refs_12_ = bf16[256,1024]{1,0:T(8,128)(2,1)} collective-permute-done((bf16[256,1024]{1,0:T(8,128)(2,1)}, bf16[256,1024]{1,0:T(8,128)(2,1)}, u32[]{:S(2)}, u32[]{:S(2)}) %collective-permute-start) | collective-permute-done | bytes 524320 | tf_op jit(solution)/shard_map/ppermute | solution.py:336
  30.1 0.1 collective-permute-start.6
  30.2 0.0 collective-permute-done.4.refs_6_.refs_7_
  30.2 1.5 %collective-permute-start.3 = (bf16[256,1024]{1,0:T(8,128)(2,1)}, bf16[256,1024]{1,0:T(8,128)(2,1)}, u32[]{:S(2)}, u32[]{:S(2)}) collective-permute-start(bf16[256,1024]{1,0:T(8,128)(2,1)} %get-tuple-element.59), channel_id=1, source_target_pairs={{0,1},{1,0},{2,3},{3,2},{4,5},{5,4},{6,7},{7,6},{8,9},{9,8},{10,11... | collective-permute-start | bytes 1572872 | tf_op jit(solution)/shard_map/ppermute | solution.py:336
  31.7 0.7 pad_add_fusion.sc_ref
  32.4 0.0 collective-permute-done.5.refs_8_.refs_9_
  32.4 0.0 collective-permute-done.6.refs_13_
  32.4 0.0 collective-permute-done.1.refs_3_.refs_4_.refs_5_.refs_11_
  32.4 21.1 %attention.2 = (bf16[512,512]{1,0:T(8,128)(2,1)}, bf16[512,512]{1,0:T(8,128)(2,1)}, bf16[512,1024]{1,0:T(8,128)(2,1)}, bf16[256,512]{1,0:T(8,128)(2,1)}, bf16[25...) custom-call(s32[2]{0:T(128)} %pad_add_fusion.sc_ref, ...), custom_call_target="tpu_custom_call" | custom-call | bytes 1024 | tf_op jit(solution)/shard_map/attention/pallas_call | solution.py:257
  53.6 0.0 collective-permute-done.3.refs_12_
  53.6 0.0 collective-permute-done.2.refs_6_.refs_7_
  53.6 0.2 collective-permute-start.7
  53.8 0.4 collective-permute-start.12
  54.2 0.1 collective-permute-start.8
  54.3 1.5 %collective-permute-start.13 = (bf16[1024,512]{1,0:T(8,128)(2,1)}, bf16[1024,512]{1,0:T(8,128)(2,1)}, u32[]{:S(2)}, u32[]{:S(2)}) collective-permute-start(bf16[1024,512]{1,0:T(8,128)(2,1)} %get-tuple-element.83), channel_id=1, source_target_pairs={{4,0},{5,1},{6,2},{7,3},{8,4},{9,5},{10,6},{11,7},{12,8},{13,9},{1... | collective-permute-start | bytes 3145736 | tf_op jit(solution)/shard_map/ppermute | solution.py:336
  55.8 0.4 collective-permute-start.9
  56.2 2.7 %collective-permute-done.8.refs_13_ = bf16[256,1024]{1,0:T(8,128)(2,1)} collective-permute-done((bf16[256,1024]{1,0:T(8,128)(2,1)}, bf16[256,1024]{1,0:T(8,128)(2,1)}, u32[]{:S(2)}, u32[]{:S(2)}) %collective-permute-start.8) | collective-permute-done | bytes 524320 | tf_op jit(solution)/shard_map/ppermute | solution.py:336
  58.9 1.5 %collective-permute-start.10 = (bf16[256,512]{1,0:T(8,128)(2,1)}, bf16[256,512]{1,0:T(8,128)(2,1)}, u32[]{:S(2)}, u32[]{:S(2)}) collective-permute-start(bf16[256,512]{1,0:T(8,128)(2,1)} %get-tuple-element.72), channel_id=1, source_target_pairs={{0,1},{1,0},{2,3},{3,2},{4,5},{5,4},{6,7},{7,6},{8,9},{9,8},{10,11... | collective-permute-start | bytes 786440 | tf_op jit(solution)/shard_map/ppermute | solution.py:336
  60.4 0.0 collective-permute-done.7.refs_8_.refs_9_
  60.4 0.0 collective-permute-start.11
  60.4 21.2 %attention.3 = (bf16[512,512]{1,0:T(8,128)(2,1)}, bf16[512,512]{1,0:T(8,128)(2,1)}, bf16[512,1024]{1,0:T(8,128)(2,1)}, bf16[256,512]{1,0:T(8,128)(2,1)}, bf16[25...) custom-call(s32[2]{0:T(128)} %pad_add_fusion.sc_ref, ...), custom_call_target="tpu_custom_call" | custom-call | flops 4000000000 | bytes 1024 | tf_op jit(solution)/shard_map/attention/pallas_call | solution.py:257
  81.6 0.0 collective-permute-done.9.refs_1_
  81.7 0.0 collective-permute-done.10.refs_2_
  81.7 0.0 collective-permute-done.11.refs_3_
  81.7 0.0 collective-permute-done.12.refs_4_.refs_2_.refs_6_
  81.7 0.7 collective-permute-start.17
  82.4 1.3 %collective-permute-start.18 = (bf16[512,512]{1,0:T(8,128)(2,1)}, bf16[512,512]{1,0:T(8,128)(2,1)}, u32[]{:S(2)}, u32[]{:S(2)}) collective-permute-start(bf16[512,512]{1,0:T(8,128)(2,1)} %get-tuple-element.93), channel_id=1, source_target_pairs={{4,0},{5,1},{6,2},{7,3},{8,4},{9,5},{10,6},{11,7},{12,8},{13,9},{1... | collective-permute-start | bytes 1572872 | tf_op jit(solution)/shard_map/ppermute | solution.py:336
  83.7 1.5 %collective-permute-start.15 = (bf16[256,512]{1,0:T(8,128)(2,1)}, bf16[256,512]{1,0:T(8,128)(2,1)}, u32[]{:S(2)}, u32[]{:S(2)}) collective-permute-start(bf16[256,512]{1,0:T(8,128)(2,1)} %get-tuple-element.85), channel_id=1, source_target_pairs={{0,1},{1,0},{2,3},{3,2},{4,5},{5,4},{6,7},{7,6},{8,9},{9,8},{10,11... | collective-permute-start | bytes 786440 | tf_op jit(solution)/shard_map/ppermute | solution.py:336
  85.2 0.0 collective-permute-start.16
  85.2 0.0 collective-permute-done.13.refs_1_.refs_5_
  85.2 1.3 %collective-permute-start.19 = (bf16[512,512]{1,0:T(8,128)(2,1)}, bf16[512,512]{1,0:T(8,128)(2,1)}, u32[]{:S(2)}, u32[]{:S(2)}) collective-permute-start(bf16[512,512]{1,0:T(8,128)(2,1)} %get-tuple-element.95), channel_id=1, source_target_pairs={{4,2},{5,3},{6,0},{7,1},{8,6},{9,7},{10,4},{11,5},{12,10},{13,11},... | collective-permute-start | bytes 1572872 | tf_op jit(solution)/shard_map/ppermute | solution.py:336
  86.5 12.9 %collective-permute-done.18.refs_1_.refs_5_ = bf16[512,512]{1,0:T(8,128)(2,1)} collective-permute-done((bf16[512,512]{1,0:T(8,128)(2,1)}, bf16[512,512]{1,0:T(8,128)(2,1)}, u32[]{:S(2)}, u32[]{:S(2)}) %collective-permute-start.18) | collective-permute-done | bytes 524320 | tf_op jit(solution)/shard_map/ppermute | solution.py:336
  99.4 0.0 collective-permute-start.14
  99.4 1.9 %constant_dynamic-slice_fusion = (bf16[512,256]{1,0:T(8,128)(2,1)}, bf16[512,256]{1,0:T(8,128)(2,1)}) fusion(bf16[1024,512]{1,0:T(8,128)(2,1)} %collective-permute-done.13.refs_1_.refs_5_, s32[]{:T(128)S(6)} %select_n.18), kind=kLoop, calls=%fused_computation.5 | loop fusion | bytes 1048580 | tf_op jit(solution)/shard_map/dynamic_slice | solution.py:502
  101.2 0.0 collective-permute-done.15.refs_8_
  101.2 0.5 collective-permute-start.21
  101.7 0.0 collective-permute-done.16.refs_9_
  101.7 0.1 collective-permute-start.20
  101.8 0.0 collective-permute-done.14.refs_7_
  101.8 0.0 collective-permute-done.17.refs_10_.refs_2_.refs_6_
  101.8 3.9 %put_together.1 = (bf16[256,4096]{1,0:T(8,128)(2,1)}, bf16[512,2048]{1,0:T(8,128)(2,1)}) custom-call(bf16[256,512]{1,0:T(8,128)(2,1)} %get-tuple-element.75.refs_0_, bf16[256,512]{1,0:T(8,128)(2,1)} %collective-permute-done.9.refs_1_, bf16[256,512]{1,0:T(8,128)(2,1)} %collective-permute-done.10.refs_2_, bf16[256,512]{1,0:T(8,128)(2,1)} %collective-permute-done.11.refs_3_, ...), custom_call_target="tpu_custom_call" | custom-call | bytes 1024 | tf_op jit(solution)/shard_map/put_together/pallas_call | solution.py:71
  105.8 0.0 collective-permute-done.21.refs_7_
  105.8 0.0 collective-permute-done.20.refs_3_
  105.8 3.4 %sum_terms.2 = (bf16[512,1024]{1,0:T(8,128)(2,1)}, bf16[512,1024]{1,0:T(8,128)(2,1)}) custom-call(s32[2]{0:T(128)} %pad_add_fusion.sc_ref, bf16[512,512]{1,0:T(8,128)(2,1)} %get-tuple-element.96.refs_0_.refs_4_, bf16[1024,512]{1,0:T(8,128)(2,1)} %collective-permute-done.13.refs_1_.refs_5_, bf16[512,1024]{1,0:T(8,128)(2,1)} %collective-permute-done.12.refs_4_.refs_2_.refs_6_, ...), custom_call_target="tpu_custom_call" | custom-call | bytes 1024 | tf_op jit(solution)/shard_map/sum_terms/pallas_call | solution.py:306
  109.2 0.0 collective-permute-done.19.refs_3_.refs_7_
  109.2 3.4 %sum_terms.3 = (bf16[512,1024]{1,0:T(8,128)(2,1)}, bf16[512,1024]{1,0:T(8,128)(2,1)}) custom-call(s32[2]{0:T(128)} %pad_add_fusion.sc_ref, bf16[512,512]{1,0:T(8,128)(2,1)} %get-tuple-element.91.refs_0_.refs_4_, bf16[512,512]{1,0:T(8,128)(2,1)} %collective-permute-done.18.refs_1_.refs_5_, ...), custom_call_target="tpu_custom_call", output_to_operand_aliasing={{0}: (9, {}), {1}: (10, {})} | custom-call | bytes 1024 | tf_op jit(solution)/shard_map/sum_terms/pallas_call | solution.py:306
  (2 shorter events, 0.0 us)
Async XLA Ops:
  0.6 22.4 %copy-start = (s32[64,9]{0,1:T(8,128)S(1)}, s32[64,9]{0,1:T(8,128)}, u32[]{:S(2)}) copy-start(s32[64,9]{0,1:T(8,128)} %param.10) | copy-start | bytes 6916
  2.7 27.5 %collective-permute-start.4 = (bf16[512,512]{1,0:T(8,128)(2,1)}, bf16[512,512]{1,0:T(8,128)(2,1)}, u32[]{:S(2)}, u32[]{:S(2)}) collective-permute-start(bf16[512,512]{1,0:T(8,128)(2,1)} %get-tuple-element.53.refs_4_), channel_id=1, source_target_pairs={{0,4},{1,5},{2,6},{3,7},{4,8},{5,9},{6,10},{7,11},{8,12},{9,13},{1... | collective-permute-start | bytes 1572872 | tf_op jit(solution)/shard_map/ppermute | solution.py:336
  8.4 24.0 %collective-permute-start.5 = (bf16[512,512]{1,0:T(8,128)(2,1)}, bf16[512,512]{1,0:T(8,128)(2,1)}, u32[]{:S(2)}, u32[]{:S(2)}) collective-permute-start(bf16[512,512]{1,0:T(8,128)(2,1)} %get-tuple-element.54.refs_5_), channel_id=1, source_target_pairs={{0,6},{1,7},{2,4},{3,5},{4,10},{5,11},{6,8},{7,9},{8,14},{9,15},{1... | collective-permute-start | bytes 1572872 | tf_op jit(solution)/shard_map/ppermute | solution.py:336
  15.0 15.2 %collective-permute-start = (bf16[256,1024]{1,0:T(8,128)(2,1)}, bf16[256,1024]{1,0:T(8,128)(2,1)}, u32[]{:S(2)}, u32[]{:S(2)}) collective-permute-start(bf16[256,1024]{1,0:T(8,128)(2,1)} %get-tuple-element.55), channel_id=1, source_target_pairs={{0,1},{1,0},{2,3},{3,2},{4,5},{5,4},{6,7},{7,6},{8,9},{9,8},{10,11... | collective-permute-start | bytes 1572872 | tf_op jit(solution)/shard_map/ppermute | solution.py:336
  16.5 7.2 %copy-start.1 = (s32[8192]{0:T(1024)S(1)}, s32[8192]{0:T(1024)}, u32[]{:S(2)}) copy-start(s32[8192]{0:T(1024)} %param.11) | copy-start | bytes 98308
  16.5 15.9 %collective-permute-start.1 = (bf16[512,2560]{1,0:T(8,128)(2,1)}, bf16[512,2560]{1,0:T(8,128)(2,1)}, u32[]{:S(2)}, u32[]{:S(2)}) collective-permute-start(bf16[512,2560]{1,0:T(8,128)(2,1)} %get-tuple-element.56.refs_2_), channel_id=1, source_target_pairs={{0,2},{1,3},{2,0},{3,1},{4,6},{5,7},{6,4},{7,5},{8,10},{9,11},{10,... | collective-permute-start | bytes 7864328 | tf_op jit(solution)/shard_map/ppermute | solution.py:336
  19.4 34.1 %collective-permute-start.2 = (bf16[512,1024]{1,0:T(8,128)(2,1)}, bf16[512,1024]{1,0:T(8,128)(2,1)}, u32[]{:S(2)}, u32[]{:S(2)}) collective-permute-start(bf16[512,1024]{1,0:T(8,128)(2,1)} %pack_halo.3), channel_id=1, source_target_pairs={{0,4},{1,5},{2,6},{3,7},{4,8},{5,9},{6,10},{7,11},{8,12},{9,13},{1... | collective-permute-start | bytes 3145736 | tf_op jit(solution)/shard_map/ppermute | solution.py:336
  30.1 2.3 %collective-permute-start.6 = (bf16[256,1024]{1,0:T(8,128)(2,1)}, bf16[256,1024]{1,0:T(8,128)(2,1)}, u32[]{:S(2)}, u32[]{:S(2)}) collective-permute-start(bf16[256,1024]{1,0:T(8,128)(2,1)} %collective-permute-done.refs_12_), channel_id=1, source_target_pairs={{0,2},{1,3},{2,0},{3,1},{4,6},{5,7},{6,4},{7,5},{8,10},{9,11},{10,... | collective-permute-start | bytes 1572872 | tf_op jit(solution)/shard_map/ppermute | solution.py:336
  30.2 23.3 %collective-permute-start.3 = (bf16[256,1024]{1,0:T(8,128)(2,1)}, bf16[256,1024]{1,0:T(8,128)(2,1)}, u32[]{:S(2)}, u32[]{:S(2)}) collective-permute-start(bf16[256,1024]{1,0:T(8,128)(2,1)} %get-tuple-element.59), channel_id=1, source_target_pairs={{0,1},{1,0},{2,3},{3,2},{4,5},{5,4},{6,7},{7,6},{8,9},{9,8},{10,11... | collective-permute-start | bytes 1572872 | tf_op jit(solution)/shard_map/ppermute | solution.py:336
  53.6 6.8 %collective-permute-start.7 = (bf16[512,1024]{1,0:T(8,128)(2,1)}, bf16[512,1024]{1,0:T(8,128)(2,1)}, u32[]{:S(2)}, u32[]{:S(2)}) collective-permute-start(bf16[512,1024]{1,0:T(8,128)(2,1)} %collective-permute-done.2.refs_6_.refs_7_), channel_id=1, source_target_pairs={{0,2},{1,3},{2,0},{3,1},{4,6},{5,7},{6,4},{7,5},{8,10},{9,11},{10,... | collective-permute-start | bytes 3145736 | tf_op jit(solution)/shard_map/ppermute | solution.py:336
  53.8 27.9 %collective-permute-start.12 = (bf16[512,1024]{1,0:T(8,128)(2,1)}, bf16[512,1024]{1,0:T(8,128)(2,1)}, u32[]{:S(2)}, u32[]{:S(2)}) collective-permute-start(bf16[512,1024]{1,0:T(8,128)(2,1)} %get-tuple-element.74), channel_id=1, source_target_pairs={{0,2},{1,3},{2,0},{3,1},{4,6},{5,7},{6,4},{7,5},{8,10},{9,11},{10,... | collective-permute-start | bytes 3145736 | tf_op jit(solution)/shard_map/ppermute | solution.py:336
  54.2 4.7 %collective-permute-start.8 = (bf16[256,1024]{1,0:T(8,128)(2,1)}, bf16[256,1024]{1,0:T(8,128)(2,1)}, u32[]{:S(2)}, u32[]{:S(2)}) collective-permute-start(bf16[256,1024]{1,0:T(8,128)(2,1)} %collective-permute-done.3.refs_12_), channel_id=1, source_target_pairs={{0,2},{1,3},{2,0},{3,1},{4,6},{5,7},{6,4},{7,5},{8,10},{9,11},{10,... | collective-permute-start | bytes 1572872 | tf_op jit(solution)/shard_map/ppermute | solution.py:336
  54.3 30.9 %collective-permute-start.13 = (bf16[1024,512]{1,0:T(8,128)(2,1)}, bf16[1024,512]{1,0:T(8,128)(2,1)}, u32[]{:S(2)}, u32[]{:S(2)}) collective-permute-start(bf16[1024,512]{1,0:T(8,128)(2,1)} %get-tuple-element.83), channel_id=1, source_target_pairs={{4,0},{5,1},{6,2},{7,3},{8,4},{9,5},{10,6},{11,7},{12,8},{13,9},{1... | collective-permute-start | bytes 3145736 | tf_op jit(solution)/shard_map/ppermute | solution.py:336
  55.8 25.9 %collective-permute-start.9 = (bf16[256,512]{1,0:T(8,128)(2,1)}, bf16[256,512]{1,0:T(8,128)(2,1)}, u32[]{:S(2)}, u32[]{:S(2)}) collective-permute-start(bf16[256,512]{1,0:T(8,128)(2,1)} %get-tuple-element.71), channel_id=1, source_target_pairs={{0,2},{1,3},{2,0},{3,1},{4,6},{5,7},{6,4},{7,5},{8,10},{9,11},{10,... | collective-permute-start | bytes 786440 | tf_op jit(solution)/shard_map/ppermute | solution.py:336
  58.9 22.8 %collective-permute-start.10 = (bf16[256,512]{1,0:T(8,128)(2,1)}, bf16[256,512]{1,0:T(8,128)(2,1)}, u32[]{:S(2)}, u32[]{:S(2)}) collective-permute-start(bf16[256,512]{1,0:T(8,128)(2,1)} %get-tuple-element.72), channel_id=1, source_target_pairs={{0,1},{1,0},{2,3},{3,2},{4,5},{5,4},{6,7},{7,6},{8,9},{9,8},{10,11... | collective-permute-start | bytes 786440 | tf_op jit(solution)/shard_map/ppermute | solution.py:336
  60.4 21.3 %collective-permute-start.11 = (bf16[256,512]{1,0:T(8,128)(2,1)}, bf16[256,512]{1,0:T(8,128)(2,1)}, u32[]{:S(2)}, u32[]{:S(2)}) collective-permute-start(bf16[256,512]{1,0:T(8,128)(2,1)} %get-tuple-element.73), channel_id=1, source_target_pairs={{0,3},{1,2},{2,1},{3,0},{4,7},{5,6},{6,5},{7,4},{8,11},{9,10},{10,... | collective-permute-start | bytes 786440 | tf_op jit(solution)/shard_map/ppermute | solution.py:336
  81.7 20.1 %collective-permute-start.17 = (bf16[512,1024]{1,0:T(8,128)(2,1)}, bf16[512,1024]{1,0:T(8,128)(2,1)}, u32[]{:S(2)}, u32[]{:S(2)}) collective-permute-start(bf16[512,1024]{1,0:T(8,128)(2,1)} %get-tuple-element.87), channel_id=1, source_target_pairs={{0,2},{1,3},{2,0},{3,1},{4,6},{5,7},{6,4},{7,5},{8,10},{9,11},{10,... | collective-permute-start | bytes 3145736 | tf_op jit(solution)/shard_map/ppermute | solution.py:336
  82.4 17.0 %collective-permute-start.18 = (bf16[512,512]{1,0:T(8,128)(2,1)}, bf16[512,512]{1,0:T(8,128)(2,1)}, u32[]{:S(2)}, u32[]{:S(2)}) collective-permute-start(bf16[512,512]{1,0:T(8,128)(2,1)} %get-tuple-element.93), channel_id=1, source_target_pairs={{4,0},{5,1},{6,2},{7,3},{8,4},{9,5},{10,6},{11,7},{12,8},{13,9},{1... | collective-permute-start | bytes 1572872 | tf_op jit(solution)/shard_map/ppermute | solution.py:336
  83.7 17.6 %collective-permute-start.15 = (bf16[256,512]{1,0:T(8,128)(2,1)}, bf16[256,512]{1,0:T(8,128)(2,1)}, u32[]{:S(2)}, u32[]{:S(2)}) collective-permute-start(bf16[256,512]{1,0:T(8,128)(2,1)} %get-tuple-element.85), channel_id=1, source_target_pairs={{0,1},{1,0},{2,3},{3,2},{4,5},{5,4},{6,7},{7,6},{8,9},{9,8},{10,11... | collective-permute-start | bytes 786440 | tf_op jit(solution)/shard_map/ppermute | solution.py:336
  85.2 16.5 %collective-permute-start.16 = (bf16[256,512]{1,0:T(8,128)(2,1)}, bf16[256,512]{1,0:T(8,128)(2,1)}, u32[]{:S(2)}, u32[]{:S(2)}) collective-permute-start(bf16[256,512]{1,0:T(8,128)(2,1)} %get-tuple-element.86), channel_id=1, source_target_pairs={{0,3},{1,2},{2,1},{3,0},{4,7},{5,6},{6,5},{7,4},{8,11},{9,10},{10,... | collective-permute-start | bytes 786440 | tf_op jit(solution)/shard_map/ppermute | solution.py:336
  85.2 24.0 %collective-permute-start.19 = (bf16[512,512]{1,0:T(8,128)(2,1)}, bf16[512,512]{1,0:T(8,128)(2,1)}, u32[]{:S(2)}, u32[]{:S(2)}) collective-permute-start(bf16[512,512]{1,0:T(8,128)(2,1)} %get-tuple-element.95), channel_id=1, source_target_pairs={{4,2},{5,3},{6,0},{7,1},{8,6},{9,7},{10,4},{11,5},{12,10},{13,11},... | collective-permute-start | bytes 1572872 | tf_op jit(solution)/shard_map/ppermute | solution.py:336
  99.4 2.4 %collective-permute-start.14 = (bf16[256,512]{1,0:T(8,128)(2,1)}, bf16[256,512]{1,0:T(8,128)(2,1)}, u32[]{:S(2)}, u32[]{:S(2)}) collective-permute-start(bf16[256,512]{1,0:T(8,128)(2,1)} %get-tuple-element.84), channel_id=1, source_target_pairs={{0,2},{1,3},{2,0},{3,1},{4,6},{5,7},{6,4},{7,5},{8,10},{9,11},{10,... | collective-permute-start | bytes 786440 | tf_op jit(solution)/shard_map/ppermute | solution.py:336
  101.2 4.5 %collective-permute-start.21 = (bf16[512,256]{1,0:T(8,128)(2,1)}, bf16[512,256]{1,0:T(8,128)(2,1)}, u32[]{:S(2)}, u32[]{:S(2)}) collective-permute-start(bf16[512,256]{1,0:T(8,128)(2,1)} %get-tuple-element.102), channel_id=1, source_target_pairs={{0,2},{1,3},{2,0},{3,1},{4,6},{5,7},{6,4},{7,5},{8,10},{9,11},{10,... | collective-permute-start | bytes 786440 | tf_op jit(solution)/shard_map/ppermute | solution.py:336
  101.7 4.0 %collective-permute-start.20 = (bf16[512,256]{1,0:T(8,128)(2,1)}, bf16[512,256]{1,0:T(8,128)(2,1)}, u32[]{:S(2)}, u32[]{:S(2)}) collective-permute-start(bf16[512,256]{1,0:T(8,128)(2,1)} %get-tuple-element.103), channel_id=1, source_target_pairs={{0,2},{1,3},{2,0},{3,1},{4,6},{5,7},{6,4},{7,5},{8,10},{9,11},{10,... | collective-permute-start | bytes 786440 | tf_op jit(solution)/shard_map/ppermute | solution.py:336

commit v8 on v7

--- a/solution.py
+++ b/solution.py
@@ -199,8 +199,8 @@
     for at in range(n_mp - 1):
         o_far[2 * at][...] = os[piece_at(0, at + 1), :]
         o_far[2 * at + 1][...] = os[piece_at(1, at + 1), :]
-    ats = (slice(0, 2 * rows),) if whole else (same, oth)
-    for out, at in ((dkv_same, same_kv), *zip(back, ats)):
+    back = (back[0].at[:rows], back[0].at[rows:]) if whole else back
+    for out, at in ((dkv_same, same_kv), (back[0], same), (back[1], oth)):
         out[:, :HEAD] = (dk[at, :] * ATTN_SCALE).astype(out.dtype)
         out[:, HEAD:] = dv[at, :].astype(out.dtype)
     across[:, pl.ds(wide + at_g, HEAD)] = (dk[oth_kv, :] * ATTN_SCALE).astype(across.dtype)
@@ -499,12 +499,12 @@
         if i < CHUNKS - 1:
             back, far_parts[-1][0] = lax.optimization_barrier((far_parts[i][0], far_parts[-1][0]))
             handed = [
-                send(lax.dynamic_slice(back, ((1 - core) * rows, g * pair), (rows, pair)), swap)
+                send(back[rows:, g * pair : (g + 1) * pair], swap)
                 for g in range(heads)
             ]
         for g in range(heads):
             last = i == CHUNKS - 1
-            terms += [(near_parts[i], False, g), (far_parts[i][0], not last, g)]
+            terms += [(near_parts[i], False, g), (far_parts[i][0], False, g)]
             terms += [(across_parts[i], False, heads + g)]
             terms += [(far_parts[i][1], False, g) if last else (handed[g], False, 0)]
         grads_kv = sum_terms(place, i, heads, heads_mp, terms, grads_kv, (attn_out,))

time: 113 us -> 113 us (level)
    dynamic_slice x1 -> x0, local copies, waits for them, and re-layouts: 1.85 us -> none  [body(): lax.dynamic_slice(back, ((1 - core) * rows, g * pair), (rows, pair))]
    slice x0 -> x1, local copies, waits for them, and re-layouts: none -> 1.85 us  [body(): back[rows:, g * pair:(g + 1) * pair]]
where the time goes in v8:
time: 113 us
  Pallas kernels  61.4 us (54%)
  starting transfers between devices  25.2 us (22%)
  waiting for transfers between devices  20.4 us (18%)
  local copies, waits for them, and re-layouts  2.63 us (2%)
  other arithmetic  2.25 us (2%)
    pallas_call x2, Pallas kernels, attention(): pl.pallas_call(functools.partial(attention_kernel, n_mp, rows, whole), gr...  42.4 us
    ppermute x22, starting transfers between devices, send(): return lax.ppermute(x, AXES, routes(target, n_ctx, n_mp))  25.2 us
    ppermute x22, waiting for transfers between devices, send(): return lax.ppermute(x, AXES, routes(target, n_ctx, n_mp))  20.4 us
    pallas_call x4, Pallas kernels, gather(): pl.pallas_call(functools.partial(gather_kernel, plan, len(arrays) + len(a...  12.1 us
    pallas_call x2, Pallas kernels, sum_terms(): pl.pallas_call(functools.partial(sum_kernel, heads), grid_spec=pltpu.Pref...  6.83 us
  transfers between devices with their start and end apart: 22, of which 3 were waited for; matrix products, arithmetic and copies ran while one was open for 4% of the time, Pallas kernels for 50%

profile of v8, /device:TPU:0, one launch (start us, length us, event | category | flops | bytes accessed | tf_op | source)
XLA Modules:
  0.0 112.7 jit_solution(13775419281621078776)
XLA Ops:
  0.6 0.0 copy-start
  0.6 2.1 %pack_halo.2 = (bf16[512,512]{1,0:T(8,128)(2,1)}, bf16[512,512]{1,0:T(8,128)(2,1)}) custom-call(bf16[512,1024]{1,0:T(8,128)(2,1)} %refs_1_.9, bf16[512,1024]{1,0:T(8,128)(2,1)} %refs_2_.5), custom_call_target="tpu_custom_call" | custom-call | flops 24999999488 | bytes 1024 | tf_op jit(solution)/shard_map/pack_halo/pallas_call | solution.py:71
  2.7 5.7 %collective-permute-start.4 = (bf16[512,512]{1,0:T(8,128)(2,1)}, bf16[512,512]{1,0:T(8,128)(2,1)}, u32[]{:S(2)}, u32[]{:S(2)}) collective-permute-start(bf16[512,512]{1,0:T(8,128)(2,1)} %get-tuple-element.53.refs_4_), channel_id=1, source_target_pairs={{0,4},{1,5},{2,6},{3,7},{4,8},{5,9},{6,10},{7,11},{8,12},{9,13},{1... | collective-permute-start | bytes 1572872 | tf_op jit(solution)/shard_map/ppermute | solution.py:336
  8.4 2.7 %collective-permute-start.5 = (bf16[512,512]{1,0:T(8,128)(2,1)}, bf16[512,512]{1,0:T(8,128)(2,1)}, u32[]{:S(2)}, u32[]{:S(2)}) collective-permute-start(bf16[512,512]{1,0:T(8,128)(2,1)} %get-tuple-element.54.refs_5_), channel_id=1, source_target_pairs={{0,6},{1,7},{2,4},{3,5},{4,10},{5,11},{6,8},{7,9},{8,14},{9,15},{1... | collective-permute-start | bytes 1572872 | tf_op jit(solution)/shard_map/ppermute | solution.py:336
  11.1 3.9 %pack_near.1 = (bf16[256,1024]{1,0:T(8,128)(2,1)}, bf16[256,1024]{1,0:T(8,128)(2,1)}, bf16[512,2560]{1,0:T(8,128)(2,1)}) custom-call(bf16[512,2048]{1,0:T(8,128)(2,1)} %refs_0_.9, bf16[512,1024]{1,0:T(8,128)(2,1)} %refs_1_.9, bf16[512,1024]{1,0:T(8,128)(2,1)} %refs_2_.5, bf16[256,4096]{1,0:T(8,128)(2,1)} %refs_10_.3, ...), custom_call_target="tpu_custom_call" | custom-call | flops 24999999488 | bytes 1024 | tf_op jit(solution)/shard_map/pack_near/pallas_call | solution.py:71
  15.0 1.6 %collective-permute-start = (bf16[256,1024]{1,0:T(8,128)(2,1)}, bf16[256,1024]{1,0:T(8,128)(2,1)}, u32[]{:S(2)}, u32[]{:S(2)}) collective-permute-start(bf16[256,1024]{1,0:T(8,128)(2,1)} %get-tuple-element.55), channel_id=1, source_target_pairs={{0,1},{1,0},{2,3},{3,2},{4,5},{5,4},{6,7},{7,6},{8,9},{9,8},{10,11... | collective-permute-start | bytes 1572872 | tf_op jit(solution)/shard_map/ppermute | solution.py:336
  16.5 0.0 copy-start.1
  16.5 0.7 collective-permute-start.1
  17.2 2.2 %pack_halo.3 = bf16[512,1024]{1,0:T(8,128)(2,1)} custom-call(bf16[512,1024]{1,0:T(8,128)(2,1)} %refs_1_.9, bf16[512,1024]{1,0:T(8,128)(2,1)} %refs_2_.5, bf16[512,2560]{1,0:T(8,128)(2,1)} %get-tuple-element.56.refs_2_), custom_call_target="tpu_custom_call" | custom-call | flops 24999999488 | bytes 1024 | tf_op jit(solution)/shard_map/pack_halo/pallas_call | solution.py:71
  19.4 3.6 %collective-permute-start.2 = (bf16[512,1024]{1,0:T(8,128)(2,1)}, bf16[512,1024]{1,0:T(8,128)(2,1)}, u32[]{:S(2)}, u32[]{:S(2)}) collective-permute-start(bf16[512,1024]{1,0:T(8,128)(2,1)} %pack_halo.3), channel_id=1, source_target_pairs={{0,4},{1,5},{2,6},{3,7},{4,8},{5,9},{6,10},{7,11},{8,12},{9,13},{1... | collective-permute-start | bytes 3145736 | tf_op jit(solution)/shard_map/ppermute | solution.py:336
  23.0 0.0 copy-done
  23.0 0.1 constant_dynamic-slice_fusion
  23.1 0.1 copy.13
  23.2 0.6 reshape.27.open_ref
  23.8 0.0 copy-done.1
  23.8 1.0 convert_reduce_fusion
  24.8 0.6 add_maximum_fusion.lo_ref
  25.4 4.8 %collective-permute-done.refs_12_ = bf16[256,1024]{1,0:T(8,128)(2,1)} collective-permute-done((bf16[256,1024]{1,0:T(8,128)(2,1)}, bf16[256,1024]{1,0:T(8,128)(2,1)}, u32[]{:S(2)}, u32[]{:S(2)}) %collective-permute-start) | collective-permute-done | bytes 524320 | tf_op jit(solution)/shard_map/ppermute | solution.py:336
  30.1 0.1 collective-permute-start.6
  30.2 0.0 collective-permute-done.4.refs_6_.refs_7_
  30.2 1.5 %collective-permute-start.3 = (bf16[256,1024]{1,0:T(8,128)(2,1)}, bf16[256,1024]{1,0:T(8,128)(2,1)}, u32[]{:S(2)}, u32[]{:S(2)}) collective-permute-start(bf16[256,1024]{1,0:T(8,128)(2,1)} %get-tuple-element.59), channel_id=1, source_target_pairs={{0,1},{1,0},{2,3},{3,2},{4,5},{5,4},{6,7},{7,6},{8,9},{9,8},{10,11... | collective-permute-start | bytes 1572872 | tf_op jit(solution)/shard_map/ppermute | solution.py:336
  31.7 0.7 pad_add_fusion.sc_ref
  32.4 0.0 collective-permute-done.5.refs_8_.refs_9_
  32.4 0.0 collective-permute-done.6.refs_13_
  32.4 0.0 collective-permute-done.1.refs_3_.refs_4_.refs_5_.refs_11_
  32.4 21.2 %attention.2 = (bf16[512,512]{1,0:T(8,128)(2,1)}, bf16[512,512]{1,0:T(8,128)(2,1)}, bf16[512,1024]{1,0:T(8,128)(2,1)}, bf16[256,512]{1,0:T(8,128)(2,1)}, bf16[25...) custom-call(s32[2]{0:T(128)} %pad_add_fusion.sc_ref, ...), custom_call_target="tpu_custom_call" | custom-call | bytes 1024 | tf_op jit(solution)/shard_map/attention/pallas_call | solution.py:257
  53.6 0.0 collective-permute-done.3.refs_12_
  53.6 0.0 collective-permute-done.2.refs_6_.refs_7_
  53.6 0.2 collective-permute-start.7
  53.8 0.4 collective-permute-start.12
  54.2 0.1 collective-permute-start.8
  54.3 1.5 %collective-permute-start.13 = (bf16[1024,512]{1,0:T(8,128)(2,1)}, bf16[1024,512]{1,0:T(8,128)(2,1)}, u32[]{:S(2)}, u32[]{:S(2)}) collective-permute-start(bf16[1024,512]{1,0:T(8,128)(2,1)} %get-tuple-element.83), channel_id=1, source_target_pairs={{4,0},{5,1},{6,2},{7,3},{8,4},{9,5},{10,6},{11,7},{12,8},{13,9},{1... | collective-permute-start | bytes 3145736 | tf_op jit(solution)/shard_map/ppermute | solution.py:336
  55.8 0.4 collective-permute-start.9
  56.2 2.7 %collective-permute-done.8.refs_13_ = bf16[256,1024]{1,0:T(8,128)(2,1)} collective-permute-done((bf16[256,1024]{1,0:T(8,128)(2,1)}, bf16[256,1024]{1,0:T(8,128)(2,1)}, u32[]{:S(2)}, u32[]{:S(2)}) %collective-permute-start.8) | collective-permute-done | bytes 524320 | tf_op jit(solution)/shard_map/ppermute | solution.py:336
  58.9 1.5 %collective-permute-start.10 = (bf16[256,512]{1,0:T(8,128)(2,1)}, bf16[256,512]{1,0:T(8,128)(2,1)}, u32[]{:S(2)}, u32[]{:S(2)}) collective-permute-start(bf16[256,512]{1,0:T(8,128)(2,1)} %get-tuple-element.72), channel_id=1, source_target_pairs={{0,1},{1,0},{2,3},{3,2},{4,5},{5,4},{6,7},{7,6},{8,9},{9,8},{10,11... | collective-permute-start | bytes 786440 | tf_op jit(solution)/shard_map/ppermute | solution.py:336
  60.4 0.0 collective-permute-done.7.refs_8_.refs_9_
  60.4 0.0 collective-permute-start.11
  60.4 21.2 %attention.3 = (bf16[512,512]{1,0:T(8,128)(2,1)}, bf16[512,512]{1,0:T(8,128)(2,1)}, bf16[512,1024]{1,0:T(8,128)(2,1)}, bf16[256,512]{1,0:T(8,128)(2,1)}, bf16[25...) custom-call(s32[2]{0:T(128)} %pad_add_fusion.sc_ref, ...), custom_call_target="tpu_custom_call" | custom-call | flops 4000000000 | bytes 1024 | tf_op jit(solution)/shard_map/attention/pallas_call | solution.py:257
  81.7 0.0 collective-permute-done.9.refs_1_
  81.7 0.0 collective-permute-done.10.refs_2_
  81.7 0.0 collective-permute-done.11.refs_3_
  81.7 0.0 collective-permute-done.12.refs_4_.refs_2_.refs_6_
  81.7 0.7 collective-permute-start.17
  82.4 1.3 %collective-permute-start.18 = (bf16[512,512]{1,0:T(8,128)(2,1)}, bf16[512,512]{1,0:T(8,128)(2,1)}, u32[]{:S(2)}, u32[]{:S(2)}) collective-permute-start(bf16[512,512]{1,0:T(8,128)(2,1)} %get-tuple-element.93), channel_id=1, source_target_pairs={{4,0},{5,1},{6,2},{7,3},{8,4},{9,5},{10,6},{11,7},{12,8},{13,9},{1... | collective-permute-start | bytes 1572872 | tf_op jit(solution)/shard_map/ppermute | solution.py:336
  83.7 1.5 %collective-permute-start.15 = (bf16[256,512]{1,0:T(8,128)(2,1)}, bf16[256,512]{1,0:T(8,128)(2,1)}, u32[]{:S(2)}, u32[]{:S(2)}) collective-permute-start(bf16[256,512]{1,0:T(8,128)(2,1)} %get-tuple-element.85), channel_id=1, source_target_pairs={{0,1},{1,0},{2,3},{3,2},{4,5},{5,4},{6,7},{7,6},{8,9},{9,8},{10,11... | collective-permute-start | bytes 786440 | tf_op jit(solution)/shard_map/ppermute | solution.py:336
  85.2 0.0 collective-permute-start.16
  85.2 0.0 collective-permute-done.13.refs_1_.refs_5_
  85.2 1.3 %collective-permute-start.19 = (bf16[512,512]{1,0:T(8,128)(2,1)}, bf16[512,512]{1,0:T(8,128)(2,1)}, u32[]{:S(2)}, u32[]{:S(2)}) collective-permute-start(bf16[512,512]{1,0:T(8,128)(2,1)} %get-tuple-element.95), channel_id=1, source_target_pairs={{4,2},{5,3},{6,0},{7,1},{8,6},{9,7},{10,4},{11,5},{12,10},{13,11},... | collective-permute-start | bytes 1572872 | tf_op jit(solution)/shard_map/ppermute | solution.py:336
  86.5 12.9 %collective-permute-done.18.refs_1_.refs_5_ = bf16[512,512]{1,0:T(8,128)(2,1)} collective-permute-done((bf16[512,512]{1,0:T(8,128)(2,1)}, bf16[512,512]{1,0:T(8,128)(2,1)}, u32[]{:S(2)}, u32[]{:S(2)}) %collective-permute-start.18) | collective-permute-done | bytes 524320 | tf_op jit(solution)/shard_map/ppermute | solution.py:336
  99.4 0.0 collective-permute-start.14
  99.4 1.9 %fusion = (bf16[512,256]{1,0:T(8,128)(2,1)}, bf16[512,256]{1,0:T(8,128)(2,1)}) fusion(bf16[1024,512]{1,0:T(8,128)(2,1)} %collective-permute-done.13.refs_1_.refs_5_), kind=kLoop, calls=%fused_computation.6 | loop fusion | bytes 1048576 | tf_op jit(solution)/shard_map/slice | solution.py:502
  101.3 0.0 collective-permute-done.15.refs_8_
  101.3 0.5 collective-permute-start.21
  101.8 0.0 collective-permute-done.16.refs_9_
  101.8 0.1 collective-permute-start.20
  101.8 0.0 collective-permute-done.14.refs_7_
  101.8 0.0 collective-permute-done.17.refs_10_.refs_2_.refs_6_
  101.8 3.9 %put_together.1 = (bf16[256,4096]{1,0:T(8,128)(2,1)}, bf16[512,2048]{1,0:T(8,128)(2,1)}) custom-call(bf16[256,512]{1,0:T(8,128)(2,1)} %get-tuple-element.75.refs_0_, bf16[256,512]{1,0:T(8,128)(2,1)} %collective-permute-done.9.refs_1_, bf16[256,512]{1,0:T(8,128)(2,1)} %collective-permute-done.10.refs_2_, bf16[256,512]{1,0:T(8,128)(2,1)} %collective-permute-done.11.refs_3_, ...), custom_call_target="tpu_custom_call" | custom-call | bytes 1024 | tf_op jit(solution)/shard_map/put_together/pallas_call | solution.py:71
  105.8 0.0 collective-permute-done.21.refs_7_
  105.8 0.0 collective-permute-done.20.refs_3_
  105.8 3.4 %sum_terms.2 = (bf16[512,1024]{1,0:T(8,128)(2,1)}, bf16[512,1024]{1,0:T(8,128)(2,1)}) custom-call(s32[2]{0:T(128)} %pad_add_fusion.sc_ref, bf16[512,512]{1,0:T(8,128)(2,1)} %get-tuple-element.96.refs_0_.refs_4_, bf16[1024,512]{1,0:T(8,128)(2,1)} %collective-permute-done.13.refs_1_.refs_5_, bf16[512,1024]{1,0:T(8,128)(2,1)} %collective-permute-done.12.refs_4_.refs_2_.refs_6_, ...), custom_call_target="tpu_custom_call" | custom-call | bytes 1024 | tf_op jit(solution)/shard_map/sum_terms/pallas_call | solution.py:306
  109.2 0.0 collective-permute-done.19.refs_3_.refs_7_
  109.2 3.4 %sum_terms.3 = (bf16[512,1024]{1,0:T(8,128)(2,1)}, bf16[512,1024]{1,0:T(8,128)(2,1)}) custom-call(s32[2]{0:T(128)} %pad_add_fusion.sc_ref, bf16[512,512]{1,0:T(8,128)(2,1)} %get-tuple-element.91.refs_0_.refs_4_, bf16[512,512]{1,0:T(8,128)(2,1)} %collective-permute-done.18.refs_1_.refs_5_, ...), custom_call_target="tpu_custom_call", output_to_operand_aliasing={{0}: (9, {}), {1}: (10, {})} | custom-call | bytes 1024 | tf_op jit(solution)/shard_map/sum_terms/pallas_call | solution.py:306
  (2 shorter events, 0.0 us)
Async XLA Ops:
  0.6 22.4 %copy-start = (s32[64,9]{0,1:T(8,128)S(1)}, s32[64,9]{0,1:T(8,128)}, u32[]{:S(2)}) copy-start(s32[64,9]{0,1:T(8,128)} %param.10) | copy-start | bytes 6916
  2.7 27.5 %collective-permute-start.4 = (bf16[512,512]{1,0:T(8,128)(2,1)}, bf16[512,512]{1,0:T(8,128)(2,1)}, u32[]{:S(2)}, u32[]{:S(2)}) collective-permute-start(bf16[512,512]{1,0:T(8,128)(2,1)} %get-tuple-element.53.refs_4_), channel_id=1, source_target_pairs={{0,4},{1,5},{2,6},{3,7},{4,8},{5,9},{6,10},{7,11},{8,12},{9,13},{1... | collective-permute-start | bytes 1572872 | tf_op jit(solution)/shard_map/ppermute | solution.py:336
  8.4 24.0 %collective-permute-start.5 = (bf16[512,512]{1,0:T(8,128)(2,1)}, bf16[512,512]{1,0:T(8,128)(2,1)}, u32[]{:S(2)}, u32[]{:S(2)}) collective-permute-start(bf16[512,512]{1,0:T(8,128)(2,1)} %get-tuple-element.54.refs_5_), channel_id=1, source_target_pairs={{0,6},{1,7},{2,4},{3,5},{4,10},{5,11},{6,8},{7,9},{8,14},{9,15},{1... | collective-permute-start | bytes 1572872 | tf_op jit(solution)/shard_map/ppermute | solution.py:336
  15.0 15.2 %collective-permute-start = (bf16[256,1024]{1,0:T(8,128)(2,1)}, bf16[256,1024]{1,0:T(8,128)(2,1)}, u32[]{:S(2)}, u32[]{:S(2)}) collective-permute-start(bf16[256,1024]{1,0:T(8,128)(2,1)} %get-tuple-element.55), channel_id=1, source_target_pairs={{0,1},{1,0},{2,3},{3,2},{4,5},{5,4},{6,7},{7,6},{8,9},{9,8},{10,11... | collective-permute-start | bytes 1572872 | tf_op jit(solution)/shard_map/ppermute | solution.py:336
  16.5 7.2 %copy-start.1 = (s32[8192]{0:T(1024)S(1)}, s32[8192]{0:T(1024)}, u32[]{:S(2)}) copy-start(s32[8192]{0:T(1024)} %param.11) | copy-start | bytes 98308
  16.5 15.9 %collective-permute-start.1 = (bf16[512,2560]{1,0:T(8,128)(2,1)}, bf16[512,2560]{1,0:T(8,128)(2,1)}, u32[]{:S(2)}, u32[]{:S(2)}) collective-permute-start(bf16[512,2560]{1,0:T(8,128)(2,1)} %get-tuple-element.56.refs_2_), channel_id=1, source_target_pairs={{0,2},{1,3},{2,0},{3,1},{4,6},{5,7},{6,4},{7,5},{8,10},{9,11},{10,... | collective-permute-start | bytes 7864328 | tf_op jit(solution)/shard_map/ppermute | solution.py:336
  19.4 34.2 %collective-permute-start.2 = (bf16[512,1024]{1,0:T(8,128)(2,1)}, bf16[512,1024]{1,0:T(8,128)(2,1)}, u32[]{:S(2)}, u32[]{:S(2)}) collective-permute-start(bf16[512,1024]{1,0:T(8,128)(2,1)} %pack_halo.3), channel_id=1, source_target_pairs={{0,4},{1,5},{2,6},{3,7},{4,8},{5,9},{6,10},{7,11},{8,12},{9,13},{1... | collective-permute-start | bytes 3145736 | tf_op jit(solution)/shard_map/ppermute | solution.py:336
  30.1 2.3 %collective-permute-start.6 = (bf16[256,1024]{1,0:T(8,128)(2,1)}, bf16[256,1024]{1,0:T(8,128)(2,1)}, u32[]{:S(2)}, u32[]{:S(2)}) collective-permute-start(bf16[256,1024]{1,0:T(8,128)(2,1)} %collective-permute-done.refs_12_), channel_id=1, source_target_pairs={{0,2},{1,3},{2,0},{3,1},{4,6},{5,7},{6,4},{7,5},{8,10},{9,11},{10,... | collective-permute-start | bytes 1572872 | tf_op jit(solution)/shard_map/ppermute | solution.py:336
  30.2 23.3 %collective-permute-start.3 = (bf16[256,1024]{1,0:T(8,128)(2,1)}, bf16[256,1024]{1,0:T(8,128)(2,1)}, u32[]{:S(2)}, u32[]{:S(2)}) collective-permute-start(bf16[256,1024]{1,0:T(8,128)(2,1)} %get-tuple-element.59), channel_id=1, source_target_pairs={{0,1},{1,0},{2,3},{3,2},{4,5},{5,4},{6,7},{7,6},{8,9},{9,8},{10,11... | collective-permute-start | bytes 1572872 | tf_op jit(solution)/shard_map/ppermute | solution.py:336
  53.6 6.8 %collective-permute-start.7 = (bf16[512,1024]{1,0:T(8,128)(2,1)}, bf16[512,1024]{1,0:T(8,128)(2,1)}, u32[]{:S(2)}, u32[]{:S(2)}) collective-permute-start(bf16[512,1024]{1,0:T(8,128)(2,1)} %collective-permute-done.2.refs_6_.refs_7_), channel_id=1, source_target_pairs={{0,2},{1,3},{2,0},{3,1},{4,6},{5,7},{6,4},{7,5},{8,10},{9,11},{10,... | collective-permute-start | bytes 3145736 | tf_op jit(solution)/shard_map/ppermute | solution.py:336
  53.8 27.9 %collective-permute-start.12 = (bf16[512,1024]{1,0:T(8,128)(2,1)}, bf16[512,1024]{1,0:T(8,128)(2,1)}, u32[]{:S(2)}, u32[]{:S(2)}) collective-permute-start(bf16[512,1024]{1,0:T(8,128)(2,1)} %get-tuple-element.74), channel_id=1, source_target_pairs={{0,2},{1,3},{2,0},{3,1},{4,6},{5,7},{6,4},{7,5},{8,10},{9,11},{10,... | collective-permute-start | bytes 3145736 | tf_op jit(solution)/shard_map/ppermute | solution.py:336
  54.2 4.7 %collective-permute-start.8 = (bf16[256,1024]{1,0:T(8,128)(2,1)}, bf16[256,1024]{1,0:T(8,128)(2,1)}, u32[]{:S(2)}, u32[]{:S(2)}) collective-permute-start(bf16[256,1024]{1,0:T(8,128)(2,1)} %collective-permute-done.3.refs_12_), channel_id=1, source_target_pairs={{0,2},{1,3},{2,0},{3,1},{4,6},{5,7},{6,4},{7,5},{8,10},{9,11},{10,... | collective-permute-start | bytes 1572872 | tf_op jit(solution)/shard_map/ppermute | solution.py:336
  54.3 30.9 %collective-permute-start.13 = (bf16[1024,512]{1,0:T(8,128)(2,1)}, bf16[1024,512]{1,0:T(8,128)(2,1)}, u32[]{:S(2)}, u32[]{:S(2)}) collective-permute-start(bf16[1024,512]{1,0:T(8,128)(2,1)} %get-tuple-element.83), channel_id=1, source_target_pairs={{4,0},{5,1},{6,2},{7,3},{8,4},{9,5},{10,6},{11,7},{12,8},{13,9},{1... | collective-permute-start | bytes 3145736 | tf_op jit(solution)/shard_map/ppermute | solution.py:336
  55.8 25.9 %collective-permute-start.9 = (bf16[256,512]{1,0:T(8,128)(2,1)}, bf16[256,512]{1,0:T(8,128)(2,1)}, u32[]{:S(2)}, u32[]{:S(2)}) collective-permute-start(bf16[256,512]{1,0:T(8,128)(2,1)} %get-tuple-element.71), channel_id=1, source_target_pairs={{0,2},{1,3},{2,0},{3,1},{4,6},{5,7},{6,4},{7,5},{8,10},{9,11},{10,... | collective-permute-start | bytes 786440 | tf_op jit(solution)/shard_map/ppermute | solution.py:336
  58.9 22.8 %collective-permute-start.10 = (bf16[256,512]{1,0:T(8,128)(2,1)}, bf16[256,512]{1,0:T(8,128)(2,1)}, u32[]{:S(2)}, u32[]{:S(2)}) collective-permute-start(bf16[256,512]{1,0:T(8,128)(2,1)} %get-tuple-element.72), channel_id=1, source_target_pairs={{0,1},{1,0},{2,3},{3,2},{4,5},{5,4},{6,7},{7,6},{8,9},{9,8},{10,11... | collective-permute-start | bytes 786440 | tf_op jit(solution)/shard_map/ppermute | solution.py:336
  60.4 21.3 %collective-permute-start.11 = (bf16[256,512]{1,0:T(8,128)(2,1)}, bf16[256,512]{1,0:T(8,128)(2,1)}, u32[]{:S(2)}, u32[]{:S(2)}) collective-permute-start(bf16[256,512]{1,0:T(8,128)(2,1)} %get-tuple-element.73), channel_id=1, source_target_pairs={{0,3},{1,2},{2,1},{3,0},{4,7},{5,6},{6,5},{7,4},{8,11},{9,10},{10,... | collective-permute-start | bytes 786440 | tf_op jit(solution)/shard_map/ppermute | solution.py:336
  81.7 20.1 %collective-permute-start.17 = (bf16[512,1024]{1,0:T(8,128)(2,1)}, bf16[512,1024]{1,0:T(8,128)(2,1)}, u32[]{:S(2)}, u32[]{:S(2)}) collective-permute-start(bf16[512,1024]{1,0:T(8,128)(2,1)} %get-tuple-element.87), channel_id=1, source_target_pairs={{0,2},{1,3},{2,0},{3,1},{4,6},{5,7},{6,4},{7,5},{8,10},{9,11},{10,... | collective-permute-start | bytes 3145736 | tf_op jit(solution)/shard_map/ppermute | solution.py:336
  82.4 17.0 %collective-permute-start.18 = (bf16[512,512]{1,0:T(8,128)(2,1)}, bf16[512,512]{1,0:T(8,128)(2,1)}, u32[]{:S(2)}, u32[]{:S(2)}) collective-permute-start(bf16[512,512]{1,0:T(8,128)(2,1)} %get-tuple-element.93), channel_id=1, source_target_pairs={{4,0},{5,1},{6,2},{7,3},{8,4},{9,5},{10,6},{11,7},{12,8},{13,9},{1... | collective-permute-start | bytes 1572872 | tf_op jit(solution)/shard_map/ppermute | solution.py:336
  83.7 17.6 %collective-permute-start.15 = (bf16[256,512]{1,0:T(8,128)(2,1)}, bf16[256,512]{1,0:T(8,128)(2,1)}, u32[]{:S(2)}, u32[]{:S(2)}) collective-permute-start(bf16[256,512]{1,0:T(8,128)(2,1)} %get-tuple-element.85), channel_id=1, source_target_pairs={{0,1},{1,0},{2,3},{3,2},{4,5},{5,4},{6,7},{7,6},{8,9},{9,8},{10,11... | collective-permute-start | bytes 786440 | tf_op jit(solution)/shard_map/ppermute | solution.py:336
  85.2 16.5 %collective-permute-start.16 = (bf16[256,512]{1,0:T(8,128)(2,1)}, bf16[256,512]{1,0:T(8,128)(2,1)}, u32[]{:S(2)}, u32[]{:S(2)}) collective-permute-start(bf16[256,512]{1,0:T(8,128)(2,1)} %get-tuple-element.86), channel_id=1, source_target_pairs={{0,3},{1,2},{2,1},{3,0},{4,7},{5,6},{6,5},{7,4},{8,11},{9,10},{10,... | collective-permute-start | bytes 786440 | tf_op jit(solution)/shard_map/ppermute | solution.py:336
  85.2 24.0 %collective-permute-start.19 = (bf16[512,512]{1,0:T(8,128)(2,1)}, bf16[512,512]{1,0:T(8,128)(2,1)}, u32[]{:S(2)}, u32[]{:S(2)}) collective-permute-start(bf16[512,512]{1,0:T(8,128)(2,1)} %get-tuple-element.95), channel_id=1, source_target_pairs={{4,2},{5,3},{6,0},{7,1},{8,6},{9,7},{10,4},{11,5},{12,10},{13,11},... | collective-permute-start | bytes 1572872 | tf_op jit(solution)/shard_map/ppermute | solution.py:336
  99.4 2.4 %collective-permute-start.14 = (bf16[256,512]{1,0:T(8,128)(2,1)}, bf16[256,512]{1,0:T(8,128)(2,1)}, u32[]{:S(2)}, u32[]{:S(2)}) collective-permute-start(bf16[256,512]{1,0:T(8,128)(2,1)} %get-tuple-element.84), channel_id=1, source_target_pairs={{0,2},{1,3},{2,0},{3,1},{4,6},{5,7},{6,4},{7,5},{8,10},{9,11},{10,... | collective-permute-start | bytes 786440 | tf_op jit(solution)/shard_map/ppermute | solution.py:336
  101.3 4.5 %collective-permute-start.21 = (bf16[512,256]{1,0:T(8,128)(2,1)}, bf16[512,256]{1,0:T(8,128)(2,1)}, u32[]{:S(2)}, u32[]{:S(2)}) collective-permute-start(bf16[512,256]{1,0:T(8,128)(2,1)} %get-tuple-element.102), channel_id=1, source_target_pairs={{0,2},{1,3},{2,0},{3,1},{4,6},{5,7},{6,4},{7,5},{8,10},{9,11},{10,... | collective-permute-start | bytes 786440 | tf_op jit(solution)/shard_map/ppermute | solution.py:336
  101.8 4.0 %collective-permute-start.20 = (bf16[512,256]{1,0:T(8,128)(2,1)}, bf16[512,256]{1,0:T(8,128)(2,1)}, u32[]{:S(2)}, u32[]{:S(2)}) collective-permute-start(bf16[512,256]{1,0:T(8,128)(2,1)} %get-tuple-element.103), channel_id=1, source_target_pairs={{0,2},{1,3},{2,0},{3,1},{4,6},{5,7},{6,4},{7,5},{8,10},{9,11},{10,... | collective-permute-start | bytes 786440 | tf_op jit(solution)/shard_map/ppermute | solution.py:336
